TPU v7x, 32 devices: a whole 2x2x4 slice. The times are simulated.
32 devices in a mesh: grp: 2 (over y), az: 4 (over z), el: 2 (over x), fq: 2 (over core).
Axes of the slice: x: 2, y: 2, z: 4, core: 2. Of those that a mesh axis runs over, the one named last changes fastest.
Arguments:
- polar: bfloat16 [2, 64, 1024, 768], P(None, ('grp', 'el'), 'az', 'fq'), parts along dimension 1, may hold values from -6 to 6
- band_offset: int32 [1024, 768], P('az', 'fq'), may hold values from -8 to 5, as said below
- tap_count: int32 [1024, 768], P('az', 'fq'), may hold values from 4 to 8
- tap_weight: bfloat16 [8, 1024, 768], P(None, 'az', 'fq'), may hold values from -2.390625 to 2.390625
Outputs:
- image_out: bfloat16 [2, 64, 768, 1024], P(None, ('grp', 'el'), ('az', 'fq')), parts along dimension 1
There are 2 independent parts, one for each index of `grp`. A program takes and returns all parts, laid end to end along the dimension named above; an argument that names none is the same for every part. Nothing has to cross between parts.
Inputs may be any that keep to these rules, and one draw needn't show every extreme that they name: band_offset[j, f] lies between -8 and 9 - tap_count[j, f], so a band reads azimuths j - 8 to j + 8; both ends are reached.
All inputs are finite; a program needn't handle non-finite values.
Results may differ from a plain program's by a relative error of at most 0.0074.
Values may be sent and summed in bfloat16 or wider, within the bound.
No kernel may reach another device: no remote copies, remote signals or barrier semaphores. Data moves between devices by JAX's collectives and lax.ppermute only.
A program may use at most 128 MiB of HBM per device.

v0:
```python
import math

import jax
import jax.numpy as jnp
from jax import lax
from jax.sharding import PartitionSpec as P

F = 768
A = 1024
E = 32
HW = 8
KT = 8


def with_halo(cells, sides, width):
    for axis, dim in sides:
        count = lax.axis_size(axis)
        ends = count - 1
        head = lax.slice_in_dim(cells, 0, width, axis=dim)
        tail = lax.slice_in_dim(cells, cells.shape[dim] - width, cells.shape[dim], axis=dim)
        cells = jnp.concatenate(
            [
                lax.ppermute(tail, axis, [(i, (i + 1) % count) for i in range(ends)]),
                cells,
                lax.ppermute(head, axis, [((i + 1) % count, i) for i in range(ends)]),
            ],
            axis=dim,
        )
    return cells


def table_pair(row_ids, col_ids, length):
    product = row_ids[:, None] * col_ids[None, :] % length
    angle = product.astype(jnp.float32) * (2.0 * math.pi / length)
    return (jnp.cos(angle).astype(jnp.bfloat16), jnp.sin(angle).astype(jnp.bfloat16))


def on_device(polar, band_offset, tap_count, tap_weight):
    shape_all = polar.shape
    col_count = shape_all[2]
    freq_count = shape_all[3]
    az_count = lax.axis_size("az")
    fq_count = lax.axis_size("fq")
    el_count = lax.axis_size("el")
    padded = with_halo(polar, (("az", 2),), HW)
    window = col_count + 2 * HW
    column = jnp.arange(col_count, dtype=jnp.int32)[:, None]
    position = jnp.arange(window, dtype=jnp.int32)[None, :, None]
    band_matrix = jnp.zeros((col_count, window, freq_count), jnp.bfloat16)
    for tap_index in range(KT):
        reach = column + HW + band_offset + tap_index
        matches = (position == reach[:, None, :]) & (tap_index < tap_count)[:, None, :]
        band_matrix = jnp.where(matches, tap_weight[tap_index][:, None, :], band_matrix)
    interpolated = jnp.einsum(
        "jaf,ceaf->cejf", band_matrix, padded, preferred_element_type=jnp.float32
    ).astype(jnp.bfloat16)
    fq_index = lax.axis_index("fq")
    bin_count = F // (fq_count * az_count)
    az_block = jnp.arange(az_count, dtype=jnp.int32)[:, None]
    bin_local = jnp.arange(bin_count, dtype=jnp.int32)[None, :]
    range_bins = ((az_block * fq_count + fq_index) * bin_count + bin_local).reshape(-1)
    cos_f, sin_f = table_pair(jnp.arange(F, dtype=jnp.int32), range_bins, F)
    shard_piece = lax.all_gather(interpolated, "fq", axis=3, tiled=True)
    cos_rows = cos_f
    sin_rows = sin_f
    real_part = jnp.einsum(
        "ejf,fk->ekj", shard_piece[0], cos_rows, preferred_element_type=jnp.float32
    ) - jnp.einsum("ejf,fk->ekj", shard_piece[1], sin_rows, preferred_element_type=jnp.float32)
    imag_part = jnp.einsum(
        "ejf,fk->ekj", shard_piece[0], sin_rows, preferred_element_type=jnp.float32
    ) + jnp.einsum("ejf,fk->ekj", shard_piece[1], cos_rows, preferred_element_type=jnp.float32)
    summed = jnp.stack([real_part, imag_part])
    ranged = (summed * (1.0 / math.sqrt(F))).astype(jnp.bfloat16)
    azim_ids = jnp.arange(A, dtype=jnp.int32)
    cos_a, sin_a = table_pair(azim_ids, azim_ids, A)
    block_data = lax.all_to_all(ranged, "az", split_axis=2, concat_axis=3, tiled=True)
    real_part = jnp.einsum(
        "ekj,jm->ekm", block_data[0], cos_a, preferred_element_type=jnp.float32
    ) - jnp.einsum("ekj,jm->ekm", block_data[1], sin_a, preferred_element_type=jnp.float32)
    imag_part = jnp.einsum(
        "ekj,jm->ekm", block_data[0], sin_a, preferred_element_type=jnp.float32
    ) + jnp.einsum("ekj,jm->ekm", block_data[1], cos_a, preferred_element_type=jnp.float32)
    crossed = (jnp.stack([real_part, imag_part]) * (1.0 / math.sqrt(A))).astype(jnp.bfloat16)
    elev_ids = jnp.arange(E, dtype=jnp.int32)
    el_index = lax.axis_index("el")
    height_count = E // el_count
    height_rows = el_index * height_count + jnp.arange(height_count, dtype=jnp.int32)
    cos_e, sin_e = table_pair(elev_ids, height_rows, E)
    shard_piece = lax.all_gather(crossed, "el", axis=1, tiled=True)
    cos_rows = cos_e
    sin_rows = sin_e
    real_part = jnp.einsum(
        "eh,ekm->hkm", cos_rows, shard_piece[0], preferred_element_type=jnp.float32
    ) - jnp.einsum("eh,ekm->hkm", sin_rows, shard_piece[1], preferred_element_type=jnp.float32)
    imag_part = jnp.einsum(
        "eh,ekm->hkm", sin_rows, shard_piece[0], preferred_element_type=jnp.float32
    ) + jnp.einsum("eh,ekm->hkm", cos_rows, shard_piece[1], preferred_element_type=jnp.float32)
    totals = jnp.stack([real_part, imag_part])
    image_out = (totals * (1.0 / math.sqrt(E))).astype(jnp.bfloat16)
    return image_out


def solution(mesh):
    in_specs = (
        P(None, ("grp", "el"), "az", "fq"),
        P("az", "fq"),
        P("az", "fq"),
        P(None, "az", "fq"),
    )
    out_specs = P(None, ("grp", "el"), ("az", "fq"), None)
    return jax.shard_map(
        on_device, mesh=mesh, in_specs=in_specs, out_specs=out_specs, check_vma=False
    )
```

profile of v0, /device:TPU:0, one launch (start us, length us, event | category | flops | bytes accessed | tf_op | source)
XLA Modules:
  0.0 831.5 jit_solution(13408476565091446861)
XLA Ops:
  6.5 1.8 fusion.157
  8.3 1.3 collective-permute-start.1
  9.6 6.2 collective-permute-start
  15.9 1.1 broadcast_add_fusion.6
  17.0 0.9 copy.67
  17.9 1.0 broadcast_add_fusion.5
  18.9 8.9 %copy.44 = bf16[2,16,256,384]{2,1,0,3:T(8,128)(2,1)} copy(bf16[2,16,256,384]{3,2,1,0:T(8,128)(2,1)} %param.4) | data formatting | bytes 12582912 | tf_op args[0]
  27.9 2.0 copy.64
  29.9 1.9 copy.61
  31.8 0.9 copy.58
  32.9 0.9 copy.52
  33.8 0.9 copy.49
  34.8 0.9 copy.46
  35.7 1.5 broadcast_compare_fusion.7
  49.6 0.8 copy.48
  50.4 5.2 copy.45
  55.6 5.8 copy.43
  61.6 8.3 %fusion.168 = bf16[2,16,272,384]{2,1,0,3:T(8,128)(2,1)S(1)} fusion(bf16[2,16,8,384]{2,1,0,3:T(8,128)(2,1)S(1)} %copy.45, bf16[2,16,256,384]{2,1,0,3:T(8,128)(2,1)} %copy.44, bf16[2,16,8,384]{2,1,0,3:T(8,128)(2,1)} %copy.43), kind=kLoop, calls=%fused_computation.49.clone.clone.clone.2 | loop fusion | flops 20054016 | bytes 13369344 | tf_op jit(solution)/shard_map/jaf,ceaf->cejf/dot_general | solution.py:54
  70.2 193.7 %convert_bitcast_fusion = bf16[2,16,256,384]{2,1,0,3:T(8,128)(2,1)} fusion(s32[256,384]{0,1:T(8,128)S(1)} %copy-done.6, s32[256,384]{0,1:T(8,128)S(1)} %copy-done.7, s32[256,384]{0,1:T(8,128)S(1)} %copy-done.8, s32[256,384]{0,1:T(8,128)S(1)} %copy-done.9, s32[256,384]{0,1:T(8,128)S(1)} %copy.55, s32[256,384]{0,1:T(8,128)S(1)} %copy-done.10, ...), kind=kOutput, calls=%fused_computation.74 | convolution fusion | flops 2356150272 | bytes 18481152 | tf_op jit(solution)/shard_map/jaf,ceaf->cejf/dot_general | solution.py:54
  264.3 25.3 %all-gather.3.cloned.1.call-done = bf16[2,16,256,768]{2,1,0,3:T(8,128)(2,1)} async-done(((bf16[2,16,256,384]{2,1,0,3:T(8,128)(2,1)}), bf16[2,16,256,768]{2,1,0,3:T(8,128)(2,1)}) %all-gather.3.cloned.1.call-update) | async-done | bytes 12582928 | tf_op jit(solution)/shard_map/all_gather | solution.py:63
  289.6 10.3 %fusion.155 = (bf16[1,16,256,768]{2,1,0,3:T(8,128)(2,1)}, bf16[1,16,256,768]{2,1,0,3:T(8,128)(2,1)}) fusion(bf16[2,16,256,768]{2,1,0,3:T(8,128)(2,1)} %all-gather.3.cloned.1.call-done), kind=kLoop, calls=%fused_computation.193 | loop fusion | bytes 25165824 | tf_op jit(solution)/shard_map/slice | solution.py:67
  299.9 9.2 %copy.81 = bf16[1,16,256,768]{3,2,1,0:T(8,128)(2,1)} copy(bf16[1,16,256,768]{2,1,0,3:T(8,128)(2,1)} %get-tuple-element.10) | data formatting | bytes 12582912
  309.1 13.1 %fusion.44 = f32[384,16,256]{2,0,1:T(8,128)} fusion(bf16[1,16,256,768]{3,2,1,0:T(8,128)(2,1)} %copy.81, s32[384]{0:T(512)S(1)} %add.157), kind=kOutput, calls=%fused_computation.56 | convolution fusion | flops 2418868224 | bytes 12584448 | tf_op jit(solution)/shard_map/ejf,fk->ekj/dot_general | solution.py:71
  322.3 11.9 %fusion.46 = f32[384,16,256]{2,0,1:T(8,128)} fusion(bf16[1,16,256,768]{3,2,1,0:T(8,128)(2,1)S(1)} %copy-done.2, s32[384]{0:T(512)S(1)} %add.157), kind=kOutput, calls=%fused_computation.58 | convolution fusion | flops 2418868224 | bytes 12584448 | tf_op jit(solution)/shard_map/ejf,fk->ekj/dot_general | solution.py:68
  334.2 9.0 %copy.80 = bf16[1,16,256,768]{3,2,1,0:T(8,128)(2,1)} copy(bf16[1,16,256,768]{2,1,0,3:T(8,128)(2,1)} %get-tuple-element.9) | data formatting | bytes 12582912
  343.2 13.0 %add_bitcast_fusion.2 = f32[1,16,384,256]{3,2,1,0:T(8,128)S(1)} fusion(f32[384,16,256]{2,0,1:T(8,128)} %fusion.44, bf16[1,16,256,768]{3,2,1,0:T(8,128)(2,1)} %copy.80, s32[384]{0:T(512)S(1)} %add.157), kind=kOutput, calls=%fused_computation.72 | convolution fusion | flops 2420441088 | bytes 18875904 | tf_op jit(solution)/shard_map/ejf,fk->ekj/dot_general | solution.py:69
  356.2 12.6 %subtract_bitcast_fusion.2 = f32[1,16,384,256]{3,2,1,0:T(8,128)S(1)} fusion(f32[384,16,256]{2,0,1:T(8,128)} %fusion.46, bf16[1,16,256,768]{3,2,1,0:T(8,128)(2,1)S(1)} %copy-done, s32[384]{0:T(512)S(1)} %add.157), kind=kOutput, calls=%fused_computation.73 | convolution fusion | flops 2420441088 | bytes 18875904 | tf_op jit(solution)/shard_map/ejf,fk->ekj/dot_general | solution.py:66
  368.8 3.9 fusion.36
  372.7 6.3 copy.72
  379.1 143.5 %all_to_all.15 = bf16[2,16,384,256]{3,1,0,2:T(8,128)(2,1)} all-to-all(bf16[2,16,384,256]{3,1,0,2:T(8,128)(2,1)S(1)} %copy.72), channel_id=1, replica_groups=mesh['grp'=2,'az'=4,'el'=2,'fq'=2] {'az'}, dimensions={2} | all-to-all | bytes 12582912 | tf_op jit(solution)/shard_map/all_to_all | solution.py:76
  522.6 7.6 copy.95
  530.2 4.3 fusion.156
  534.5 4.7 squeeze.26
  539.2 1.7 copy-done.4
  540.9 19.0 %fusion.80 = f32[16,96,1024]{2,1,0:T(8,128)} fusion(bf16[16,96,1024]{2,1,0:T(8,128)(2,1)S(1)} %squeeze.26), kind=kOutput, calls=%fused_computation.93 | convolution fusion | flops 3236954112 | bytes 9437184 | tf_op jit(solution)/shard_map/ekj,jm->ekm/dot_general | solution.py:80
  559.9 21.5 %fusion.84 = f32[16,96,1024]{2,1,0:T(8,128)} fusion(bf16[16,96,1024]{2,1,0:T(8,128)(2,1)} %copy-done.4), kind=kOutput, calls=%fused_computation.94 | convolution fusion | flops 3236954112 | bytes 9437184 | tf_op jit(solution)/shard_map/ekj,jm->ekm/dot_general | solution.py:77
  581.4 3.9 squeeze.27
  585.3 22.2 %add_bitcast_fusion.1 = f32[1,16,96,1024]{3,2,1,0:T(8,128)S(1)} fusion(f32[16,96,1024]{2,1,0:T(8,128)} %fusion.80, bf16[16,96,1024]{2,1,0:T(8,128)(2,1)} %squeeze.27), kind=kOutput, calls=%fused_computation.67 | convolution fusion | flops 3238526976 | bytes 15728640 | tf_op jit(solution)/shard_map/ekj,jm->ekm/dot_general | solution.py:82
  607.6 19.7 %subtract_bitcast_fusion.1 = f32[1,16,96,1024]{3,2,1,0:T(8,128)S(1)} fusion(f32[16,96,1024]{2,1,0:T(8,128)S(1)} %copy-done.29, bf16[16,96,1024]{2,1,0:T(8,128)(2,1)S(1)} %copy-done.3), kind=kOutput, calls=%fused_computation.68 | convolution fusion | flops 3238526976 | bytes 15728640 | tf_op jit(solution)/shard_map/ekj,jm->ekm/dot_general | solution.py:79
  627.3 3.8 fusion.37
  631.2 150.7 %all-gather.5.cloned.1.call-done = bf16[2,32,96,1024]{3,2,1,0:T(8,128)(2,1)} async-done(((bf16[2,16,96,1024]{3,2,1,0:T(8,128)(2,1)}), bf16[2,32,96,1024]{3,2,1,0:T(8,128)(2,1)}) %all-gather.5.cloned.1.call-update) | async-done | bytes 12582928 | tf_op jit(solution)/shard_map/all_gather | solution.py:89
  781.8 5.7 slice_bitcast_fusion.1
  787.6 7.0 fusion.52
  794.6 7.2 fusion.54
  801.7 7.1 add_bitcast_fusion
  808.8 7.3 subtract_bitcast_fusion
  816.2 1.8 fusion.38
  818.0 6.2 copy.78
  (87 shorter events, 13.1 us)
Async XLA Ops:
  6.5 283.1 %all-gather.3.cloned.1.call-start = ((), (), s32[]{:S(2)}) async-start(), calls=%async_computation.1 | async-start | bytes 18874368 | tf_op jit(solution)/shard_map/all_gather | solution.py:63
  8.3 42.1 %collective-permute-start.1 = (bf16[2,16,8,384]{3,2,1,0:T(8,128)(2,1)}, bf16[2,16,8,384]{3,2,1,0:T(8,128)(2,1)}, u32[]{:S(2)}, u32[]{:S(2)}) collective-permute-start(bf16[2,16,8,384]{3,2,1,0:T(8,128)(2,1)} %get-tuple-element.14), channel_id=1, source_target_pairs={{4,0},{8,4},{12,8},{5,1},{9,5},{13,9},{6,2},{10,6},{14,10},{7,3},{... | collective-permute-start | bytes 589832 | tf_op jit(solution)/shard_map/ppermute | solution.py:25
  9.6 46.0 %collective-permute-start = (bf16[2,16,8,384]{3,2,1,0:T(8,128)(2,1)}, bf16[2,16,8,384]{3,2,1,0:T(8,128)(2,1)}, u32[]{:S(2)}, u32[]{:S(2)}) collective-permute-start(bf16[2,16,8,384]{3,2,1,0:T(8,128)(2,1)} %get-tuple-element.13), channel_id=1, source_target_pairs={{0,4},{4,8},{8,12},{1,5},{5,9},{9,13},{2,6},{6,10},{10,14},{3,7},{... | collective-permute-start | bytes 589832 | tf_op jit(solution)/shard_map/ppermute | solution.py:23
  27.9 15.8 %copy-start.5 = (bf16[8,256,384]{2,1,0:T(8,128)(2,1)S(1)}, bf16[8,256,384]{2,1,0:T(8,128)(2,1)}, u32[]{:S(2)}) copy-start(bf16[8,256,384]{2,1,0:T(8,128)(2,1)} %param.7) | copy-start | bytes 4718596
  61.4 8.6 %copy-start.6 = (s32[256,384]{0,1:T(8,128)S(1)}, s32[256,384]{0,1:T(8,128)}, u32[]{:S(2)}) copy-start(s32[256,384]{0,1:T(8,128)} %copy.67) | copy-start | bytes 1179652
  61.4 8.6 %copy-start.7 = (s32[256,384]{0,1:T(8,128)S(1)}, s32[256,384]{0,1:T(8,128)}, u32[]{:S(2)}) copy-start(s32[256,384]{0,1:T(8,128)} %copy.64) | copy-start | bytes 1179652
  61.4 8.6 %copy-start.8 = (s32[256,384]{0,1:T(8,128)S(1)}, s32[256,384]{0,1:T(8,128)}, u32[]{:S(2)}) copy-start(s32[256,384]{0,1:T(8,128)} %copy.61) | copy-start | bytes 1179652
  61.4 8.6 %copy-start.9 = (s32[256,384]{0,1:T(8,128)S(1)}, s32[256,384]{0,1:T(8,128)}, u32[]{:S(2)}) copy-start(s32[256,384]{0,1:T(8,128)} %copy.58) | copy-start | bytes 1179652
  61.4 8.6 %copy-start.10 = (s32[256,384]{0,1:T(8,128)S(1)}, s32[256,384]{0,1:T(8,128)}, u32[]{:S(2)}) copy-start(s32[256,384]{0,1:T(8,128)} %copy.52) | copy-start | bytes 1179652
  61.4 8.6 %copy-start.11 = (s32[256,384]{0,1:T(8,128)S(1)}, s32[256,384]{0,1:T(8,128)}, u32[]{:S(2)}) copy-start(s32[256,384]{0,1:T(8,128)} %copy.49) | copy-start | bytes 1179652
  61.4 8.6 %copy-start.12 = (s32[256,384]{0,1:T(8,128)S(1)}, s32[256,384]{0,1:T(8,128)}, u32[]{:S(2)}) copy-start(s32[256,384]{0,1:T(8,128)} %copy.46) | copy-start | bytes 1179652
  61.4 8.6 %copy-start.13 = (bf16[256,384]{0,1:T(8,128)(2,1)S(1)}, bf16[256,384]{0,1:T(8,128)(2,1)}, u32[]{:S(2)}) copy-start(bf16[256,384]{0,1:T(8,128)(2,1)} %copy.69) | copy-start | bytes 589828
  61.5 8.6 %copy-start.14 = (bf16[256,384]{0,1:T(8,128)(2,1)S(1)}, bf16[256,384]{0,1:T(8,128)(2,1)}, u32[]{:S(2)}) copy-start(bf16[256,384]{0,1:T(8,128)(2,1)} %copy.66) | copy-start | bytes 589828
  61.5 8.6 %copy-start.15 = (bf16[256,384]{0,1:T(8,128)(2,1)S(1)}, bf16[256,384]{0,1:T(8,128)(2,1)}, u32[]{:S(2)}) copy-start(bf16[256,384]{0,1:T(8,128)(2,1)} %copy.63) | copy-start | bytes 589828
  61.5 8.6 %copy-start.16 = (bf16[256,384]{0,1:T(8,128)(2,1)S(1)}, bf16[256,384]{0,1:T(8,128)(2,1)}, u32[]{:S(2)}) copy-start(bf16[256,384]{0,1:T(8,128)(2,1)} %copy.60) | copy-start | bytes 589828
  61.5 8.6 %copy-start.17 = (bf16[256,384]{0,1:T(8,128)(2,1)S(1)}, bf16[256,384]{0,1:T(8,128)(2,1)}, u32[]{:S(2)}) copy-start(bf16[256,384]{0,1:T(8,128)(2,1)} %copy.57) | copy-start | bytes 589828
  61.5 8.6 %copy-start.18 = (bf16[256,384]{0,1:T(8,128)(2,1)S(1)}, bf16[256,384]{0,1:T(8,128)(2,1)}, u32[]{:S(2)}) copy-start(bf16[256,384]{0,1:T(8,128)(2,1)} %copy.54) | copy-start | bytes 589828
  61.5 8.6 %copy-start.19 = (bf16[256,384]{0,1:T(8,128)(2,1)S(1)}, bf16[256,384]{0,1:T(8,128)(2,1)}, u32[]{:S(2)}) copy-start(bf16[256,384]{0,1:T(8,128)(2,1)} %copy.51) | copy-start | bytes 589828
  61.5 8.6 %copy-start.20 = (bf16[256,384]{0,1:T(8,128)(2,1)S(1)}, bf16[256,384]{0,1:T(8,128)(2,1)}, u32[]{:S(2)}) copy-start(bf16[256,384]{0,1:T(8,128)(2,1)} %copy.48) | copy-start | bytes 589828
  61.5 8.6 %copy-start.21 = (pred[256,384]{0,1:T(8,128)(4,1)S(1)}, pred[256,384]{0,1:T(8,128)(4,1)}, u32[]{:S(2)}) copy-start(pred[256,384]{0,1:T(8,128)(4,1)} %copy.68) | copy-start | bytes 294916
  61.5 8.6 %copy-start.22 = (pred[256,384]{0,1:T(8,128)(4,1)S(1)}, pred[256,384]{0,1:T(8,128)(4,1)}, u32[]{:S(2)}) copy-start(pred[256,384]{0,1:T(8,128)(4,1)} %copy.65) | copy-start | bytes 294916
  61.5 8.6 %copy-start.23 = (pred[256,384]{0,1:T(8,128)(4,1)S(1)}, pred[256,384]{0,1:T(8,128)(4,1)}, u32[]{:S(2)}) copy-start(pred[256,384]{0,1:T(8,128)(4,1)} %copy.62) | copy-start | bytes 294916
  61.6 8.6 %copy-start.24 = (pred[256,384]{0,1:T(8,128)(4,1)S(1)}, pred[256,384]{0,1:T(8,128)(4,1)}, u32[]{:S(2)}) copy-start(pred[256,384]{0,1:T(8,128)(4,1)} %copy.59) | copy-start | bytes 294916
  61.6 8.6 %copy-start.25 = (pred[256,384]{0,1:T(8,128)(4,1)S(1)}, pred[256,384]{0,1:T(8,128)(4,1)}, u32[]{:S(2)}) copy-start(pred[256,384]{0,1:T(8,128)(4,1)} %copy.56) | copy-start | bytes 294916
  61.6 8.6 %copy-start.26 = (pred[256,384]{0,1:T(8,128)(4,1)S(1)}, pred[256,384]{0,1:T(8,128)(4,1)}, u32[]{:S(2)}) copy-start(pred[256,384]{0,1:T(8,128)(4,1)} %copy.53) | copy-start | bytes 294916
  61.6 8.6 %copy-start.27 = (pred[256,384]{0,1:T(8,128)(4,1)S(1)}, pred[256,384]{0,1:T(8,128)(4,1)}, u32[]{:S(2)}) copy-start(pred[256,384]{0,1:T(8,128)(4,1)} %copy.50) | copy-start | bytes 294916
  61.6 8.6 %copy-start.28 = (pred[256,384]{0,1:T(8,128)(4,1)S(1)}, pred[256,384]{0,1:T(8,128)(4,1)}, u32[]{:S(2)}) copy-start(pred[256,384]{0,1:T(8,128)(4,1)} %copy.47) | copy-start | bytes 294916
  263.9 517.9 %all-gather.5.cloned.1.call-start = ((), (), s32[]{:S(2)}) async-start(), calls=%async_computation.2 | async-start | bytes 18874368 | tf_op jit(solution)/shard_map/all_gather | solution.py:89
  309.1 13.1 %copy-start.2 = (bf16[1,16,256,768]{3,2,1,0:T(8,128)(2,1)S(1)}, bf16[1,16,256,768]{3,2,1,0:T(8,128)(2,1)}, u32[]{:S(2)}) copy-start(bf16[1,16,256,768]{3,2,1,0:T(8,128)(2,1)} %copy.81) | copy-start | bytes 18874372
  343.2 13.0 %copy-start = (bf16[1,16,256,768]{3,2,1,0:T(8,128)(2,1)S(1)}, bf16[1,16,256,768]{3,2,1,0:T(8,128)(2,1)}, u32[]{:S(2)}) copy-start(bf16[1,16,256,768]{3,2,1,0:T(8,128)(2,1)} %copy.80) | copy-start | bytes 18874372
  539.2 1.7 copy-start.4
  559.9 21.5 %copy-start.1 = (bf16[1,16,96,4,256]{4,3,2,1,0:T(4,128)(2,1)S(1)}, bf16[1,16,96,4,256]{4,3,2,1,0:T(4,128)(2,1)}, u32[]{:S(2)}) copy-start(bf16[1,16,96,4,256]{4,3,2,1,0:T(4,128)(2,1)} %get-tuple-element.11) | copy-start | bytes 9437188
  585.3 22.2 %copy-start.3 = (bf16[16,96,1024]{2,1,0:T(8,128)(2,1)S(1)}, bf16[16,96,1024]{2,1,0:T(8,128)(2,1)}, u32[]{:S(2)}) copy-start(bf16[16,96,1024]{2,1,0:T(8,128)(2,1)} %squeeze.27) | copy-start | bytes 9437188
  585.3 22.2 %copy-start.29 = (f32[16,96,1024]{2,1,0:T(8,128)S(1)}, f32[16,96,1024]{2,1,0:T(8,128)}, u32[]{:S(2)}) copy-start(f32[16,96,1024]{2,1,0:T(8,128)} %fusion.84) | copy-start | bytes 18874372
Sparse Core Ops, SparseCore 0:
  264.0 25.5 all-gather.2
  631.3 150.5 all-gather.4
where the time goes:
time: 841 us; the launch traced here: 832 us
  matrix products  355 us (42%)
  waiting for transfers between devices  176 us (21%)
  blocking collectives  143 us (17%)
  local copies, waits for them, and re-layouts  113 us (13%)
  other arithmetic  21.6 us (3%)
  between operations  14.4 us (2%)
    dot_general x1, matrix products, on_device(): jnp.einsum('jaf,ceaf->cejf', band_matrix, padded, preferred_element_type=...  194 us
    all_gather x1, waiting for transfers between devices, on_device(): shard_piece = lax.all_gather(crossed, 'el', axis=1, tiled=True)  151 us
    all_to_all x1, blocking collectives, on_device(): lax.all_to_all(ranged, 'az', split_axis=2, concat_axis=3, tiled=True)  143 us
    unnamed x63, local copies, waits for them, and re-layouts  29 us
    all_gather x1, waiting for transfers between devices, on_device(): shard_piece = lax.all_gather(interpolated, 'fq', axis=3, tiled=True)  25.3 us
    dot_general x1, matrix products, on_device(): jnp.einsum('ekj,jm->ekm', block_data[1], cos_a, preferred_element_type=jn...  22.2 us
    dot_general x1, matrix products, on_device(): jnp.einsum('ekj,jm->ekm', block_data[0], cos_a, preferred_element_type=jn...  21.5 us
    dot_general x1, matrix products, on_device(): jnp.einsum('ekj,jm->ekm', block_data[1], sin_a, preferred_element_type=jn...  19.7 us
  transfers between devices with their start and end apart: 4, of which 2 were waited for; matrix products, arithmetic and copies ran while one was open for 5% of the time, Pallas kernels for 0%

commit v1 on v0

--- a/solution.py
+++ b/solution.py
@@ -2,7 +2,11 @@
 
 import jax
 import jax.numpy as jnp
+import ml_dtypes
+import numpy as np
 from jax import lax
+from jax.experimental import pallas as pl
+from jax.experimental.pallas import tpu as pltpu
 from jax.sharding import PartitionSpec as P
 
 F = 768
@@ -10,6 +14,9 @@
 E = 32
 HW = 8
 KT = 8
+
+LANES = 128
+ROWS = 16
 
 
 def with_halo(cells, sides, width):
@@ -35,7 +42,7 @@
     return (jnp.cos(angle).astype(jnp.bfloat16), jnp.sin(angle).astype(jnp.bfloat16))
 
 
-def on_device(polar, band_offset, tap_count, tap_weight):
+def general_path(polar, band_offset, tap_count, tap_weight):
     shape_all = polar.shape
     col_count = shape_all[2]
     freq_count = shape_all[3]
@@ -100,6 +107,473 @@
     return image_out
 
 
+CUTS = (2, 4, 4, 6)
+SPLIT = 32
+VMEM = 56 * 1024 * 1024
+
+
+def host_table(row_ids, col_ids, length):
+    product = (row_ids[:, None] * col_ids[None, :]) % length
+    angle = product.astype(np.float32) * np.float32(2.0 * math.pi / length)
+    return (np.cos(angle).astype(ml_dtypes.bfloat16), np.sin(angle).astype(ml_dtypes.bfloat16))
+
+
+def params():
+    return pltpu.CompilerParams(vmem_limit_bytes=VMEM)
+
+
+def cost(flops, nbytes):
+    return pl.CostEstimate(flops=int(flops), bytes_accessed=int(nbytes), transcendentals=0)
+
+
+def band_kernel(offset_ref, count_ref, weight_ref, out_ref):
+    rows, freqs = offset_ref.shape
+
+    def tile(index, carry):
+        row = pl.ds(pl.multiple_of(index * ROWS, ROWS), ROWS)
+        for start in range(0, freqs, LANES):
+            lane = pl.ds(start, LANES)
+            base = offset_ref[row, lane] + HW
+            count = count_ref[row, lane]
+            zero = jnp.zeros((ROWS, LANES), jnp.float32)
+            slots = [
+                jnp.where(count > tap, weight_ref[tap, row, lane].astype(jnp.float32), zero)
+                for tap in range(KT)
+            ]
+            step = 1
+            while step < 2 * HW:
+                chosen = (base & step) != 0
+                size = min(len(slots) + step, 2 * HW + 1)
+                slots = [
+                    jnp.where(
+                        chosen,
+                        slots[d - step] if 0 <= d - step < len(slots) else zero,
+                        slots[d] if d < len(slots) else zero,
+                    )
+                    for d in range(size)
+                ]
+                step *= 2
+            for d in range(2 * HW + 1):
+                value = slots[d] if d < len(slots) else zero
+                out_ref[d, row, lane] = value.astype(jnp.bfloat16)
+        return carry
+
+    lax.fori_loop(0, rows // ROWS, tile, 0)
+
+
+def expand_bands(band_offset, tap_count, tap_weight):
+    cols, freqs = band_offset.shape
+    step = cols // 4
+    return pl.pallas_call(
+        band_kernel,
+        grid=(4,),
+        in_specs=[
+            pl.BlockSpec((step, freqs), lambda i: (i, 0)),
+            pl.BlockSpec((step, freqs), lambda i: (i, 0)),
+            pl.BlockSpec((KT, step, freqs), lambda i: (0, i, 0)),
+        ],
+        out_specs=pl.BlockSpec((2 * HW + 1, step, freqs), lambda i: (0, i, 0)),
+        out_shape=jax.ShapeDtypeStruct((2 * HW + 1, cols, freqs), jnp.bfloat16),
+        compiler_params=params(),
+        cost_estimate=cost(100 * cols * freqs, 58 * cols * freqs),
+        name="expand_bands",
+    )(band_offset, tap_count, tap_weight)
+
+
+def interp_kernel(polar_ref, halo_ref, band_ref, out_ref, pad_ref):
+    _, cuts, cols, freqs = polar_ref.shape
+    for part in range(2):
+        for cut in range(cuts):
+            plane = part * cuts + cut
+            for f in range(freqs // LANES):
+                lane = pl.ds(f * LANES, LANES)
+                halo = halo_ref[part, cut, :, lane].astype(jnp.float32)
+                pad_ref[plane, f, pl.ds(0, HW), :] = halo[:HW]
+                pad_ref[plane, f, pl.ds(HW, cols), :] = polar_ref[part, cut, :, lane].astype(jnp.float32)
+                pad_ref[plane, f, pl.ds(HW + cols, HW), :] = halo[HW:]
+
+    def tile(index, carry):
+        row = pl.multiple_of(index * ROWS, ROWS)
+        for f in range(freqs // LANES):
+            lane = pl.ds(f * LANES, LANES)
+            bands = [
+                band_ref[d, pl.ds(row, ROWS), lane].astype(jnp.float32) for d in range(2 * HW + 1)
+            ]
+            for part in range(2):
+                for cut in range(cuts):
+                    plane = part * cuts + cut
+                    total = bands[0] * pad_ref[plane, f, pl.ds(row, ROWS), :]
+                    for d in range(1, 2 * HW + 1):
+                        total = total + bands[d] * pad_ref[plane, f, pl.ds(row + d, ROWS), :]
+                    out_ref[part, cut, pl.ds(row, ROWS), lane] = total.astype(jnp.bfloat16)
+        return carry
+
+    lax.fori_loop(0, cols // ROWS, tile, 0)
+
+
+def interpolate(polar, halo, bands, first, count):
+    _, _, cols, freqs = polar.shape
+    group = 2
+    skip = first // group
+    return pl.pallas_call(
+        interp_kernel,
+        grid=(count // group,),
+        in_specs=[
+            pl.BlockSpec((2, group, cols, freqs), lambda i: (0, skip + i, 0, 0)),
+            pl.BlockSpec((2, group, 2 * HW, freqs), lambda i: (0, skip + i, 0, 0)),
+            pl.BlockSpec((2 * HW + 1, cols, freqs), lambda i: (0, 0, 0)),
+        ],
+        out_specs=pl.BlockSpec((2, group, cols, freqs), lambda i: (0, i, 0, 0)),
+        out_shape=jax.ShapeDtypeStruct((2, count, cols, freqs), jnp.bfloat16),
+        scratch_shapes=[
+            pltpu.VMEM((2 * group, freqs // LANES, cols + 2 * HW, LANES), jnp.float32)
+        ],
+        compiler_params=params(),
+        cost_estimate=cost(2 * count * cols * freqs * 34, 8 * count * cols * freqs),
+        name="interpolate",
+    )(polar, halo, bands)
+
+
+def range_kernel(ids_ref, own_ref, other_ref, table_ref, *refs):
+    first_ref, rest, product = refs[0], refs[1:-1], refs[-1]
+    blocks, rows2, _ = product.shape[1:]
+    bins = rows2 // 2
+    split = first_ref.shape[3]
+    table = table_ref[0].reshape(blocks * rows2, table_ref.shape[3])
+    for part in range(2):
+        values = jnp.concatenate([own_ref[part, 0], other_ref[part, 0]], axis=1)
+        product[part] = lax.dot_general(
+            table, values, (((1,), (1,)), ((), ())), preferred_element_type=jnp.float32
+        ).reshape(product.shape[1:])
+    az = ids_ref[0]
+    scale = 1.0 / math.sqrt(F)
+    for s in range(blocks):
+        block = az ^ s
+        real = (product[0, block, :bins] - product[1, block, bins:]) * scale
+        imag = (product[0, block, bins:] + product[1, block, :bins]) * scale
+        for part, value in ((0, real), (1, imag)):
+            value = value.astype(jnp.bfloat16)
+            first_ref[part, 0, s] = value[:split]
+            rest[s][part, 0] = value[split:]
+
+
+def range_transform(ids, own, other, table, split):
+    _, count, cols, freqs = own.shape
+    _, blocks, rows2, full = table.shape
+    bins = rows2 // 2
+    rest = bins - split
+    return pl.pallas_call(
+        range_kernel,
+        grid_spec=pltpu.PrefetchScalarGridSpec(
+            num_scalar_prefetch=1,
+            grid=(count,),
+            in_specs=[
+                pl.BlockSpec((2, 1, cols, freqs), lambda i, ids: (0, i, 0, 0)),
+                pl.BlockSpec((2, 1, cols, freqs), lambda i, ids: (0, i, 0, 0)),
+                pl.BlockSpec((1, blocks, rows2, full), lambda i, ids: (ids[1], 0, 0, 0)),
+            ],
+            out_specs=[pl.BlockSpec((2, 1, blocks, split, cols), lambda i, ids: (0, i, 0, 0, 0))]
+            + [pl.BlockSpec((2, 1, rest, cols), lambda i, ids: (0, i, 0, 0))] * blocks,
+            scratch_shapes=[pltpu.VMEM((2, blocks, rows2, cols), jnp.float32)],
+        ),
+        out_shape=[jax.ShapeDtypeStruct((2, count, blocks, split, cols), jnp.bfloat16)]
+        + [jax.ShapeDtypeStruct((2, count, rest, cols), jnp.bfloat16)] * blocks,
+        compiler_params=params(),
+        cost_estimate=cost(4 * count * cols * full * blocks * rows2, 12 * count * cols * freqs),
+        name="range_transform",
+    )(ids, own, other, table)
+
+
+def spin(value, real, imag):
+    return (value[0] * real - value[1] * imag, value[0] * imag + value[1] * real)
+
+
+def add(a, b):
+    return (a[0] + b[0], a[1] + b[1])
+
+
+def sub(a, b):
+    return (a[0] - b[0], a[1] - b[1])
+
+
+def turned(value, num, den):
+    num %= den
+    if num == 0:
+        return value
+    if 4 * num == den:
+        return (-value[1], value[0])
+    if 2 * num == den:
+        return (-value[0], -value[1])
+    angle = 2.0 * math.pi * num / den
+    if 8 * num == den:
+        root = math.sqrt(0.5)
+        return ((value[0] - value[1]) * root, (value[0] + value[1]) * root)
+    if 8 * num == 3 * den:
+        root = math.sqrt(0.5)
+        return ((value[0] + value[1]) * -root, (value[0] - value[1]) * root)
+    return spin(value, math.cos(angle), math.sin(angle))
+
+
+def fourier(points):
+    n = len(points)
+    if n == 1:
+        return points
+    even, odd = fourier(points[0::2]), fourier(points[1::2])
+    odd = [turned(v, g, n) for g, v in enumerate(odd)]
+    return [add(a, b) for a, b in zip(even, odd)] + [sub(a, b) for a, b in zip(even, odd)]
+
+
+def half_fourier(points, sign):
+    n = len(points)
+    even, odd = fourier(points[0::2]), fourier(points[1::2])
+    out = []
+    for g in range(n // 2):
+        angle = 2.0 * math.pi * g / n
+        if g == 0:
+            turn = (odd[g][0] * sign, odd[g][1] * sign)
+        else:
+            turn = spin(odd[g], sign * math.cos(angle), sign * math.sin(angle))
+        out.append(add(even[g], turn))
+    return out
+
+
+def heights(own, other, sign):
+    n = len(own)
+    even = half_fourier([add(a, b) for a, b in zip(own, other)], sign)
+    odd = []
+    for e, (a, b) in enumerate(zip(own, other)):
+        angle = math.pi * e / n
+        odd.append(spin(sub(a, b), sign * math.cos(angle), sign * math.sin(angle)))
+    odd = half_fourier(odd, sign)
+    return [v for pair in zip(even, odd) for v in pair]
+
+
+def height_kernel(ids_ref, *refs, chunks, outs, scale, aliased):
+    ins = refs[: 2 * chunks]
+    out_refs = refs[2 * chunks + aliased : 2 * chunks + aliased + outs]
+    sign = (1 - 2 * ids_ref[2]).astype(jnp.float32)
+    lanes = ins[0].shape[-1]
+
+    def tile(index, carry):
+        lane = pl.ds(pl.multiple_of(index * LANES, LANES), LANES)
+
+        def cuts_of(group):
+            found = []
+            for ref in group:
+                for e in range(ref.shape[1]):
+                    pad = (0,) * (len(ref.shape) - 4)
+                    found.append(
+                        tuple(
+                            ref[(part, e) + pad + (slice(None), lane)].astype(jnp.float32)
+                            for part in range(2)
+                        )
+                    )
+            return found
+
+        result = heights(cuts_of(ins[:chunks]), cuts_of(ins[chunks:]), sign)
+        h = 0
+        for ref in out_refs:
+            for row in range(ref.shape[1]):
+                for part in range(2):
+                    value = result[h][part]
+                    if scale is not None:
+                        value = value * scale
+                    ref[part, row, :, lane] = value.astype(jnp.bfloat16)
+                h += 1
+        return carry
+
+    lax.fori_loop(0, lanes // LANES, tile, 0)
+
+
+def first_heights(ids, own, other, s, parts):
+    chunks = len(own)
+    _, _, _, split, cols = own[0].shape
+    total = sum(v.shape[1] for v in own)
+    spec = [
+        pl.BlockSpec((2, v.shape[1], 1, ROWS, cols), lambda i, ids: (0, 0, s, i, 0)) for v in own
+    ]
+    return pl.pallas_call(
+        lambda *refs: height_kernel(*refs, chunks=chunks, outs=len(parts), scale=None, aliased=0),
+        grid_spec=pltpu.PrefetchScalarGridSpec(
+            num_scalar_prefetch=1,
+            grid=(split // ROWS,),
+            in_specs=spec + spec,
+            out_specs=[
+                pl.BlockSpec((2, h, ROWS, cols), lambda i, ids: (0, 0, i, 0)) for h in parts
+            ],
+        ),
+        out_shape=[jax.ShapeDtypeStruct((2, h, split, cols), jnp.bfloat16) for h in parts],
+        compiler_params=params(),
+        cost_estimate=cost(split * cols * 700, 12 * total * split * cols),
+        name="first_heights",
+    )(ids, *own, *other)
+
+
+def last_heights(ids, own, other, image, shape, skip, rows, offset):
+    chunks = len(own)
+    full = own[0].shape[3]
+    width = min(full, 512)
+    total = sum(v.shape[1] for v in own)
+    spec = [
+        pl.BlockSpec((2, v.shape[1], ROWS, width), lambda i, j, ids: (0, 0, offset // ROWS + i, j))
+        for v in own
+    ]
+    extra = [] if image is None else [image]
+    first = skip // ROWS
+    return pl.pallas_call(
+        lambda *refs: height_kernel(
+            *refs, chunks=chunks, outs=1, scale=1.0 / math.sqrt(2 * total), aliased=len(extra)
+        ),
+        grid_spec=pltpu.PrefetchScalarGridSpec(
+            num_scalar_prefetch=1,
+            grid=(rows // ROWS, full // width),
+            in_specs=spec + spec + [pl.BlockSpec(memory_space=pl.ANY)] * len(extra),
+            out_specs=pl.BlockSpec((2, total, ROWS, width), lambda i, j, ids: (0, 0, first + i, j)),
+        ),
+        out_shape=jax.ShapeDtypeStruct(shape, jnp.bfloat16),
+        input_output_aliases={1 + 2 * chunks: 0} if extra else {},
+        compiler_params=params(),
+        cost_estimate=cost(rows * full * 700, 12 * total * rows * full),
+        name="last_heights",
+    )(ids, *own, *other, *extra)
+
+
+def cross_kernel(ids_ref, *refs, blocks, scale, aliased):
+    ins = refs[:blocks]
+    cos_ref, sin_ref = refs[blocks : blocks + 2]
+    out_ref, rows_ref = refs[blocks + 2 + aliased :]
+    _, cuts, bins, cols = ins[0].shape
+    rows = cuts * bins
+
+    @pl.when(pl.program_id(0) == 0)
+    def _():
+        for s, ref in enumerate(ins):
+            start = pl.multiple_of((ids_ref[0] ^ s) * cols, cols)
+            rows_ref[:, pl.ds(start, cols)] = ref[...].reshape(2 * rows, cols)
+
+    values = rows_ref[...]
+    with_cos = jnp.dot(values, cos_ref[...], preferred_element_type=jnp.float32)
+    with_sin = jnp.dot(values, sin_ref[...], preferred_element_type=jnp.float32)
+    real = (with_cos[:rows] - with_sin[rows:]) * scale
+    imag = (with_sin[:rows] + with_cos[rows:]) * scale
+    out_ref[0] = real.astype(jnp.bfloat16).reshape(out_ref.shape[1:])
+    out_ref[1] = imag.astype(jnp.bfloat16).reshape(out_ref.shape[1:])
+
+
+def cross_transform(ids, ins, tables, scale, image=None, shape=None, place=0):
+    blocks = len(ins)
+    _, cuts, bins, cols = ins[0].shape
+    full = tables[0].shape[1]
+    width = min(full, 256)
+    extra = [] if image is None else [image]
+    if shape is None:
+        shape = (2, cuts, bins, full)
+    return pl.pallas_call(
+        lambda *refs: cross_kernel(*refs, blocks=blocks, scale=scale, aliased=len(extra)),
+        grid_spec=pltpu.PrefetchScalarGridSpec(
+            num_scalar_prefetch=1,
+            grid=(full // width,),
+            in_specs=[pl.BlockSpec((2, cuts, bins, cols), lambda i, ids: (0, 0, 0, 0))] * blocks
+            + [pl.BlockSpec((full, width), lambda i, ids: (0, i))] * 2
+            + [pl.BlockSpec(memory_space=pl.ANY)] * len(extra),
+            out_specs=pl.BlockSpec((2, cuts, bins, width), lambda i, ids: (0, place, 0, i)),
+            scratch_shapes=[pltpu.VMEM((2 * cuts * bins, full), jnp.bfloat16)],
+        ),
+        out_shape=jax.ShapeDtypeStruct(shape, jnp.bfloat16),
+        input_output_aliases={1 + blocks + 2: 0} if extra else {},
+        compiler_params=params(),
+        cost_estimate=cost(8 * cuts * bins * full * full, 8 * cuts * bins * full + 4 * full * full),
+        name="cross_transform",
+    )(ids, *ins, *tables, *extra)
+
+
+def exchange(value, axis, s):
+    return lax.ppermute(value, axis, [(i, i ^ s) for i in range(lax.axis_size(axis))])
+
+
+def halo_rows(polar):
+    count = lax.axis_size("az")
+    cols = polar.shape[2]
+    ends = count - 1
+    head = lax.slice_in_dim(polar, 0, HW, axis=2)
+    tail = lax.slice_in_dim(polar, cols - HW, cols, axis=2)
+    return jnp.concatenate(
+        [
+            lax.ppermute(tail, "az", [(i, i + 1) for i in range(ends)]),
+            lax.ppermute(head, "az", [(i + 1, i) for i in range(ends)]),
+        ],
+        axis=2,
+    )
+
+
+def planned_path(polar, band_offset, tap_count, tap_weight):
+    _, cuts, cols, freqs = polar.shape
+    az_count = lax.axis_size("az")
+    fq_count = lax.axis_size("fq")
+    bins = F // (az_count * fq_count)
+    split = SPLIT
+    ids = jnp.stack([lax.axis_index("az"), lax.axis_index("fq"), lax.axis_index("el")])
+    tables = []
+    for core in range(fq_count):
+        order = np.concatenate([np.arange(freqs) + freqs * (core ^ s) for s in range(fq_count)])
+        blocks = []
+        for az in range(az_count):
+            ks = (az * fq_count + core) * bins + np.arange(bins)
+            blocks.append(np.concatenate(host_table(ks, order, F)))
+        tables.append(np.stack(blocks))
+    range_table = jnp.asarray(np.stack(tables))
+    cross_tables = [jnp.asarray(t) for t in host_table(np.arange(A), np.arange(A), A)]
+
+    halo = halo_rows(polar)
+    bands = expand_bands(band_offset, tap_count, tap_weight)
+    own_first, other_first = [], []
+    own_last, other_last = [], []
+    start = 0
+    for count in CUTS:
+        own = interpolate(polar, halo, bands, start, count)
+        other = exchange(own, "fq", 1)
+        first, *rest = range_transform(ids, own, other, range_table, split)
+        own_first.append(first)
+        other_first.append(exchange(first, "el", 1))
+        landed = [rest[0]] + [exchange(rest[s], "az", s) for s in range(1, az_count)]
+        crossed = cross_transform(ids, landed, cross_tables, 1.0 / math.sqrt(A))
+        own_last.append(crossed)
+        other_last.append(exchange(crossed, "el", 1))
+        start += count
+    parts = (cuts // 2, cuts // 2)
+    landed = [[] for _ in parts]
+    for s in reversed(range(az_count)):
+        made = first_heights(ids, own_first, other_first, s, parts)
+        for p, value in enumerate(made):
+            landed[p].insert(0, exchange(value, "az", s) if s else value)
+    shape = (2, cuts, bins, A)
+    scale = 1.0 / math.sqrt(A * 2 * cuts)
+    image = cross_transform(ids, landed[0], cross_tables, scale, None, shape, 0)
+    image = last_heights(ids, own_last, other_last, image, shape, split, bins - split, 0)
+    image = cross_transform(ids, landed[1], cross_tables, scale, image, shape, 1)
+    return image
+
+
+def on_device(polar, band_offset, tap_count, tap_weight):
+    _, cuts, cols, freqs = polar.shape
+    az_count = lax.axis_size("az")
+    bins = F // (az_count * lax.axis_size("fq"))
+    fits = (
+        lax.axis_size("el") == 2
+        and lax.axis_size("fq") == 2
+        and az_count in (2, 4)
+        and cuts == sum(CUTS)
+        and cols % (2 * LANES) == 0
+        and freqs % LANES == 0
+        and bins > SPLIT
+        and bins % SPLIT == 0
+        and A % 512 == 0
+        and 2 * HW == ROWS
+    )
+    chosen = planned_path if fits else general_path
+    return chosen(polar, band_offset, tap_count, tap_weight)
+
+
 def solution(mesh):
     in_specs = (
         P(None, ("grp", "el"), "az", "fq"),

time: 841 us -> 315 us (0.37)
  matrix products: 355 us -> 0 us
  blocking collectives: 143 us -> 0 us
  Pallas kernels: 0 us -> 133 us
  local copies, waits for them, and re-layouts: 113 us -> 6.84 us
  waiting for transfers between devices: 176 us -> 120 us
  starting transfers between devices: 7.78 us -> 53.2 us
  other arithmetic: 21.6 us -> 0.56 us
  between operations: 14.4 us -> 0.36 us
    dot_general x13 -> x0, matrix products: 355 us -> none  [the longest x1 194 us: on_device(): jnp.einsum('jaf,ceaf->cejf', band_matrix, padded, preferred_element_type=...]
    all_gather x2 -> x0, waiting for transfers between devices: 176 us -> none  [the longest x1 151 us: on_device(): shard_piece = lax.all_gather(crossed, 'el', axis=1, tiled=True)]
    all_to_all x1 -> x0, blocking collectives: 143 us -> none  [on_device(): lax.all_to_all(ranged, 'az', split_axis=2, concat_axis=3, tiled=True)]
    pallas_call x0 -> x20, Pallas kernels: none -> 133 us  [the longest x6 40.3 us: cross_transform(): pl.pallas_call(lambda *refs: cross_kernel(*refs, blocks=blocks, scale=sca...]
    ppermute x2 -> x32, waiting for transfers between devices: 0.01 us -> 120 us  [the longest x30 118 us: exchange(): lax.ppermute(value, axis, [(i, i ^ s) for i in range(lax.axis_size(axis))])]
    ppermute x2 -> x32, starting transfers between devices: 7.52 us -> 53.2 us  [the longest x30 47 us: exchange(): lax.ppermute(value, axis, [(i, i ^ s) for i in range(lax.axis_size(axis))])]
    unnamed x63 -> x81, local copies, waits for them, and re-layouts: 29 us -> 5.74 us
    slice x3 -> x1, local copies, waits for them, and re-layouts: 16.4 us -> 1.06 us  [halo_rows(): head = lax.slice_in_dim(polar, 0, HW, axis=2)]
  transfers between devices with their start and end apart: 4 -> 32, of which waited for: 2 -> 10; matrix products, arithmetic and copies ran while one was open for 5% -> 0% of each run, Pallas kernels for 0% -> 37%
where the time goes in v1:
time: 315 us; the launch traced here: 314 us
  Pallas kernels  133 us (42%)
  waiting for transfers between devices  120 us (38%)
  starting transfers between devices  53.2 us (17%)
  local copies, waits for them, and re-layouts  6.84 us (2%)
    ppermute x30, waiting for transfers between devices, exchange(): lax.ppermute(value, axis, [(i, i ^ s) for i in range(lax.axis_size(axis))])  118 us
    ppermute x30, starting transfers between devices, exchange(): lax.ppermute(value, axis, [(i, i ^ s) for i in range(lax.axis_size(axis))])  47 us
    pallas_call x6, Pallas kernels, cross_transform(): pl.pallas_call(lambda *refs: cross_kernel(*refs, blocks=blocks, scale=sca...  40.3 us
    pallas_call x4, Pallas kernels, interpolate(): pl.pallas_call(interp_kernel, grid=(count // group,), in_specs=[pl.BlockS...  33.8 us
    pallas_call x4, Pallas kernels, range_transform(): pl.pallas_call(range_kernel, grid_spec=pltpu.PrefetchScalarGridSpec(num_s...  28.4 us
    pallas_call x4, Pallas kernels, first_heights(): pl.pallas_call(lambda *refs: height_kernel(*refs, chunks=chunks, outs=len...  13.8 us
    pallas_call x1, Pallas kernels, last_heights(): pl.pallas_call(lambda *refs: height_kernel(*refs, chunks=chunks, outs=1,...  11.8 us
  transfers between devices with their start and end apart: 32, of which 10 were waited for; matrix products, arithmetic and copies ran while one was open for 0% of the time, Pallas kernels for 37%

profile of v1, /device:TPU:0, one launch (start us, length us, event | category | flops | bytes accessed | tf_op | source)
XLA Modules:
  0.0 313.6 jit_solution(14134458623202450517)
XLA Ops:
  1.1 4.9 %collective-permute-start = (bf16[2,16,8,384]{3,2,1,0:T(8,128)(2,1)S(1)}, bf16[2,16,8,384]{3,2,1,0:T(8,128)(2,1)S(1)}, u32[]{:S(2)}, u32[]{:S(2)}) collective-permute-start(bf16[2,16,8,384]{3,2,1,0:T(8,128)(2,1)S(1)} %get-tuple-element.62), channel_id=1, source_target_pairs={{0,4},{4,8},{8,12},{1,5},{5,9},{9,13},{2,6},{6,10},{10,14},{3,7},{... | collective-permute-start | bytes 589832 | tf_op jit(solution)/shard_map/ppermute | solution.py:502
  6.0 1.3 collective-permute-start.1
  7.3 4.7 %expand_bands.1.band_ref = bf16[17,256,384]{2,1,0:T(8,128)(2,1)} custom-call(s32[256,384]{1,0:T(8,128)} %offset_ref.1, s32[256,384]{1,0:T(8,128)} %count_ref.1, bf16[8,256,384]{2,1,0:T(8,128)(2,1)} %weight_ref.1), custom_call_target="tpu_custom_call" | custom-call | flops 9830400 | bytes 5701632 | tf_op jit(solution)/shard_map/expand_bands/pallas_call | solution.py:167
  12.0 2.2 collective-permute-done.1
  15.1 11.1 %interpolate.7.own_ref = bf16[2,6,256,384]{3,2,1,0:T(8,128)(2,1)} custom-call(bf16[2,16,256,384]{3,2,1,0:T(8,128)(2,1)} %polar_ref.7, bf16[2,16,16,384]{3,2,1,0:T(8,128)(2,1)} %copy-done.6, bf16[17,256,384]{2,1,0:T(8,128)(2,1)} %expand_bands.1.band_ref), custom_call_target="tpu_custom_call" | custom-call | flops 40108032 | bytes 4718592 | tf_op jit(solution)/shard_map/interpolate/pallas_call | solution.py:218
  26.2 8.5 %interpolate.5.own_ref = bf16[2,4,256,384]{3,2,1,0:T(8,128)(2,1)} custom-call(bf16[2,16,256,384]{3,2,1,0:T(8,128)(2,1)} %polar_ref.7, bf16[2,16,16,384]{3,2,1,0:T(8,128)(2,1)} %copy-done.6, bf16[17,256,384]{2,1,0:T(8,128)(2,1)} %expand_bands.1.band_ref), custom_call_target="tpu_custom_call" | custom-call | flops 26738688 | bytes 3145728 | tf_op jit(solution)/shard_map/interpolate/pallas_call | solution.py:218
  35.2 8.4 %interpolate.6.own_ref = bf16[2,4,256,384]{3,2,1,0:T(8,128)(2,1)} custom-call(bf16[2,16,256,384]{3,2,1,0:T(8,128)(2,1)} %polar_ref.7, bf16[2,16,16,384]{3,2,1,0:T(8,128)(2,1)} %copy-done.6, bf16[17,256,384]{2,1,0:T(8,128)(2,1)} %expand_bands.1.band_ref), custom_call_target="tpu_custom_call" | custom-call | flops 26738688 | bytes 3145728 | tf_op jit(solution)/shard_map/interpolate/pallas_call | solution.py:218
  43.6 5.8 %interpolate.4.own_ref = bf16[2,2,256,384]{3,2,1,0:T(8,128)(2,1)} custom-call(bf16[2,16,256,384]{3,2,1,0:T(8,128)(2,1)} %polar_ref.7, bf16[2,16,16,384]{3,2,1,0:T(8,128)(2,1)} %copy-done.6, bf16[17,256,384]{2,1,0:T(8,128)(2,1)} %expand_bands.1.band_ref), custom_call_target="tpu_custom_call" | custom-call | flops 13369344 | bytes 1572864 | tf_op jit(solution)/shard_map/interpolate/pallas_call | solution.py:218
  50.4 1.6 collective-permute-done.2.other_ref
  52.9 4.9 %range_transform.4 = (bf16[2,2,4,32,256]{4,3,2,1,0:T(8,128)(2,1)}, bf16[2,2,64,256]{3,2,1,0:T(8,128)(2,1)}, bf16[2,2,64,256]{3,2,1,0:T(8,128)(2,1)}, bf16[2,2,64...) custom-call(s32[3]{0:T(128)} %pad_add_fusion.ids_ref.refs_0_, bf16[2,2,256,384]{3,2,1,0:T(8,128)(2,1)} %interpolate.4.own_ref, ...), custom_call_target="tpu_custom_call" | custom-call | flops 1207959552 | bytes 2359296 | tf_op jit(solution)/shard_map/range_transform/pallas_call | solution.py:265
  57.8 1.6 collective-permute-start.13
  59.3 1.4 collective-permute-start.14
  60.8 1.5 collective-permute-start.6
  62.3 9.4 %range_transform.7 = (bf16[2,6,4,32,256]{4,3,2,1,0:T(8,128)(2,1)}, bf16[2,6,64,256]{3,2,1,0:T(8,128)(2,1)}, bf16[2,6,64,256]{3,2,1,0:T(8,128)(2,1)}, bf16[2,6,64...) custom-call(s32[3]{0:T(128)} %pad_add_fusion.ids_ref.refs_0_, bf16[2,6,256,384]{3,2,1,0:T(8,128)(2,1)} %interpolate.7.own_ref, ...), custom_call_target="tpu_custom_call" | custom-call | flops 3623878656 | bytes 7077888 | tf_op jit(solution)/shard_map/range_transform/pallas_call | solution.py:265
  71.6 1.7 collective-permute-start.22
  73.7 2.4 collective-permute-start.24
  76.1 7.1 %range_transform.5 = (bf16[2,4,4,32,256]{4,3,2,1,0:T(8,128)(2,1)}, bf16[2,4,64,256]{3,2,1,0:T(8,128)(2,1)}, bf16[2,4,64,256]{3,2,1,0:T(8,128)(2,1)}, bf16[2,4,64...) custom-call(s32[3]{0:T(128)} %pad_add_fusion.ids_ref.refs_0_, bf16[2,4,256,384]{3,2,1,0:T(8,128)(2,1)} %interpolate.5.own_ref, ...), custom_call_target="tpu_custom_call" | custom-call | flops 2415919104 | bytes 4718592 | tf_op jit(solution)/shard_map/range_transform/pallas_call | solution.py:265
  83.3 1.4 collective-permute-start.15
  84.7 7.1 %range_transform.6 = (bf16[2,4,4,32,256]{4,3,2,1,0:T(8,128)(2,1)}, bf16[2,4,64,256]{3,2,1,0:T(8,128)(2,1)}, bf16[2,4,64,256]{3,2,1,0:T(8,128)(2,1)}, bf16[2,4,64...) custom-call(s32[3]{0:T(128)} %pad_add_fusion.ids_ref.refs_0_, bf16[2,4,256,384]{3,2,1,0:T(8,128)(2,1)} %interpolate.6.own_ref, ...), custom_call_target="tpu_custom_call" | custom-call | flops 2415919104 | bytes 4718592 | tf_op jit(solution)/shard_map/range_transform/pallas_call | solution.py:265
  91.8 11.3 %collective-permute-done.15.refs_4_ = bf16[2,2,64,256]{3,2,1,0:T(8,128)(2,1)S(1)} collective-permute-done((bf16[2,2,64,256]{3,2,1,0:T(8,128)(2,1)S(1)}, bf16[2,2,64,256]{3,2,1,0:T(8,128)(2,1)S(1)}, u32[]{:S(2)}, u32[]{:S(2)}) %collective-permute-start.15) | collective-permute-done | bytes 131104 | tf_op jit(solution)/shard_map/ppermute | solution.py:491
  103.1 13.1 %collective-permute-start.16 = (bf16[2,4,64,256]{3,2,1,0:T(8,128)(2,1)S(1)}, bf16[2,4,64,256]{3,2,1,0:T(8,128)(2,1)S(1)}, u32[]{:S(2)}, u32[]{:S(2)}) collective-permute-start(bf16[2,4,64,256]{3,2,1,0:T(8,128)(2,1)S(1)} %copy-done.33), channel_id=1, source_target_pairs={{0,4},{4,0},{8,12},{12,8},{1,5},{5,1},{9,13},{13,9},{2,6},{6,2},{1... | collective-permute-start | bytes 786440 | tf_op jit(solution)/shard_map/ppermute | solution.py:491
  116.3 2.4 collective-permute-start.18
  120.8 8.0 %cross_transform.9.refs_4_ = bf16[2,6,64,1024]{3,2,1,0:T(8,128)(2,1)} custom-call(s32[3]{0:T(128)} %pad_add_fusion.ids_ref.refs_0_, bf16[2,6,64,256]{3,2,1,0:T(8,128)(2,1)} %get-tuple-element.53.refs_1_, bf16[2,6,64,256]{3,2,1,0:T(8,128)(2,1)} %copy-done.23, bf16[2,6,64,256]{3,2,1,0:T(8,128)(2,1)} %copy-done.24, bf16[2,6,64,256]{3,2,1,0:T(8,128)(2,1)} %copy-done.25, ...), custom_call_target="tpu_custom_call" | custom-call | flops 3221225472 | bytes 7340032 | tf_op jit(solution)/shard_map/cross_transform/pallas_call | solution.py:471
  129.9 7.8 %collective-permute-done.17.refs_3_ = bf16[2,4,64,256]{3,2,1,0:T(8,128)(2,1)S(1)} collective-permute-done((bf16[2,4,64,256]{3,2,1,0:T(8,128)(2,1)S(1)}, bf16[2,4,64,256]{3,2,1,0:T(8,128)(2,1)S(1)}, u32[]{:S(2)}, u32[]{:S(2)}) %collective-permute-start.17) | collective-permute-done | bytes 262176 | tf_op jit(solution)/shard_map/ppermute | solution.py:491
  137.7 1.3 collective-permute-start.21
  140.0 1.1 collective-permute-start.28
  141.1 6.8 %cross_transform.7.refs_2_ = bf16[2,4,64,1024]{3,2,1,0:T(8,128)(2,1)} custom-call(s32[3]{0:T(128)} %pad_add_fusion.ids_ref.refs_0_, bf16[2,4,64,256]{3,2,1,0:T(8,128)(2,1)} %get-tuple-element.45.refs_1_, bf16[2,4,64,256]{3,2,1,0:T(8,128)(2,1)} %copy-done.31, bf16[2,4,64,256]{3,2,1,0:T(8,128)(2,1)} %copy-done.34, bf16[2,4,64,256]{3,2,1,0:T(8,128)(2,1)} %copy-done.36, ...), custom_call_target="tpu_custom_call" | custom-call | flops 2147483648 | bytes 6291456 | tf_op jit(solution)/shard_map/cross_transform/pallas_call | solution.py:471
  147.9 11.5 %collective-permute-done.20.refs_3_ = bf16[2,4,64,256]{3,2,1,0:T(8,128)(2,1)S(1)} collective-permute-done((bf16[2,4,64,256]{3,2,1,0:T(8,128)(2,1)}, bf16[2,4,64,256]{3,2,1,0:T(8,128)(2,1)S(1)}, u32[]{:S(2)}, u32[]{:S(2)}) %collective-permute-start.20) | collective-permute-done | bytes 262176 | tf_op jit(solution)/shard_map/ppermute | solution.py:491
  160.0 1.6 collective-permute-start.9
  161.6 6.7 %cross_transform.8.refs_3_ = bf16[2,4,64,1024]{3,2,1,0:T(8,128)(2,1)} custom-call(s32[3]{0:T(128)} %pad_add_fusion.ids_ref.refs_0_, bf16[2,4,64,256]{3,2,1,0:T(8,128)(2,1)} %get-tuple-element.49.refs_1_, bf16[2,4,64,256]{3,2,1,0:T(8,128)(2,1)} %copy-done.32, bf16[2,4,64,256]{3,2,1,0:T(8,128)(2,1)} %copy-done.35, bf16[2,4,64,256]{3,2,1,0:T(8,128)(2,1)} %copy-done.37, ...), custom_call_target="tpu_custom_call" | custom-call | flops 2147483648 | bytes 6291456 | tf_op jit(solution)/shard_map/cross_transform/pallas_call | solution.py:471
  168.9 5.6 %cross_transform.6.refs_1_ = bf16[2,2,64,1024]{3,2,1,0:T(8,128)(2,1)} custom-call(s32[3]{0:T(128)} %pad_add_fusion.ids_ref.refs_0_, bf16[2,2,64,256]{3,2,1,0:T(8,128)(2,1)} %get-tuple-element.41.refs_1_, bf16[2,2,64,256]{3,2,1,0:T(8,128)(2,1)} %copy-done.18, bf16[2,2,64,256]{3,2,1,0:T(8,128)(2,1)} %copy-done.19, bf16[2,2,64,256]{3,2,1,0:T(8,128)(2,1)} %copy-done.20, ...), custom_call_target="tpu_custom_call" | custom-call | flops 1073741824 | bytes 5242880 | tf_op jit(solution)/shard_map/cross_transform/pallas_call | solution.py:471
  174.6 1.5 collective-permute-start.25
  176.0 52.5 %collective-permute-done.9.refs_8_ = bf16[2,6,4,32,256]{4,3,2,1,0:T(8,128)(2,1)S(1)} collective-permute-done((bf16[2,6,4,32,256]{4,3,2,1,0:T(8,128)(2,1)S(1)}, bf16[2,6,4,32,256]{4,3,2,1,0:T(8,128)(2,1)S(1)}, u32[]{:S(2)}, u32[]{:S(2)}) %collective-permute-start.9) | collective-permute-done | bytes 786464 | tf_op jit(solution)/shard_map/ppermute | solution.py:491
  229.4 3.4 %first_heights.7 = (bf16[2,8,32,256]{3,2,1,0:T(8,128)(2,1)}, bf16[2,8,32,256]{3,2,1,0:T(8,128)(2,1)}) custom-call(s32[3]{0:T(128)} %pad_add_fusion.ids_ref.refs_0_, bf16[2,2,4,32,256]{4,3,2,1,0:T(8,128)(2,1)} %get-tuple-element.33.refs_1_, bf16[2,4,4,32,256]{4,3,2,1,0:T(8,128)(2,1)} %get-tuple-element.34.refs_2_, ...), custom_call_target="tpu_custom_call" | custom-call | flops 5734400 | bytes 1572864 | tf_op jit(solution)/shard_map/first_heights/pallas_call | solution.py:395
  232.8 1.9 collective-permute-start.31
  234.7 3.4 %first_heights.6 = (bf16[2,8,32,256]{3,2,1,0:T(8,128)(2,1)}, bf16[2,8,32,256]{3,2,1,0:T(8,128)(2,1)}) custom-call(s32[3]{0:T(128)} %pad_add_fusion.ids_ref.refs_0_, bf16[2,2,4,32,256]{4,3,2,1,0:T(8,128)(2,1)} %get-tuple-element.33.refs_1_, bf16[2,4,4,32,256]{4,3,2,1,0:T(8,128)(2,1)} %get-tuple-element.34.refs_2_, ...), custom_call_target="tpu_custom_call" | custom-call | flops 5734400 | bytes 1572864 | tf_op jit(solution)/shard_map/first_heights/pallas_call | solution.py:395
  238.2 3.5 %first_heights.5 = (bf16[2,8,32,256]{3,2,1,0:T(8,128)(2,1)}, bf16[2,8,32,256]{3,2,1,0:T(8,128)(2,1)}) custom-call(s32[3]{0:T(128)} %pad_add_fusion.ids_ref.refs_0_, bf16[2,2,4,32,256]{4,3,2,1,0:T(8,128)(2,1)} %get-tuple-element.33.refs_1_, bf16[2,4,4,32,256]{4,3,2,1,0:T(8,128)(2,1)} %get-tuple-element.34.refs_2_, ...), custom_call_target="tpu_custom_call" | custom-call | flops 5734400 | bytes 1572864 | tf_op jit(solution)/shard_map/first_heights/pallas_call | solution.py:395
  241.7 16.2 %collective-permute-done.25.refs_5_ = bf16[2,2,64,1024]{3,2,1,0:T(8,128)(2,1)S(1)} collective-permute-done((bf16[2,2,64,1024]{3,2,1,0:T(8,128)(2,1)}, bf16[2,2,64,1024]{3,2,1,0:T(8,128)(2,1)S(1)}, u32[]{:S(2)}, u32[]{:S(2)}) %collective-permute-start.25) | collective-permute-done | bytes 524320 | tf_op jit(solution)/shard_map/ppermute | solution.py:491
  257.9 1.7 collective-permute-start.30
  259.7 1.6 collective-permute-start.29
  261.3 2.4 collective-permute-start.12
  263.7 15.7 %collective-permute-done.30.refs_3_ = bf16[2,8,32,256]{3,2,1,0:T(8,128)(2,1)S(1)} collective-permute-done((bf16[2,8,32,256]{3,2,1,0:T(8,128)(2,1)S(1)}, bf16[2,8,32,256]{3,2,1,0:T(8,128)(2,1)S(1)}, u32[]{:S(2)}, u32[]{:S(2)}) %collective-permute-start.30) | collective-permute-done | bytes 262176 | tf_op jit(solution)/shard_map/ppermute | solution.py:491
  279.3 2.5 collective-permute-start.10
  281.9 3.4 %first_heights.4 = (bf16[2,8,32,256]{3,2,1,0:T(8,128)(2,1)}, bf16[2,8,32,256]{3,2,1,0:T(8,128)(2,1)}) custom-call(s32[3]{0:T(128)} %pad_add_fusion.ids_ref.refs_0_, bf16[2,2,4,32,256]{4,3,2,1,0:T(8,128)(2,1)} %get-tuple-element.33.refs_1_, bf16[2,4,4,32,256]{4,3,2,1,0:T(8,128)(2,1)} %get-tuple-element.34.refs_2_, ...), custom_call_target="tpu_custom_call" | custom-call | flops 5734400 | bytes 1572864 | tf_op jit(solution)/shard_map/first_heights/pallas_call | solution.py:395
  285.3 6.6 %cross_transform.10.refs_9_ = bf16[2,16,96,1024]{3,2,1,0:T(8,128)(2,1)} custom-call(s32[3]{0:T(128)} %pad_add_fusion.ids_ref.refs_0_, bf16[2,8,32,256]{3,2,1,0:T(8,128)(2,1)} %get-tuple-element.57.refs_1_, bf16[2,8,32,256]{3,2,1,0:T(8,128)(2,1)} %copy-done.17, bf16[2,8,32,256]{3,2,1,0:T(8,128)(2,1)} %copy-done.16, bf16[2,8,32,256]{3,2,1,0:T(8,128)(2,1)} %copy-done.15, ...), custom_call_target="tpu_custom_call" | custom-call | flops 2147483648 | bytes 6291456 | tf_op jit(solution)/shard_map/cross_transform/pallas_call | solution.py:471
  293.0 1.2 copy-done.8
  294.2 11.8 %last_heights.1.refs_7_ = bf16[2,16,96,1024]{3,2,1,0:T(8,128)(2,1)} custom-call(s32[3]{0:T(128)} %pad_add_fusion.ids_ref.refs_0_, bf16[2,2,64,1024]{3,2,1,0:T(8,128)(2,1)} %cross_transform.6.refs_1_, bf16[2,4,64,1024]{3,2,1,0:T(8,128)(2,1)} %cross_transform.7.refs_2_, ...), custom_call_target="tpu_custom_call", output_to_operand_aliasing={{}: (9, {})} | custom-call | flops 45875200 | bytes 12582912 | tf_op jit(solution)/shard_map/last_heights/pallas_call | solution.py:423
  306.9 6.6 %cross_transform.11 = bf16[2,16,96,1024]{3,2,1,0:T(8,128)(2,1)} custom-call(s32[3]{0:T(128)} %pad_add_fusion.ids_ref.refs_0_, bf16[2,8,32,256]{3,2,1,0:T(8,128)(2,1)} %get-tuple-element.37.refs_1_, bf16[2,8,32,256]{3,2,1,0:T(8,128)(2,1)} %copy-done.14, bf16[2,8,32,256]{3,2,1,0:T(8,128)(2,1)} %copy-done.13, ...), custom_call_target="tpu_custom_call", output_to_operand_aliasing={{}: (7, {})} | custom-call | flops 2147483648 | bytes 6291456 | tf_op jit(solution)/shard_map/cross_transform/pallas_call | solution.py:471
  (120 shorter events, 13.0 us)
Async XLA Ops:
  1.1 10.9 %collective-permute-start = (bf16[2,16,8,384]{3,2,1,0:T(8,128)(2,1)S(1)}, bf16[2,16,8,384]{3,2,1,0:T(8,128)(2,1)S(1)}, u32[]{:S(2)}, u32[]{:S(2)}) collective-permute-start(bf16[2,16,8,384]{3,2,1,0:T(8,128)(2,1)S(1)} %get-tuple-element.62), channel_id=1, source_target_pairs={{0,4},{4,8},{8,12},{1,5},{5,9},{9,13},{2,6},{6,10},{10,14},{3,7},{... | collective-permute-start | bytes 589832 | tf_op jit(solution)/shard_map/ppermute | solution.py:502
  6.0 8.3 %collective-permute-start.1 = (bf16[2,16,8,384]{3,2,1,0:T(8,128)(2,1)S(1)}, bf16[2,16,8,384]{3,2,1,0:T(8,128)(2,1)S(1)}, u32[]{:S(2)}, u32[]{:S(2)}) collective-permute-start(bf16[2,16,8,384]{3,2,1,0:T(8,128)(2,1)S(1)} %get-tuple-element.61), channel_id=1, source_target_pairs={{4,0},{8,4},{12,8},{5,1},{9,5},{13,9},{6,2},{10,6},{14,10},{7,3},{... | collective-permute-start | bytes 589832 | tf_op jit(solution)/shard_map/ppermute | solution.py:503
  26.2 34.6 %collective-permute-start.5 = (bf16[2,6,256,384]{3,2,1,0:T(8,128)(2,1)}, bf16[2,6,256,384]{3,2,1,0:T(8,128)(2,1)}, u32[]{:S(2)}, u32[]{:S(2)}) collective-permute-start(bf16[2,6,256,384]{3,2,1,0:T(8,128)(2,1)} %interpolate.7.own_ref), channel_id=1, source_target_pairs={{0,1},{1,0},{2,3},{3,2},{4,5},{5,4},{6,7},{7,6},{8,9},{9,8},{10,11... | collective-permute-start | bytes 7077896 | tf_op jit(solution)/shard_map/ppermute | solution.py:491
  34.7 39.0 %collective-permute-start.3 = (bf16[2,4,256,384]{3,2,1,0:T(8,128)(2,1)}, bf16[2,4,256,384]{3,2,1,0:T(8,128)(2,1)}, u32[]{:S(2)}, u32[]{:S(2)}) collective-permute-start(bf16[2,4,256,384]{3,2,1,0:T(8,128)(2,1)} %interpolate.5.own_ref), channel_id=1, source_target_pairs={{0,1},{1,0},{2,3},{3,2},{4,5},{5,4},{6,7},{7,6},{8,9},{9,8},{10,11... | collective-permute-start | bytes 4718600 | tf_op jit(solution)/shard_map/ppermute | solution.py:491
  43.6 39.6 %collective-permute-start.4 = (bf16[2,4,256,384]{3,2,1,0:T(8,128)(2,1)}, bf16[2,4,256,384]{3,2,1,0:T(8,128)(2,1)S(1)}, u32[]{:S(2)}, u32[]{:S(2)}) collective-permute-start(bf16[2,4,256,384]{3,2,1,0:T(8,128)(2,1)} %interpolate.6.own_ref), channel_id=1, source_target_pairs={{0,1},{1,0},{2,3},{3,2},{4,5},{5,4},{6,7},{7,6},{8,9},{9,8},{10,11... | collective-permute-start | bytes 4718600 | tf_op jit(solution)/shard_map/ppermute | solution.py:491
  49.4 2.6 collective-permute-start.2
  57.8 13.9 %collective-permute-start.13 = (bf16[2,2,64,256]{3,2,1,0:T(8,128)(2,1)}, bf16[2,2,64,256]{3,2,1,0:T(8,128)(2,1)S(1)}, u32[]{:S(2)}, u32[]{:S(2)}) collective-permute-start(bf16[2,2,64,256]{3,2,1,0:T(8,128)(2,1)} %get-tuple-element.42), channel_id=1, source_target_pairs={{0,4},{4,0},{8,12},{12,8},{1,5},{5,1},{9,13},{13,9},{2,6},{6,2},{1... | collective-permute-start | bytes 393224 | tf_op jit(solution)/shard_map/ppermute | solution.py:491
  59.3 14.0 %collective-permute-start.14 = (bf16[2,2,64,256]{3,2,1,0:T(8,128)(2,1)}, bf16[2,2,64,256]{3,2,1,0:T(8,128)(2,1)S(1)}, u32[]{:S(2)}, u32[]{:S(2)}) collective-permute-start(bf16[2,2,64,256]{3,2,1,0:T(8,128)(2,1)} %get-tuple-element.43), channel_id=1, source_target_pairs={{0,8},{4,12},{8,0},{12,4},{1,9},{5,13},{9,1},{13,5},{2,10},{6,14},... | collective-permute-start | bytes 393224 | tf_op jit(solution)/shard_map/ppermute | solution.py:491
  60.8 55.4 %collective-permute-start.6 = (bf16[2,2,4,32,256]{4,3,2,1,0:T(8,128)(2,1)}, bf16[2,2,4,32,256]{4,3,2,1,0:T(8,128)(2,1)S(1)}, u32[]{:S(2)}, u32[]{:S(2)}) collective-permute-start(bf16[2,2,4,32,256]{4,3,2,1,0:T(8,128)(2,1)} %get-tuple-element.33.refs_1_), channel_id=1, source_target_pairs={{0,2},{2,0},{1,3},{3,1},{4,6},{6,4},{5,7},{7,5},{8,10},{10,8},{9,1... | collective-permute-start | bytes 786440 | tf_op jit(solution)/shard_map/ppermute | solution.py:491
  71.6 44.6 %collective-permute-start.22 = (bf16[2,6,64,256]{3,2,1,0:T(8,128)(2,1)}, bf16[2,6,64,256]{3,2,1,0:T(8,128)(2,1)S(1)}, u32[]{:S(2)}, u32[]{:S(2)}) collective-permute-start(bf16[2,6,64,256]{3,2,1,0:T(8,128)(2,1)} %get-tuple-element.54), channel_id=1, source_target_pairs={{0,4},{4,0},{8,12},{12,8},{1,5},{5,1},{9,13},{13,9},{2,6},{6,2},{1... | collective-permute-start | bytes 1179656 | tf_op jit(solution)/shard_map/ppermute | solution.py:491
  73.3 45.4 %collective-permute-start.23 = (bf16[2,6,64,256]{3,2,1,0:T(8,128)(2,1)}, bf16[2,6,64,256]{3,2,1,0:T(8,128)(2,1)S(1)}, u32[]{:S(2)}, u32[]{:S(2)}) collective-permute-start(bf16[2,6,64,256]{3,2,1,0:T(8,128)(2,1)} %get-tuple-element.55), channel_id=1, source_target_pairs={{0,8},{4,12},{8,0},{12,4},{1,9},{5,13},{9,1},{13,5},{2,10},{6,14},... | collective-permute-start | bytes 1179656 | tf_op jit(solution)/shard_map/ppermute | solution.py:491
  73.7 46.2 %collective-permute-start.24 = (bf16[2,6,64,256]{3,2,1,0:T(8,128)(2,1)}, bf16[2,6,64,256]{3,2,1,0:T(8,128)(2,1)S(1)}, u32[]{:S(2)}, u32[]{:S(2)}) collective-permute-start(bf16[2,6,64,256]{3,2,1,0:T(8,128)(2,1)} %get-tuple-element.56), channel_id=1, source_target_pairs={{0,12},{4,8},{8,4},{12,0},{1,13},{5,9},{9,5},{13,1},{2,14},{6,10},... | collective-permute-start | bytes 1179656 | tf_op jit(solution)/shard_map/ppermute | solution.py:491
  83.3 19.9 %copy-start.33 = (bf16[2,4,64,256]{3,2,1,0:T(8,128)(2,1)S(1)}, bf16[2,4,64,256]{3,2,1,0:T(8,128)(2,1)}, u32[]{:S(2)}) copy-start(bf16[2,4,64,256]{3,2,1,0:T(8,128)(2,1)} %get-tuple-element.46) | copy-start | bytes 786436
  83.3 33.0 %copy-start.30 = (bf16[2,4,64,256]{3,2,1,0:T(8,128)(2,1)S(1)}, bf16[2,4,64,256]{3,2,1,0:T(8,128)(2,1)}, u32[]{:S(2)}) copy-start(bf16[2,4,64,256]{3,2,1,0:T(8,128)(2,1)} %get-tuple-element.47) | copy-start | bytes 786436
  83.3 33.0 %copy-start.28 = (bf16[2,4,64,256]{3,2,1,0:T(8,128)(2,1)S(1)}, bf16[2,4,64,256]{3,2,1,0:T(8,128)(2,1)}, u32[]{:S(2)}) copy-start(bf16[2,4,64,256]{3,2,1,0:T(8,128)(2,1)} %get-tuple-element.48) | copy-start | bytes 786436
  83.3 19.9 %collective-permute-start.15 = (bf16[2,2,64,256]{3,2,1,0:T(8,128)(2,1)S(1)}, bf16[2,2,64,256]{3,2,1,0:T(8,128)(2,1)S(1)}, u32[]{:S(2)}, u32[]{:S(2)}) collective-permute-start(bf16[2,2,64,256]{3,2,1,0:T(8,128)(2,1)S(1)} %copy-done.39), channel_id=1, source_target_pairs={{0,12},{4,8},{8,4},{12,0},{1,13},{5,9},{9,5},{13,1},{2,14},{6,10},... | collective-permute-start | bytes 393224 | tf_op jit(solution)/shard_map/ppermute | solution.py:491
  103.1 25.6 %copy-start.20 = (bf16[2,2,64,256]{3,2,1,0:T(8,128)(2,1)}, bf16[2,2,64,256]{3,2,1,0:T(8,128)(2,1)S(1)}, u32[]{:S(2)}) copy-start(bf16[2,2,64,256]{3,2,1,0:T(8,128)(2,1)S(1)} %collective-permute-done.15.refs_4_) | copy-start | bytes 393220
  103.1 26.2 %collective-permute-start.16 = (bf16[2,4,64,256]{3,2,1,0:T(8,128)(2,1)S(1)}, bf16[2,4,64,256]{3,2,1,0:T(8,128)(2,1)S(1)}, u32[]{:S(2)}, u32[]{:S(2)}) collective-permute-start(bf16[2,4,64,256]{3,2,1,0:T(8,128)(2,1)S(1)} %copy-done.33), channel_id=1, source_target_pairs={{0,4},{4,0},{8,12},{12,8},{1,5},{5,1},{9,13},{13,9},{2,6},{6,2},{1... | collective-permute-start | bytes 786440 | tf_op jit(solution)/shard_map/ppermute | solution.py:491
  116.2 12.6 %copy-start.7 = (bf16[2,2,4,32,256]{4,3,2,1,0:T(8,128)(2,1)}, bf16[2,2,4,32,256]{4,3,2,1,0:T(8,128)(2,1)S(1)}, u32[]{:S(2)}) copy-start(bf16[2,2,4,32,256]{4,3,2,1,0:T(8,128)(2,1)S(1)} %collective-permute-done.6.refs_5_) | copy-start | bytes 786436
  116.2 21.5 %collective-permute-start.17 = (bf16[2,4,64,256]{3,2,1,0:T(8,128)(2,1)S(1)}, bf16[2,4,64,256]{3,2,1,0:T(8,128)(2,1)S(1)}, u32[]{:S(2)}, u32[]{:S(2)}) collective-permute-start(bf16[2,4,64,256]{3,2,1,0:T(8,128)(2,1)S(1)} %copy-done.30), channel_id=1, source_target_pairs={{0,8},{4,12},{8,0},{12,4},{1,9},{5,13},{9,1},{13,5},{2,10},{6,14},... | collective-permute-start | bytes 786440 | tf_op jit(solution)/shard_map/ppermute | solution.py:491
  116.3 22.7 %collective-permute-start.18 = (bf16[2,4,64,256]{3,2,1,0:T(8,128)(2,1)S(1)}, bf16[2,4,64,256]{3,2,1,0:T(8,128)(2,1)S(1)}, u32[]{:S(2)}, u32[]{:S(2)}) collective-permute-start(bf16[2,4,64,256]{3,2,1,0:T(8,128)(2,1)S(1)} %copy-done.28), channel_id=1, source_target_pairs={{0,12},{4,8},{8,4},{12,0},{1,13},{5,9},{9,5},{13,1},{2,14},{6,10},... | collective-permute-start | bytes 786440 | tf_op jit(solution)/shard_map/ppermute | solution.py:491
  118.7 21.2 %collective-permute-start.19 = (bf16[2,4,64,256]{3,2,1,0:T(8,128)(2,1)}, bf16[2,4,64,256]{3,2,1,0:T(8,128)(2,1)S(1)}, u32[]{:S(2)}, u32[]{:S(2)}) collective-permute-start(bf16[2,4,64,256]{3,2,1,0:T(8,128)(2,1)} %get-tuple-element.50), channel_id=1, source_target_pairs={{0,4},{4,0},{8,12},{12,8},{1,5},{5,1},{9,13},{13,9},{2,6},{6,2},{1... | collective-permute-start | bytes 786440 | tf_op jit(solution)/shard_map/ppermute | solution.py:491
  119.8 39.6 %collective-permute-start.20 = (bf16[2,4,64,256]{3,2,1,0:T(8,128)(2,1)}, bf16[2,4,64,256]{3,2,1,0:T(8,128)(2,1)S(1)}, u32[]{:S(2)}, u32[]{:S(2)}) collective-permute-start(bf16[2,4,64,256]{3,2,1,0:T(8,128)(2,1)} %get-tuple-element.51), channel_id=1, source_target_pairs={{0,8},{4,12},{8,0},{12,4},{1,9},{5,13},{9,1},{13,5},{2,10},{6,14},... | collective-permute-start | bytes 786440 | tf_op jit(solution)/shard_map/ppermute | solution.py:491
  120.8 16.9 %copy-start.26 = (bf16[2,4,64,256]{3,2,1,0:T(8,128)(2,1)S(1)}, bf16[2,4,64,256]{3,2,1,0:T(8,128)(2,1)}, u32[]{:S(2)}) copy-start(bf16[2,4,64,256]{3,2,1,0:T(8,128)(2,1)} %get-tuple-element.52) | copy-start | bytes 786436
  120.8 18.2 %copy-start.3 = (bf16[2,4,4,32,256]{4,3,2,1,0:T(8,128)(2,1)S(1)}, bf16[2,4,4,32,256]{4,3,2,1,0:T(8,128)(2,1)}, u32[]{:S(2)}) copy-start(bf16[2,4,4,32,256]{4,3,2,1,0:T(8,128)(2,1)} %get-tuple-element.35.refs_3_) | copy-start | bytes 1572868
  129.4 11.7 %copy-start.31 = (bf16[2,4,64,256]{3,2,1,0:T(8,128)(2,1)}, bf16[2,4,64,256]{3,2,1,0:T(8,128)(2,1)S(1)}, u32[]{:S(2)}) copy-start(bf16[2,4,64,256]{3,2,1,0:T(8,128)(2,1)S(1)} %collective-permute-done.16.refs_2_) | copy-start | bytes 786436
  129.4 38.8 %collective-permute-start.7 = (bf16[2,4,4,32,256]{4,3,2,1,0:T(8,128)(2,1)S(1)}, bf16[2,4,4,32,256]{4,3,2,1,0:T(8,128)(2,1)S(1)}, u32[]{:S(2)}, u32[]{:S(2)}) collective-permute-start(bf16[2,4,4,32,256]{4,3,2,1,0:T(8,128)(2,1)S(1)} %copy-done.2), channel_id=1, source_target_pairs={{0,2},{2,0},{1,3},{3,1},{4,6},{6,4},{5,7},{7,5},{8,10},{10,8},{9,1... | collective-permute-start | bytes 1572872 | tf_op jit(solution)/shard_map/ppermute | solution.py:491
  137.7 22.3 %collective-permute-start.21 = (bf16[2,4,64,256]{3,2,1,0:T(8,128)(2,1)S(1)}, bf16[2,4,64,256]{3,2,1,0:T(8,128)(2,1)S(1)}, u32[]{:S(2)}, u32[]{:S(2)}) collective-permute-start(bf16[2,4,64,256]{3,2,1,0:T(8,128)(2,1)S(1)} %copy-done.26), channel_id=1, source_target_pairs={{0,12},{4,8},{8,4},{12,0},{1,13},{5,9},{9,5},{13,1},{2,14},{6,10},... | collective-permute-start | bytes 786440 | tf_op jit(solution)/shard_map/ppermute | solution.py:491
  139.0 35.5 %collective-permute-start.8 = (bf16[2,4,4,32,256]{4,3,2,1,0:T(8,128)(2,1)S(1)}, bf16[2,4,4,32,256]{4,3,2,1,0:T(8,128)(2,1)S(1)}, u32[]{:S(2)}, u32[]{:S(2)}) collective-permute-start(bf16[2,4,4,32,256]{4,3,2,1,0:T(8,128)(2,1)S(1)} %copy-done.3), channel_id=1, source_target_pairs={{0,2},{2,0},{1,3},{3,1},{4,6},{6,4},{5,7},{7,5},{8,10},{10,8},{9,1... | collective-permute-start | bytes 1572872 | tf_op jit(solution)/shard_map/ppermute | solution.py:491
  140.0 152.0 %collective-permute-start.28 = (bf16[2,6,64,1024]{3,2,1,0:T(8,128)(2,1)}, bf16[2,6,64,1024]{3,2,1,0:T(8,128)(2,1)S(1)}, u32[]{:S(2)}, u32[]{:S(2)}) collective-permute-start(bf16[2,6,64,1024]{3,2,1,0:T(8,128)(2,1)} %cross_transform.9.refs_4_), channel_id=1, source_target_pairs={{0,2},{2,0},{1,3},{3,1},{4,6},{6,4},{5,7},{7,5},{8,10},{10,8},{9,1... | collective-permute-start | bytes 4718600 | tf_op jit(solution)/shard_map/ppermute | solution.py:491
  141.1 18.9 %copy-start = (bf16[2,6,4,32,256]{4,3,2,1,0:T(8,128)(2,1)S(1)}, bf16[2,6,4,32,256]{4,3,2,1,0:T(8,128)(2,1)}, u32[]{:S(2)}) copy-start(bf16[2,6,4,32,256]{4,3,2,1,0:T(8,128)(2,1)} %get-tuple-element.36.refs_4_) | copy-start | bytes 2359300
  159.5 100.2 %collective-permute-start.26 = (bf16[2,4,64,1024]{3,2,1,0:T(8,128)(2,1)}, bf16[2,4,64,1024]{3,2,1,0:T(8,128)(2,1)S(1)}, u32[]{:S(2)}, u32[]{:S(2)}) collective-permute-start(bf16[2,4,64,1024]{3,2,1,0:T(8,128)(2,1)} %cross_transform.7.refs_2_), channel_id=1, source_target_pairs={{0,2},{2,0},{1,3},{3,1},{4,6},{6,4},{5,7},{7,5},{8,10},{10,8},{9,1... | collective-permute-start | bytes 3145736 | tf_op jit(solution)/shard_map/ppermute | solution.py:491
  160.0 68.5 %collective-permute-start.9 = (bf16[2,6,4,32,256]{4,3,2,1,0:T(8,128)(2,1)S(1)}, bf16[2,6,4,32,256]{4,3,2,1,0:T(8,128)(2,1)S(1)}, u32[]{:S(2)}, u32[]{:S(2)}) collective-permute-start(bf16[2,6,4,32,256]{4,3,2,1,0:T(8,128)(2,1)S(1)} %copy-done), channel_id=1, source_target_pairs={{0,2},{2,0},{1,3},{3,1},{4,6},{6,4},{5,7},{7,5},{8,10},{10,8},{9,1... | collective-permute-start | bytes 2359304 | tf_op jit(solution)/shard_map/ppermute | solution.py:491
  168.2 123.8 %collective-permute-start.27 = (bf16[2,4,64,1024]{3,2,1,0:T(8,128)(2,1)}, bf16[2,4,64,1024]{3,2,1,0:T(8,128)(2,1)S(1)}, u32[]{:S(2)}, u32[]{:S(2)}) collective-permute-start(bf16[2,4,64,1024]{3,2,1,0:T(8,128)(2,1)} %cross_transform.8.refs_3_), channel_id=1, source_target_pairs={{0,2},{2,0},{1,3},{3,1},{4,6},{6,4},{5,7},{7,5},{8,10},{10,8},{9,1... | collective-permute-start | bytes 3145736 | tf_op jit(solution)/shard_map/ppermute | solution.py:491
  174.6 54.0 %copy-start.5 = (bf16[2,4,4,32,256]{4,3,2,1,0:T(8,128)(2,1)}, bf16[2,4,4,32,256]{4,3,2,1,0:T(8,128)(2,1)S(1)}, u32[]{:S(2)}) copy-start(bf16[2,4,4,32,256]{4,3,2,1,0:T(8,128)(2,1)S(1)} %collective-permute-done.8.refs_7_) | copy-start | bytes 1572868
  174.6 83.4 %collective-permute-start.25 = (bf16[2,2,64,1024]{3,2,1,0:T(8,128)(2,1)}, bf16[2,2,64,1024]{3,2,1,0:T(8,128)(2,1)S(1)}, u32[]{:S(2)}, u32[]{:S(2)}) collective-permute-start(bf16[2,2,64,1024]{3,2,1,0:T(8,128)(2,1)} %cross_transform.6.refs_1_), channel_id=1, source_target_pairs={{0,2},{2,0},{1,3},{3,1},{4,6},{6,4},{5,7},{7,5},{8,10},{10,8},{9,1... | collective-permute-start | bytes 1572872 | tf_op jit(solution)/shard_map/ppermute | solution.py:491
  232.8 28.5 %collective-permute-start.31 = (bf16[2,8,32,256]{3,2,1,0:T(8,128)(2,1)}, bf16[2,8,32,256]{3,2,1,0:T(8,128)(2,1)S(1)}, u32[]{:S(2)}, u32[]{:S(2)}) collective-permute-start(bf16[2,8,32,256]{3,2,1,0:T(8,128)(2,1)} %get-tuple-element.60), channel_id=1, source_target_pairs={{0,12},{4,8},{8,4},{12,0},{1,13},{5,9},{9,5},{13,1},{2,14},{6,10},... | collective-permute-start | bytes 786440 | tf_op jit(solution)/shard_map/ppermute | solution.py:491
  238.1 19.8 %copy-start.38 = (bf16[2,8,32,256]{3,2,1,0:T(8,128)(2,1)S(1)}, bf16[2,8,32,256]{3,2,1,0:T(8,128)(2,1)}, u32[]{:S(2)}) copy-start(bf16[2,8,32,256]{3,2,1,0:T(8,128)(2,1)} %get-tuple-element.59) | copy-start | bytes 786436
  238.1 23.2 %copy-start.27 = (bf16[2,8,32,256]{3,2,1,0:T(8,128)(2,1)S(1)}, bf16[2,8,32,256]{3,2,1,0:T(8,128)(2,1)}, u32[]{:S(2)}) copy-start(bf16[2,8,32,256]{3,2,1,0:T(8,128)(2,1)} %get-tuple-element.40) | copy-start | bytes 786436
  238.1 41.2 %copy-start.29 = (bf16[2,8,32,256]{3,2,1,0:T(8,128)(2,1)S(1)}, bf16[2,8,32,256]{3,2,1,0:T(8,128)(2,1)}, u32[]{:S(2)}) copy-start(bf16[2,8,32,256]{3,2,1,0:T(8,128)(2,1)} %get-tuple-element.39) | copy-start | bytes 786436
  257.9 34.0 %copy-start.11 = (bf16[2,2,64,1024]{3,2,1,0:T(8,128)(2,1)}, bf16[2,2,64,1024]{3,2,1,0:T(8,128)(2,1)S(1)}, u32[]{:S(2)}) copy-start(bf16[2,2,64,1024]{3,2,1,0:T(8,128)(2,1)S(1)} %collective-permute-done.25.refs_5_) | copy-start | bytes 1572868
  257.9 21.4 %collective-permute-start.30 = (bf16[2,8,32,256]{3,2,1,0:T(8,128)(2,1)S(1)}, bf16[2,8,32,256]{3,2,1,0:T(8,128)(2,1)S(1)}, u32[]{:S(2)}, u32[]{:S(2)}) collective-permute-start(bf16[2,8,32,256]{3,2,1,0:T(8,128)(2,1)S(1)} %copy-done.38), channel_id=1, source_target_pairs={{0,8},{4,12},{8,0},{12,4},{1,9},{5,13},{9,1},{13,5},{2,10},{6,14},... | collective-permute-start | bytes 786440 | tf_op jit(solution)/shard_map/ppermute | solution.py:491
  259.7 32.3 %copy-start.9 = (bf16[2,4,64,1024]{3,2,1,0:T(8,128)(2,1)}, bf16[2,4,64,1024]{3,2,1,0:T(8,128)(2,1)S(1)}, u32[]{:S(2)}) copy-start(bf16[2,4,64,1024]{3,2,1,0:T(8,128)(2,1)S(1)} %collective-permute-done.26.refs_6_) | copy-start | bytes 3145732
  259.7 19.6 %collective-permute-start.29 = (bf16[2,8,32,256]{3,2,1,0:T(8,128)(2,1)}, bf16[2,8,32,256]{3,2,1,0:T(8,128)(2,1)S(1)}, u32[]{:S(2)}, u32[]{:S(2)}) collective-permute-start(bf16[2,8,32,256]{3,2,1,0:T(8,128)(2,1)} %get-tuple-element.58), channel_id=1, source_target_pairs={{0,4},{4,0},{8,12},{12,8},{1,5},{5,1},{9,13},{13,9},{2,6},{6,2},{1... | collective-permute-start | bytes 786440 | tf_op jit(solution)/shard_map/ppermute | solution.py:491
  261.3 24.0 %copy-start.15 = (bf16[2,8,32,256]{3,2,1,0:T(8,128)(2,1)}, bf16[2,8,32,256]{3,2,1,0:T(8,128)(2,1)S(1)}, u32[]{:S(2)}) copy-start(bf16[2,8,32,256]{3,2,1,0:T(8,128)(2,1)S(1)} %collective-permute-done.31.refs_4_) | copy-start | bytes 786436
  261.3 44.7 %collective-permute-start.12 = (bf16[2,8,32,256]{3,2,1,0:T(8,128)(2,1)S(1)}, bf16[2,8,32,256]{3,2,1,0:T(8,128)(2,1)S(1)}, u32[]{:S(2)}, u32[]{:S(2)}) collective-permute-start(bf16[2,8,32,256]{3,2,1,0:T(8,128)(2,1)S(1)} %copy-done.27), channel_id=1, source_target_pairs={{0,12},{4,8},{8,4},{12,0},{1,13},{5,9},{9,5},{13,1},{2,14},{6,10},... | collective-permute-start | bytes 786440 | tf_op jit(solution)/shard_map/ppermute | solution.py:491
  279.3 26.7 %collective-permute-start.11 = (bf16[2,8,32,256]{3,2,1,0:T(8,128)(2,1)S(1)}, bf16[2,8,32,256]{3,2,1,0:T(8,128)(2,1)S(1)}, u32[]{:S(2)}, u32[]{:S(2)}) collective-permute-start(bf16[2,8,32,256]{3,2,1,0:T(8,128)(2,1)S(1)} %copy-done.29), channel_id=1, source_target_pairs={{0,8},{4,12},{8,0},{12,4},{1,9},{5,13},{9,1},{13,5},{2,10},{6,14},... | collective-permute-start | bytes 786440 | tf_op jit(solution)/shard_map/ppermute | solution.py:491
  279.3 26.7 %collective-permute-start.10 = (bf16[2,8,32,256]{3,2,1,0:T(8,128)(2,1)}, bf16[2,8,32,256]{3,2,1,0:T(8,128)(2,1)S(1)}, u32[]{:S(2)}, u32[]{:S(2)}) collective-permute-start(bf16[2,8,32,256]{3,2,1,0:T(8,128)(2,1)} %get-tuple-element.38), channel_id=1, source_target_pairs={{0,4},{4,0},{8,12},{12,8},{1,5},{5,1},{9,13},{13,9},{2,6},{6,2},{1... | collective-permute-start | bytes 786440 | tf_op jit(solution)/shard_map/ppermute | solution.py:491
  (24 other events, 91.3 us)

commit v2 on v0

--- a/solution.py
+++ b/solution.py
@@ -2,7 +2,11 @@
 
 import jax
 import jax.numpy as jnp
+import ml_dtypes
+import numpy as np
 from jax import lax
+from jax.experimental import pallas as pl
+from jax.experimental.pallas import tpu as pltpu
 from jax.sharding import PartitionSpec as P
 
 F = 768
@@ -10,6 +14,9 @@
 E = 32
 HW = 8
 KT = 8
+
+LANES = 128
+ROWS = 16
 
 
 def with_halo(cells, sides, width):
@@ -35,7 +42,7 @@
     return (jnp.cos(angle).astype(jnp.bfloat16), jnp.sin(angle).astype(jnp.bfloat16))
 
 
-def on_device(polar, band_offset, tap_count, tap_weight):
+def general_path(polar, band_offset, tap_count, tap_weight):
     shape_all = polar.shape
     col_count = shape_all[2]
     freq_count = shape_all[3]
@@ -100,6 +107,595 @@
     return image_out
 
 
+CUTS = (6, 6, 4)
+PARTS = (8, 4, 4)
+SPLIT = 48
+VMEM = 60 * 1024 * 1024
+
+
+def host_table(row_ids, col_ids, length):
+    product = (row_ids[:, None] * col_ids[None, :]) % length
+    angle = product.astype(np.float32) * np.float32(2.0 * math.pi / length)
+    return (np.cos(angle).astype(ml_dtypes.bfloat16), np.sin(angle).astype(ml_dtypes.bfloat16))
+
+
+def params():
+    return pltpu.CompilerParams(vmem_limit_bytes=VMEM)
+
+
+def cost(flops, nbytes):
+    return pl.CostEstimate(flops=int(flops) // 1000, bytes_accessed=int(nbytes) // 1000, transcendentals=0)
+
+
+def after(values):
+    return [pl.BlockSpec(memory_space=pl.ANY)] * len(values)
+
+
+def band_kernel(offset_ref, count_ref, weight_ref, out_ref):
+    rows, freqs = offset_ref.shape
+
+    def tile(index, carry):
+        row = pl.ds(pl.multiple_of(index * ROWS, ROWS), ROWS)
+        for start in range(0, freqs, LANES):
+            lane = pl.ds(start, LANES)
+            base = offset_ref[row, lane] + HW
+            count = count_ref[row, lane]
+            zero = jnp.zeros((ROWS, LANES), jnp.float32)
+            slots = [
+                jnp.where(count > tap, weight_ref[tap, row, lane].astype(jnp.float32), zero)
+                for tap in range(KT)
+            ]
+            step = 1
+            while step < KT:
+                chosen = (base & step) != 0
+                slots = [jnp.where(chosen, slots[(r - step) % KT], slots[r]) for r in range(KT)]
+                step *= 2
+            for r in range(KT):
+                out_ref[r, row, lane] = slots[r].astype(jnp.bfloat16)
+        return carry
+
+    lax.fori_loop(0, rows // ROWS, tile, 0)
+
+
+def place_taps(band_offset, tap_count, tap_weight):
+    cols, freqs = band_offset.shape
+    step = cols // 2
+    return pl.pallas_call(
+        band_kernel,
+        grid=(2,),
+        in_specs=[
+            pl.BlockSpec((step, freqs), lambda i: (i, 0)),
+            pl.BlockSpec((step, freqs), lambda i: (i, 0)),
+            pl.BlockSpec((KT, step, freqs), lambda i: (0, i, 0)),
+        ],
+        out_specs=pl.BlockSpec((KT, step, freqs), lambda i: (0, i, 0)),
+        out_shape=jax.ShapeDtypeStruct((KT, cols, freqs), jnp.bfloat16),
+        compiler_params=params(),
+        cost_estimate=cost(100 * cols * freqs, 40 * cols * freqs),
+        name="place_taps",
+    )(band_offset, tap_count, tap_weight)
+
+
+def interp_rows(pad_ref, band_ref, offset_ref, out_ref):
+    _, cuts, cols, freqs = out_ref.shape
+
+    def tile(index, carry):
+        row = pl.multiple_of(index * ROWS, ROWS)
+        for f in range(freqs // LANES):
+            lane = pl.ds(f * LANES, LANES)
+            taps = [band_ref[r, pl.ds(row, ROWS), lane].astype(jnp.float32) for r in range(KT)]
+            base = offset_ref[pl.ds(row, ROWS), lane] + HW
+            past = [base > r for r in range(KT + 1)]
+            for part in range(2):
+                for cut in range(cuts):
+                    plane = part * cuts + cut
+                    near = [
+                        pad_ref[plane, f, pl.ds(row + d, ROWS), :] for d in range(2 * HW + 1)
+                    ]
+                    total = None
+                    for r in range(KT):
+                        value = jnp.where(past[r], near[r + KT], near[r])
+                        if r == 0:
+                            value = jnp.where(past[KT], near[2 * KT], value)
+                        value = value * taps[r]
+                        total = value if total is None else total + value
+                    out_ref[part, cut, pl.ds(row, ROWS), lane] = total.astype(jnp.bfloat16)
+        return carry
+
+    lax.fori_loop(0, cols // ROWS, tile, 0)
+
+
+def interp_kernel(polar_ref, band_ref, offset_ref, *refs, bordered):
+    out_ref, pad_ref = refs[-2:]
+    _, cuts, cols, freqs = polar_ref.shape
+    for part in range(2):
+        for cut in range(cuts):
+            plane = part * cuts + cut
+            for f in range(freqs // LANES):
+                lane = pl.ds(f * LANES, LANES)
+                if bordered:
+                    halo = refs[0][part, cut, :, lane].astype(jnp.float32)
+                else:
+                    halo = jnp.zeros((2 * HW, LANES), jnp.float32)
+                pad_ref[plane, f, pl.ds(0, HW), :] = halo[:HW]
+                pad_ref[plane, f, pl.ds(HW, cols), :] = polar_ref[part, cut, :, lane].astype(jnp.float32)
+                pad_ref[plane, f, pl.ds(HW + cols, HW), :] = halo[HW:]
+    interp_rows(pad_ref, band_ref, offset_ref, out_ref)
+
+
+def interpolate(polar, halo, taps, band_offset, first, count, earlier=()):
+    _, _, cols, freqs = polar.shape
+    group = 2
+    skip = first // group
+    border = [] if halo is None else [halo]
+    return pl.pallas_call(
+        lambda *refs: interp_kernel(*refs, bordered=len(border) == 1),
+        grid=(count // group,),
+        in_specs=[
+            pl.BlockSpec((2, group, cols, freqs), lambda i: (0, skip + i, 0, 0)),
+            pl.BlockSpec((KT, cols, freqs), lambda i: (0, 0, 0)),
+            pl.BlockSpec((cols, freqs), lambda i: (0, 0)),
+        ]
+        + [pl.BlockSpec((2, group, 2 * HW, freqs), lambda i: (0, skip + i, 0, 0))] * len(border)
+        + after(earlier),
+        out_specs=pl.BlockSpec((2, group, cols, freqs), lambda i: (0, i, 0, 0)),
+        out_shape=jax.ShapeDtypeStruct((2, count, cols, freqs), jnp.bfloat16),
+        scratch_shapes=[
+            pltpu.VMEM((2 * group, freqs // LANES, cols + 2 * HW, LANES), jnp.float32)
+        ],
+        compiler_params=params(),
+        cost_estimate=cost(2 * count * cols * freqs * 34, 8 * count * cols * freqs),
+        name="interpolate",
+    )(polar, taps, band_offset, *border, *earlier)
+
+
+def edge_kernel(polar_ref, halo_ref, band_ref, offset_ref, made_ref, out_ref, pad_ref):
+    del made_ref
+    _, cuts, rows, freqs = polar_ref.shape
+    for part in range(2):
+        for cut in range(cuts):
+            for f in range(freqs // LANES):
+                plane, lane = part * cuts + cut, pl.ds(f * LANES, LANES)
+                halo = halo_ref[part, cut, :, lane].astype(jnp.float32)
+                body = polar_ref[part, cut, :, lane].astype(jnp.float32)
+
+                @pl.when(pl.program_id(0) == 0)
+                def _():
+                    pad_ref[plane, f, pl.ds(0, HW), :] = halo[:HW]
+                    pad_ref[plane, f, pl.ds(HW, rows - HW), :] = body[: rows - HW]
+
+                @pl.when(pl.program_id(0) == 1)
+                def _():
+                    pad_ref[plane, f, pl.ds(0, rows - HW), :] = body[HW:]
+                    pad_ref[plane, f, pl.ds(rows - HW, HW), :] = halo[HW:]
+
+    interp_rows(pad_ref, band_ref, offset_ref, out_ref)
+
+
+def interpolate_edges(polar, halo, taps, band_offset, made):
+    _, count, cols, freqs = made.shape
+    wide = cols // (2 * ROWS) - 1
+    last = cols // ROWS - 1
+    return pl.pallas_call(
+        edge_kernel,
+        grid=(2,),
+        in_specs=[
+            pl.BlockSpec((2, count, 2 * ROWS, freqs), lambda i: (0, 0, i * wide, 0)),
+            pl.BlockSpec((2, count, 2 * HW, freqs), lambda i: (0, 0, 0, 0)),
+            pl.BlockSpec((KT, ROWS, freqs), lambda i: (0, i * last, 0)),
+            pl.BlockSpec((ROWS, freqs), lambda i: (i * last, 0)),
+            pl.BlockSpec(memory_space=pl.ANY),
+        ],
+        out_specs=pl.BlockSpec((2, count, ROWS, freqs), lambda i: (0, 0, i * last, 0)),
+        out_shape=jax.ShapeDtypeStruct(made.shape, jnp.bfloat16),
+        scratch_shapes=[pltpu.VMEM((2 * count, freqs // LANES, 2 * ROWS, LANES), jnp.float32)],
+        input_output_aliases={4: 0},
+        compiler_params=params(),
+        cost_estimate=cost(4 * count * ROWS * freqs * 34, 16 * count * ROWS * freqs),
+        name="interpolate_edges",
+    )(polar, halo, taps, band_offset, made)
+
+
+def range_kernel(ids_ref, own_ref, other_ref, *refs, blocks, earlier):
+    tables = refs[:blocks]
+    first_ref, *rest = refs[blocks + earlier :]
+    cuts, cols = own_ref.shape[1:3]
+    bins = tables[0].shape[2]
+    split = first_ref.shape[3]
+    scale = 1.0 / math.sqrt(F)
+    table = jnp.concatenate([ref[0, 0] for ref in tables], axis=0)
+    for cut in range(cuts):
+        real = [own_ref[0, cut], other_ref[0, cut]]
+        imag = [own_ref[1, cut], other_ref[1, cut]]
+        values = jnp.concatenate(
+            [
+                jnp.concatenate(real + [-v for v in imag], axis=1),
+                jnp.concatenate(imag + real, axis=1),
+            ],
+            axis=0,
+        )
+        product = lax.dot_general(
+            table, values, (((1,), (1,)), ((), ())), preferred_element_type=jnp.float32
+        )
+        product = (product * scale).astype(jnp.bfloat16)
+        for s in range(blocks):
+            for part in range(2):
+                value = product[s * bins : (s + 1) * bins, part * cols : (part + 1) * cols]
+                first_ref[part, cut, s] = value[:split]
+                rest[s][part, cut] = value[split:]
+
+
+def range_transform(ids, own, other, table, split, earlier=()):
+    _, count, cols, freqs = own.shape
+    _, blocks, bins, full = table.shape
+    rest = bins - split
+    group = 2
+
+    def block_of(s):
+        return pl.BlockSpec((1, 1, bins, full), lambda i, ids: (ids[1], ids[0] ^ s, 0, 0))
+
+    return pl.pallas_call(
+        lambda *refs: range_kernel(*refs, blocks=blocks, earlier=len(earlier)),
+        grid_spec=pltpu.PrefetchScalarGridSpec(
+            num_scalar_prefetch=1,
+            grid=(count // group,),
+            in_specs=[pl.BlockSpec((2, group, cols, freqs), lambda i, ids: (0, i, 0, 0))] * 2
+            + [block_of(s) for s in range(blocks)]
+            + after(earlier),
+            out_specs=[
+                pl.BlockSpec((2, group, blocks, split, cols), lambda i, ids: (0, i, 0, 0, 0))
+            ]
+            + [pl.BlockSpec((2, group, rest, cols), lambda i, ids: (0, i, 0, 0))] * blocks,
+        ),
+        out_shape=[jax.ShapeDtypeStruct((2, count, blocks, split, cols), jnp.bfloat16)]
+        + [jax.ShapeDtypeStruct((2, count, rest, cols), jnp.bfloat16)] * blocks,
+        compiler_params=params(),
+        cost_estimate=cost(4 * count * cols * full * blocks * bins, 12 * count * cols * freqs),
+        name="range_transform",
+    )(ids, own, other, *([table] * blocks), *earlier)
+
+
+def height_table(cuts, rows):
+    heights = []
+    for el in range(2):
+        pair = []
+        for parity in range(2):
+            h = el * cuts + parity + 2 * np.arange(cuts // 2)
+            cos, sin = (t.astype(np.float32) for t in host_table(h, np.arange(cuts), 2 * cuts))
+            sign = -1.0 if el and parity else 1.0
+            whole = sign * np.block([[cos, -sin], [sin, cos]])
+            pair.append(np.kron(whole, np.eye(rows, dtype=np.float32)))
+        heights.append(np.stack(pair))
+    return np.stack(heights).astype(ml_dtypes.bfloat16)
+
+
+def height_kernel(ids_ref, matrix_ref, *refs, chunks, sets, outs, scale, skipped):
+    ins = refs[: 2 * chunks]
+    out_refs = refs[2 * chunks + skipped :]
+    rows, lanes = ins[0].shape[-2:]
+    half = matrix_ref.shape[2] // (2 * rows)
+    for index in range(sets):
+        sums, differences = [], []
+        for part in range(2):
+            for own, other in zip(ins[:chunks], ins[chunks:]):
+                pad = (index,) if len(own.shape) == 5 else ()
+                for e in range(own.shape[1]):
+                    a, b = own[(part, e) + pad], other[(part, e) + pad]
+                    sums.append(a + b)
+                    differences.append(a - b)
+        results = [
+            jnp.dot(
+                matrix_ref[0, parity],
+                jnp.concatenate(values, axis=0),
+                preferred_element_type=jnp.float32,
+            )
+            for parity, values in enumerate((sums, differences))
+        ]
+        h = 0
+        for ref in out_refs[index * outs : (index + 1) * outs]:
+            for row in range(ref.shape[1]):
+                for part in range(2):
+                    start = (part * half + h // 2) * rows
+                    value = results[h % 2][start : start + rows]
+                    if scale is not None:
+                        value = value * scale
+                    ref[part, row] = value.astype(jnp.bfloat16)
+                h += 1
+
+
+def first_heights(ids, matrix, own, other, pair, parts, earlier=()):
+    chunks = len(own)
+    _, _, blocks, split, cols = own[0].shape
+    total = sum(v.shape[1] for v in own)
+    sets = 2
+    spec = [
+        pl.BlockSpec((2, v.shape[1], sets, ROWS, cols), lambda i, ids: (0, 0, pair, i, 0))
+        for v in own
+    ]
+    outs = list(parts) * sets
+    return pl.pallas_call(
+        lambda *refs: height_kernel(
+            *refs, chunks=chunks, sets=sets, outs=len(parts), scale=None, skipped=len(earlier)
+        ),
+        grid_spec=pltpu.PrefetchScalarGridSpec(
+            num_scalar_prefetch=1,
+            grid=(split // ROWS,),
+            in_specs=[pl.BlockSpec((1,) + matrix.shape[1:], lambda i, ids: (ids[2], 0, 0, 0))]
+            + spec
+            + spec
+            + after(earlier),
+            out_specs=[pl.BlockSpec((2, h, ROWS, cols), lambda i, ids: (0, 0, i, 0)) for h in outs],
+        ),
+        out_shape=[jax.ShapeDtypeStruct((2, h, split, cols), jnp.bfloat16) for h in outs],
+        compiler_params=params(),
+        cost_estimate=cost(sets * split * cols * 32768, 12 * sets * total * split * cols),
+        name="first_heights",
+    )(ids, matrix, *own, *other, *earlier)
+
+
+def last_heights(ids, matrix, own, other, places, image, shape, skip, rows, earlier=()):
+    chunks = len(own)
+    full = own[0].shape[3]
+    width = min(full, 512)
+    total = sum(v.shape[1] for v in own)
+
+    def chunk(v, place):
+        return pl.BlockSpec(
+            (2, v.shape[1], ROWS, width), lambda i, j, ids: (0, 0, place // ROWS + i, j)
+        )
+
+    spec = [chunk(v, place) for v, place in zip(own, places)]
+    extra = [] if image is None else [image]
+    first = skip // ROWS
+    return pl.pallas_call(
+        lambda *refs: height_kernel(
+            *refs,
+            chunks=chunks,
+            sets=1,
+            outs=1,
+            scale=1.0 / math.sqrt(2 * total),
+            skipped=len(earlier) + len(extra),
+        ),
+        grid_spec=pltpu.PrefetchScalarGridSpec(
+            num_scalar_prefetch=1,
+            grid=(rows // ROWS, full // width),
+            in_specs=[pl.BlockSpec((1,) + matrix.shape[1:], lambda i, j, ids: (ids[2], 0, 0, 0))]
+            + spec
+            + spec
+            + after(extra)
+            + after(earlier),
+            out_specs=pl.BlockSpec((2, total, ROWS, width), lambda i, j, ids: (0, 0, first + i, j)),
+        ),
+        out_shape=jax.ShapeDtypeStruct(shape, jnp.bfloat16),
+        input_output_aliases={2 + 2 * chunks: 0} if extra else {},
+        compiler_params=params(),
+        cost_estimate=cost(rows * full * 32768, 12 * total * rows * full),
+        name="last_heights",
+    )(ids, matrix, *own, *other, *extra, *earlier)
+
+
+def cross_kernel(ids_ref, *refs, groups, blocks, scale, skipped, outs):
+    ins = [refs[g * blocks : (g + 1) * blocks] for g in range(groups)]
+    cos_ref, sin_ref = refs[groups * blocks : groups * blocks + 2]
+    out_refs = refs[groups * blocks + 2 + skipped : -1]
+    rows_ref = refs[-1]
+    bins, cols = ins[0][0].shape[2:]
+    cuts = [group[0].shape[1] for group in ins]
+    rows = sum(cuts) * bins
+
+    @pl.when(pl.program_id(0) == 0)
+    def _():
+        for s in range(blocks):
+            start = pl.multiple_of((ids_ref[0] ^ s) * cols, cols)
+            for part in range(2):
+                place = part * rows
+                for group, count in zip(ins, cuts):
+                    rows_ref[pl.ds(place, count * bins), pl.ds(start, cols)] = group[s][
+                        part
+                    ].reshape(count * bins, cols)
+                    place += count * bins
+
+    values = rows_ref[...]
+    with_cos = jnp.dot(values, cos_ref[...], preferred_element_type=jnp.float32)
+    with_sin = jnp.dot(values, sin_ref[...], preferred_element_type=jnp.float32)
+    real = (with_cos[:rows] - with_sin[rows:]) * scale
+    imag = (with_sin[:rows] + with_cos[rows:]) * scale
+    for part, value in ((0, real), (1, imag)):
+        value = value.astype(jnp.bfloat16).reshape(sum(cuts), bins, value.shape[1])
+        place = 0
+        for ref in out_refs:
+            size = ref.shape[2]
+            ref[part] = value[:, place : place + size]
+            place += size
+
+
+def cross_transform(ids, ins, tables, scale, sizes=None, image=None, shape=None, place=0, earlier=()):
+    groups, blocks = len(ins), len(ins[0])
+    bins, cols = ins[0][0].shape[2:]
+    total = sum(group[0].shape[1] for group in ins)
+    full = tables[0].shape[1]
+    width = min(full, 512)
+    extra = [] if image is None else [image]
+    if shape is None:
+        shapes = [(2, total, size, full) for size in sizes]
+    else:
+        sizes, shapes = [bins], [shape]
+    result = pl.pallas_call(
+        lambda *refs: cross_kernel(
+            *refs,
+            groups=groups,
+            blocks=blocks,
+            scale=scale,
+            skipped=len(extra) + len(earlier),
+            outs=len(sizes),
+        ),
+        grid_spec=pltpu.PrefetchScalarGridSpec(
+            num_scalar_prefetch=1,
+            grid=(full // width,),
+            in_specs=[
+                pl.BlockSpec((2, v.shape[1], bins, cols), lambda i, ids: (0, 0, 0, 0))
+                for group in ins
+                for v in group
+            ]
+            + [pl.BlockSpec((full, width), lambda i, ids: (0, i))] * 2
+            + after(extra)
+            + after(earlier),
+            out_specs=[
+                pl.BlockSpec((2, total, size, width), lambda i, ids: (0, place, 0, i))
+                for size in sizes
+            ],
+            scratch_shapes=[pltpu.VMEM((2 * total * bins, full), jnp.bfloat16)],
+        ),
+        out_shape=[jax.ShapeDtypeStruct(v, jnp.bfloat16) for v in shapes],
+        input_output_aliases={1 + groups * blocks + 2: 0} if extra else {},
+        compiler_params=params(),
+        cost_estimate=cost(8 * total * bins * full * full, 8 * total * bins * full + 4 * full * full),
+        name="cross_transform",
+    )(ids, *[v for group in ins for v in group], *tables, *extra, *earlier)
+    return result if image is None and len(sizes) > 1 else result[0]
+
+
+def exchange(value, axis, s):
+    return lax.ppermute(value, axis, [(i, i ^ s) for i in range(lax.axis_size(axis))])
+
+
+def halo_rows(polar):
+    count = lax.axis_size("az")
+    cols = polar.shape[2]
+    ends = count - 1
+    head = lax.slice_in_dim(polar, 0, HW, axis=2)
+    tail = lax.slice_in_dim(polar, cols - HW, cols, axis=2)
+    return jnp.concatenate(
+        [
+            lax.ppermute(tail, "az", [(i, i + 1) for i in range(ends)]),
+            lax.ppermute(head, "az", [(i + 1, i) for i in range(ends)]),
+        ],
+        axis=2,
+    )
+
+
+def planned_path(polar, band_offset, tap_count, tap_weight):
+    _, cuts, cols, freqs = polar.shape
+    az_count = lax.axis_size("az")
+    fq_count = lax.axis_size("fq")
+    bins = F // (az_count * fq_count)
+    split = SPLIT
+    rest = bins - split
+    ids = jnp.stack([lax.axis_index("az"), lax.axis_index("fq"), lax.axis_index("el")])
+    tables = []
+    for core in range(fq_count):
+        order = np.concatenate([np.arange(freqs) + freqs * (core ^ s) for s in range(fq_count)])
+        blocks = []
+        for az in range(az_count):
+            ks = (az * fq_count + core) * bins + np.arange(bins)
+            blocks.append(np.concatenate(host_table(ks, order, F), axis=1))
+        tables.append(np.stack(blocks))
+    range_table = jnp.asarray(np.stack(tables))
+    cross_tables = [jnp.asarray(t) for t in host_table(np.arange(A), np.arange(A), A)]
+    matrix = jnp.asarray(height_table(cuts, ROWS))
+
+    taps = place_taps(band_offset, tap_count, tap_weight)
+    polar, taps = lax.optimization_barrier((polar, taps))
+    halo = halo_rows(polar)
+    starts = np.cumsum((0,) + CUTS)
+    last = len(CUTS) - 1
+    scale = 1.0 / math.sqrt(A)
+
+    def interp(i, earlier=()):
+        return interpolate(polar, halo, taps, band_offset, int(starts[i]), CUTS[i], earlier)
+
+    def to_owners(blocks):
+        come = {s: exchange(blocks[s], "az", s) for s in reversed(range(1, az_count))}
+        return [blocks[0]] + [come[s] for s in range(1, az_count)]
+
+    bare = interpolate(polar, None, taps, band_offset, 0, CUTS[0])
+    made = interpolate_edges(polar, halo, taps, band_offset, bare)
+    other = exchange(made, "fq", 1)
+    ahead = interp(1, (made,))
+    own_first, other_first, landed = [], [], []
+    moving = ([], ())
+    for i in range(last + 1):
+        first, *blocks = range_transform(ids, made, other, range_table, split, (ahead,))
+        if 0 < i < last:
+            ahead = interp(i + 1, (first,))
+        held = (first, blocks, ahead, moving)
+        first, blocks, ahead, moving = lax.optimization_barrier(held)
+        if i > 0:
+            landed.append(moving[0])
+            other_first.append(moving[1])
+        own_first.append(first)
+        moving = (to_owners(blocks), exchange(first, "el", 1))
+        if i < last:
+            made, other = ahead, exchange(ahead, "fq", 1)
+    c0 = cross_transform(ids, landed, cross_tables, scale, [rest], earlier=(first,))
+    c0, moving = lax.optimization_barrier((c0, moving))
+    landed.append(moving[0])
+    other_first.append(moving[1])
+    other_c0 = exchange(c0, "el", 1)
+
+    h1 = first_heights(ids, matrix, own_first, other_first, 1, PARTS, (c0,))
+    count = len(PARTS)
+    far = [h1[:count], h1[count:]]
+    h0 = first_heights(ids, matrix, own_first, other_first, 0, PARTS, (h1[0],))
+    near = [h0[:count], h0[count:]]
+    made = [[near[0][p], near[1][p], far[0][p], far[1][p]] for p in range(count)]
+    late = [rest - ROWS, ROWS]
+    c1, c2 = cross_transform(ids, landed[-1:], cross_tables, scale, late, earlier=(h0[0],))
+    other_c1 = exchange(c1, "el", 1)
+    arrived = [to_owners(made[0])]
+    shape = (2, cuts, bins, A)
+    full_scale = 1.0 / math.sqrt(A * 2 * cuts)
+    made[1], arrived[0] = lax.optimization_barrier((made[1], arrived[0]))
+    arrived.append(to_owners(made[1]))
+    image = cross_transform(
+        ids, [arrived[0]], cross_tables, full_scale, image=None, shape=shape, place=0, earlier=(c1,)
+    )
+    made[2], arrived[1], c2, other_c0, image = lax.optimization_barrier(
+        (made[2], arrived[1], c2, other_c0, image)
+    )
+    arrived.append(to_owners(made[2]))
+    other_c2 = exchange(c2, "el", 1)
+    image = cross_transform(
+        ids, [arrived[1]], cross_tables, full_scale, image=image, shape=shape, place=PARTS[0] // PARTS[1]
+    )
+    image = last_heights(
+        ids, matrix, [c0, c1], [other_c0, other_c1], (0, 0), image, shape, split, late[0]
+    )
+    image = last_heights(
+        ids, matrix, [c0, c2], [other_c0, other_c2], (late[0], 0), image, shape, split + late[0], late[1]
+    )
+    image = cross_transform(
+        ids,
+        [arrived[2]],
+        cross_tables,
+        full_scale,
+        image=image,
+        shape=shape,
+        place=(PARTS[0] + PARTS[1]) // PARTS[2],
+    )
+    return image
+
+
+def on_device(polar, band_offset, tap_count, tap_weight):
+    _, cuts, cols, freqs = polar.shape
+    az_count = lax.axis_size("az")
+    bins = F // (az_count * lax.axis_size("fq"))
+    fits = (
+        lax.axis_size("el") == 2
+        and lax.axis_size("fq") == 2
+        and az_count == 4
+        and cuts == sum(CUTS) == sum(PARTS)
+        and cols % (2 * LANES) == 0
+        and freqs % LANES == 0
+        and bins > SPLIT
+        and bins == 2 * SPLIT
+        and A % 512 == 0
+        and 2 * HW == ROWS
+    )
+    chosen = planned_path if fits else general_path
+    return chosen(polar, band_offset, tap_count, tap_weight)
+
+
 def solution(mesh):
     in_specs = (
         P(None, ("grp", "el"), "az", "fq"),

time: 841 us -> 212 us (0.25); the launches traced: 832 us -> 212 us
  matrix products: 355 us -> 0 us
  blocking collectives: 143 us -> 0 us
  waiting for transfers between devices: 176 us -> 47.5 us
  local copies, waits for them, and re-layouts: 113 us -> 6.2 us
  Pallas kernels: 0 us -> 105 us
  starting transfers between devices: 7.78 us -> 51.7 us
  other arithmetic: 21.6 us -> 0.61 us
  between operations: 14.4 us -> 0.21 us
    dot_general x13 -> x0, matrix products: 355 us -> none  [the longest x1 194 us: on_device(): jnp.einsum('jaf,ceaf->cejf', band_matrix, padded, preferred_element_type=...]
    all_gather x2 -> x0, waiting for transfers between devices: 176 us -> none  [the longest x1 151 us: on_device(): shard_piece = lax.all_gather(crossed, 'el', axis=1, tiled=True)]
    all_to_all x1 -> x0, blocking collectives: 143 us -> none  [on_device(): lax.all_to_all(ranged, 'az', split_axis=2, concat_axis=3, tiled=True)]
    pallas_call x0 -> x17, Pallas kernels: none -> 105 us  [the longest x5 32.9 us: cross_transform(): pl.pallas_call(lambda *refs: cross_kernel(*refs, groups=groups, blocks=bl...]
    ppermute x2 -> x29, waiting for transfers between devices: 0.01 us -> 47.5 us  [the longest x27 47.5 us: exchange(): lax.ppermute(value, axis, [(i, i ^ s) for i in range(lax.axis_size(axis))])]
    ppermute x2 -> x29, starting transfers between devices: 7.52 us -> 51.7 us  [the longest x27 45.5 us: exchange(): lax.ppermute(value, axis, [(i, i ^ s) for i in range(lax.axis_size(axis))])]
    unnamed x63 -> x41, local copies, waits for them, and re-layouts: 29 us -> 5.11 us
    slice x3 -> x1, local copies, waits for them, and re-layouts: 16.4 us -> 1.06 us  [halo_rows(): head = lax.slice_in_dim(polar, 0, HW, axis=2)]
  transfers between devices with their start and end apart: 4 -> 29, of which waited for: 2 -> 7; matrix products, arithmetic and copies ran while one was open for 5% -> 0% of each run, Pallas kernels for 0% -> 41%
where the time goes in v2:
time: 212 us
  Pallas kernels  105 us (50%)
  starting transfers between devices  51.7 us (24%)
  waiting for transfers between devices  47.5 us (22%)
  local copies, waits for them, and re-layouts  6.2 us (3%)
    ppermute x27, waiting for transfers between devices, exchange(): lax.ppermute(value, axis, [(i, i ^ s) for i in range(lax.axis_size(axis))])  47.5 us
    ppermute x27, starting transfers between devices, exchange(): lax.ppermute(value, axis, [(i, i ^ s) for i in range(lax.axis_size(axis))])  45.5 us
    pallas_call x5, Pallas kernels, cross_transform(): pl.pallas_call(lambda *refs: cross_kernel(*refs, groups=groups, blocks=bl...  32.9 us
    pallas_call x3, Pallas kernels, interpolate(): pl.pallas_call(lambda *refs: interp_kernel(*refs, bordered=len(border) ==...  23.9 us
    pallas_call x3, Pallas kernels, range_transform(): pl.pallas_call(lambda *refs: range_kernel(*refs, blocks=blocks, earlier=l...  22 us
    pallas_call x2, Pallas kernels, first_heights(): pl.pallas_call(lambda *refs: height_kernel(*refs, chunks=chunks, sets=set...  11.1 us
    pallas_call x2, Pallas kernels, last_heights(): pl.pallas_call(lambda *refs: height_kernel(*refs, chunks=chunks, sets=1,...  9.64 us
    unnamed x41, local copies, waits for them, and re-layouts  5.11 us
  transfers between devices with their start and end apart: 29, of which 7 were waited for; matrix products, arithmetic and copies ran while one was open for 0% of the time, Pallas kernels for 41%

profile of v2, /device:TPU:0, one launch (start us, length us, event | category | flops | bytes accessed | tf_op | source)
XLA Modules:
  0.0 211.7 jit_solution(6074429768095904475)
XLA Ops:
  0.0 3.2 %place_taps.1.refs_1_.band_ref = bf16[8,256,384]{2,1,0:T(8,128)(2,1)} custom-call(s32[256,384]{1,0:T(8,128)} %refs_2_.5, s32[256,384]{1,0:T(8,128)} %count_ref.1, bf16[8,256,384]{2,1,0:T(8,128)(2,1)} %weight_ref.1), custom_call_target="tpu_custom_call" | custom-call | flops 9830 | bytes 3932 | tf_op jit(solution)/shard_map/place_taps/pallas_call | solution.py:163
  3.2 1.1 fusion
  4.3 4.9 %collective-permute-start = (bf16[2,16,8,384]{3,2,1,0:T(8,128)(2,1)S(1)}, bf16[2,16,8,384]{3,2,1,0:T(8,128)(2,1)S(1)}, u32[]{:S(2)}, u32[]{:S(2)}) collective-permute-start(bf16[2,16,8,384]{3,2,1,0:T(8,128)(2,1)S(1)} %get-tuple-element.172), channel_id=1, source_target_pairs={{0,4},{4,8},{8,12},{1,5},{5,9},{9,13},{2,6},{6,10},{10,14},{3,7},{... | collective-permute-start | bytes 589832 | tf_op jit(solution)/shard_map/ppermute | solution.py:570
  9.2 1.3 collective-permute-start.1
  10.5 8.6 %interpolate.3.made_ref = bf16[2,6,256,384]{3,2,1,0:T(8,128)(2,1)} custom-call(bf16[2,16,256,384]{3,2,1,0:T(8,128)(2,1)} %refs_0_.2, bf16[8,256,384]{2,1,0:T(8,128)(2,1)} %place_taps.1.refs_1_.band_ref, s32[256,384]{1,0:T(8,128)} %refs_2_.5), custom_call_target="tpu_custom_call" | custom-call | flops 40108 | bytes 4718 | tf_op jit(solution)/shard_map/interpolate/pallas_call | solution.py:231
  19.2 0.7 copy-done.3
  19.9 2.8 %interpolate_edges.1.refs_4_.refs_1_ = bf16[2,6,256,384]{3,2,1,0:T(8,128)(2,1)} custom-call(bf16[2,16,256,384]{3,2,1,0:T(8,128)(2,1)} %refs_0_.2, bf16[2,16,16,384]{3,2,1,0:T(8,128)(2,1)} %copy-done.3, bf16[8,256,384]{2,1,0:T(8,128)(2,1)} %place_taps.1.refs_1_.band_ref, s32[256,384]{1,0:T(8,128)} %refs_2_.5, ...), custom_call_target="tpu_custom_call", output_to_operand_aliasing={{}: (4, {})} | custom-call | flops 5013 | bytes 589 | tf_op jit(solution)/shard_map/interpolate_edges/pallas_call | solution.py:279
  23.3 8.6 %interpolate.4.refs_7_.refs_1_ = bf16[2,6,256,384]{3,2,1,0:T(8,128)(2,1)} custom-call(bf16[2,16,256,384]{3,2,1,0:T(8,128)(2,1)} %refs_0_.2, bf16[8,256,384]{2,1,0:T(8,128)(2,1)} %place_taps.1.refs_1_.band_ref, s32[256,384]{1,0:T(8,128)} %refs_2_.5, bf16[2,16,16,384]{3,2,1,0:T(8,128)(2,1)} %copy-done.3, bf16[2,6,256,384]{3,2,1,0:T(8,128)(2,1)} %interpolate_edges.1.refs_4_.refs_1_), custom_call_target="tpu_custom_call" | custom-call | flops 40108 | bytes 4718 | tf_op jit(solution)/shard_map/interpolate/pallas_call | solution.py:231
  31.9 8.0 %range_transform.3 = (bf16[2,6,4,48,256]{4,3,2,1,0:T(8,128)(2,1)}, bf16[2,6,48,256]{3,2,1,0:T(8,128)(2,1)}, bf16[2,6,48,256]{3,2,1,0:T(8,128)(2,1)}, bf16[2,6,48...) custom-call(s32[3]{0:T(128)} %pad_add_fusion.refs_0_, bf16[2,6,256,384]{3,2,1,0:T(8,128)(2,1)} %interpolate_edges.1.refs_4_.refs_1_, ...), custom_call_target="tpu_custom_call" | custom-call | flops 3623878 | bytes 7077 | tf_op jit(solution)/shard_map/range_transform/pallas_call | solution.py:337
  40.4 1.5 collective-permute-start.7
  41.9 2.6 %collective-permute-start.4 = (bf16[2,6,48,256]{3,2,1,0:T(8,128)(2,1)}, bf16[2,6,48,256]{3,2,1,0:T(8,128)(2,1)S(1)}, u32[]{:S(2)}, u32[]{:S(2)}) collective-permute-start(bf16[2,6,48,256]{3,2,1,0:T(8,128)(2,1)} %get-tuple-element.103), channel_id=1, source_target_pairs={{0,4},{4,0},{8,12},{12,8},{1,5},{5,1},{9,13},{13,9},{2,6},{6,2},{1... | collective-permute-start | bytes 884744 | tf_op jit(solution)/shard_map/ppermute | solution.py:559
  44.6 2.6 %collective-permute-start.5 = (bf16[2,6,48,256]{3,2,1,0:T(8,128)(2,1)}, bf16[2,6,48,256]{3,2,1,0:T(8,128)(2,1)S(1)}, u32[]{:S(2)}, u32[]{:S(2)}) collective-permute-start(bf16[2,6,48,256]{3,2,1,0:T(8,128)(2,1)} %get-tuple-element.104), channel_id=1, source_target_pairs={{0,8},{4,12},{8,0},{12,4},{1,9},{5,13},{9,1},{13,5},{2,10},{6,14},... | collective-permute-start | bytes 884744 | tf_op jit(solution)/shard_map/ppermute | solution.py:559
  47.2 7.8 %range_transform.4 = (bf16[2,6,4,48,256]{4,3,2,1,0:T(8,128)(2,1)}, bf16[2,6,48,256]{3,2,1,0:T(8,128)(2,1)}, bf16[2,6,48,256]{3,2,1,0:T(8,128)(2,1)}, bf16[2,6,48...) custom-call(s32[3]{0:T(128)} %pad_add_fusion.refs_0_, bf16[2,6,256,384]{3,2,1,0:T(8,128)(2,1)} %interpolate.4.refs_7_.refs_1_, ...), custom_call_target="tpu_custom_call" | custom-call | flops 3623878 | bytes 7077 | tf_op jit(solution)/shard_map/range_transform/pallas_call | solution.py:337
  55.0 6.7 %interpolate.5.refs_1_.refs_7_ = bf16[2,4,256,384]{3,2,1,0:T(8,128)(2,1)} custom-call(bf16[2,16,256,384]{3,2,1,0:T(8,128)(2,1)} %refs_0_.2, bf16[8,256,384]{2,1,0:T(8,128)(2,1)} %place_taps.1.refs_1_.band_ref, s32[256,384]{1,0:T(8,128)} %refs_2_.5, bf16[2,16,16,384]{3,2,1,0:T(8,128)(2,1)} %copy-done.3, ...), custom_call_target="tpu_custom_call" | custom-call | flops 26738 | bytes 3145 | tf_op jit(solution)/shard_map/interpolate/pallas_call | solution.py:231
  61.7 6.6 %collective-permute-done.5.refs_3_ = bf16[2,6,48,256]{3,2,1,0:T(8,128)(2,1)S(1)} collective-permute-done((bf16[2,6,48,256]{3,2,1,0:T(8,128)(2,1)}, bf16[2,6,48,256]{3,2,1,0:T(8,128)(2,1)S(1)}, u32[]{:S(2)}, u32[]{:S(2)}) %collective-permute-start.5) | collective-permute-done | bytes 294944 | tf_op jit(solution)/shard_map/ppermute | solution.py:559
  68.6 1.6 collective-permute-start.12
  70.2 5.2 %collective-permute-start.10 = (bf16[2,6,48,256]{3,2,1,0:T(8,128)(2,1)}, bf16[2,6,48,256]{3,2,1,0:T(8,128)(2,1)}, u32[]{:S(2)}, u32[]{:S(2)}) collective-permute-start(bf16[2,6,48,256]{3,2,1,0:T(8,128)(2,1)} %get-tuple-element.115), channel_id=1, source_target_pairs={{0,8},{4,12},{8,0},{12,4},{1,9},{5,13},{9,1},{13,5},{2,10},{6,14},... | collective-permute-start | bytes 884744 | tf_op jit(solution)/shard_map/ppermute | solution.py:559
  75.4 1.4 collective-permute-start.11
  76.8 6.2 %range_transform.5 = (bf16[2,4,4,48,256]{4,3,2,1,0:T(8,128)(2,1)}, bf16[2,4,48,256]{3,2,1,0:T(8,128)(2,1)}, bf16[2,4,48,256]{3,2,1,0:T(8,128)(2,1)}, bf16[2,4,48...) custom-call(s32[3]{0:T(128)} %pad_add_fusion.refs_0_, bf16[2,4,256,384]{3,2,1,0:T(8,128)(2,1)} %interpolate.5.refs_1_.refs_7_, ...), custom_call_target="tpu_custom_call" | custom-call | flops 2415919 | bytes 4718 | tf_op jit(solution)/shard_map/range_transform/pallas_call | solution.py:337
  83.0 13.2 %collective-permute-done.10.refs_7_ = bf16[2,6,48,256]{3,2,1,0:T(8,128)(2,1)} collective-permute-done((bf16[2,6,48,256]{3,2,1,0:T(8,128)(2,1)}, bf16[2,6,48,256]{3,2,1,0:T(8,128)(2,1)}, u32[]{:S(2)}, u32[]{:S(2)}) %collective-permute-start.10) | collective-permute-done | bytes 294944 | tf_op jit(solution)/shard_map/ppermute | solution.py:559
  96.2 0.9 collective-permute-done.9.refs_6_
  97.1 1.5 collective-permute-start.16
  98.6 5.6 %collective-permute-start.13 = (bf16[2,4,48,256]{3,2,1,0:T(8,128)(2,1)}, bf16[2,4,48,256]{3,2,1,0:T(8,128)(2,1)S(1)}, u32[]{:S(2)}, u32[]{:S(2)}) collective-permute-start(bf16[2,4,48,256]{3,2,1,0:T(8,128)(2,1)} %get-tuple-element.129), channel_id=1, source_target_pairs={{0,4},{4,0},{8,12},{12,8},{1,5},{5,1},{9,13},{13,9},{2,6},{6,2},{1... | collective-permute-start | bytes 589832 | tf_op jit(solution)/shard_map/ppermute | solution.py:559
  104.2 2.4 %collective-permute-start.15 = (bf16[2,4,48,256]{3,2,1,0:T(8,128)(2,1)}, bf16[2,4,48,256]{3,2,1,0:T(8,128)(2,1)S(1)}, u32[]{:S(2)}, u32[]{:S(2)}) collective-permute-start(bf16[2,4,48,256]{3,2,1,0:T(8,128)(2,1)} %get-tuple-element.131), channel_id=1, source_target_pairs={{0,12},{4,8},{8,4},{12,0},{1,13},{5,9},{9,5},{13,1},{2,14},{6,10},... | collective-permute-start | bytes 589832 | tf_op jit(solution)/shard_map/ppermute | solution.py:559
  106.6 9.6 %cross_transform.5.refs_8_.refs_2_ = bf16[2,12,48,1024]{3,2,1,0:T(8,128)(2,1)} custom-call(s32[3]{0:T(128)} %pad_add_fusion.refs_0_, bf16[2,6,48,256]{3,2,1,0:T(8,128)(2,1)} %get-tuple-element.120.refs_1_, bf16[2,6,48,256]{3,2,1,0:T(8,128)(2,1)} %copy-done.11, bf16[2,6,48,256]{3,2,1,0:T(8,128)(2,1)} %copy-done.12, ...), custom_call_target="tpu_custom_call" | custom-call | flops 4831838 | bytes 8912 | tf_op jit(solution)/shard_map/cross_transform/pallas_call | solution.py:523
  116.2 5.0 %collective-permute-done.14.refs_3_ = bf16[2,4,48,256]{3,2,1,0:T(8,128)(2,1)S(1)} collective-permute-done((bf16[2,4,48,256]{3,2,1,0:T(8,128)(2,1)}, bf16[2,4,48,256]{3,2,1,0:T(8,128)(2,1)S(1)}, u32[]{:S(2)}, u32[]{:S(2)}) %collective-permute-start.14) | collective-permute-done | bytes 196640 | tf_op jit(solution)/shard_map/ppermute | solution.py:559
  122.6 0.9 collective-permute-start.23
  123.5 5.5 %first_heights.2 = (bf16[2,8,48,256]{3,2,1,0:T(8,128)(2,1)}, bf16[2,4,48,256]{3,2,1,0:T(8,128)(2,1)}, bf16[2,4,48,256]{3,2,1,0:T(8,128)(2,1)}, bf16[2,8,48,256]{...) custom-call(s32[3]{0:T(128)} %pad_add_fusion.refs_0_, ...), custom_call_target="tpu_custom_call" | custom-call | flops 805306 | bytes 4718 | tf_op jit(solution)/shard_map/first_heights/pallas_call | solution.py:416
  129.0 2.9 %collective-permute-start.18 = (bf16[2,8,48,256]{3,2,1,0:T(8,128)(2,1)}, bf16[2,8,48,256]{3,2,1,0:T(8,128)(2,1)S(1)}, u32[]{:S(2)}, u32[]{:S(2)}) collective-permute-start(bf16[2,8,48,256]{3,2,1,0:T(8,128)(2,1)} %get-tuple-element.134.refs_8_), channel_id=1, source_target_pairs={{0,8},{4,12},{8,0},{12,4},{1,9},{5,13},{9,1},{13,5},{2,10},{6,14},... | collective-permute-start | bytes 1179656 | tf_op jit(solution)/shard_map/ppermute | solution.py:559
  131.9 5.6 %first_heights.3 = (bf16[2,8,48,256]{3,2,1,0:T(8,128)(2,1)}, bf16[2,4,48,256]{3,2,1,0:T(8,128)(2,1)}, bf16[2,4,48,256]{3,2,1,0:T(8,128)(2,1)}, bf16[2,8,48,256]{...) custom-call(s32[3]{0:T(128)} %pad_add_fusion.refs_0_, ...), custom_call_target="tpu_custom_call" | custom-call | flops 805306 | bytes 4718 | tf_op jit(solution)/shard_map/first_heights/pallas_call | solution.py:416
  137.5 2.2 %collective-permute-start.19 = (bf16[2,8,48,256]{3,2,1,0:T(8,128)(2,1)}, bf16[2,8,48,256]{3,2,1,0:T(8,128)(2,1)S(1)}, u32[]{:S(2)}, u32[]{:S(2)}) collective-permute-start(bf16[2,8,48,256]{3,2,1,0:T(8,128)(2,1)} %get-tuple-element.145), channel_id=1, source_target_pairs={{0,12},{4,8},{8,4},{12,0},{1,13},{5,9},{9,5},{13,1},{2,14},{6,10},... | collective-permute-start | bytes 1179656 | tf_op jit(solution)/shard_map/ppermute | solution.py:559
  139.7 5.3 %cross_transform.6 = (bf16[2,4,32,1024]{3,2,1,0:T(8,128)(2,1)}, bf16[2,4,16,1024]{3,2,1,0:T(8,128)(2,1)}) custom-call(s32[3]{0:T(128)} %pad_add_fusion.refs_0_, bf16[2,4,48,256]{3,2,1,0:T(8,128)(2,1)} %get-tuple-element.150.refs_1_, bf16[2,4,48,256]{3,2,1,0:T(8,128)(2,1)} %copy-done.17, bf16[2,4,48,256]{3,2,1,0:T(8,128)(2,1)} %copy-done.18, ...), custom_call_target="tpu_custom_call" | custom-call | flops 1610612 | bytes 5767 | tf_op jit(solution)/shard_map/cross_transform/pallas_call | solution.py:523
  145.0 1.1 collective-permute-start.28
  146.2 14.7 %collective-permute-done.17.refs_2_ = bf16[2,8,48,256]{3,2,1,0:T(8,128)(2,1)S(1)} collective-permute-done((bf16[2,8,48,256]{3,2,1,0:T(8,128)(2,1)}, bf16[2,8,48,256]{3,2,1,0:T(8,128)(2,1)S(1)}, u32[]{:S(2)}, u32[]{:S(2)}) %collective-permute-start.17) | collective-permute-done | bytes 393248 | tf_op jit(solution)/shard_map/ppermute | solution.py:559
  160.9 4.4 %collective-permute-start.20 = (bf16[2,4,48,256]{3,2,1,0:T(8,128)(2,1)}, bf16[2,4,48,256]{3,2,1,0:T(8,128)(2,1)}, u32[]{:S(2)}, u32[]{:S(2)}) collective-permute-start(bf16[2,4,48,256]{3,2,1,0:T(8,128)(2,1)} %get-tuple-element.147), channel_id=1, source_target_pairs={{0,4},{4,0},{8,12},{12,8},{1,5},{5,1},{9,13},{13,9},{2,6},{6,2},{1... | collective-permute-start | bytes 589832 | tf_op jit(solution)/shard_map/ppermute | solution.py:559
  165.3 1.2 collective-permute-start.21
  166.5 1.5 collective-permute-start.22
  168.0 7.4 %cross_transform.7.refs_7_ = bf16[2,16,96,1024]{3,2,1,0:T(8,128)(2,1)} custom-call(s32[3]{0:T(128)} %pad_add_fusion.refs_0_, bf16[2,8,48,256]{3,2,1,0:T(8,128)(2,1)} %get-tuple-element.155.refs_7_.refs_1_, bf16[2,8,48,256]{3,2,1,0:T(8,128)(2,1)} %copy-done.9, bf16[2,8,48,256]{3,2,1,0:T(8,128)(2,1)} %copy-done.8, bf16[2,8,48,256]{3,2,1,0:T(8,128)(2,1)} %copy-done.10, ...), custom_call_target="tpu_custom_call" | custom-call | flops 3221225 | bytes 7340 | tf_op jit(solution)/shard_map/cross_transform/pallas_call | solution.py:523
  175.3 6.7 %collective-permute-done.21.refs_3_ = bf16[2,4,48,256]{3,2,1,0:T(8,128)(2,1)} collective-permute-done((bf16[2,4,48,256]{3,2,1,0:T(8,128)(2,1)}, bf16[2,4,48,256]{3,2,1,0:T(8,128)(2,1)}, u32[]{:S(2)}, u32[]{:S(2)}) %collective-permute-start.21) | collective-permute-done | bytes 196640 | tf_op jit(solution)/shard_map/ppermute | solution.py:559
  182.1 0.7 collective-permute-start.27
  182.8 2.6 %collective-permute-start.24 = (bf16[2,4,48,256]{3,2,1,0:T(8,128)(2,1)}, bf16[2,4,48,256]{3,2,1,0:T(8,128)(2,1)S(1)}, u32[]{:S(2)}, u32[]{:S(2)}) collective-permute-start(bf16[2,4,48,256]{3,2,1,0:T(8,128)(2,1)} %get-tuple-element.161), channel_id=1, source_target_pairs={{0,4},{4,0},{8,12},{12,8},{1,5},{5,1},{9,13},{13,9},{2,6},{6,2},{1... | collective-permute-start | bytes 589832 | tf_op jit(solution)/shard_map/ppermute | solution.py:559
  185.4 1.6 collective-permute-start.25
  187.0 1.5 collective-permute-start.26
  188.5 5.3 %cross_transform.8.refs_6_ = bf16[2,16,96,1024]{3,2,1,0:T(8,128)(2,1)} custom-call(s32[3]{0:T(128)} %pad_add_fusion.refs_0_, bf16[2,4,48,256]{3,2,1,0:T(8,128)(2,1)} %get-tuple-element.166.refs_1_, bf16[2,4,48,256]{3,2,1,0:T(8,128)(2,1)} %collective-permute-done.20.refs_2_, ...), custom_call_target="tpu_custom_call", output_to_operand_aliasing={{}: (7, {})} | custom-call | flops 1610612 | bytes 5767 | tf_op jit(solution)/shard_map/cross_transform/pallas_call | solution.py:523
  193.8 0.8 copy-done.7
  194.6 5.8 %last_heights.2.refs_6_ = bf16[2,16,96,1024]{3,2,1,0:T(8,128)(2,1)} custom-call(s32[3]{0:T(128)} %pad_add_fusion.refs_0_, bf16[2,2,256,512]{3,2,1,0:T(8,128)(2,1)} %constant.22.clone.refs_1_, bf16[2,12,48,1024]{3,2,1,0:T(8,128)(2,1)} %cross_transform.5.refs_8_.refs_2_, ...), custom_call_target="tpu_custom_call", output_to_operand_aliasing={{}: (6, {})} | custom-call | flops 1073741 | bytes 6291 | tf_op jit(solution)/shard_map/last_heights/pallas_call | solution.py:450
  201.1 3.8 %last_heights.3.refs_7_ = bf16[2,16,96,1024]{3,2,1,0:T(8,128)(2,1)} custom-call(s32[3]{0:T(128)} %pad_add_fusion.refs_0_, bf16[2,2,256,512]{3,2,1,0:T(8,128)(2,1)} %constant.22.clone.refs_1_, bf16[2,12,48,1024]{3,2,1,0:T(8,128)(2,1)} %cross_transform.5.refs_8_.refs_2_, ...), custom_call_target="tpu_custom_call", output_to_operand_aliasing={{}: (6, {})} | custom-call | flops 536870 | bytes 3145 | tf_op jit(solution)/shard_map/last_heights/pallas_call | solution.py:450
  206.4 5.3 %cross_transform.9 = bf16[2,16,96,1024]{3,2,1,0:T(8,128)(2,1)} custom-call(s32[3]{0:T(128)} %pad_add_fusion.refs_0_, bf16[2,4,48,256]{3,2,1,0:T(8,128)(2,1)} %get-tuple-element.160.refs_1_, bf16[2,4,48,256]{3,2,1,0:T(8,128)(2,1)} %copy-done.14, bf16[2,4,48,256]{3,2,1,0:T(8,128)(2,1)} %copy-done.15, ...), custom_call_target="tpu_custom_call", output_to_operand_aliasing={{}: (7, {})} | custom-call | flops 1610612 | bytes 5767 | tf_op jit(solution)/shard_map/cross_transform/pallas_call | solution.py:523
  (71 shorter events, 5.2 us)
Async XLA Ops:
  4.3 14.8 %collective-permute-start = (bf16[2,16,8,384]{3,2,1,0:T(8,128)(2,1)S(1)}, bf16[2,16,8,384]{3,2,1,0:T(8,128)(2,1)S(1)}, u32[]{:S(2)}, u32[]{:S(2)}) collective-permute-start(bf16[2,16,8,384]{3,2,1,0:T(8,128)(2,1)S(1)} %get-tuple-element.172), channel_id=1, source_target_pairs={{0,4},{4,8},{8,12},{1,5},{5,9},{9,13},{2,6},{6,10},{10,14},{3,7},{... | collective-permute-start | bytes 589832 | tf_op jit(solution)/shard_map/ppermute | solution.py:570
  9.2 9.9 %collective-permute-start.1 = (bf16[2,16,8,384]{3,2,1,0:T(8,128)(2,1)S(1)}, bf16[2,16,8,384]{3,2,1,0:T(8,128)(2,1)S(1)}, u32[]{:S(2)}, u32[]{:S(2)}) collective-permute-start(bf16[2,16,8,384]{3,2,1,0:T(8,128)(2,1)S(1)} %get-tuple-element.171), channel_id=1, source_target_pairs={{4,0},{8,4},{12,8},{5,1},{9,5},{13,9},{6,2},{10,6},{14,10},{7,3},{... | collective-permute-start | bytes 589832 | tf_op jit(solution)/shard_map/ppermute | solution.py:571
  19.2 0.8 copy-start.3
  22.7 9.2 %collective-permute-start.2 = (bf16[2,6,256,384]{3,2,1,0:T(8,128)(2,1)}, bf16[2,6,256,384]{3,2,1,0:T(8,128)(2,1)}, u32[]{:S(2)}, u32[]{:S(2)}) collective-permute-start(bf16[2,6,256,384]{3,2,1,0:T(8,128)(2,1)} %interpolate_edges.1.refs_4_.refs_1_), channel_id=1, source_target_pairs={{0,1},{1,0},{2,3},{3,2},{4,5},{5,4},{6,7},{7,6},{8,9},{9,8},{10,11... | collective-permute-start | bytes 7077896 | tf_op jit(solution)/shard_map/ppermute | solution.py:559
  31.9 8.0 %copy-start = (bf16[2,6,256,384]{3,2,1,0:T(8,128)(2,1)S(1)}, bf16[2,6,256,384]{3,2,1,0:T(8,128)(2,1)}, u32[]{:S(2)}) copy-start(bf16[2,6,256,384]{3,2,1,0:T(8,128)(2,1)} %interpolate.4.refs_7_.refs_1_) | copy-start | bytes 7077892
  39.9 7.3 %collective-permute-start.3 = (bf16[2,6,256,384]{3,2,1,0:T(8,128)(2,1)S(1)}, bf16[2,6,256,384]{3,2,1,0:T(8,128)(2,1)}, u32[]{:S(2)}, u32[]{:S(2)}) collective-permute-start(bf16[2,6,256,384]{3,2,1,0:T(8,128)(2,1)S(1)} %copy-done), channel_id=1, source_target_pairs={{0,1},{1,0},{2,3},{3,2},{4,5},{5,4},{6,7},{7,6},{8,9},{9,8},{10,11... | collective-permute-start | bytes 7077896 | tf_op jit(solution)/shard_map/ppermute | solution.py:559
  40.4 28.2 %collective-permute-start.7 = (bf16[2,6,4,48,256]{4,3,2,1,0:T(8,128)(2,1)}, bf16[2,6,4,48,256]{4,3,2,1,0:T(8,128)(2,1)S(1)}, u32[]{:S(2)}, u32[]{:S(2)}) collective-permute-start(bf16[2,6,4,48,256]{4,3,2,1,0:T(8,128)(2,1)} %get-tuple-element.95.refs_2_), channel_id=1, source_target_pairs={{0,2},{2,0},{1,3},{3,1},{4,6},{6,4},{5,7},{7,5},{8,10},{10,8},{9,1... | collective-permute-start | bytes 3538952 | tf_op jit(solution)/shard_map/ppermute | solution.py:559
  41.9 19.7 %collective-permute-start.4 = (bf16[2,6,48,256]{3,2,1,0:T(8,128)(2,1)}, bf16[2,6,48,256]{3,2,1,0:T(8,128)(2,1)S(1)}, u32[]{:S(2)}, u32[]{:S(2)}) collective-permute-start(bf16[2,6,48,256]{3,2,1,0:T(8,128)(2,1)} %get-tuple-element.103), channel_id=1, source_target_pairs={{0,4},{4,0},{8,12},{12,8},{1,5},{5,1},{9,13},{13,9},{2,6},{6,2},{1... | collective-permute-start | bytes 884744 | tf_op jit(solution)/shard_map/ppermute | solution.py:559
  44.6 23.7 %collective-permute-start.5 = (bf16[2,6,48,256]{3,2,1,0:T(8,128)(2,1)}, bf16[2,6,48,256]{3,2,1,0:T(8,128)(2,1)S(1)}, u32[]{:S(2)}, u32[]{:S(2)}) collective-permute-start(bf16[2,6,48,256]{3,2,1,0:T(8,128)(2,1)} %get-tuple-element.104), channel_id=1, source_target_pairs={{0,8},{4,12},{8,0},{12,4},{1,9},{5,13},{9,1},{13,5},{2,10},{6,14},... | collective-permute-start | bytes 884744 | tf_op jit(solution)/shard_map/ppermute | solution.py:559
  47.1 21.1 %collective-permute-start.6 = (bf16[2,6,48,256]{3,2,1,0:T(8,128)(2,1)}, bf16[2,6,48,256]{3,2,1,0:T(8,128)(2,1)}, u32[]{:S(2)}, u32[]{:S(2)}) collective-permute-start(bf16[2,6,48,256]{3,2,1,0:T(8,128)(2,1)} %get-tuple-element.105), channel_id=1, source_target_pairs={{0,12},{4,8},{8,4},{12,0},{1,13},{5,9},{9,5},{13,1},{2,14},{6,10},... | collective-permute-start | bytes 884744 | tf_op jit(solution)/shard_map/ppermute | solution.py:559
  55.0 13.6 %copy-start.1 = (bf16[2,6,4,48,256]{4,3,2,1,0:T(8,128)(2,1)S(1)}, bf16[2,6,4,48,256]{4,3,2,1,0:T(8,128)(2,1)}, u32[]{:S(2)}) copy-start(bf16[2,6,4,48,256]{4,3,2,1,0:T(8,128)(2,1)} %get-tuple-element.106.refs_4_.refs_3_) | copy-start | bytes 3538948
  61.7 21.3 %copy-start.11 = (bf16[2,6,48,256]{3,2,1,0:T(8,128)(2,1)}, bf16[2,6,48,256]{3,2,1,0:T(8,128)(2,1)S(1)}, u32[]{:S(2)}) copy-start(bf16[2,6,48,256]{3,2,1,0:T(8,128)(2,1)S(1)} %collective-permute-done.4.refs_2_) | copy-start | bytes 884740
  68.3 14.7 %copy-start.12 = (bf16[2,6,48,256]{3,2,1,0:T(8,128)(2,1)}, bf16[2,6,48,256]{3,2,1,0:T(8,128)(2,1)S(1)}, u32[]{:S(2)}) copy-start(bf16[2,6,48,256]{3,2,1,0:T(8,128)(2,1)S(1)} %collective-permute-done.5.refs_3_) | copy-start | bytes 884740
  68.6 14.4 %copy-start.4 = (bf16[2,6,4,48,256]{4,3,2,1,0:T(8,128)(2,1)}, bf16[2,6,4,48,256]{4,3,2,1,0:T(8,128)(2,1)S(1)}, u32[]{:S(2)}) copy-start(bf16[2,6,4,48,256]{4,3,2,1,0:T(8,128)(2,1)S(1)} %collective-permute-done.7.refs_5_) | copy-start | bytes 3538948
  68.6 8.2 %collective-permute-start.8 = (bf16[2,4,256,384]{3,2,1,0:T(8,128)(2,1)}, bf16[2,4,256,384]{3,2,1,0:T(8,128)(2,1)}, u32[]{:S(2)}, u32[]{:S(2)}) collective-permute-start(bf16[2,4,256,384]{3,2,1,0:T(8,128)(2,1)} %interpolate.5.refs_1_.refs_7_), channel_id=1, source_target_pairs={{0,1},{1,0},{2,3},{3,2},{4,5},{5,4},{6,7},{7,6},{8,9},{9,8},{10,11... | collective-permute-start | bytes 4718600 | tf_op jit(solution)/shard_map/ppermute | solution.py:559
  68.6 28.5 %collective-permute-start.12 = (bf16[2,6,4,48,256]{4,3,2,1,0:T(8,128)(2,1)S(1)}, bf16[2,6,4,48,256]{4,3,2,1,0:T(8,128)(2,1)S(1)}, u32[]{:S(2)}, u32[]{:S(2)}) collective-permute-start(bf16[2,6,4,48,256]{4,3,2,1,0:T(8,128)(2,1)S(1)} %copy-done.1), channel_id=1, source_target_pairs={{0,2},{2,0},{1,3},{3,1},{4,6},{6,4},{5,7},{7,5},{8,10},{10,8},{9,1... | collective-permute-start | bytes 3538952 | tf_op jit(solution)/shard_map/ppermute | solution.py:559
  70.2 26.0 %collective-permute-start.10 = (bf16[2,6,48,256]{3,2,1,0:T(8,128)(2,1)}, bf16[2,6,48,256]{3,2,1,0:T(8,128)(2,1)}, u32[]{:S(2)}, u32[]{:S(2)}) collective-permute-start(bf16[2,6,48,256]{3,2,1,0:T(8,128)(2,1)} %get-tuple-element.115), channel_id=1, source_target_pairs={{0,8},{4,12},{8,0},{12,4},{1,9},{5,13},{9,1},{13,5},{2,10},{6,14},... | collective-permute-start | bytes 884744 | tf_op jit(solution)/shard_map/ppermute | solution.py:559
  75.4 20.8 %collective-permute-start.11 = (bf16[2,6,48,256]{3,2,1,0:T(8,128)(2,1)}, bf16[2,6,48,256]{3,2,1,0:T(8,128)(2,1)}, u32[]{:S(2)}, u32[]{:S(2)}) collective-permute-start(bf16[2,6,48,256]{3,2,1,0:T(8,128)(2,1)} %get-tuple-element.116), channel_id=1, source_target_pairs={{0,12},{4,8},{8,4},{12,0},{1,13},{5,9},{9,5},{13,1},{2,14},{6,10},... | collective-permute-start | bytes 884744 | tf_op jit(solution)/shard_map/ppermute | solution.py:559
  76.8 20.3 %collective-permute-start.9 = (bf16[2,6,48,256]{3,2,1,0:T(8,128)(2,1)}, bf16[2,6,48,256]{3,2,1,0:T(8,128)(2,1)}, u32[]{:S(2)}, u32[]{:S(2)}) collective-permute-start(bf16[2,6,48,256]{3,2,1,0:T(8,128)(2,1)} %get-tuple-element.114), channel_id=1, source_target_pairs={{0,4},{4,0},{8,12},{12,8},{1,5},{5,1},{9,13},{13,9},{2,6},{6,2},{1... | collective-permute-start | bytes 884744 | tf_op jit(solution)/shard_map/ppermute | solution.py:559
  97.1 19.1 %copy-start.5 = (bf16[2,6,4,48,256]{4,3,2,1,0:T(8,128)(2,1)}, bf16[2,6,4,48,256]{4,3,2,1,0:T(8,128)(2,1)S(1)}, u32[]{:S(2)}) copy-start(bf16[2,6,4,48,256]{4,3,2,1,0:T(8,128)(2,1)S(1)} %collective-permute-done.12.refs_6_) | copy-start | bytes 3538948
  97.1 25.5 %collective-permute-start.16 = (bf16[2,4,4,48,256]{4,3,2,1,0:T(8,128)(2,1)}, bf16[2,4,4,48,256]{4,3,2,1,0:T(8,128)(2,1)S(1)}, u32[]{:S(2)}, u32[]{:S(2)}) collective-permute-start(bf16[2,4,4,48,256]{4,3,2,1,0:T(8,128)(2,1)} %get-tuple-element.117.refs_11_.refs_4_), channel_id=1, source_target_pairs={{0,2},{2,0},{1,3},{3,1},{4,6},{6,4},{5,7},{7,5},{8,10},{10,8},{9,1... | collective-permute-start | bytes 2359304 | tf_op jit(solution)/shard_map/ppermute | solution.py:559
  98.6 17.6 %collective-permute-start.13 = (bf16[2,4,48,256]{3,2,1,0:T(8,128)(2,1)}, bf16[2,4,48,256]{3,2,1,0:T(8,128)(2,1)S(1)}, u32[]{:S(2)}, u32[]{:S(2)}) collective-permute-start(bf16[2,4,48,256]{3,2,1,0:T(8,128)(2,1)} %get-tuple-element.129), channel_id=1, source_target_pairs={{0,4},{4,0},{8,12},{12,8},{1,5},{5,1},{9,13},{13,9},{2,6},{6,2},{1... | collective-permute-start | bytes 589832 | tf_op jit(solution)/shard_map/ppermute | solution.py:559
  104.2 17.0 %collective-permute-start.14 = (bf16[2,4,48,256]{3,2,1,0:T(8,128)(2,1)}, bf16[2,4,48,256]{3,2,1,0:T(8,128)(2,1)S(1)}, u32[]{:S(2)}, u32[]{:S(2)}) collective-permute-start(bf16[2,4,48,256]{3,2,1,0:T(8,128)(2,1)} %get-tuple-element.130), channel_id=1, source_target_pairs={{0,8},{4,12},{8,0},{12,4},{1,9},{5,13},{9,1},{13,5},{2,10},{6,14},... | collective-permute-start | bytes 589832 | tf_op jit(solution)/shard_map/ppermute | solution.py:559
  104.2 17.0 %collective-permute-start.15 = (bf16[2,4,48,256]{3,2,1,0:T(8,128)(2,1)}, bf16[2,4,48,256]{3,2,1,0:T(8,128)(2,1)S(1)}, u32[]{:S(2)}, u32[]{:S(2)}) collective-permute-start(bf16[2,4,48,256]{3,2,1,0:T(8,128)(2,1)} %get-tuple-element.131), channel_id=1, source_target_pairs={{0,12},{4,8},{8,4},{12,0},{1,13},{5,9},{9,5},{13,1},{2,14},{6,10},... | collective-permute-start | bytes 589832 | tf_op jit(solution)/shard_map/ppermute | solution.py:559
  116.2 5.1 %copy-start.17 = (bf16[2,4,48,256]{3,2,1,0:T(8,128)(2,1)}, bf16[2,4,48,256]{3,2,1,0:T(8,128)(2,1)S(1)}, u32[]{:S(2)}) copy-start(bf16[2,4,48,256]{3,2,1,0:T(8,128)(2,1)S(1)} %collective-permute-done.13.refs_2_) | copy-start | bytes 589828
  121.9 0.7 copy-start.19
  122.6 0.9 copy-start.6
  122.6 59.5 %collective-permute-start.23 = (bf16[2,12,48,1024]{3,2,1,0:T(8,128)(2,1)}, bf16[2,12,48,1024]{3,2,1,0:T(8,128)(2,1)S(1)}, u32[]{:S(2)}, u32[]{:S(2)}) collective-permute-start(bf16[2,12,48,1024]{3,2,1,0:T(8,128)(2,1)} %cross_transform.5.refs_8_.refs_2_), channel_id=1, source_target_pairs={{0,2},{2,0},{1,3},{3,1},{4,6},{6,4},{5,7},{7,5},{8,10},{10,8},{9,1... | collective-permute-start | bytes 7077896 | tf_op jit(solution)/shard_map/ppermute | solution.py:559
  129.0 31.9 %collective-permute-start.18 = (bf16[2,8,48,256]{3,2,1,0:T(8,128)(2,1)}, bf16[2,8,48,256]{3,2,1,0:T(8,128)(2,1)S(1)}, u32[]{:S(2)}, u32[]{:S(2)}) collective-permute-start(bf16[2,8,48,256]{3,2,1,0:T(8,128)(2,1)} %get-tuple-element.134.refs_8_), channel_id=1, source_target_pairs={{0,8},{4,12},{8,0},{12,4},{1,9},{5,13},{9,1},{13,5},{2,10},{6,14},... | collective-permute-start | bytes 1179656 | tf_op jit(solution)/shard_map/ppermute | solution.py:559
  137.4 23.4 %collective-permute-start.17 = (bf16[2,8,48,256]{3,2,1,0:T(8,128)(2,1)}, bf16[2,8,48,256]{3,2,1,0:T(8,128)(2,1)S(1)}, u32[]{:S(2)}, u32[]{:S(2)}) collective-permute-start(bf16[2,8,48,256]{3,2,1,0:T(8,128)(2,1)} %get-tuple-element.144), channel_id=1, source_target_pairs={{0,4},{4,0},{8,12},{12,8},{1,5},{5,1},{9,13},{13,9},{2,6},{6,2},{1... | collective-permute-start | bytes 1179656 | tf_op jit(solution)/shard_map/ppermute | solution.py:559
  137.5 23.4 %collective-permute-start.19 = (bf16[2,8,48,256]{3,2,1,0:T(8,128)(2,1)}, bf16[2,8,48,256]{3,2,1,0:T(8,128)(2,1)S(1)}, u32[]{:S(2)}, u32[]{:S(2)}) collective-permute-start(bf16[2,8,48,256]{3,2,1,0:T(8,128)(2,1)} %get-tuple-element.145), channel_id=1, source_target_pairs={{0,12},{4,8},{8,4},{12,0},{1,13},{5,9},{9,5},{13,1},{2,14},{6,10},... | collective-permute-start | bytes 1179656 | tf_op jit(solution)/shard_map/ppermute | solution.py:559
  145.0 48.7 %collective-permute-start.28 = (bf16[2,4,32,1024]{3,2,1,0:T(8,128)(2,1)}, bf16[2,4,32,1024]{3,2,1,0:T(8,128)(2,1)S(1)}, u32[]{:S(2)}, u32[]{:S(2)}) collective-permute-start(bf16[2,4,32,1024]{3,2,1,0:T(8,128)(2,1)} %get-tuple-element.159.refs_7_.refs_3_), channel_id=1, source_target_pairs={{0,2},{2,0},{1,3},{3,1},{4,6},{6,4},{5,7},{7,5},{8,10},{10,8},{9,1... | collective-permute-start | bytes 1572872 | tf_op jit(solution)/shard_map/ppermute | solution.py:559
  160.9 7.1 %copy-start.9 = (bf16[2,8,48,256]{3,2,1,0:T(8,128)(2,1)}, bf16[2,8,48,256]{3,2,1,0:T(8,128)(2,1)S(1)}, u32[]{:S(2)}) copy-start(bf16[2,8,48,256]{3,2,1,0:T(8,128)(2,1)S(1)} %collective-permute-done.17.refs_2_) | copy-start | bytes 1179652
  160.9 7.1 %copy-start.8 = (bf16[2,8,48,256]{3,2,1,0:T(8,128)(2,1)}, bf16[2,8,48,256]{3,2,1,0:T(8,128)(2,1)S(1)}, u32[]{:S(2)}) copy-start(bf16[2,8,48,256]{3,2,1,0:T(8,128)(2,1)S(1)} %collective-permute-done.18.refs_3_) | copy-start | bytes 1179652
  160.9 7.1 %copy-start.10 = (bf16[2,8,48,256]{3,2,1,0:T(8,128)(2,1)}, bf16[2,8,48,256]{3,2,1,0:T(8,128)(2,1)S(1)}, u32[]{:S(2)}) copy-start(bf16[2,8,48,256]{3,2,1,0:T(8,128)(2,1)S(1)} %collective-permute-done.19.refs_4_) | copy-start | bytes 1179652
  160.9 14.4 %collective-permute-start.20 = (bf16[2,4,48,256]{3,2,1,0:T(8,128)(2,1)}, bf16[2,4,48,256]{3,2,1,0:T(8,128)(2,1)}, u32[]{:S(2)}, u32[]{:S(2)}) collective-permute-start(bf16[2,4,48,256]{3,2,1,0:T(8,128)(2,1)} %get-tuple-element.147), channel_id=1, source_target_pairs={{0,4},{4,0},{8,12},{12,8},{1,5},{5,1},{9,13},{13,9},{2,6},{6,2},{1... | collective-permute-start | bytes 589832 | tf_op jit(solution)/shard_map/ppermute | solution.py:559
  165.3 16.8 %collective-permute-start.21 = (bf16[2,4,48,256]{3,2,1,0:T(8,128)(2,1)}, bf16[2,4,48,256]{3,2,1,0:T(8,128)(2,1)}, u32[]{:S(2)}, u32[]{:S(2)}) collective-permute-start(bf16[2,4,48,256]{3,2,1,0:T(8,128)(2,1)} %get-tuple-element.148), channel_id=1, source_target_pairs={{0,8},{4,12},{8,0},{12,4},{1,9},{5,13},{9,1},{13,5},{2,10},{6,14},... | collective-permute-start | bytes 589832 | tf_op jit(solution)/shard_map/ppermute | solution.py:559
  166.5 15.6 %collective-permute-start.22 = (bf16[2,4,48,256]{3,2,1,0:T(8,128)(2,1)}, bf16[2,4,48,256]{3,2,1,0:T(8,128)(2,1)}, u32[]{:S(2)}, u32[]{:S(2)}) collective-permute-start(bf16[2,4,48,256]{3,2,1,0:T(8,128)(2,1)} %get-tuple-element.149), channel_id=1, source_target_pairs={{0,12},{4,8},{8,4},{12,0},{1,13},{5,9},{9,5},{13,1},{2,14},{6,10},... | collective-permute-start | bytes 589832 | tf_op jit(solution)/shard_map/ppermute | solution.py:559
  182.1 11.7 %copy-start.2 = (bf16[2,12,48,1024]{3,2,1,0:T(8,128)(2,1)}, bf16[2,12,48,1024]{3,2,1,0:T(8,128)(2,1)S(1)}, u32[]{:S(2)}) copy-start(bf16[2,12,48,1024]{3,2,1,0:T(8,128)(2,1)S(1)} %collective-permute-done.23.refs_4_) | copy-start | bytes 7077892
  182.1 18.4 %collective-permute-start.27 = (bf16[2,4,16,1024]{3,2,1,0:T(8,128)(2,1)}, bf16[2,4,16,1024]{3,2,1,0:T(8,128)(2,1)S(1)}, u32[]{:S(2)}, u32[]{:S(2)}) collective-permute-start(bf16[2,4,16,1024]{3,2,1,0:T(8,128)(2,1)} %get-tuple-element.164.refs_3_), channel_id=1, source_target_pairs={{0,2},{2,0},{1,3},{3,1},{4,6},{6,4},{5,7},{7,5},{8,10},{10,8},{9,1... | collective-permute-start | bytes 786440 | tf_op jit(solution)/shard_map/ppermute | solution.py:559
  182.8 22.1 %collective-permute-start.24 = (bf16[2,4,48,256]{3,2,1,0:T(8,128)(2,1)}, bf16[2,4,48,256]{3,2,1,0:T(8,128)(2,1)S(1)}, u32[]{:S(2)}, u32[]{:S(2)}) collective-permute-start(bf16[2,4,48,256]{3,2,1,0:T(8,128)(2,1)} %get-tuple-element.161), channel_id=1, source_target_pairs={{0,4},{4,0},{8,12},{12,8},{1,5},{5,1},{9,13},{13,9},{2,6},{6,2},{1... | collective-permute-start | bytes 589832 | tf_op jit(solution)/shard_map/ppermute | solution.py:559
  185.4 19.5 %collective-permute-start.25 = (bf16[2,4,48,256]{3,2,1,0:T(8,128)(2,1)}, bf16[2,4,48,256]{3,2,1,0:T(8,128)(2,1)S(1)}, u32[]{:S(2)}, u32[]{:S(2)}) collective-permute-start(bf16[2,4,48,256]{3,2,1,0:T(8,128)(2,1)} %get-tuple-element.162), channel_id=1, source_target_pairs={{0,8},{4,12},{8,0},{12,4},{1,9},{5,13},{9,1},{13,5},{2,10},{6,14},... | collective-permute-start | bytes 589832 | tf_op jit(solution)/shard_map/ppermute | solution.py:559
  187.0 18.0 %collective-permute-start.26 = (bf16[2,4,48,256]{3,2,1,0:T(8,128)(2,1)}, bf16[2,4,48,256]{3,2,1,0:T(8,128)(2,1)S(1)}, u32[]{:S(2)}, u32[]{:S(2)}) collective-permute-start(bf16[2,4,48,256]{3,2,1,0:T(8,128)(2,1)} %get-tuple-element.163), channel_id=1, source_target_pairs={{0,12},{4,8},{8,4},{12,0},{1,13},{5,9},{9,5},{13,1},{2,14},{6,10},... | collective-permute-start | bytes 589832 | tf_op jit(solution)/shard_map/ppermute | solution.py:559
  193.8 0.8 copy-start.7
  200.4 0.7 copy-start.13
  204.9 0.7 copy-start.14
  204.9 0.7 copy-start.15
  205.7 0.7 copy-start.16
  (1 other events, 0.7 us)

commit v3 on v2

--- a/solution.py
+++ b/solution.py
@@ -107,10 +107,11 @@
     return image_out
 
 
-CUTS = (6, 6, 4)
-PARTS = (8, 4, 4)
+CHUNKS = ((0, 6), (6, 6), (12, 4))
+PARTS = (8, 8)
 SPLIT = 48
-VMEM = 60 * 1024 * 1024
+VMEM = 20 * 1024 * 1024
+WIDE_VMEM = 60 * 1024 * 1024
 
 
 def host_table(row_ids, col_ids, length):
@@ -119,8 +120,8 @@
     return (np.cos(angle).astype(ml_dtypes.bfloat16), np.sin(angle).astype(ml_dtypes.bfloat16))
 
 
-def params():
-    return pltpu.CompilerParams(vmem_limit_bytes=VMEM)
+def params(limit=VMEM):
+    return pltpu.CompilerParams(vmem_limit_bytes=limit)
 
 
 def cost(flops, nbytes):
@@ -131,148 +132,112 @@
     return [pl.BlockSpec(memory_space=pl.ANY)] * len(values)
 
 
-def band_kernel(offset_ref, count_ref, weight_ref, out_ref):
-    rows, freqs = offset_ref.shape
-
-    def tile(index, carry):
-        row = pl.ds(pl.multiple_of(index * ROWS, ROWS), ROWS)
-        for start in range(0, freqs, LANES):
-            lane = pl.ds(start, LANES)
-            base = offset_ref[row, lane] + HW
-            count = count_ref[row, lane]
-            zero = jnp.zeros((ROWS, LANES), jnp.float32)
-            slots = [
-                jnp.where(count > tap, weight_ref[tap, row, lane].astype(jnp.float32), zero)
-                for tap in range(KT)
-            ]
-            step = 1
-            while step < KT:
-                chosen = (base & step) != 0
-                slots = [jnp.where(chosen, slots[(r - step) % KT], slots[r]) for r in range(KT)]
-                step *= 2
-            for r in range(KT):
-                out_ref[r, row, lane] = slots[r].astype(jnp.bfloat16)
-        return carry
-
-    lax.fori_loop(0, rows // ROWS, tile, 0)
-
-
-def place_taps(band_offset, tap_count, tap_weight):
-    cols, freqs = band_offset.shape
-    step = cols // 2
-    return pl.pallas_call(
-        band_kernel,
-        grid=(2,),
-        in_specs=[
-            pl.BlockSpec((step, freqs), lambda i: (i, 0)),
-            pl.BlockSpec((step, freqs), lambda i: (i, 0)),
-            pl.BlockSpec((KT, step, freqs), lambda i: (0, i, 0)),
-        ],
-        out_specs=pl.BlockSpec((KT, step, freqs), lambda i: (0, i, 0)),
-        out_shape=jax.ShapeDtypeStruct((KT, cols, freqs), jnp.bfloat16),
-        compiler_params=params(),
-        cost_estimate=cost(100 * cols * freqs, 40 * cols * freqs),
-        name="place_taps",
-    )(band_offset, tap_count, tap_weight)
-
-
-def interp_rows(pad_ref, band_ref, offset_ref, out_ref):
-    _, cuts, cols, freqs = out_ref.shape
+def interp_rows(pad_ref, offset_ref, count_ref, weight_ref, out_ref, lane=slice(None)):
+    _, cuts, cols, _ = out_ref.shape
+    lanes = pad_ref.shape[2]
+    step = 8
 
     def tile(index, carry):
         row = pl.multiple_of(index * ROWS, ROWS)
-        for f in range(freqs // LANES):
-            lane = pl.ds(f * LANES, LANES)
-            taps = [band_ref[r, pl.ds(row, ROWS), lane].astype(jnp.float32) for r in range(KT)]
-            base = offset_ref[pl.ds(row, ROWS), lane] + HW
-            past = [base > r for r in range(KT + 1)]
-            for part in range(2):
-                for cut in range(cuts):
-                    plane = part * cuts + cut
-                    near = [
-                        pad_ref[plane, f, pl.ds(row + d, ROWS), :] for d in range(2 * HW + 1)
-                    ]
+        rows = pl.ds(row, ROWS)
+        base = offset_ref[rows, lane] + HW
+        count = count_ref[rows, lane]
+        zero = jnp.zeros((ROWS, lanes), jnp.float32)
+        taps = [
+            jnp.where(count > tap, weight_ref[tap, rows, lane].astype(jnp.float32), zero)
+            for tap in range(KT)
+        ]
+        shift = 1
+        while shift < KT:
+            chosen = (base & shift) != 0
+            taps = [jnp.where(chosen, taps[(r - shift) % KT], taps[r]) for r in range(KT)]
+            shift *= 2
+        halves = [slice(i, i + step) for i in range(0, ROWS, step)]
+        past = [[base[half] > r for r in range(KT + 1)] for half in halves]
+        taps = [[tap[half] for tap in taps] for half in halves]
+        for part in range(2):
+            for cut in range(cuts):
+                plane = part * cuts + cut
+                near = [
+                    pad_ref[plane, pl.ds(row + d, step), :] for d in range(2 * HW + 1 + ROWS - step)
+                ]
+                totals = []
+                for i in range(len(halves)):
+                    here = near[i * step :]
                     total = None
                     for r in range(KT):
-                        value = jnp.where(past[r], near[r + KT], near[r])
+                        value = jnp.where(past[i][r], here[r + KT], here[r])
                         if r == 0:
-                            value = jnp.where(past[KT], near[2 * KT], value)
-                        value = value * taps[r]
+                            value = jnp.where(past[i][KT], here[2 * KT], value)
+                        value = value * taps[i][r]
                         total = value if total is None else total + value
-                    out_ref[part, cut, pl.ds(row, ROWS), lane] = total.astype(jnp.bfloat16)
+                    totals.append(total)
+                out_ref[part, cut, rows, lane] = jnp.concatenate(totals, axis=0).astype(jnp.bfloat16)
         return carry
 
     lax.fori_loop(0, cols // ROWS, tile, 0)
 
 
-def interp_kernel(polar_ref, band_ref, offset_ref, *refs, bordered):
+def interp_kernel(polar_ref, offset_ref, count_ref, weight_ref, *refs, bordered):
     out_ref, pad_ref = refs[-2:]
-    _, cuts, cols, freqs = polar_ref.shape
+    _, cuts, cols, lanes = polar_ref.shape
     for part in range(2):
         for cut in range(cuts):
             plane = part * cuts + cut
-            for f in range(freqs // LANES):
-                lane = pl.ds(f * LANES, LANES)
-                if bordered:
-                    halo = refs[0][part, cut, :, lane].astype(jnp.float32)
-                else:
-                    halo = jnp.zeros((2 * HW, LANES), jnp.float32)
-                pad_ref[plane, f, pl.ds(0, HW), :] = halo[:HW]
-                pad_ref[plane, f, pl.ds(HW, cols), :] = polar_ref[part, cut, :, lane].astype(jnp.float32)
-                pad_ref[plane, f, pl.ds(HW + cols, HW), :] = halo[HW:]
-    interp_rows(pad_ref, band_ref, offset_ref, out_ref)
-
-
-def interpolate(polar, halo, taps, band_offset, first, count, earlier=()):
+            if bordered:
+                halo = refs[0][part, cut].astype(jnp.float32)
+            else:
+                halo = jnp.zeros((2 * HW, lanes), jnp.float32)
+            pad_ref[plane, pl.ds(0, HW), :] = halo[:HW]
+            pad_ref[plane, pl.ds(HW, cols), :] = polar_ref[part, cut].astype(jnp.float32)
+            pad_ref[plane, pl.ds(HW + cols, HW), :] = halo[HW:]
+    interp_rows(pad_ref, offset_ref, count_ref, weight_ref, out_ref)
+
+
+def chunk_spec(count, rows, first):
+    return pl.BlockSpec((2, count, rows, LANES), lambda i: (0, first // count, 0, i))
+
+
+def interpolate(polar, halo, bands, first, count, earlier=(), limit=VMEM):
     _, _, cols, freqs = polar.shape
-    group = 2
-    skip = first // group
     border = [] if halo is None else [halo]
     return pl.pallas_call(
         lambda *refs: interp_kernel(*refs, bordered=len(border) == 1),
-        grid=(count // group,),
+        grid=(freqs // LANES,),
         in_specs=[
-            pl.BlockSpec((2, group, cols, freqs), lambda i: (0, skip + i, 0, 0)),
-            pl.BlockSpec((KT, cols, freqs), lambda i: (0, 0, 0)),
-            pl.BlockSpec((cols, freqs), lambda i: (0, 0)),
+            chunk_spec(count, cols, first),
+            pl.BlockSpec((cols, LANES), lambda i: (0, i)),
+            pl.BlockSpec((cols, LANES), lambda i: (0, i)),
+            pl.BlockSpec((KT, cols, LANES), lambda i: (0, 0, i)),
         ]
-        + [pl.BlockSpec((2, group, 2 * HW, freqs), lambda i: (0, skip + i, 0, 0))] * len(border)
+        + [chunk_spec(count, 2 * HW, first)] * len(border)
         + after(earlier),
-        out_specs=pl.BlockSpec((2, group, cols, freqs), lambda i: (0, i, 0, 0)),
+        out_specs=chunk_spec(count, cols, 0),
         out_shape=jax.ShapeDtypeStruct((2, count, cols, freqs), jnp.bfloat16),
-        scratch_shapes=[
-            pltpu.VMEM((2 * group, freqs // LANES, cols + 2 * HW, LANES), jnp.float32)
-        ],
-        compiler_params=params(),
+        scratch_shapes=[pltpu.VMEM((2 * count, cols + 2 * HW, LANES), jnp.float32)],
+        compiler_params=params(limit),
         cost_estimate=cost(2 * count * cols * freqs * 34, 8 * count * cols * freqs),
         name="interpolate",
-    )(polar, taps, band_offset, *border, *earlier)
-
-
-def edge_kernel(polar_ref, halo_ref, band_ref, offset_ref, made_ref, out_ref, pad_ref):
+    )(polar, *bands, *border, *earlier)
+
+
+def edge_kernel(polar_ref, halo_ref, offset_ref, count_ref, weight_ref, made_ref, out_ref, pad_ref):
     del made_ref
     _, cuts, rows, freqs = polar_ref.shape
-    for part in range(2):
-        for cut in range(cuts):
-            for f in range(freqs // LANES):
-                plane, lane = part * cuts + cut, pl.ds(f * LANES, LANES)
+    for start in range(0, freqs, LANES):
+        lane = pl.ds(start, LANES)
+        for part in range(2):
+            for cut in range(cuts):
+                plane = part * cuts + cut
                 halo = halo_ref[part, cut, :, lane].astype(jnp.float32)
                 body = polar_ref[part, cut, :, lane].astype(jnp.float32)
-
-                @pl.when(pl.program_id(0) == 0)
-                def _():
-                    pad_ref[plane, f, pl.ds(0, HW), :] = halo[:HW]
-                    pad_ref[plane, f, pl.ds(HW, rows - HW), :] = body[: rows - HW]
-
-                @pl.when(pl.program_id(0) == 1)
-                def _():
-                    pad_ref[plane, f, pl.ds(0, rows - HW), :] = body[HW:]
-                    pad_ref[plane, f, pl.ds(rows - HW, HW), :] = halo[HW:]
-
-    interp_rows(pad_ref, band_ref, offset_ref, out_ref)
-
-
-def interpolate_edges(polar, halo, taps, band_offset, made):
+                left = jnp.concatenate([halo[:HW], body[: rows - HW]], axis=0)
+                right = jnp.concatenate([body[HW:], halo[HW:]], axis=0)
+                pad_ref[plane] = jnp.where(pl.program_id(0) == 0, left, right)
+        interp_rows(pad_ref, offset_ref, count_ref, weight_ref, out_ref, lane)
+
+
+def interpolate_edges(polar, halo, bands, first, made):
     _, count, cols, freqs = made.shape
     wide = cols // (2 * ROWS) - 1
     last = cols // ROWS - 1
@@ -280,20 +245,21 @@
         edge_kernel,
         grid=(2,),
         in_specs=[
-            pl.BlockSpec((2, count, 2 * ROWS, freqs), lambda i: (0, 0, i * wide, 0)),
-            pl.BlockSpec((2, count, 2 * HW, freqs), lambda i: (0, 0, 0, 0)),
+            pl.BlockSpec((2, count, 2 * ROWS, freqs), lambda i: (0, first // count, i * wide, 0)),
+            pl.BlockSpec((2, count, 2 * HW, freqs), lambda i: (0, first // count, 0, 0)),
+            pl.BlockSpec((ROWS, freqs), lambda i: (i * last, 0)),
+            pl.BlockSpec((ROWS, freqs), lambda i: (i * last, 0)),
             pl.BlockSpec((KT, ROWS, freqs), lambda i: (0, i * last, 0)),
-            pl.BlockSpec((ROWS, freqs), lambda i: (i * last, 0)),
             pl.BlockSpec(memory_space=pl.ANY),
         ],
         out_specs=pl.BlockSpec((2, count, ROWS, freqs), lambda i: (0, 0, i * last, 0)),
         out_shape=jax.ShapeDtypeStruct(made.shape, jnp.bfloat16),
-        scratch_shapes=[pltpu.VMEM((2 * count, freqs // LANES, 2 * ROWS, LANES), jnp.float32)],
-        input_output_aliases={4: 0},
-        compiler_params=params(),
+        scratch_shapes=[pltpu.VMEM((2 * count, 2 * ROWS, LANES), jnp.float32)],
+        input_output_aliases={5: 0},
+        compiler_params=params(WIDE_VMEM),
         cost_estimate=cost(4 * count * ROWS * freqs * 34, 16 * count * ROWS * freqs),
         name="interpolate_edges",
-    )(polar, halo, taps, band_offset, made)
+    )(polar, halo, *bands, made)
 
 
 def range_kernel(ids_ref, own_ref, other_ref, *refs, blocks, earlier):
@@ -325,7 +291,7 @@
                 rest[s][part, cut] = value[split:]
 
 
-def range_transform(ids, own, other, table, split, earlier=()):
+def range_transform(ids, own, other, table, split, earlier=(), limit=VMEM):
     _, count, cols, freqs = own.shape
     _, blocks, bins, full = table.shape
     rest = bins - split
@@ -349,19 +315,19 @@
         ),
         out_shape=[jax.ShapeDtypeStruct((2, count, blocks, split, cols), jnp.bfloat16)]
         + [jax.ShapeDtypeStruct((2, count, rest, cols), jnp.bfloat16)] * blocks,
-        compiler_params=params(),
+        compiler_params=params(limit),
         cost_estimate=cost(4 * count * cols * full * blocks * bins, 12 * count * cols * freqs),
         name="range_transform",
     )(ids, own, other, *([table] * blocks), *earlier)
 
 
-def height_table(cuts, rows):
+def height_table(cuts, rows, order):
     heights = []
     for el in range(2):
         pair = []
         for parity in range(2):
             h = el * cuts + parity + 2 * np.arange(cuts // 2)
-            cos, sin = (t.astype(np.float32) for t in host_table(h, np.arange(cuts), 2 * cuts))
+            cos, sin = (t.astype(np.float32) for t in host_table(h, order, 2 * cuts))
             sign = -1.0 if el and parity else 1.0
             whole = sign * np.block([[cos, -sin], [sin, cos]])
             pair.append(np.kron(whole, np.eye(rows, dtype=np.float32)))
@@ -403,19 +369,18 @@
                 h += 1
 
 
-def first_heights(ids, matrix, own, other, pair, parts, earlier=()):
+def first_heights(ids, matrix, own, other, parts, earlier=()):
     chunks = len(own)
     _, _, blocks, split, cols = own[0].shape
     total = sum(v.shape[1] for v in own)
-    sets = 2
     spec = [
-        pl.BlockSpec((2, v.shape[1], sets, ROWS, cols), lambda i, ids: (0, 0, pair, i, 0))
+        pl.BlockSpec((2, v.shape[1], blocks, ROWS, cols), lambda i, ids: (0, 0, 0, i, 0))
         for v in own
     ]
-    outs = list(parts) * sets
-    return pl.pallas_call(
+    outs = list(parts) * blocks
+    made = pl.pallas_call(
         lambda *refs: height_kernel(
-            *refs, chunks=chunks, sets=sets, outs=len(parts), scale=None, skipped=len(earlier)
+            *refs, chunks=chunks, sets=blocks, outs=len(parts), scale=None, skipped=len(earlier)
         ),
         grid_spec=pltpu.PrefetchScalarGridSpec(
             num_scalar_prefetch=1,
@@ -428,9 +393,10 @@
         ),
         out_shape=[jax.ShapeDtypeStruct((2, h, split, cols), jnp.bfloat16) for h in outs],
         compiler_params=params(),
-        cost_estimate=cost(sets * split * cols * 32768, 12 * sets * total * split * cols),
+        cost_estimate=cost(blocks * split * cols * 32768, 12 * blocks * total * split * cols),
         name="first_heights",
     )(ids, matrix, *own, *other, *earlier)
+    return [[made[s * len(parts) + p] for s in range(blocks)] for p in range(len(parts))]
 
 
 def last_heights(ids, matrix, own, other, places, image, shape, skip, rows, earlier=()):
@@ -592,86 +558,72 @@
         tables.append(np.stack(blocks))
     range_table = jnp.asarray(np.stack(tables))
     cross_tables = [jnp.asarray(t) for t in host_table(np.arange(A), np.arange(A), A)]
-    matrix = jnp.asarray(height_table(cuts, ROWS))
-
-    taps = place_taps(band_offset, tap_count, tap_weight)
-    polar, taps = lax.optimization_barrier((polar, taps))
+    order = np.concatenate([start + np.arange(count) for start, count in CHUNKS])
+    matrix = jnp.asarray(height_table(cuts, ROWS, order))
+
+    bands = (band_offset, tap_count, tap_weight)
     halo = halo_rows(polar)
-    starts = np.cumsum((0,) + CUTS)
-    last = len(CUTS) - 1
+    last = len(CHUNKS) - 1
     scale = 1.0 / math.sqrt(A)
 
-    def interp(i, earlier=()):
-        return interpolate(polar, halo, taps, band_offset, int(starts[i]), CUTS[i], earlier)
-
-    def to_owners(blocks):
-        come = {s: exchange(blocks[s], "az", s) for s in reversed(range(1, az_count))}
+    def interp(i, earlier=(), limit=VMEM):
+        return interpolate(polar, halo, bands, *CHUNKS[i], earlier, limit)
+
+    def to_owners(blocks, which=range(az_count - 1, 0, -1)):
+        return {s: exchange(blocks[s], "az", s) for s in which}
+
+    def in_order(blocks, come):
         return [blocks[0]] + [come[s] for s in range(1, az_count)]
 
-    bare = interpolate(polar, None, taps, band_offset, 0, CUTS[0])
-    made = interpolate_edges(polar, halo, taps, band_offset, bare)
+    bare = interpolate(polar, None, bands, *CHUNKS[0], (), WIDE_VMEM)
+    made = interpolate_edges(polar, halo, bands, CHUNKS[0][0], bare)
     other = exchange(made, "fq", 1)
-    ahead = interp(1, (made,))
+    ahead = interp(1, (made,), WIDE_VMEM)
     own_first, other_first, landed = [], [], []
-    moving = ([], ())
+    moving = None
     for i in range(last + 1):
-        first, *blocks = range_transform(ids, made, other, range_table, split, (ahead,))
+        limit = VMEM if i else WIDE_VMEM
+        first, *blocks = range_transform(ids, made, other, range_table, split, (ahead,), limit)
         if 0 < i < last:
             ahead = interp(i + 1, (first,))
-        held = (first, blocks, ahead, moving)
-        first, blocks, ahead, moving = lax.optimization_barrier(held)
+        first, blocks, ahead, moving = lax.optimization_barrier((first, blocks, ahead, moving))
         if i > 0:
-            landed.append(moving[0])
+            landed.append(in_order(held, moving[0]))
             other_first.append(moving[1])
         own_first.append(first)
+        held = blocks
         moving = (to_owners(blocks), exchange(first, "el", 1))
         if i < last:
             made, other = ahead, exchange(ahead, "fq", 1)
     c0 = cross_transform(ids, landed, cross_tables, scale, [rest], earlier=(first,))
     c0, moving = lax.optimization_barrier((c0, moving))
-    landed.append(moving[0])
+    landed.append(in_order(held, moving[0]))
     other_first.append(moving[1])
     other_c0 = exchange(c0, "el", 1)
 
-    h1 = first_heights(ids, matrix, own_first, other_first, 1, PARTS, (c0,))
-    count = len(PARTS)
-    far = [h1[:count], h1[count:]]
-    h0 = first_heights(ids, matrix, own_first, other_first, 0, PARTS, (h1[0],))
-    near = [h0[:count], h0[count:]]
-    made = [[near[0][p], near[1][p], far[0][p], far[1][p]] for p in range(count)]
-    late = [rest - ROWS, ROWS]
-    c1, c2 = cross_transform(ids, landed[-1:], cross_tables, scale, late, earlier=(h0[0],))
+    made = first_heights(ids, matrix, own_first, other_first, PARTS, (c0,))
+    come = to_owners(made[0])
+    c1 = cross_transform(ids, landed[-1:], cross_tables, scale, [rest], earlier=(made[0][0],))
     other_c1 = exchange(c1, "el", 1)
-    arrived = [to_owners(made[0])]
     shape = (2, cuts, bins, A)
     full_scale = 1.0 / math.sqrt(A * 2 * cuts)
-    made[1], arrived[0] = lax.optimization_barrier((made[1], arrived[0]))
-    arrived.append(to_owners(made[1]))
+    made, come, c1 = lax.optimization_barrier((made, come, c1))
+    arrived = in_order(made[0], come)
+    come = to_owners(made[1])
     image = cross_transform(
-        ids, [arrived[0]], cross_tables, full_scale, image=None, shape=shape, place=0, earlier=(c1,)
-    )
-    made[2], arrived[1], c2, other_c0, image = lax.optimization_barrier(
-        (made[2], arrived[1], c2, other_c0, image)
-    )
-    arrived.append(to_owners(made[2]))
-    other_c2 = exchange(c2, "el", 1)
-    image = cross_transform(
-        ids, [arrived[1]], cross_tables, full_scale, image=image, shape=shape, place=PARTS[0] // PARTS[1]
+        ids, [arrived], cross_tables, full_scale, image=None, shape=shape, place=0, earlier=(c1,)
     )
     image = last_heights(
-        ids, matrix, [c0, c1], [other_c0, other_c1], (0, 0), image, shape, split, late[0]
-    )
-    image = last_heights(
-        ids, matrix, [c0, c2], [other_c0, other_c2], (late[0], 0), image, shape, split + late[0], late[1]
+        ids, matrix, [c0, c1], [other_c0, other_c1], (0, 0), image, shape, split, rest
     )
     image = cross_transform(
         ids,
-        [arrived[2]],
+        [in_order(made[1], come)],
         cross_tables,
         full_scale,
         image=image,
         shape=shape,
-        place=(PARTS[0] + PARTS[1]) // PARTS[2],
+        place=PARTS[0] // PARTS[1],
     )
     return image
 
@@ -684,7 +636,7 @@
         lax.axis_size("el") == 2
         and lax.axis_size("fq") == 2
         and az_count == 4
-        and cuts == sum(CUTS) == sum(PARTS)
+        and cuts == sum(count for _, count in CHUNKS) == sum(PARTS)
         and cols % (2 * LANES) == 0
         and freqs % LANES == 0
         and bins > SPLIT

time: 212 us -> 199 us (0.939); the launches traced: 212 us -> 196 us
  Pallas kernels: 105 us -> 72.4 us
  waiting for transfers between devices: 47.5 us -> 69.4 us
  starting transfers between devices: 51.7 us -> 46.7 us
    ppermute x27 -> x23, waiting for transfers between devices: 47.5 us -> 69.4 us  [exchange(): lax.ppermute(value, axis, [(i, i ^ s) for i in range(lax.axis_size(axis))])]
    pallas_call x5 -> x4, Pallas kernels: 32.9 us -> 20.9 us  [cross_transform(): pl.pallas_call(lambda *refs: cross_kernel(*refs, groups=groups, blocks=bl...]
    pallas_call x3 -> x1, Pallas kernels: 14.3 us -> 3.4 us  [first_heights(): pl.pallas_call(lambda *refs: height_kernel(*refs, chunks=chunks, sets=blo...]
    ppermute x27 -> x23, starting transfers between devices: 45.5 us -> 40.4 us  [exchange(): lax.ppermute(value, axis, [(i, i ^ s) for i in range(lax.axis_size(axis))])]
    pallas_call x2 -> x1, Pallas kernels: 9.64 us -> 5.11 us  [last_heights(): pl.pallas_call(lambda *refs: height_kernel(*refs, chunks=chunks, sets=1,...]
    pallas_call x3, Pallas kernels: 22 us -> 17.8 us  [range_transform(): pl.pallas_call(lambda *refs: range_kernel(*refs, blocks=blocks, earlier=l...]
    unnamed x41 -> x29, local copies, waits for them, and re-layouts: 5.11 us -> 5.25 us
  transfers between devices with their start and end apart: 29 -> 25, of which waited for: 7 -> 9; matrix products, arithmetic and copies ran while one was open for 0% -> 0% of each run, Pallas kernels for 41% -> 29%
where the time goes in v3:
time: 199 us; the launch traced here: 196 us
  Pallas kernels  72.4 us (36%)
  waiting for transfers between devices  69.4 us (35%)
  starting transfers between devices  46.7 us (23%)
  local copies, waits for them, and re-layouts  6.35 us (3%)
    ppermute x23, waiting for transfers between devices, exchange(): lax.ppermute(value, axis, [(i, i ^ s) for i in range(lax.axis_size(axis))])  69.4 us
    ppermute x23, starting transfers between devices, exchange(): lax.ppermute(value, axis, [(i, i ^ s) for i in range(lax.axis_size(axis))])  40.4 us
    pallas_call x3, Pallas kernels, interpolate(): pl.pallas_call(lambda *refs: interp_kernel(*refs, bordered=len(border) ==...  22.7 us
    pallas_call x4, Pallas kernels, cross_transform(): pl.pallas_call(lambda *refs: cross_kernel(*refs, groups=groups, blocks=bl...  20.9 us
    pallas_call x3, Pallas kernels, range_transform(): pl.pallas_call(lambda *refs: range_kernel(*refs, blocks=blocks, earlier=l...  17.8 us
    unnamed x29, local copies, waits for them, and re-layouts  5.25 us
    pallas_call x1, Pallas kernels, last_heights(): pl.pallas_call(lambda *refs: height_kernel(*refs, chunks=chunks, sets=1,...  5.11 us
    ppermute x1, starting transfers between devices, halo_rows(): lax.ppermute(tail, 'az', [(i, i + 1) for i in range(ends)])  4.94 us
  transfers between devices with their start and end apart: 25, of which 9 were waited for; matrix products, arithmetic and copies ran while one was open for 0% of the time, Pallas kernels for 29%

profile of v3, /device:TPU:0, one launch (start us, length us, event | category | flops | bytes accessed | tf_op | source)
XLA Modules:
  0.0 195.6 jit_solution(13165566844384784443)
XLA Ops:
  0.0 1.1 fusion
  1.1 4.9 %collective-permute-start = (bf16[2,16,8,384]{3,2,1,0:T(8,128)(2,1)S(1)}, bf16[2,16,8,384]{3,2,1,0:T(8,128)(2,1)S(1)}, u32[]{:S(2)}, u32[]{:S(2)}) collective-permute-start(bf16[2,16,8,384]{3,2,1,0:T(8,128)(2,1)S(1)} %get-tuple-element.130), channel_id=1, source_target_pairs={{0,4},{4,8},{8,12},{1,5},{5,9},{9,13},{2,6},{6,10},{10,14},{3,7},{... | collective-permute-start | bytes 589832 | tf_op jit(solution)/shard_map/ppermute | solution.py:536
  6.0 1.3 collective-permute-start.1
  7.3 8.6 %interpolate.3.made_ref = bf16[2,6,256,384]{3,2,1,0:T(8,128)(2,1)} custom-call(bf16[2,16,256,384]{3,2,1,0:T(8,128)(2,1)} %refs_0_.5, s32[256,384]{1,0:T(8,128)} %refs_1_.7, s32[256,384]{1,0:T(8,128)} %refs_2_.5, bf16[8,256,384]{2,1,0:T(8,128)(2,1)} %refs_3_.8), custom_call_target="tpu_custom_call" | custom-call | flops 40108 | bytes 4718 | tf_op jit(solution)/shard_map/interpolate/pallas_call | solution.py:204
  16.0 0.8 copy-done.8
  16.7 2.5 %interpolate_edges.1.refs_5_.refs_1_ = bf16[2,6,256,384]{3,2,1,0:T(8,128)(2,1)} custom-call(bf16[2,16,256,384]{3,2,1,0:T(8,128)(2,1)} %refs_0_.5, bf16[2,16,16,384]{3,2,1,0:T(8,128)(2,1)} %copy-done.8, s32[256,384]{1,0:T(8,128)} %refs_1_.7, s32[256,384]{1,0:T(8,128)} %refs_2_.5, bf16[8,256,384]{2,1,0:T(8,128)(2,1)} %refs_3_.8, ...), custom_call_target="tpu_custom_call", output_to_operand_aliasing={{}: (5, {})} | custom-call | flops 5013 | bytes 589 | tf_op jit(solution)/shard_map/interpolate_edges/pallas_call | solution.py:244
  19.3 0.6 pad_add_fusion.refs_0_
  19.9 8.6 %interpolate.4.refs_7_.refs_1_ = bf16[2,6,256,384]{3,2,1,0:T(8,128)(2,1)} custom-call(bf16[2,16,256,384]{3,2,1,0:T(8,128)(2,1)} %refs_0_.5, s32[256,384]{1,0:T(8,128)} %refs_1_.7, s32[256,384]{1,0:T(8,128)} %refs_2_.5, bf16[8,256,384]{2,1,0:T(8,128)(2,1)} %refs_3_.8, bf16[2,16,16,384]{3,2,1,0:T(8,128)(2,1)} %copy-done.8, ...), custom_call_target="tpu_custom_call" | custom-call | flops 40108 | bytes 4718 | tf_op jit(solution)/shard_map/interpolate/pallas_call | solution.py:204
  28.5 8.3 %range_transform.3 = (bf16[2,6,4,48,256]{4,3,2,1,0:T(8,128)(2,1)}, bf16[2,6,48,256]{3,2,1,0:T(8,128)(2,1)}, bf16[2,6,48,256]{3,2,1,0:T(8,128)(2,1)}, bf16[2,6,48...) custom-call(s32[3]{0:T(128)} %pad_add_fusion.refs_0_, bf16[2,6,256,384]{3,2,1,0:T(8,128)(2,1)} %interpolate_edges.1.refs_5_.refs_1_, ...), custom_call_target="tpu_custom_call" | custom-call | flops 3623878 | bytes 7077 | tf_op jit(solution)/shard_map/range_transform/pallas_call | solution.py:303
  37.0 1.5 collective-permute-start.7
  38.5 2.6 %collective-permute-start.4 = (bf16[2,6,48,256]{3,2,1,0:T(8,128)(2,1)}, bf16[2,6,48,256]{3,2,1,0:T(8,128)(2,1)S(1)}, u32[]{:S(2)}, u32[]{:S(2)}) collective-permute-start(bf16[2,6,48,256]{3,2,1,0:T(8,128)(2,1)} %get-tuple-element.79), channel_id=1, source_target_pairs={{0,4},{4,0},{8,12},{12,8},{1,5},{5,1},{9,13},{13,9},{2,6},{6,2},{1... | collective-permute-start | bytes 884744 | tf_op jit(solution)/shard_map/ppermute | solution.py:525
  41.1 2.6 %collective-permute-start.5 = (bf16[2,6,48,256]{3,2,1,0:T(8,128)(2,1)}, bf16[2,6,48,256]{3,2,1,0:T(8,128)(2,1)S(1)}, u32[]{:S(2)}, u32[]{:S(2)}) collective-permute-start(bf16[2,6,48,256]{3,2,1,0:T(8,128)(2,1)} %get-tuple-element.80), channel_id=1, source_target_pairs={{0,8},{4,12},{8,0},{12,4},{1,9},{5,13},{9,1},{13,5},{2,10},{6,14},... | collective-permute-start | bytes 884744 | tf_op jit(solution)/shard_map/ppermute | solution.py:525
  43.8 1.7 copy-done.2
  45.5 5.6 %range_transform.4 = (bf16[2,6,4,48,256]{4,3,2,1,0:T(8,128)(2,1)S(1)}, bf16[2,6,48,256]{3,2,1,0:T(8,128)(2,1)S(1)}, bf16[2,6,48,256]{3,2,1,0:T(8,128)(2,1)S(1)},...) custom-call(s32[3]{0:T(128)S(1)} %copy-done.13, bf16[2,6,256,384]{3,2,1,0:T(8,128)(2,1)S(1)} %copy-done.2, ...), custom_call_target="tpu_custom_call" | custom-call | flops 3623878 | bytes 7077 | tf_op jit(solution)/shard_map/range_transform/pallas_call | solution.py:303
  51.1 2.8 %copy-done.1 = bf16[2,16,256,384]{3,2,1,0:T(8,128)(2,1)S(1)} copy-done((bf16[2,16,256,384]{3,2,1,0:T(8,128)(2,1)S(1)}, bf16[2,16,256,384]{3,2,1,0:T(8,128)(2,1)}, u32[]{:S(2)}) %copy-start.1) | copy-done | bytes 6291480
  53.9 5.5 %interpolate.5.refs_1_.refs_7_ = bf16[2,4,256,384]{3,2,1,0:T(8,128)(2,1)S(1)} custom-call(bf16[2,16,256,384]{3,2,1,0:T(8,128)(2,1)S(1)} %copy-done.1, s32[256,384]{1,0:T(8,128)S(1)} %copy-done.6, s32[256,384]{1,0:T(8,128)S(1)} %copy-done.7, bf16[8,256,384]{2,1,0:T(8,128)(2,1)S(1)} %copy-done.5, bf16[2,16,16,384]{3,2,1,0:T(8,128)(2,1)S(1)} %copy-done.9, ...), custom_call_target="tpu_custom_call" | custom-call | flops 26738 | bytes 3145 | tf_op jit(solution)/shard_map/interpolate/pallas_call | solution.py:204
  59.4 5.5 %collective-permute-done.5.refs_3_ = bf16[2,6,48,256]{3,2,1,0:T(8,128)(2,1)S(1)} collective-permute-done((bf16[2,6,48,256]{3,2,1,0:T(8,128)(2,1)}, bf16[2,6,48,256]{3,2,1,0:T(8,128)(2,1)S(1)}, u32[]{:S(2)}, u32[]{:S(2)}) %collective-permute-start.5) | collective-permute-done | bytes 294944 | tf_op jit(solution)/shard_map/ppermute | solution.py:525
  64.8 0.6 collective-permute-done.7.refs_5_
  65.5 1.6 collective-permute-start.12
  67.0 4.2 %collective-permute-start.9 = (bf16[2,6,48,256]{3,2,1,0:T(8,128)(2,1)S(1)}, bf16[2,6,48,256]{3,2,1,0:T(8,128)(2,1)S(1)}, u32[]{:S(2)}, u32[]{:S(2)}) collective-permute-start(bf16[2,6,48,256]{3,2,1,0:T(8,128)(2,1)S(1)} %get-tuple-element.89), channel_id=1, source_target_pairs={{0,4},{4,0},{8,12},{12,8},{1,5},{5,1},{9,13},{13,9},{2,6},{6,2},{1... | collective-permute-start | bytes 884744 | tf_op jit(solution)/shard_map/ppermute | solution.py:525
  71.2 1.1 collective-permute-start.10
  72.3 1.3 collective-permute-start.11
  73.6 3.9 %range_transform.5 = (bf16[2,4,4,48,256]{4,3,2,1,0:T(8,128)(2,1)S(1)}, bf16[2,4,48,256]{3,2,1,0:T(8,128)(2,1)S(1)}, bf16[2,4,48,256]{3,2,1,0:T(8,128)(2,1)S(1)},...) custom-call(s32[3]{0:T(128)S(1)} %copy-done.13, bf16[2,4,256,384]{3,2,1,0:T(8,128)(2,1)S(1)} %interpolate.5.refs_1_.refs_7_, ...), custom_call_target="tpu_custom_call" | custom-call | flops 2415919 | bytes 4718 | tf_op jit(solution)/shard_map/range_transform/pallas_call | solution.py:303
  77.5 6.7 %collective-permute-done.9.refs_6_ = bf16[2,6,48,256]{3,2,1,0:T(8,128)(2,1)S(1)} collective-permute-done((bf16[2,6,48,256]{3,2,1,0:T(8,128)(2,1)S(1)}, bf16[2,6,48,256]{3,2,1,0:T(8,128)(2,1)S(1)}, u32[]{:S(2)}, u32[]{:S(2)}) %collective-permute-start.9) | collective-permute-done | bytes 294944 | tf_op jit(solution)/shard_map/ppermute | solution.py:525
  84.2 10.4 %collective-permute-done.10.refs_7_ = bf16[2,6,48,256]{3,2,1,0:T(8,128)(2,1)S(1)} collective-permute-done((bf16[2,6,48,256]{3,2,1,0:T(8,128)(2,1)S(1)}, bf16[2,6,48,256]{3,2,1,0:T(8,128)(2,1)S(1)}, u32[]{:S(2)}, u32[]{:S(2)}) %collective-permute-start.10) | collective-permute-done | bytes 294944 | tf_op jit(solution)/shard_map/ppermute | solution.py:525
  94.7 1.6 collective-permute-start.16
  96.2 5.8 %collective-permute-start.13 = (bf16[2,4,48,256]{3,2,1,0:T(8,128)(2,1)S(1)}, bf16[2,4,48,256]{3,2,1,0:T(8,128)(2,1)S(1)}, u32[]{:S(2)}, u32[]{:S(2)}) collective-permute-start(bf16[2,4,48,256]{3,2,1,0:T(8,128)(2,1)S(1)} %get-tuple-element.103), channel_id=1, source_target_pairs={{0,4},{4,0},{8,12},{12,8},{1,5},{5,1},{9,13},{13,9},{2,6},{6,2},{1... | collective-permute-start | bytes 589832 | tf_op jit(solution)/shard_map/ppermute | solution.py:525
  102.0 1.0 collective-permute-start.14
  103.0 1.5 collective-permute-start.15
  104.5 6.6 %cross_transform.4.refs_8_.refs_2_ = bf16[2,12,48,1024]{3,2,1,0:T(8,128)(2,1)S(1)} custom-call(s32[3]{0:T(128)S(1)} %copy-done.13, bf16[2,6,48,256]{3,2,1,0:T(8,128)(2,1)S(1)} %copy-done.12, bf16[2,6,48,256]{3,2,1,0:T(8,128)(2,1)S(1)} %collective-permute-done.4.refs_2_, bf16[2,6,48,256]{3,2,1,0:T(8,128)(2,1)S(1)} %collective-permute-done.5.refs_3_, ...), custom_call_target="tpu_custom_call" | custom-call | flops 4831838 | bytes 8912 | tf_op jit(solution)/shard_map/cross_transform/pallas_call | solution.py:489
  111.1 7.7 %collective-permute-done.14.refs_3_ = bf16[2,4,48,256]{3,2,1,0:T(8,128)(2,1)S(1)} collective-permute-done((bf16[2,4,48,256]{3,2,1,0:T(8,128)(2,1)S(1)}, bf16[2,4,48,256]{3,2,1,0:T(8,128)(2,1)S(1)}, u32[]{:S(2)}, u32[]{:S(2)}) %collective-permute-start.14) | collective-permute-done | bytes 196640 | tf_op jit(solution)/shard_map/ppermute | solution.py:525
  118.8 0.5 collective-permute-start.23
  119.4 3.4 %first_heights.1 = (bf16[2,8,48,256]{3,2,1,0:T(8,128)(2,1)S(1)}, bf16[2,8,48,256]{3,2,1,0:T(8,128)(2,1)S(1)}, bf16[2,8,48,256]{3,2,1,0:T(8,128)(2,1)S(1)}, bf16[...) custom-call(s32[3]{0:T(128)S(1)} %copy-done.13, ...), custom_call_target="tpu_custom_call" | custom-call | flops 1610612 | bytes 9437 | tf_op jit(solution)/shard_map/first_heights/pallas_call | solution.py:381
  122.8 2.7 %collective-permute-start.17 = (bf16[2,8,48,256]{3,2,1,0:T(8,128)(2,1)S(1)}, bf16[2,8,48,256]{3,2,1,0:T(8,128)(2,1)S(1)}, u32[]{:S(2)}, u32[]{:S(2)}) collective-permute-start(bf16[2,8,48,256]{3,2,1,0:T(8,128)(2,1)S(1)} %get-tuple-element.109), channel_id=1, source_target_pairs={{0,4},{4,0},{8,12},{12,8},{1,5},{5,1},{9,13},{13,9},{2,6},{6,2},{1... | collective-permute-start | bytes 1179656 | tf_op jit(solution)/shard_map/ppermute | solution.py:525
  125.5 1.0 collective-permute-start.18
  126.5 1.4 collective-permute-start.19
  128.0 3.0 %cross_transform.5.refs_7_.refs_3_ = bf16[2,4,48,1024]{3,2,1,0:T(8,128)(2,1)S(1)} custom-call(s32[3]{0:T(128)S(1)} %copy-done.13, bf16[2,4,48,256]{3,2,1,0:T(8,128)(2,1)S(1)} %get-tuple-element.116.refs_1_, bf16[2,4,48,256]{3,2,1,0:T(8,128)(2,1)S(1)} %collective-permute-done.13.refs_2_, bf16[2,4,48,256]{3,2,1,0:T(8,128)(2,1)S(1)} %collective-permute-done.14.refs_3_, ...), custom_call_target="tpu_custom_call" | custom-call | flops 1610612 | bytes 5767 | tf_op jit(solution)/shard_map/cross_transform/pallas_call | solution.py:489
  130.9 1.6 collective-permute-start.24
  132.5 6.8 %collective-permute-done.17.refs_2_ = bf16[2,8,48,256]{3,2,1,0:T(8,128)(2,1)S(1)} collective-permute-done((bf16[2,8,48,256]{3,2,1,0:T(8,128)(2,1)S(1)}, bf16[2,8,48,256]{3,2,1,0:T(8,128)(2,1)S(1)}, u32[]{:S(2)}, u32[]{:S(2)}) %collective-permute-start.17) | collective-permute-done | bytes 393248 | tf_op jit(solution)/shard_map/ppermute | solution.py:525
  139.3 16.0 %collective-permute-done.18.refs_3_ = bf16[2,8,48,256]{3,2,1,0:T(8,128)(2,1)S(1)} collective-permute-done((bf16[2,8,48,256]{3,2,1,0:T(8,128)(2,1)S(1)}, bf16[2,8,48,256]{3,2,1,0:T(8,128)(2,1)S(1)}, u32[]{:S(2)}, u32[]{:S(2)}) %collective-permute-start.18) | collective-permute-done | bytes 393248 | tf_op jit(solution)/shard_map/ppermute | solution.py:525
  155.3 5.4 %collective-permute-start.20 = (bf16[2,8,48,256]{3,2,1,0:T(8,128)(2,1)S(1)}, bf16[2,8,48,256]{3,2,1,0:T(8,128)(2,1)S(1)}, u32[]{:S(2)}, u32[]{:S(2)}) collective-permute-start(bf16[2,8,48,256]{3,2,1,0:T(8,128)(2,1)S(1)} %get-tuple-element.121), channel_id=1, source_target_pairs={{0,4},{4,0},{8,12},{12,8},{1,5},{5,1},{9,13},{13,9},{2,6},{6,2},{1... | collective-permute-start | bytes 1179656 | tf_op jit(solution)/shard_map/ppermute | solution.py:525
  160.7 1.4 collective-permute-start.21
  162.1 1.5 collective-permute-start.22
  163.6 5.7 %cross_transform.6.refs_6_ = bf16[2,16,96,1024]{3,2,1,0:T(8,128)(2,1)} custom-call(s32[3]{0:T(128)S(1)} %copy-done.13, bf16[2,8,48,256]{3,2,1,0:T(8,128)(2,1)S(1)} %get-tuple-element.125.refs_7_.refs_1_, bf16[2,8,48,256]{3,2,1,0:T(8,128)(2,1)S(1)} %collective-permute-done.17.refs_2_, bf16[2,8,48,256]{3,2,1,0:T(8,128)(2,1)S(1)} %collective-permute-done.18.refs_3_, ...), custom_call_target="tpu_custom_call" | custom-call | flops 3221225 | bytes 7340 | tf_op jit(solution)/shard_map/cross_transform/pallas_call | solution.py:489
  169.3 14.7 %collective-permute-done.24.refs_5_ = bf16[2,4,48,1024]{3,2,1,0:T(8,128)(2,1)S(1)} collective-permute-done((bf16[2,4,48,1024]{3,2,1,0:T(8,128)(2,1)S(1)}, bf16[2,4,48,1024]{3,2,1,0:T(8,128)(2,1)S(1)}, u32[]{:S(2)}, u32[]{:S(2)}) %collective-permute-start.24) | collective-permute-done | bytes 786464 | tf_op jit(solution)/shard_map/ppermute | solution.py:525
  184.0 5.1 %last_heights.1.refs_7_ = bf16[2,16,96,1024]{3,2,1,0:T(8,128)(2,1)} custom-call(s32[3]{0:T(128)S(1)} %copy-done.13, bf16[2,2,256,512]{3,2,1,0:T(8,128)(2,1)S(1)} %copy-done.10, bf16[2,12,48,1024]{3,2,1,0:T(8,128)(2,1)S(1)} %cross_transform.4.refs_8_.refs_2_, ...), custom_call_target="tpu_custom_call", output_to_operand_aliasing={{}: (6, {})} | custom-call | flops 1610612 | bytes 9437 | tf_op jit(solution)/shard_map/last_heights/pallas_call | solution.py:416
  189.1 0.9 collective-permute-done.21.refs_3_
  190.1 5.6 %cross_transform.7 = bf16[2,16,96,1024]{3,2,1,0:T(8,128)(2,1)} custom-call(s32[3]{0:T(128)S(1)} %copy-done.13, bf16[2,8,48,256]{3,2,1,0:T(8,128)(2,1)S(1)} %get-tuple-element.120.refs_1_, bf16[2,8,48,256]{3,2,1,0:T(8,128)(2,1)S(1)} %collective-permute-done.20.refs_2_, ...), custom_call_target="tpu_custom_call", output_to_operand_aliasing={{}: (7, {})} | custom-call | flops 3221225 | bytes 7340 | tf_op jit(solution)/shard_map/cross_transform/pallas_call | solution.py:489
  (47 shorter events, 0.3 us)
Async XLA Ops:
  1.1 14.8 %collective-permute-start = (bf16[2,16,8,384]{3,2,1,0:T(8,128)(2,1)S(1)}, bf16[2,16,8,384]{3,2,1,0:T(8,128)(2,1)S(1)}, u32[]{:S(2)}, u32[]{:S(2)}) collective-permute-start(bf16[2,16,8,384]{3,2,1,0:T(8,128)(2,1)S(1)} %get-tuple-element.130), channel_id=1, source_target_pairs={{0,4},{4,8},{8,12},{1,5},{5,9},{9,13},{2,6},{6,10},{10,14},{3,7},{... | collective-permute-start | bytes 589832 | tf_op jit(solution)/shard_map/ppermute | solution.py:536
  6.0 9.9 %collective-permute-start.1 = (bf16[2,16,8,384]{3,2,1,0:T(8,128)(2,1)S(1)}, bf16[2,16,8,384]{3,2,1,0:T(8,128)(2,1)S(1)}, u32[]{:S(2)}, u32[]{:S(2)}) collective-permute-start(bf16[2,16,8,384]{3,2,1,0:T(8,128)(2,1)S(1)} %get-tuple-element.129), channel_id=1, source_target_pairs={{4,0},{8,4},{12,8},{5,1},{9,5},{13,9},{6,2},{10,6},{14,10},{7,3},{... | collective-permute-start | bytes 589832 | tf_op jit(solution)/shard_map/ppermute | solution.py:537
  16.0 0.8 copy-start.8
  19.3 9.2 %collective-permute-start.2 = (bf16[2,6,256,384]{3,2,1,0:T(8,128)(2,1)}, bf16[2,6,256,384]{3,2,1,0:T(8,128)(2,1)}, u32[]{:S(2)}, u32[]{:S(2)}) collective-permute-start(bf16[2,6,256,384]{3,2,1,0:T(8,128)(2,1)} %interpolate_edges.1.refs_5_.refs_1_), channel_id=1, source_target_pairs={{0,1},{1,0},{2,3},{3,2},{4,5},{5,4},{6,7},{7,6},{8,9},{9,8},{10,11... | collective-permute-start | bytes 7077896 | tf_op jit(solution)/shard_map/ppermute | solution.py:525
  28.5 15.3 %copy-start = (bf16[2,4,96,1536]{3,2,1,0:T(8,128)(2,1)S(1)}, bf16[2,4,96,1536]{3,2,1,0:T(8,128)(2,1)}, u32[]{:S(2)}) copy-start(bf16[2,4,96,1536]{3,2,1,0:T(8,128)(2,1)} %constant.19.clone.refs_3_.refs_4_.refs_5_.refs_6_) | copy-start | bytes 7077892
  28.5 15.3 %copy-start.13 = (s32[3]{0:T(128)S(1)}, s32[3]{0:T(128)}, u32[]{:S(2)}) copy-start(s32[3]{0:T(128)} %pad_add_fusion.refs_0_) | copy-start | bytes 40
  36.8 6.9 %collective-permute-start.3 = (bf16[2,6,256,384]{3,2,1,0:T(8,128)(2,1)}, bf16[2,6,256,384]{3,2,1,0:T(8,128)(2,1)S(1)}, u32[]{:S(2)}, u32[]{:S(2)}) collective-permute-start(bf16[2,6,256,384]{3,2,1,0:T(8,128)(2,1)} %interpolate.4.refs_7_.refs_1_), channel_id=1, source_target_pairs={{0,1},{1,0},{2,3},{3,2},{4,5},{5,4},{6,7},{7,6},{8,9},{9,8},{10,11... | collective-permute-start | bytes 7077896 | tf_op jit(solution)/shard_map/ppermute | solution.py:525
  37.0 28.4 %collective-permute-start.7 = (bf16[2,6,4,48,256]{4,3,2,1,0:T(8,128)(2,1)}, bf16[2,6,4,48,256]{4,3,2,1,0:T(8,128)(2,1)S(1)}, u32[]{:S(2)}, u32[]{:S(2)}) collective-permute-start(bf16[2,6,4,48,256]{4,3,2,1,0:T(8,128)(2,1)} %get-tuple-element.72.refs_2_), channel_id=1, source_target_pairs={{0,2},{2,0},{1,3},{3,1},{4,6},{6,4},{5,7},{7,5},{8,10},{10,8},{9,1... | collective-permute-start | bytes 3538952 | tf_op jit(solution)/shard_map/ppermute | solution.py:525
  38.5 20.8 %collective-permute-start.4 = (bf16[2,6,48,256]{3,2,1,0:T(8,128)(2,1)}, bf16[2,6,48,256]{3,2,1,0:T(8,128)(2,1)S(1)}, u32[]{:S(2)}, u32[]{:S(2)}) collective-permute-start(bf16[2,6,48,256]{3,2,1,0:T(8,128)(2,1)} %get-tuple-element.79), channel_id=1, source_target_pairs={{0,4},{4,0},{8,12},{12,8},{1,5},{5,1},{9,13},{13,9},{2,6},{6,2},{1... | collective-permute-start | bytes 884744 | tf_op jit(solution)/shard_map/ppermute | solution.py:525
  41.1 23.7 %collective-permute-start.5 = (bf16[2,6,48,256]{3,2,1,0:T(8,128)(2,1)}, bf16[2,6,48,256]{3,2,1,0:T(8,128)(2,1)S(1)}, u32[]{:S(2)}, u32[]{:S(2)}) collective-permute-start(bf16[2,6,48,256]{3,2,1,0:T(8,128)(2,1)} %get-tuple-element.80), channel_id=1, source_target_pairs={{0,8},{4,12},{8,0},{12,4},{1,9},{5,13},{9,1},{13,5},{2,10},{6,14},... | collective-permute-start | bytes 884744 | tf_op jit(solution)/shard_map/ppermute | solution.py:525
  43.8 21.0 %collective-permute-start.6 = (bf16[2,6,48,256]{3,2,1,0:T(8,128)(2,1)}, bf16[2,6,48,256]{3,2,1,0:T(8,128)(2,1)S(1)}, u32[]{:S(2)}, u32[]{:S(2)}) collective-permute-start(bf16[2,6,48,256]{3,2,1,0:T(8,128)(2,1)} %get-tuple-element.81), channel_id=1, source_target_pairs={{0,12},{4,8},{8,4},{12,0},{1,13},{5,9},{9,5},{13,1},{2,14},{6,10},... | collective-permute-start | bytes 884744 | tf_op jit(solution)/shard_map/ppermute | solution.py:525
  43.8 1.7 copy-start.2
  45.5 5.6 %copy-start.5 = (bf16[8,256,384]{2,1,0:T(8,128)(2,1)S(1)}, bf16[8,256,384]{2,1,0:T(8,128)(2,1)}, u32[]{:S(2)}) copy-start(bf16[8,256,384]{2,1,0:T(8,128)(2,1)} %refs_3_.8) | copy-start | bytes 4718596
  45.5 5.6 %copy-start.6 = (s32[256,384]{1,0:T(8,128)S(1)}, s32[256,384]{1,0:T(8,128)}, u32[]{:S(2)}) copy-start(s32[256,384]{1,0:T(8,128)} %refs_1_.7) | copy-start | bytes 1179652
  45.5 5.6 %copy-start.7 = (s32[256,384]{1,0:T(8,128)S(1)}, s32[256,384]{1,0:T(8,128)}, u32[]{:S(2)}) copy-start(s32[256,384]{1,0:T(8,128)} %refs_2_.5) | copy-start | bytes 1179652
  45.5 5.6 %copy-start.9 = (bf16[2,16,16,384]{3,2,1,0:T(8,128)(2,1)S(1)}, bf16[2,16,16,384]{3,2,1,0:T(8,128)(2,1)}, u32[]{:S(2)}) copy-start(bf16[2,16,16,384]{3,2,1,0:T(8,128)(2,1)} %copy-done.8) | copy-start | bytes 1179652
  51.1 2.8 %copy-start.1 = (bf16[2,16,256,384]{3,2,1,0:T(8,128)(2,1)S(1)}, bf16[2,16,256,384]{3,2,1,0:T(8,128)(2,1)}, u32[]{:S(2)}) copy-start(bf16[2,16,256,384]{3,2,1,0:T(8,128)(2,1)} %refs_0_.5) | copy-start | bytes 18874372
  65.5 39.0 %copy-start.3 = (bf16[1024,1024]{1,0:T(8,128)(2,1)S(1)}, bf16[1024,1024]{1,0:T(8,128)(2,1)}, u32[]{:S(2)}) copy-start(bf16[1024,1024]{1,0:T(8,128)(2,1)} %constant.21.clone.refs_10_.refs_6_) | copy-start | bytes 6291460
  65.5 39.0 %copy-start.4 = (bf16[1024,1024]{1,0:T(8,128)(2,1)S(1)}, bf16[1024,1024]{1,0:T(8,128)(2,1)}, u32[]{:S(2)}) copy-start(bf16[1024,1024]{1,0:T(8,128)(2,1)} %constant.20.clone.refs_9_.refs_5_) | copy-start | bytes 6291460
  65.5 39.0 %copy-start.12 = (bf16[2,6,48,256]{3,2,1,0:T(8,128)(2,1)S(1)}, bf16[2,6,48,256]{3,2,1,0:T(8,128)(2,1)}, u32[]{:S(2)}) copy-start(bf16[2,6,48,256]{3,2,1,0:T(8,128)(2,1)} %get-tuple-element.95.refs_1_) | copy-start | bytes 884740
  65.5 8.2 %collective-permute-start.8 = (bf16[2,4,256,384]{3,2,1,0:T(8,128)(2,1)S(1)}, bf16[2,4,256,384]{3,2,1,0:T(8,128)(2,1)S(1)}, u32[]{:S(2)}, u32[]{:S(2)}) collective-permute-start(bf16[2,4,256,384]{3,2,1,0:T(8,128)(2,1)S(1)} %interpolate.5.refs_1_.refs_7_), channel_id=1, source_target_pairs={{0,1},{1,0},{2,3},{3,2},{4,5},{5,4},{6,7},{7,6},{8,9},{9,8},{10,11... | collective-permute-start | bytes 4718600 | tf_op jit(solution)/shard_map/ppermute | solution.py:525
  65.5 29.2 %collective-permute-start.12 = (bf16[2,6,4,48,256]{4,3,2,1,0:T(8,128)(2,1)S(1)}, bf16[2,6,4,48,256]{4,3,2,1,0:T(8,128)(2,1)S(1)}, u32[]{:S(2)}, u32[]{:S(2)}) collective-permute-start(bf16[2,6,4,48,256]{4,3,2,1,0:T(8,128)(2,1)S(1)} %get-tuple-element.82.refs_5_.refs_3_), channel_id=1, source_target_pairs={{0,2},{2,0},{1,3},{3,1},{4,6},{6,4},{5,7},{7,5},{8,10},{10,8},{9,1... | collective-permute-start | bytes 3538952 | tf_op jit(solution)/shard_map/ppermute | solution.py:525
  67.0 17.2 %collective-permute-start.9 = (bf16[2,6,48,256]{3,2,1,0:T(8,128)(2,1)S(1)}, bf16[2,6,48,256]{3,2,1,0:T(8,128)(2,1)S(1)}, u32[]{:S(2)}, u32[]{:S(2)}) collective-permute-start(bf16[2,6,48,256]{3,2,1,0:T(8,128)(2,1)S(1)} %get-tuple-element.89), channel_id=1, source_target_pairs={{0,4},{4,0},{8,12},{12,8},{1,5},{5,1},{9,13},{13,9},{2,6},{6,2},{1... | collective-permute-start | bytes 884744 | tf_op jit(solution)/shard_map/ppermute | solution.py:525
  71.2 23.4 %collective-permute-start.10 = (bf16[2,6,48,256]{3,2,1,0:T(8,128)(2,1)S(1)}, bf16[2,6,48,256]{3,2,1,0:T(8,128)(2,1)S(1)}, u32[]{:S(2)}, u32[]{:S(2)}) collective-permute-start(bf16[2,6,48,256]{3,2,1,0:T(8,128)(2,1)S(1)} %get-tuple-element.90), channel_id=1, source_target_pairs={{0,8},{4,12},{8,0},{12,4},{1,9},{5,13},{9,1},{13,5},{2,10},{6,14},... | collective-permute-start | bytes 884744 | tf_op jit(solution)/shard_map/ppermute | solution.py:525
  72.3 22.3 %collective-permute-start.11 = (bf16[2,6,48,256]{3,2,1,0:T(8,128)(2,1)S(1)}, bf16[2,6,48,256]{3,2,1,0:T(8,128)(2,1)S(1)}, u32[]{:S(2)}, u32[]{:S(2)}) collective-permute-start(bf16[2,6,48,256]{3,2,1,0:T(8,128)(2,1)S(1)} %get-tuple-element.91), channel_id=1, source_target_pairs={{0,12},{4,8},{8,4},{12,0},{1,13},{5,9},{9,5},{13,1},{2,14},{6,10},... | collective-permute-start | bytes 884744 | tf_op jit(solution)/shard_map/ppermute | solution.py:525
  94.6 24.7 %copy-start.10 = (bf16[2,2,256,512]{3,2,1,0:T(8,128)(2,1)S(1)}, bf16[2,2,256,512]{3,2,1,0:T(8,128)(2,1)}, u32[]{:S(2)}) copy-start(bf16[2,2,256,512]{3,2,1,0:T(8,128)(2,1)} %constant.22.clone.refs_1_) | copy-start | bytes 3145732
  94.6 24.7 %copy-start.11 = (bf16[2,6,4,48,256]{4,3,2,1,0:T(8,128)(2,1)S(1)}, bf16[2,6,4,48,256]{4,3,2,1,0:T(8,128)(2,1)}, u32[]{:S(2)}) copy-start(bf16[2,6,4,48,256]{4,3,2,1,0:T(8,128)(2,1)} %get-tuple-element.72.refs_2_) | copy-start | bytes 3538948
  94.7 24.2 %collective-permute-start.16 = (bf16[2,4,4,48,256]{4,3,2,1,0:T(8,128)(2,1)S(1)}, bf16[2,4,4,48,256]{4,3,2,1,0:T(8,128)(2,1)S(1)}, u32[]{:S(2)}, u32[]{:S(2)}) collective-permute-start(bf16[2,4,4,48,256]{4,3,2,1,0:T(8,128)(2,1)S(1)} %get-tuple-element.92.refs_11_.refs_4_), channel_id=1, source_target_pairs={{0,2},{2,0},{1,3},{3,1},{4,6},{6,4},{5,7},{7,5},{8,10},{10,8},{9,1... | collective-permute-start | bytes 2359304 | tf_op jit(solution)/shard_map/ppermute | solution.py:525
  96.2 14.9 %collective-permute-start.13 = (bf16[2,4,48,256]{3,2,1,0:T(8,128)(2,1)S(1)}, bf16[2,4,48,256]{3,2,1,0:T(8,128)(2,1)S(1)}, u32[]{:S(2)}, u32[]{:S(2)}) collective-permute-start(bf16[2,4,48,256]{3,2,1,0:T(8,128)(2,1)S(1)} %get-tuple-element.103), channel_id=1, source_target_pairs={{0,4},{4,0},{8,12},{12,8},{1,5},{5,1},{9,13},{13,9},{2,6},{6,2},{1... | collective-permute-start | bytes 589832 | tf_op jit(solution)/shard_map/ppermute | solution.py:525
  102.0 16.8 %collective-permute-start.14 = (bf16[2,4,48,256]{3,2,1,0:T(8,128)(2,1)S(1)}, bf16[2,4,48,256]{3,2,1,0:T(8,128)(2,1)S(1)}, u32[]{:S(2)}, u32[]{:S(2)}) collective-permute-start(bf16[2,4,48,256]{3,2,1,0:T(8,128)(2,1)S(1)} %get-tuple-element.104), channel_id=1, source_target_pairs={{0,8},{4,12},{8,0},{12,4},{1,9},{5,13},{9,1},{13,5},{2,10},{6,14},... | collective-permute-start | bytes 589832 | tf_op jit(solution)/shard_map/ppermute | solution.py:525
  103.0 15.8 %collective-permute-start.15 = (bf16[2,4,48,256]{3,2,1,0:T(8,128)(2,1)S(1)}, bf16[2,4,48,256]{3,2,1,0:T(8,128)(2,1)S(1)}, u32[]{:S(2)}, u32[]{:S(2)}) collective-permute-start(bf16[2,4,48,256]{3,2,1,0:T(8,128)(2,1)S(1)} %get-tuple-element.105), channel_id=1, source_target_pairs={{0,12},{4,8},{8,4},{12,0},{1,13},{5,9},{9,5},{13,1},{2,14},{6,10},... | collective-permute-start | bytes 589832 | tf_op jit(solution)/shard_map/ppermute | solution.py:525
  118.8 65.2 %collective-permute-start.23 = (bf16[2,12,48,1024]{3,2,1,0:T(8,128)(2,1)S(1)}, bf16[2,12,48,1024]{3,2,1,0:T(8,128)(2,1)S(1)}, u32[]{:S(2)}, u32[]{:S(2)}) collective-permute-start(bf16[2,12,48,1024]{3,2,1,0:T(8,128)(2,1)S(1)} %cross_transform.4.refs_8_.refs_2_), channel_id=1, source_target_pairs={{0,2},{2,0},{1,3},{3,1},{4,6},{6,4},{5,7},{7,5},{8,10},{10,8},{9,1... | collective-permute-start | bytes 7077896 | tf_op jit(solution)/shard_map/ppermute | solution.py:525
  122.8 16.5 %collective-permute-start.17 = (bf16[2,8,48,256]{3,2,1,0:T(8,128)(2,1)S(1)}, bf16[2,8,48,256]{3,2,1,0:T(8,128)(2,1)S(1)}, u32[]{:S(2)}, u32[]{:S(2)}) collective-permute-start(bf16[2,8,48,256]{3,2,1,0:T(8,128)(2,1)S(1)} %get-tuple-element.109), channel_id=1, source_target_pairs={{0,4},{4,0},{8,12},{12,8},{1,5},{5,1},{9,13},{13,9},{2,6},{6,2},{1... | collective-permute-start | bytes 1179656 | tf_op jit(solution)/shard_map/ppermute | solution.py:525
  125.5 29.8 %collective-permute-start.18 = (bf16[2,8,48,256]{3,2,1,0:T(8,128)(2,1)S(1)}, bf16[2,8,48,256]{3,2,1,0:T(8,128)(2,1)S(1)}, u32[]{:S(2)}, u32[]{:S(2)}) collective-permute-start(bf16[2,8,48,256]{3,2,1,0:T(8,128)(2,1)S(1)} %get-tuple-element.110), channel_id=1, source_target_pairs={{0,8},{4,12},{8,0},{12,4},{1,9},{5,13},{9,1},{13,5},{2,10},{6,14},... | collective-permute-start | bytes 1179656 | tf_op jit(solution)/shard_map/ppermute | solution.py:525
  126.5 28.8 %collective-permute-start.19 = (bf16[2,8,48,256]{3,2,1,0:T(8,128)(2,1)S(1)}, bf16[2,8,48,256]{3,2,1,0:T(8,128)(2,1)S(1)}, u32[]{:S(2)}, u32[]{:S(2)}) collective-permute-start(bf16[2,8,48,256]{3,2,1,0:T(8,128)(2,1)S(1)} %get-tuple-element.111), channel_id=1, source_target_pairs={{0,12},{4,8},{8,4},{12,0},{1,13},{5,9},{9,5},{13,1},{2,14},{6,10},... | collective-permute-start | bytes 1179656 | tf_op jit(solution)/shard_map/ppermute | solution.py:525
  130.9 53.1 %collective-permute-start.24 = (bf16[2,4,48,1024]{3,2,1,0:T(8,128)(2,1)S(1)}, bf16[2,4,48,1024]{3,2,1,0:T(8,128)(2,1)S(1)}, u32[]{:S(2)}, u32[]{:S(2)}) collective-permute-start(bf16[2,4,48,1024]{3,2,1,0:T(8,128)(2,1)S(1)} %cross_transform.5.refs_7_.refs_3_), channel_id=1, source_target_pairs={{0,2},{2,0},{1,3},{3,1},{4,6},{6,4},{5,7},{7,5},{8,10},{10,8},{9,1... | collective-permute-start | bytes 2359304 | tf_op jit(solution)/shard_map/ppermute | solution.py:525
  155.3 33.8 %collective-permute-start.20 = (bf16[2,8,48,256]{3,2,1,0:T(8,128)(2,1)S(1)}, bf16[2,8,48,256]{3,2,1,0:T(8,128)(2,1)S(1)}, u32[]{:S(2)}, u32[]{:S(2)}) collective-permute-start(bf16[2,8,48,256]{3,2,1,0:T(8,128)(2,1)S(1)} %get-tuple-element.121), channel_id=1, source_target_pairs={{0,4},{4,0},{8,12},{12,8},{1,5},{5,1},{9,13},{13,9},{2,6},{6,2},{1... | collective-permute-start | bytes 1179656 | tf_op jit(solution)/shard_map/ppermute | solution.py:525
  160.7 29.3 %collective-permute-start.21 = (bf16[2,8,48,256]{3,2,1,0:T(8,128)(2,1)S(1)}, bf16[2,8,48,256]{3,2,1,0:T(8,128)(2,1)S(1)}, u32[]{:S(2)}, u32[]{:S(2)}) collective-permute-start(bf16[2,8,48,256]{3,2,1,0:T(8,128)(2,1)S(1)} %get-tuple-element.122), channel_id=1, source_target_pairs={{0,8},{4,12},{8,0},{12,4},{1,9},{5,13},{9,1},{13,5},{2,10},{6,14},... | collective-permute-start | bytes 1179656 | tf_op jit(solution)/shard_map/ppermute | solution.py:525
  162.1 27.9 %collective-permute-start.22 = (bf16[2,8,48,256]{3,2,1,0:T(8,128)(2,1)S(1)}, bf16[2,8,48,256]{3,2,1,0:T(8,128)(2,1)S(1)}, u32[]{:S(2)}, u32[]{:S(2)}) collective-permute-start(bf16[2,8,48,256]{3,2,1,0:T(8,128)(2,1)S(1)} %get-tuple-element.123), channel_id=1, source_target_pairs={{0,12},{4,8},{8,4},{12,0},{1,13},{5,9},{9,5},{13,1},{2,14},{6,10},... | collective-permute-start | bytes 1179656 | tf_op jit(solution)/shard_map/ppermute | solution.py:525

commit v4 on v3

--- a/solution.py
+++ b/solution.py
@@ -570,10 +570,10 @@
         return interpolate(polar, halo, bands, *CHUNKS[i], earlier, limit)
 
     def to_owners(blocks, which=range(az_count - 1, 0, -1)):
-        return {s: exchange(blocks[s], "az", s) for s in which}
+        return {4 - s: exchange(blocks[s], "az", s) for s in which}
 
     def in_order(blocks, come):
-        return [blocks[0]] + [come[s] for s in range(1, az_count)]
+        return [blocks[0]] + [come[4 - s] for s in range(1, az_count)]
 
     bare = interpolate(polar, None, bands, *CHUNKS[0], (), WIDE_VMEM)
     made = interpolate_edges(polar, halo, bands, CHUNKS[0][0], bare)

time: 199 us -> 196 us (0.985); the launches traced: 196 us -> 196 us
  starting transfers between devices: 46.7 us -> 39.1 us
  waiting for transfers between devices: 69.4 us -> 76.8 us
    ppermute x23, starting transfers between devices: 40.4 us -> 32.9 us  [exchange(): lax.ppermute(value, axis, [(i, i ^ s) for i in range(lax.axis_size(axis))])]
    ppermute x23, waiting for transfers between devices: 69.4 us -> 76.8 us  [exchange(): lax.ppermute(value, axis, [(i, i ^ s) for i in range(lax.axis_size(axis))])]
where the time goes in v4:
time: 196 us
  waiting for transfers between devices  76.8 us (39%)
  Pallas kernels  72.4 us (37%)
  starting transfers between devices  39.1 us (20%)
  local copies, waits for them, and re-layouts  6.35 us (3%)
    ppermute x23, waiting for transfers between devices, exchange(): lax.ppermute(value, axis, [(i, i ^ s) for i in range(lax.axis_size(axis))])  76.8 us
    ppermute x23, starting transfers between devices, exchange(): lax.ppermute(value, axis, [(i, i ^ s) for i in range(lax.axis_size(axis))])  32.9 us
    pallas_call x3, Pallas kernels, interpolate(): pl.pallas_call(lambda *refs: interp_kernel(*refs, bordered=len(border) ==...  22.7 us
    pallas_call x4, Pallas kernels, cross_transform(): pl.pallas_call(lambda *refs: cross_kernel(*refs, groups=groups, blocks=bl...  20.9 us
    pallas_call x3, Pallas kernels, range_transform(): pl.pallas_call(lambda *refs: range_kernel(*refs, blocks=blocks, earlier=l...  17.8 us
    unnamed x29, local copies, waits for them, and re-layouts  5.26 us
    pallas_call x1, Pallas kernels, last_heights(): pl.pallas_call(lambda *refs: height_kernel(*refs, chunks=chunks, sets=1,...  5.11 us
    ppermute x1, starting transfers between devices, halo_rows(): lax.ppermute(tail, 'az', [(i, i + 1) for i in range(ends)])  4.94 us
  transfers between devices with their start and end apart: 25, of which 9 were waited for; matrix products, arithmetic and copies ran while one was open for 0% of the time, Pallas kernels for 29%

profile of v4, /device:TPU:0, one launch (start us, length us, event | category | flops | bytes accessed | tf_op | source)
XLA Modules:
  0.0 195.6 jit_solution(6895495831226136589)
XLA Ops:
  0.0 1.1 fusion
  1.1 4.9 %collective-permute-start = (bf16[2,16,8,384]{3,2,1,0:T(8,128)(2,1)S(1)}, bf16[2,16,8,384]{3,2,1,0:T(8,128)(2,1)S(1)}, u32[]{:S(2)}, u32[]{:S(2)}) collective-permute-start(bf16[2,16,8,384]{3,2,1,0:T(8,128)(2,1)S(1)} %get-tuple-element.130), channel_id=1, source_target_pairs={{0,4},{4,8},{8,12},{1,5},{5,9},{9,13},{2,6},{6,10},{10,14},{3,7},{... | collective-permute-start | bytes 589832 | tf_op jit(solution)/shard_map/ppermute | solution.py:536
  6.0 1.3 collective-permute-start.1
  7.3 8.6 %interpolate.3.made_ref = bf16[2,6,256,384]{3,2,1,0:T(8,128)(2,1)} custom-call(bf16[2,16,256,384]{3,2,1,0:T(8,128)(2,1)} %refs_0_.5, s32[256,384]{1,0:T(8,128)} %refs_1_.7, s32[256,384]{1,0:T(8,128)} %refs_2_.5, bf16[8,256,384]{2,1,0:T(8,128)(2,1)} %refs_3_.8), custom_call_target="tpu_custom_call" | custom-call | flops 40108 | bytes 4718 | tf_op jit(solution)/shard_map/interpolate/pallas_call | solution.py:204
  16.0 0.8 copy-done.8
  16.7 2.5 %interpolate_edges.1.refs_5_.refs_1_ = bf16[2,6,256,384]{3,2,1,0:T(8,128)(2,1)} custom-call(bf16[2,16,256,384]{3,2,1,0:T(8,128)(2,1)} %refs_0_.5, bf16[2,16,16,384]{3,2,1,0:T(8,128)(2,1)} %copy-done.8, s32[256,384]{1,0:T(8,128)} %refs_1_.7, s32[256,384]{1,0:T(8,128)} %refs_2_.5, bf16[8,256,384]{2,1,0:T(8,128)(2,1)} %refs_3_.8, ...), custom_call_target="tpu_custom_call", output_to_operand_aliasing={{}: (5, {})} | custom-call | flops 5013 | bytes 589 | tf_op jit(solution)/shard_map/interpolate_edges/pallas_call | solution.py:244
  19.3 0.6 pad_add_fusion.refs_0_
  19.9 8.6 %interpolate.4.refs_7_.refs_1_ = bf16[2,6,256,384]{3,2,1,0:T(8,128)(2,1)} custom-call(bf16[2,16,256,384]{3,2,1,0:T(8,128)(2,1)} %refs_0_.5, s32[256,384]{1,0:T(8,128)} %refs_1_.7, s32[256,384]{1,0:T(8,128)} %refs_2_.5, bf16[8,256,384]{2,1,0:T(8,128)(2,1)} %refs_3_.8, bf16[2,16,16,384]{3,2,1,0:T(8,128)(2,1)} %copy-done.8, ...), custom_call_target="tpu_custom_call" | custom-call | flops 40108 | bytes 4718 | tf_op jit(solution)/shard_map/interpolate/pallas_call | solution.py:204
  28.5 8.3 %range_transform.3 = (bf16[2,6,4,48,256]{4,3,2,1,0:T(8,128)(2,1)}, bf16[2,6,48,256]{3,2,1,0:T(8,128)(2,1)}, bf16[2,6,48,256]{3,2,1,0:T(8,128)(2,1)}, bf16[2,6,48...) custom-call(s32[3]{0:T(128)} %pad_add_fusion.refs_0_, bf16[2,6,256,384]{3,2,1,0:T(8,128)(2,1)} %interpolate_edges.1.refs_5_.refs_1_, ...), custom_call_target="tpu_custom_call" | custom-call | flops 3623878 | bytes 7077 | tf_op jit(solution)/shard_map/range_transform/pallas_call | solution.py:303
  36.8 0.2 collective-permute-start.3
  37.0 1.5 collective-permute-start.7
  38.5 4.7 %collective-permute-start.4 = (bf16[2,6,48,256]{3,2,1,0:T(8,128)(2,1)}, bf16[2,6,48,256]{3,2,1,0:T(8,128)(2,1)S(1)}, u32[]{:S(2)}, u32[]{:S(2)}) collective-permute-start(bf16[2,6,48,256]{3,2,1,0:T(8,128)(2,1)} %get-tuple-element.79), channel_id=1, source_target_pairs={{0,12},{4,8},{8,4},{12,0},{1,13},{5,9},{9,5},{13,1},{2,14},{6,10},... | collective-permute-start | bytes 884744 | tf_op jit(solution)/shard_map/ppermute | solution.py:525
  43.2 0.6 collective-permute-start.6
  43.8 1.7 copy-done.2
  45.5 5.6 %range_transform.4 = (bf16[2,6,4,48,256]{4,3,2,1,0:T(8,128)(2,1)S(1)}, bf16[2,6,48,256]{3,2,1,0:T(8,128)(2,1)S(1)}, bf16[2,6,48,256]{3,2,1,0:T(8,128)(2,1)S(1)},...) custom-call(s32[3]{0:T(128)S(1)} %copy-done.13, bf16[2,6,256,384]{3,2,1,0:T(8,128)(2,1)S(1)} %copy-done.2, ...), custom_call_target="tpu_custom_call" | custom-call | flops 3623878 | bytes 7077 | tf_op jit(solution)/shard_map/range_transform/pallas_call | solution.py:303
  51.1 2.8 %copy-done.1 = bf16[2,16,256,384]{3,2,1,0:T(8,128)(2,1)S(1)} copy-done((bf16[2,16,256,384]{3,2,1,0:T(8,128)(2,1)S(1)}, bf16[2,16,256,384]{3,2,1,0:T(8,128)(2,1)}, u32[]{:S(2)}) %copy-start.1) | copy-done | bytes 6291480
  53.9 5.5 %interpolate.5.refs_1_.refs_7_ = bf16[2,4,256,384]{3,2,1,0:T(8,128)(2,1)S(1)} custom-call(bf16[2,16,256,384]{3,2,1,0:T(8,128)(2,1)S(1)} %copy-done.1, s32[256,384]{1,0:T(8,128)S(1)} %copy-done.6, s32[256,384]{1,0:T(8,128)S(1)} %copy-done.7, bf16[8,256,384]{2,1,0:T(8,128)(2,1)S(1)} %copy-done.5, bf16[2,16,16,384]{3,2,1,0:T(8,128)(2,1)S(1)} %copy-done.9, ...), custom_call_target="tpu_custom_call" | custom-call | flops 26738 | bytes 3145 | tf_op jit(solution)/shard_map/interpolate/pallas_call | solution.py:204
  59.3 9.2 %collective-permute-done.5.refs_3_ = bf16[2,6,48,256]{3,2,1,0:T(8,128)(2,1)S(1)} collective-permute-done((bf16[2,6,48,256]{3,2,1,0:T(8,128)(2,1)}, bf16[2,6,48,256]{3,2,1,0:T(8,128)(2,1)S(1)}, u32[]{:S(2)}, u32[]{:S(2)}) %collective-permute-start.5) | collective-permute-done | bytes 294944 | tf_op jit(solution)/shard_map/ppermute | solution.py:525
  68.5 0.1 collective-permute-start.8
  68.6 0.6 collective-permute-start.12
  69.2 2.6 %collective-permute-start.9 = (bf16[2,6,48,256]{3,2,1,0:T(8,128)(2,1)S(1)}, bf16[2,6,48,256]{3,2,1,0:T(8,128)(2,1)S(1)}, u32[]{:S(2)}, u32[]{:S(2)}) collective-permute-start(bf16[2,6,48,256]{3,2,1,0:T(8,128)(2,1)S(1)} %get-tuple-element.89), channel_id=1, source_target_pairs={{0,12},{4,8},{8,4},{12,0},{1,13},{5,9},{9,5},{13,1},{2,14},{6,10},... | collective-permute-start | bytes 884744 | tf_op jit(solution)/shard_map/ppermute | solution.py:525
  71.9 1.7 collective-permute-start.11
  73.6 3.9 %range_transform.5 = (bf16[2,4,4,48,256]{4,3,2,1,0:T(8,128)(2,1)S(1)}, bf16[2,4,48,256]{3,2,1,0:T(8,128)(2,1)S(1)}, bf16[2,4,48,256]{3,2,1,0:T(8,128)(2,1)S(1)},...) custom-call(s32[3]{0:T(128)S(1)} %copy-done.13, bf16[2,4,256,384]{3,2,1,0:T(8,128)(2,1)S(1)} %interpolate.5.refs_1_.refs_7_, ...), custom_call_target="tpu_custom_call" | custom-call | flops 2415919 | bytes 4718 | tf_op jit(solution)/shard_map/range_transform/pallas_call | solution.py:303
  77.5 3.5 %collective-permute-done.9.refs_8_ = bf16[2,6,48,256]{3,2,1,0:T(8,128)(2,1)S(1)} collective-permute-done((bf16[2,6,48,256]{3,2,1,0:T(8,128)(2,1)S(1)}, bf16[2,6,48,256]{3,2,1,0:T(8,128)(2,1)S(1)}, u32[]{:S(2)}, u32[]{:S(2)}) %collective-permute-start.9) | collective-permute-done | bytes 294944 | tf_op jit(solution)/shard_map/ppermute | solution.py:525
  81.0 15.9 %collective-permute-done.10.refs_7_ = bf16[2,6,48,256]{3,2,1,0:T(8,128)(2,1)S(1)} collective-permute-done((bf16[2,6,48,256]{3,2,1,0:T(8,128)(2,1)S(1)}, bf16[2,6,48,256]{3,2,1,0:T(8,128)(2,1)S(1)}, u32[]{:S(2)}, u32[]{:S(2)}) %collective-permute-start.10) | collective-permute-done | bytes 294944 | tf_op jit(solution)/shard_map/ppermute | solution.py:525
  96.9 0.1 collective-permute-done.12.refs_6_
  97.0 1.2 collective-permute-start.16
  98.2 2.0 %collective-permute-start.13 = (bf16[2,4,48,256]{3,2,1,0:T(8,128)(2,1)S(1)}, bf16[2,4,48,256]{3,2,1,0:T(8,128)(2,1)S(1)}, u32[]{:S(2)}, u32[]{:S(2)}) collective-permute-start(bf16[2,4,48,256]{3,2,1,0:T(8,128)(2,1)S(1)} %get-tuple-element.103), channel_id=1, source_target_pairs={{0,12},{4,8},{8,4},{12,0},{1,13},{5,9},{9,5},{13,1},{2,14},{6,10},... | collective-permute-start | bytes 589832 | tf_op jit(solution)/shard_map/ppermute | solution.py:525
  100.2 2.4 %collective-permute-start.15 = (bf16[2,4,48,256]{3,2,1,0:T(8,128)(2,1)S(1)}, bf16[2,4,48,256]{3,2,1,0:T(8,128)(2,1)S(1)}, u32[]{:S(2)}, u32[]{:S(2)}) collective-permute-start(bf16[2,4,48,256]{3,2,1,0:T(8,128)(2,1)S(1)} %get-tuple-element.105), channel_id=1, source_target_pairs={{0,4},{4,0},{8,12},{12,8},{1,5},{5,1},{9,13},{13,9},{2,6},{6,2},{1... | collective-permute-start | bytes 589832 | tf_op jit(solution)/shard_map/ppermute | solution.py:525
  102.6 6.6 %cross_transform.4.refs_8_.refs_2_ = bf16[2,12,48,1024]{3,2,1,0:T(8,128)(2,1)S(1)} custom-call(s32[3]{0:T(128)S(1)} %copy-done.13, bf16[2,6,48,256]{3,2,1,0:T(8,128)(2,1)S(1)} %copy-done.12, bf16[2,6,48,256]{3,2,1,0:T(8,128)(2,1)S(1)} %collective-permute-done.6.refs_2_, bf16[2,6,48,256]{3,2,1,0:T(8,128)(2,1)S(1)} %collective-permute-done.5.refs_3_, ...), custom_call_target="tpu_custom_call" | custom-call | flops 4831838 | bytes 8912 | tf_op jit(solution)/shard_map/cross_transform/pallas_call | solution.py:489
  109.2 6.8 %collective-permute-done.14.refs_3_ = bf16[2,4,48,256]{3,2,1,0:T(8,128)(2,1)S(1)} collective-permute-done((bf16[2,4,48,256]{3,2,1,0:T(8,128)(2,1)S(1)}, bf16[2,4,48,256]{3,2,1,0:T(8,128)(2,1)S(1)}, u32[]{:S(2)}, u32[]{:S(2)}) %collective-permute-start.14) | collective-permute-done | bytes 196640 | tf_op jit(solution)/shard_map/ppermute | solution.py:525
  116.0 0.1 collective-permute-done.16.refs_7_
  116.1 1.1 collective-permute-start.23
  117.3 3.4 %first_heights.1 = (bf16[2,8,48,256]{3,2,1,0:T(8,128)(2,1)S(1)}, bf16[2,8,48,256]{3,2,1,0:T(8,128)(2,1)S(1)}, bf16[2,8,48,256]{3,2,1,0:T(8,128)(2,1)S(1)}, bf16[...) custom-call(s32[3]{0:T(128)S(1)} %copy-done.13, ...), custom_call_target="tpu_custom_call" | custom-call | flops 1610612 | bytes 9437 | tf_op jit(solution)/shard_map/first_heights/pallas_call | solution.py:381
  120.7 0.1 collective-permute-start.19
  120.7 2.6 %collective-permute-start.18 = (bf16[2,8,48,256]{3,2,1,0:T(8,128)(2,1)S(1)}, bf16[2,8,48,256]{3,2,1,0:T(8,128)(2,1)S(1)}, u32[]{:S(2)}, u32[]{:S(2)}) collective-permute-start(bf16[2,8,48,256]{3,2,1,0:T(8,128)(2,1)S(1)} %get-tuple-element.110), channel_id=1, source_target_pairs={{0,8},{4,12},{8,0},{12,4},{1,9},{5,13},{9,1},{13,5},{2,10},{6,14},... | collective-permute-start | bytes 1179656 | tf_op jit(solution)/shard_map/ppermute | solution.py:525
  123.3 1.8 collective-permute-start.17
  125.1 3.0 %cross_transform.5.refs_7_.refs_3_ = bf16[2,4,48,1024]{3,2,1,0:T(8,128)(2,1)S(1)} custom-call(s32[3]{0:T(128)S(1)} %copy-done.13, bf16[2,4,48,256]{3,2,1,0:T(8,128)(2,1)S(1)} %get-tuple-element.116.refs_1_, bf16[2,4,48,256]{3,2,1,0:T(8,128)(2,1)S(1)} %collective-permute-done.15.refs_2_, bf16[2,4,48,256]{3,2,1,0:T(8,128)(2,1)S(1)} %collective-permute-done.14.refs_3_, ...), custom_call_target="tpu_custom_call" | custom-call | flops 1610612 | bytes 5767 | tf_op jit(solution)/shard_map/cross_transform/pallas_call | solution.py:489
  128.1 1.0 collective-permute-start.24
  129.1 7.8 %collective-permute-done.19.refs_2_ = bf16[2,8,48,256]{3,2,1,0:T(8,128)(2,1)S(1)} collective-permute-done((bf16[2,8,48,256]{3,2,1,0:T(8,128)(2,1)S(1)}, bf16[2,8,48,256]{3,2,1,0:T(8,128)(2,1)S(1)}, u32[]{:S(2)}, u32[]{:S(2)}) %collective-permute-start.19) | collective-permute-done | bytes 393248 | tf_op jit(solution)/shard_map/ppermute | solution.py:525
  136.9 13.7 %collective-permute-done.18.refs_3_ = bf16[2,8,48,256]{3,2,1,0:T(8,128)(2,1)S(1)} collective-permute-done((bf16[2,8,48,256]{3,2,1,0:T(8,128)(2,1)S(1)}, bf16[2,8,48,256]{3,2,1,0:T(8,128)(2,1)S(1)}, u32[]{:S(2)}, u32[]{:S(2)}) %collective-permute-start.18) | collective-permute-done | bytes 393248 | tf_op jit(solution)/shard_map/ppermute | solution.py:525
  150.6 6.3 %collective-permute-start.20 = (bf16[2,8,48,256]{3,2,1,0:T(8,128)(2,1)S(1)}, bf16[2,8,48,256]{3,2,1,0:T(8,128)(2,1)S(1)}, u32[]{:S(2)}, u32[]{:S(2)}) collective-permute-start(bf16[2,8,48,256]{3,2,1,0:T(8,128)(2,1)S(1)} %get-tuple-element.121), channel_id=1, source_target_pairs={{0,4},{4,0},{8,12},{12,8},{1,5},{5,1},{9,13},{13,9},{2,6},{6,2},{1... | collective-permute-start | bytes 1179656 | tf_op jit(solution)/shard_map/ppermute | solution.py:525
  157.0 1.0 collective-permute-start.21
  157.9 1.5 collective-permute-start.22
  159.4 5.7 %cross_transform.6.refs_6_ = bf16[2,16,96,1024]{3,2,1,0:T(8,128)(2,1)} custom-call(s32[3]{0:T(128)S(1)} %copy-done.13, bf16[2,8,48,256]{3,2,1,0:T(8,128)(2,1)S(1)} %get-tuple-element.125.refs_7_.refs_1_, bf16[2,8,48,256]{3,2,1,0:T(8,128)(2,1)S(1)} %collective-permute-done.19.refs_2_, bf16[2,8,48,256]{3,2,1,0:T(8,128)(2,1)S(1)} %collective-permute-done.18.refs_3_, ...), custom_call_target="tpu_custom_call" | custom-call | flops 3221225 | bytes 7340 | tf_op jit(solution)/shard_map/cross_transform/pallas_call | solution.py:489
  165.1 19.7 %collective-permute-done.24.refs_5_ = bf16[2,4,48,1024]{3,2,1,0:T(8,128)(2,1)S(1)} collective-permute-done((bf16[2,4,48,1024]{3,2,1,0:T(8,128)(2,1)S(1)}, bf16[2,4,48,1024]{3,2,1,0:T(8,128)(2,1)S(1)}, u32[]{:S(2)}, u32[]{:S(2)}) %collective-permute-start.24) | collective-permute-done | bytes 786464 | tf_op jit(solution)/shard_map/ppermute | solution.py:525
  184.9 5.1 %last_heights.1.refs_7_ = bf16[2,16,96,1024]{3,2,1,0:T(8,128)(2,1)} custom-call(s32[3]{0:T(128)S(1)} %copy-done.13, bf16[2,2,256,512]{3,2,1,0:T(8,128)(2,1)S(1)} %copy-done.10, bf16[2,12,48,1024]{3,2,1,0:T(8,128)(2,1)S(1)} %cross_transform.4.refs_8_.refs_2_, ...), custom_call_target="tpu_custom_call", output_to_operand_aliasing={{}: (6, {})} | custom-call | flops 1610612 | bytes 9437 | tf_op jit(solution)/shard_map/last_heights/pallas_call | solution.py:416
  190.0 5.6 %cross_transform.7 = bf16[2,16,96,1024]{3,2,1,0:T(8,128)(2,1)} custom-call(s32[3]{0:T(128)S(1)} %copy-done.13, bf16[2,8,48,256]{3,2,1,0:T(8,128)(2,1)S(1)} %get-tuple-element.120.refs_1_, bf16[2,8,48,256]{3,2,1,0:T(8,128)(2,1)S(1)} %collective-permute-done.20.refs_2_, ...), custom_call_target="tpu_custom_call", output_to_operand_aliasing={{}: (7, {})} | custom-call | flops 3221225 | bytes 7340 | tf_op jit(solution)/shard_map/cross_transform/pallas_call | solution.py:489
  (47 shorter events, 0.2 us)
Async XLA Ops:
  1.1 14.8 %collective-permute-start = (bf16[2,16,8,384]{3,2,1,0:T(8,128)(2,1)S(1)}, bf16[2,16,8,384]{3,2,1,0:T(8,128)(2,1)S(1)}, u32[]{:S(2)}, u32[]{:S(2)}) collective-permute-start(bf16[2,16,8,384]{3,2,1,0:T(8,128)(2,1)S(1)} %get-tuple-element.130), channel_id=1, source_target_pairs={{0,4},{4,8},{8,12},{1,5},{5,9},{9,13},{2,6},{6,10},{10,14},{3,7},{... | collective-permute-start | bytes 589832 | tf_op jit(solution)/shard_map/ppermute | solution.py:536
  6.0 9.9 %collective-permute-start.1 = (bf16[2,16,8,384]{3,2,1,0:T(8,128)(2,1)S(1)}, bf16[2,16,8,384]{3,2,1,0:T(8,128)(2,1)S(1)}, u32[]{:S(2)}, u32[]{:S(2)}) collective-permute-start(bf16[2,16,8,384]{3,2,1,0:T(8,128)(2,1)S(1)} %get-tuple-element.129), channel_id=1, source_target_pairs={{4,0},{8,4},{12,8},{5,1},{9,5},{13,9},{6,2},{10,6},{14,10},{7,3},{... | collective-permute-start | bytes 589832 | tf_op jit(solution)/shard_map/ppermute | solution.py:537
  16.0 0.8 copy-start.8
  19.3 9.2 %collective-permute-start.2 = (bf16[2,6,256,384]{3,2,1,0:T(8,128)(2,1)}, bf16[2,6,256,384]{3,2,1,0:T(8,128)(2,1)}, u32[]{:S(2)}, u32[]{:S(2)}) collective-permute-start(bf16[2,6,256,384]{3,2,1,0:T(8,128)(2,1)} %interpolate_edges.1.refs_5_.refs_1_), channel_id=1, source_target_pairs={{0,1},{1,0},{2,3},{3,2},{4,5},{5,4},{6,7},{7,6},{8,9},{9,8},{10,11... | collective-permute-start | bytes 7077896 | tf_op jit(solution)/shard_map/ppermute | solution.py:525
  28.5 15.3 %copy-start = (bf16[2,4,96,1536]{3,2,1,0:T(8,128)(2,1)S(1)}, bf16[2,4,96,1536]{3,2,1,0:T(8,128)(2,1)}, u32[]{:S(2)}) copy-start(bf16[2,4,96,1536]{3,2,1,0:T(8,128)(2,1)} %constant.19.clone.refs_3_.refs_4_.refs_5_.refs_6_) | copy-start | bytes 7077892
  28.5 15.3 %copy-start.13 = (s32[3]{0:T(128)S(1)}, s32[3]{0:T(128)}, u32[]{:S(2)}) copy-start(s32[3]{0:T(128)} %pad_add_fusion.refs_0_) | copy-start | bytes 40
  36.8 6.9 %collective-permute-start.3 = (bf16[2,6,256,384]{3,2,1,0:T(8,128)(2,1)}, bf16[2,6,256,384]{3,2,1,0:T(8,128)(2,1)S(1)}, u32[]{:S(2)}, u32[]{:S(2)}) collective-permute-start(bf16[2,6,256,384]{3,2,1,0:T(8,128)(2,1)} %interpolate.4.refs_7_.refs_1_), channel_id=1, source_target_pairs={{0,1},{1,0},{2,3},{3,2},{4,5},{5,4},{6,7},{7,6},{8,9},{9,8},{10,11... | collective-permute-start | bytes 7077896 | tf_op jit(solution)/shard_map/ppermute | solution.py:525
  37.0 31.5 %collective-permute-start.7 = (bf16[2,6,4,48,256]{4,3,2,1,0:T(8,128)(2,1)}, bf16[2,6,4,48,256]{4,3,2,1,0:T(8,128)(2,1)S(1)}, u32[]{:S(2)}, u32[]{:S(2)}) collective-permute-start(bf16[2,6,4,48,256]{4,3,2,1,0:T(8,128)(2,1)} %get-tuple-element.72.refs_2_), channel_id=1, source_target_pairs={{0,2},{2,0},{1,3},{3,1},{4,6},{6,4},{5,7},{7,5},{8,10},{10,8},{9,1... | collective-permute-start | bytes 3538952 | tf_op jit(solution)/shard_map/ppermute | solution.py:525
  38.5 20.8 %collective-permute-start.4 = (bf16[2,6,48,256]{3,2,1,0:T(8,128)(2,1)}, bf16[2,6,48,256]{3,2,1,0:T(8,128)(2,1)S(1)}, u32[]{:S(2)}, u32[]{:S(2)}) collective-permute-start(bf16[2,6,48,256]{3,2,1,0:T(8,128)(2,1)} %get-tuple-element.79), channel_id=1, source_target_pairs={{0,12},{4,8},{8,4},{12,0},{1,13},{5,9},{9,5},{13,1},{2,14},{6,10},... | collective-permute-start | bytes 884744 | tf_op jit(solution)/shard_map/ppermute | solution.py:525
  43.2 25.3 %collective-permute-start.5 = (bf16[2,6,48,256]{3,2,1,0:T(8,128)(2,1)}, bf16[2,6,48,256]{3,2,1,0:T(8,128)(2,1)S(1)}, u32[]{:S(2)}, u32[]{:S(2)}) collective-permute-start(bf16[2,6,48,256]{3,2,1,0:T(8,128)(2,1)} %get-tuple-element.80), channel_id=1, source_target_pairs={{0,8},{4,12},{8,0},{12,4},{1,9},{5,13},{9,1},{13,5},{2,10},{6,14},... | collective-permute-start | bytes 884744 | tf_op jit(solution)/shard_map/ppermute | solution.py:525
  43.2 25.3 %collective-permute-start.6 = (bf16[2,6,48,256]{3,2,1,0:T(8,128)(2,1)}, bf16[2,6,48,256]{3,2,1,0:T(8,128)(2,1)S(1)}, u32[]{:S(2)}, u32[]{:S(2)}) collective-permute-start(bf16[2,6,48,256]{3,2,1,0:T(8,128)(2,1)} %get-tuple-element.81), channel_id=1, source_target_pairs={{0,4},{4,0},{8,12},{12,8},{1,5},{5,1},{9,13},{13,9},{2,6},{6,2},{1... | collective-permute-start | bytes 884744 | tf_op jit(solution)/shard_map/ppermute | solution.py:525
  43.8 1.7 copy-start.2
  45.4 5.6 %copy-start.5 = (bf16[8,256,384]{2,1,0:T(8,128)(2,1)S(1)}, bf16[8,256,384]{2,1,0:T(8,128)(2,1)}, u32[]{:S(2)}) copy-start(bf16[8,256,384]{2,1,0:T(8,128)(2,1)} %refs_3_.8) | copy-start | bytes 4718596
  45.4 5.6 %copy-start.6 = (s32[256,384]{1,0:T(8,128)S(1)}, s32[256,384]{1,0:T(8,128)}, u32[]{:S(2)}) copy-start(s32[256,384]{1,0:T(8,128)} %refs_1_.7) | copy-start | bytes 1179652
  45.4 5.6 %copy-start.7 = (s32[256,384]{1,0:T(8,128)S(1)}, s32[256,384]{1,0:T(8,128)}, u32[]{:S(2)}) copy-start(s32[256,384]{1,0:T(8,128)} %refs_2_.5) | copy-start | bytes 1179652
  45.4 5.6 %copy-start.9 = (bf16[2,16,16,384]{3,2,1,0:T(8,128)(2,1)S(1)}, bf16[2,16,16,384]{3,2,1,0:T(8,128)(2,1)}, u32[]{:S(2)}) copy-start(bf16[2,16,16,384]{3,2,1,0:T(8,128)(2,1)} %copy-done.8) | copy-start | bytes 1179652
  51.1 2.8 %copy-start.1 = (bf16[2,16,256,384]{3,2,1,0:T(8,128)(2,1)S(1)}, bf16[2,16,256,384]{3,2,1,0:T(8,128)(2,1)}, u32[]{:S(2)}) copy-start(bf16[2,16,256,384]{3,2,1,0:T(8,128)(2,1)} %refs_0_.5) | copy-start | bytes 18874372
  68.5 34.1 %copy-start.3 = (bf16[1024,1024]{1,0:T(8,128)(2,1)S(1)}, bf16[1024,1024]{1,0:T(8,128)(2,1)}, u32[]{:S(2)}) copy-start(bf16[1024,1024]{1,0:T(8,128)(2,1)} %constant.21.clone.refs_10_.refs_6_) | copy-start | bytes 6291460
  68.5 34.1 %copy-start.4 = (bf16[1024,1024]{1,0:T(8,128)(2,1)S(1)}, bf16[1024,1024]{1,0:T(8,128)(2,1)}, u32[]{:S(2)}) copy-start(bf16[1024,1024]{1,0:T(8,128)(2,1)} %constant.20.clone.refs_9_.refs_5_) | copy-start | bytes 6291460
  68.5 34.1 %copy-start.12 = (bf16[2,6,48,256]{3,2,1,0:T(8,128)(2,1)S(1)}, bf16[2,6,48,256]{3,2,1,0:T(8,128)(2,1)}, u32[]{:S(2)}) copy-start(bf16[2,6,48,256]{3,2,1,0:T(8,128)(2,1)} %get-tuple-element.95.refs_1_) | copy-start | bytes 884740
  68.5 5.1 %collective-permute-start.8 = (bf16[2,4,256,384]{3,2,1,0:T(8,128)(2,1)S(1)}, bf16[2,4,256,384]{3,2,1,0:T(8,128)(2,1)S(1)}, u32[]{:S(2)}, u32[]{:S(2)}) collective-permute-start(bf16[2,4,256,384]{3,2,1,0:T(8,128)(2,1)S(1)} %interpolate.5.refs_1_.refs_7_), channel_id=1, source_target_pairs={{0,1},{1,0},{2,3},{3,2},{4,5},{5,4},{6,7},{7,6},{8,9},{9,8},{10,11... | collective-permute-start | bytes 4718600 | tf_op jit(solution)/shard_map/ppermute | solution.py:525
  68.6 28.4 %collective-permute-start.12 = (bf16[2,6,4,48,256]{4,3,2,1,0:T(8,128)(2,1)S(1)}, bf16[2,6,4,48,256]{4,3,2,1,0:T(8,128)(2,1)S(1)}, u32[]{:S(2)}, u32[]{:S(2)}) collective-permute-start(bf16[2,6,4,48,256]{4,3,2,1,0:T(8,128)(2,1)S(1)} %get-tuple-element.82.refs_5_.refs_3_), channel_id=1, source_target_pairs={{0,2},{2,0},{1,3},{3,1},{4,6},{6,4},{5,7},{7,5},{8,10},{10,8},{9,1... | collective-permute-start | bytes 3538952 | tf_op jit(solution)/shard_map/ppermute | solution.py:525
  69.2 11.8 %collective-permute-start.9 = (bf16[2,6,48,256]{3,2,1,0:T(8,128)(2,1)S(1)}, bf16[2,6,48,256]{3,2,1,0:T(8,128)(2,1)S(1)}, u32[]{:S(2)}, u32[]{:S(2)}) collective-permute-start(bf16[2,6,48,256]{3,2,1,0:T(8,128)(2,1)S(1)} %get-tuple-element.89), channel_id=1, source_target_pairs={{0,12},{4,8},{8,4},{12,0},{1,13},{5,9},{9,5},{13,1},{2,14},{6,10},... | collective-permute-start | bytes 884744 | tf_op jit(solution)/shard_map/ppermute | solution.py:525
  71.9 25.0 %collective-permute-start.10 = (bf16[2,6,48,256]{3,2,1,0:T(8,128)(2,1)S(1)}, bf16[2,6,48,256]{3,2,1,0:T(8,128)(2,1)S(1)}, u32[]{:S(2)}, u32[]{:S(2)}) collective-permute-start(bf16[2,6,48,256]{3,2,1,0:T(8,128)(2,1)S(1)} %get-tuple-element.90), channel_id=1, source_target_pairs={{0,8},{4,12},{8,0},{12,4},{1,9},{5,13},{9,1},{13,5},{2,10},{6,14},... | collective-permute-start | bytes 884744 | tf_op jit(solution)/shard_map/ppermute | solution.py:525
  71.9 25.0 %collective-permute-start.11 = (bf16[2,6,48,256]{3,2,1,0:T(8,128)(2,1)S(1)}, bf16[2,6,48,256]{3,2,1,0:T(8,128)(2,1)S(1)}, u32[]{:S(2)}, u32[]{:S(2)}) collective-permute-start(bf16[2,6,48,256]{3,2,1,0:T(8,128)(2,1)S(1)} %get-tuple-element.91), channel_id=1, source_target_pairs={{0,4},{4,0},{8,12},{12,8},{1,5},{5,1},{9,13},{13,9},{2,6},{6,2},{1... | collective-permute-start | bytes 884744 | tf_op jit(solution)/shard_map/ppermute | solution.py:525
  97.0 20.2 %copy-start.10 = (bf16[2,2,256,512]{3,2,1,0:T(8,128)(2,1)S(1)}, bf16[2,2,256,512]{3,2,1,0:T(8,128)(2,1)}, u32[]{:S(2)}) copy-start(bf16[2,2,256,512]{3,2,1,0:T(8,128)(2,1)} %constant.22.clone.refs_1_) | copy-start | bytes 3145732
  97.0 20.3 %copy-start.11 = (bf16[2,6,4,48,256]{4,3,2,1,0:T(8,128)(2,1)S(1)}, bf16[2,6,4,48,256]{4,3,2,1,0:T(8,128)(2,1)}, u32[]{:S(2)}) copy-start(bf16[2,6,4,48,256]{4,3,2,1,0:T(8,128)(2,1)} %get-tuple-element.72.refs_2_) | copy-start | bytes 3538948
  97.0 19.1 %collective-permute-start.16 = (bf16[2,4,4,48,256]{4,3,2,1,0:T(8,128)(2,1)S(1)}, bf16[2,4,4,48,256]{4,3,2,1,0:T(8,128)(2,1)S(1)}, u32[]{:S(2)}, u32[]{:S(2)}) collective-permute-start(bf16[2,4,4,48,256]{4,3,2,1,0:T(8,128)(2,1)S(1)} %get-tuple-element.92.refs_11_.refs_4_), channel_id=1, source_target_pairs={{0,2},{2,0},{1,3},{3,1},{4,6},{6,4},{5,7},{7,5},{8,10},{10,8},{9,1... | collective-permute-start | bytes 2359304 | tf_op jit(solution)/shard_map/ppermute | solution.py:525
  98.2 11.0 %collective-permute-start.13 = (bf16[2,4,48,256]{3,2,1,0:T(8,128)(2,1)S(1)}, bf16[2,4,48,256]{3,2,1,0:T(8,128)(2,1)S(1)}, u32[]{:S(2)}, u32[]{:S(2)}) collective-permute-start(bf16[2,4,48,256]{3,2,1,0:T(8,128)(2,1)S(1)} %get-tuple-element.103), channel_id=1, source_target_pairs={{0,12},{4,8},{8,4},{12,0},{1,13},{5,9},{9,5},{13,1},{2,14},{6,10},... | collective-permute-start | bytes 589832 | tf_op jit(solution)/shard_map/ppermute | solution.py:525
  100.2 15.8 %collective-permute-start.14 = (bf16[2,4,48,256]{3,2,1,0:T(8,128)(2,1)S(1)}, bf16[2,4,48,256]{3,2,1,0:T(8,128)(2,1)S(1)}, u32[]{:S(2)}, u32[]{:S(2)}) collective-permute-start(bf16[2,4,48,256]{3,2,1,0:T(8,128)(2,1)S(1)} %get-tuple-element.104), channel_id=1, source_target_pairs={{0,8},{4,12},{8,0},{12,4},{1,9},{5,13},{9,1},{13,5},{2,10},{6,14},... | collective-permute-start | bytes 589832 | tf_op jit(solution)/shard_map/ppermute | solution.py:525
  100.2 15.8 %collective-permute-start.15 = (bf16[2,4,48,256]{3,2,1,0:T(8,128)(2,1)S(1)}, bf16[2,4,48,256]{3,2,1,0:T(8,128)(2,1)S(1)}, u32[]{:S(2)}, u32[]{:S(2)}) collective-permute-start(bf16[2,4,48,256]{3,2,1,0:T(8,128)(2,1)S(1)} %get-tuple-element.105), channel_id=1, source_target_pairs={{0,4},{4,0},{8,12},{12,8},{1,5},{5,1},{9,13},{13,9},{2,6},{6,2},{1... | collective-permute-start | bytes 589832 | tf_op jit(solution)/shard_map/ppermute | solution.py:525
  116.1 68.8 %collective-permute-start.23 = (bf16[2,12,48,1024]{3,2,1,0:T(8,128)(2,1)S(1)}, bf16[2,12,48,1024]{3,2,1,0:T(8,128)(2,1)S(1)}, u32[]{:S(2)}, u32[]{:S(2)}) collective-permute-start(bf16[2,12,48,1024]{3,2,1,0:T(8,128)(2,1)S(1)} %cross_transform.4.refs_8_.refs_2_), channel_id=1, source_target_pairs={{0,2},{2,0},{1,3},{3,1},{4,6},{6,4},{5,7},{7,5},{8,10},{10,8},{9,1... | collective-permute-start | bytes 7077896 | tf_op jit(solution)/shard_map/ppermute | solution.py:525
  120.7 16.3 %collective-permute-start.19 = (bf16[2,8,48,256]{3,2,1,0:T(8,128)(2,1)S(1)}, bf16[2,8,48,256]{3,2,1,0:T(8,128)(2,1)S(1)}, u32[]{:S(2)}, u32[]{:S(2)}) collective-permute-start(bf16[2,8,48,256]{3,2,1,0:T(8,128)(2,1)S(1)} %get-tuple-element.109), channel_id=1, source_target_pairs={{0,4},{4,0},{8,12},{12,8},{1,5},{5,1},{9,13},{13,9},{2,6},{6,2},{1... | collective-permute-start | bytes 1179656 | tf_op jit(solution)/shard_map/ppermute | solution.py:525
  120.7 29.9 %collective-permute-start.18 = (bf16[2,8,48,256]{3,2,1,0:T(8,128)(2,1)S(1)}, bf16[2,8,48,256]{3,2,1,0:T(8,128)(2,1)S(1)}, u32[]{:S(2)}, u32[]{:S(2)}) collective-permute-start(bf16[2,8,48,256]{3,2,1,0:T(8,128)(2,1)S(1)} %get-tuple-element.110), channel_id=1, source_target_pairs={{0,8},{4,12},{8,0},{12,4},{1,9},{5,13},{9,1},{13,5},{2,10},{6,14},... | collective-permute-start | bytes 1179656 | tf_op jit(solution)/shard_map/ppermute | solution.py:525
  123.3 27.3 %collective-permute-start.17 = (bf16[2,8,48,256]{3,2,1,0:T(8,128)(2,1)S(1)}, bf16[2,8,48,256]{3,2,1,0:T(8,128)(2,1)S(1)}, u32[]{:S(2)}, u32[]{:S(2)}) collective-permute-start(bf16[2,8,48,256]{3,2,1,0:T(8,128)(2,1)S(1)} %get-tuple-element.111), channel_id=1, source_target_pairs={{0,12},{4,8},{8,4},{12,0},{1,13},{5,9},{9,5},{13,1},{2,14},{6,10},... | collective-permute-start | bytes 1179656 | tf_op jit(solution)/shard_map/ppermute | solution.py:525
  128.1 56.8 %collective-permute-start.24 = (bf16[2,4,48,1024]{3,2,1,0:T(8,128)(2,1)S(1)}, bf16[2,4,48,1024]{3,2,1,0:T(8,128)(2,1)S(1)}, u32[]{:S(2)}, u32[]{:S(2)}) collective-permute-start(bf16[2,4,48,1024]{3,2,1,0:T(8,128)(2,1)S(1)} %cross_transform.5.refs_7_.refs_3_), channel_id=1, source_target_pairs={{0,2},{2,0},{1,3},{3,1},{4,6},{6,4},{5,7},{7,5},{8,10},{10,8},{9,1... | collective-permute-start | bytes 2359304 | tf_op jit(solution)/shard_map/ppermute | solution.py:525
  150.6 39.4 %collective-permute-start.20 = (bf16[2,8,48,256]{3,2,1,0:T(8,128)(2,1)S(1)}, bf16[2,8,48,256]{3,2,1,0:T(8,128)(2,1)S(1)}, u32[]{:S(2)}, u32[]{:S(2)}) collective-permute-start(bf16[2,8,48,256]{3,2,1,0:T(8,128)(2,1)S(1)} %get-tuple-element.121), channel_id=1, source_target_pairs={{0,4},{4,0},{8,12},{12,8},{1,5},{5,1},{9,13},{13,9},{2,6},{6,2},{1... | collective-permute-start | bytes 1179656 | tf_op jit(solution)/shard_map/ppermute | solution.py:525
  157.0 33.0 %collective-permute-start.21 = (bf16[2,8,48,256]{3,2,1,0:T(8,128)(2,1)S(1)}, bf16[2,8,48,256]{3,2,1,0:T(8,128)(2,1)S(1)}, u32[]{:S(2)}, u32[]{:S(2)}) collective-permute-start(bf16[2,8,48,256]{3,2,1,0:T(8,128)(2,1)S(1)} %get-tuple-element.122), channel_id=1, source_target_pairs={{0,8},{4,12},{8,0},{12,4},{1,9},{5,13},{9,1},{13,5},{2,10},{6,14},... | collective-permute-start | bytes 1179656 | tf_op jit(solution)/shard_map/ppermute | solution.py:525
  157.9 32.1 %collective-permute-start.22 = (bf16[2,8,48,256]{3,2,1,0:T(8,128)(2,1)S(1)}, bf16[2,8,48,256]{3,2,1,0:T(8,128)(2,1)S(1)}, u32[]{:S(2)}, u32[]{:S(2)}) collective-permute-start(bf16[2,8,48,256]{3,2,1,0:T(8,128)(2,1)S(1)} %get-tuple-element.123), channel_id=1, source_target_pairs={{0,12},{4,8},{8,4},{12,0},{1,13},{5,9},{9,5},{13,1},{2,14},{6,10},... | collective-permute-start | bytes 1179656 | tf_op jit(solution)/shard_map/ppermute | solution.py:525

commit v5 on v4

--- a/solution.py
+++ b/solution.py
@@ -107,7 +107,7 @@
     return image_out
 
 
-CHUNKS = ((0, 6), (6, 6), (12, 4))
+CHUNKS = ((0, 4), (4, 4), (8, 4), (12, 4))
 PARTS = (8, 8)
 SPLIT = 48
 VMEM = 20 * 1024 * 1024
@@ -603,18 +603,24 @@
 
     made = first_heights(ids, matrix, own_first, other_first, PARTS, (c0,))
     come = to_owners(made[0])
-    c1 = cross_transform(ids, landed[-1:], cross_tables, scale, [rest], earlier=(made[0][0],))
+    late = [rest - ROWS, ROWS]
+    c1, c2 = cross_transform(ids, landed[-1:], cross_tables, scale, late, earlier=(made[0][0],))
     other_c1 = exchange(c1, "el", 1)
     shape = (2, cuts, bins, A)
     full_scale = 1.0 / math.sqrt(A * 2 * cuts)
-    made, come, c1 = lax.optimization_barrier((made, come, c1))
+    made, come, c2 = lax.optimization_barrier((made, come, c2))
     arrived = in_order(made[0], come)
     come = to_owners(made[1])
     image = cross_transform(
         ids, [arrived], cross_tables, full_scale, image=None, shape=shape, place=0, earlier=(c1,)
     )
+    image, c2, other_c0 = lax.optimization_barrier((image, c2, other_c0))
+    other_c2 = exchange(c2, "el", 1)
     image = last_heights(
-        ids, matrix, [c0, c1], [other_c0, other_c1], (0, 0), image, shape, split, rest
+        ids, matrix, [c0, c1], [other_c0, other_c1], (0, 0), image, shape, split, late[0]
+    )
+    image = last_heights(
+        ids, matrix, [c0, c2], [other_c0, other_c2], (late[0], 0), image, shape, split + late[0], late[1]
     )
     image = cross_transform(
         ids,

time: 196 us -> 193 us (0.985)
  waiting for transfers between devices: 76.8 us -> 64.4 us
  starting transfers between devices: 39.1 us -> 45.6 us
  Pallas kernels: 72.4 us -> 75.7 us
    ppermute x23 -> x29, waiting for transfers between devices: 76.8 us -> 64.2 us  [exchange(): lax.ppermute(value, axis, [(i, i ^ s) for i in range(lax.axis_size(axis))])]
    ppermute x23 -> x29, starting transfers between devices: 32.9 us -> 39.3 us  [exchange(): lax.ppermute(value, axis, [(i, i ^ s) for i in range(lax.axis_size(axis))])]
    pallas_call x3 -> x4, Pallas kernels: 22.7 us -> 24.3 us  [interpolate(): pl.pallas_call(lambda *refs: interp_kernel(*refs, bordered=len(border) ==...]
    unnamed x29 -> x33, local copies, waits for them, and re-layouts: 5.26 us -> 3.63 us
    pallas_call x1 -> x2, Pallas kernels: 5.11 us -> 6.33 us  [last_heights(): pl.pallas_call(lambda *refs: height_kernel(*refs, chunks=chunks, sets=1,...]
    pallas_call x3 -> x4, Pallas kernels: 17.8 us -> 18.3 us  [range_transform(): pl.pallas_call(lambda *refs: range_kernel(*refs, blocks=blocks, earlier=l...]
  transfers between devices with their start and end apart: 25 -> 31, of which waited for: 9 -> 13; matrix products, arithmetic and copies ran while one was open for 0% -> 0% of each run, Pallas kernels for 29% -> 32%
where the time goes in v5:
time: 193 us; the launch traced here: 191 us
  Pallas kernels  75.7 us (39%)
  waiting for transfers between devices  64.4 us (33%)
  starting transfers between devices  45.6 us (24%)
  local copies, waits for them, and re-layouts  4.73 us (2%)
    ppermute x29, waiting for transfers between devices, exchange(): lax.ppermute(value, axis, [(i, i ^ s) for i in range(lax.axis_size(axis))])  64.2 us
    ppermute x29, starting transfers between devices, exchange(): lax.ppermute(value, axis, [(i, i ^ s) for i in range(lax.axis_size(axis))])  39.3 us
    pallas_call x4, Pallas kernels, interpolate(): pl.pallas_call(lambda *refs: interp_kernel(*refs, bordered=len(border) ==...  24.3 us
    pallas_call x4, Pallas kernels, cross_transform(): pl.pallas_call(lambda *refs: cross_kernel(*refs, groups=groups, blocks=bl...  20.9 us
    pallas_call x4, Pallas kernels, range_transform(): pl.pallas_call(lambda *refs: range_kernel(*refs, blocks=blocks, earlier=l...  18.3 us
    pallas_call x2, Pallas kernels, last_heights(): pl.pallas_call(lambda *refs: height_kernel(*refs, chunks=chunks, sets=1,...  6.33 us
    ppermute x1, starting transfers between devices, halo_rows(): lax.ppermute(tail, 'az', [(i, i + 1) for i in range(ends)])  4.94 us
  transfers between devices with their start and end apart: 31, of which 13 were waited for; matrix products, arithmetic and copies ran while one was open for 0% of the time, Pallas kernels for 32%

profile of v5, /device:TPU:0, one launch (start us, length us, event | category | flops | bytes accessed | tf_op | source)
XLA Modules:
  0.0 191.3 jit_solution(10295781690185216298)
XLA Ops:
  0.0 1.1 fusion
  1.1 4.9 %collective-permute-start = (bf16[2,16,8,384]{3,2,1,0:T(8,128)(2,1)S(1)}, bf16[2,16,8,384]{3,2,1,0:T(8,128)(2,1)S(1)}, u32[]{:S(2)}, u32[]{:S(2)}) collective-permute-start(bf16[2,16,8,384]{3,2,1,0:T(8,128)(2,1)S(1)} %get-tuple-element.170), channel_id=1, source_target_pairs={{0,4},{4,8},{8,12},{1,5},{5,9},{9,13},{2,6},{6,10},{10,14},{3,7},{... | collective-permute-start | bytes 589832 | tf_op jit(solution)/shard_map/ppermute | solution.py:536
  6.0 1.3 collective-permute-start.1
  7.3 6.7 %interpolate.4.made_ref = bf16[2,4,256,384]{3,2,1,0:T(8,128)(2,1)} custom-call(bf16[2,16,256,384]{3,2,1,0:T(8,128)(2,1)} %refs_0_.7, s32[256,384]{1,0:T(8,128)} %refs_1_.10, s32[256,384]{1,0:T(8,128)} %refs_2_.7, bf16[8,256,384]{2,1,0:T(8,128)(2,1)} %refs_3_.11), custom_call_target="tpu_custom_call" | custom-call | flops 26738 | bytes 3145 | tf_op jit(solution)/shard_map/interpolate/pallas_call | solution.py:204
  14.3 0.8 copy-done.9
  15.1 2.3 %interpolate_edges.1.refs_5_.refs_1_ = bf16[2,4,256,384]{3,2,1,0:T(8,128)(2,1)} custom-call(bf16[2,16,256,384]{3,2,1,0:T(8,128)(2,1)} %refs_0_.7, bf16[2,16,16,384]{3,2,1,0:T(8,128)(2,1)} %copy-done.9, s32[256,384]{1,0:T(8,128)} %refs_1_.10, s32[256,384]{1,0:T(8,128)} %refs_2_.7, bf16[8,256,384]{2,1,0:T(8,128)(2,1)} %refs_3_.11, ...), custom_call_target="tpu_custom_call", output_to_operand_aliasing={{}: (5, {})} | custom-call | flops 3342 | bytes 393 | tf_op jit(solution)/shard_map/interpolate_edges/pallas_call | solution.py:244
  18.0 6.7 %interpolate.5.refs_7_.refs_1_ = bf16[2,4,256,384]{3,2,1,0:T(8,128)(2,1)} custom-call(bf16[2,16,256,384]{3,2,1,0:T(8,128)(2,1)} %refs_0_.7, s32[256,384]{1,0:T(8,128)} %refs_1_.10, s32[256,384]{1,0:T(8,128)} %refs_2_.7, bf16[8,256,384]{2,1,0:T(8,128)(2,1)} %refs_3_.11, bf16[2,16,16,384]{3,2,1,0:T(8,128)(2,1)} %copy-done.9, ...), custom_call_target="tpu_custom_call" | custom-call | flops 26738 | bytes 3145 | tf_op jit(solution)/shard_map/interpolate/pallas_call | solution.py:204
  24.7 6.7 %range_transform.4 = (bf16[2,4,4,48,256]{4,3,2,1,0:T(8,128)(2,1)}, bf16[2,4,48,256]{3,2,1,0:T(8,128)(2,1)}, bf16[2,4,48,256]{3,2,1,0:T(8,128)(2,1)}, bf16[2,4,48...) custom-call(s32[3]{0:T(128)} %pad_add_fusion.refs_0_, bf16[2,4,256,384]{3,2,1,0:T(8,128)(2,1)} %interpolate_edges.1.refs_5_.refs_1_, ...), custom_call_target="tpu_custom_call" | custom-call | flops 2415919 | bytes 4718 | tf_op jit(solution)/shard_map/range_transform/pallas_call | solution.py:303
  32.0 1.5 collective-permute-start.7
  33.5 4.4 %collective-permute-start.4 = (bf16[2,4,48,256]{3,2,1,0:T(8,128)(2,1)}, bf16[2,4,48,256]{3,2,1,0:T(8,128)(2,1)S(1)}, u32[]{:S(2)}, u32[]{:S(2)}) collective-permute-start(bf16[2,4,48,256]{3,2,1,0:T(8,128)(2,1)} %get-tuple-element.99), channel_id=1, source_target_pairs={{0,12},{4,8},{8,4},{12,0},{1,13},{5,9},{9,5},{13,1},{2,14},{6,10},... | collective-permute-start | bytes 589832 | tf_op jit(solution)/shard_map/ppermute | solution.py:525
  38.5 3.9 %range_transform.5 = (bf16[2,4,4,48,256]{4,3,2,1,0:T(8,128)(2,1)S(1)}, bf16[2,4,48,256]{3,2,1,0:T(8,128)(2,1)S(1)}, bf16[2,4,48,256]{3,2,1,0:T(8,128)(2,1)S(1)},...) custom-call(s32[3]{0:T(128)S(1)} %copy-done.13, bf16[2,4,256,384]{3,2,1,0:T(8,128)(2,1)S(1)} %copy-done.5, ...), custom_call_target="tpu_custom_call" | custom-call | flops 2415919 | bytes 4718 | tf_op jit(solution)/shard_map/range_transform/pallas_call | solution.py:303
  42.4 2.8 %copy-done.1 = bf16[2,16,256,384]{3,2,1,0:T(8,128)(2,1)S(1)} copy-done((bf16[2,16,256,384]{3,2,1,0:T(8,128)(2,1)S(1)}, bf16[2,16,256,384]{3,2,1,0:T(8,128)(2,1)}, u32[]{:S(2)}) %copy-start.1) | copy-done | bytes 6291480
  45.2 5.5 %interpolate.6.refs_1_.refs_7_ = bf16[2,4,256,384]{3,2,1,0:T(8,128)(2,1)S(1)} custom-call(bf16[2,16,256,384]{3,2,1,0:T(8,128)(2,1)S(1)} %copy-done.1, s32[256,384]{1,0:T(8,128)S(1)} %copy-done.6, s32[256,384]{1,0:T(8,128)S(1)} %copy-done.7, bf16[8,256,384]{2,1,0:T(8,128)(2,1)S(1)} %copy-done.2, bf16[2,16,16,384]{3,2,1,0:T(8,128)(2,1)S(1)} %copy-done.10, ...), custom_call_target="tpu_custom_call" | custom-call | flops 26738 | bytes 3145 | tf_op jit(solution)/shard_map/interpolate/pallas_call | solution.py:204
  50.7 4.1 %collective-permute-done.5.refs_3_ = bf16[2,4,48,256]{3,2,1,0:T(8,128)(2,1)S(1)} collective-permute-done((bf16[2,4,48,256]{3,2,1,0:T(8,128)(2,1)}, bf16[2,4,48,256]{3,2,1,0:T(8,128)(2,1)S(1)}, u32[]{:S(2)}, u32[]{:S(2)}) %collective-permute-start.5) | collective-permute-done | bytes 196640 | tf_op jit(solution)/shard_map/ppermute | solution.py:525
  55.5 2.5 %collective-permute-start.9 = (bf16[2,4,48,256]{3,2,1,0:T(8,128)(2,1)S(1)}, bf16[2,4,48,256]{3,2,1,0:T(8,128)(2,1)S(1)}, u32[]{:S(2)}, u32[]{:S(2)}) collective-permute-start(bf16[2,4,48,256]{3,2,1,0:T(8,128)(2,1)S(1)} %get-tuple-element.109), channel_id=1, source_target_pairs={{0,12},{4,8},{8,4},{12,0},{1,13},{5,9},{9,5},{13,1},{2,14},{6,10},... | collective-permute-start | bytes 589832 | tf_op jit(solution)/shard_map/ppermute | solution.py:525
  58.0 1.9 %collective-permute-start.11 = (bf16[2,4,48,256]{3,2,1,0:T(8,128)(2,1)S(1)}, bf16[2,4,48,256]{3,2,1,0:T(8,128)(2,1)S(1)}, u32[]{:S(2)}, u32[]{:S(2)}) collective-permute-start(bf16[2,4,48,256]{3,2,1,0:T(8,128)(2,1)S(1)} %get-tuple-element.111), channel_id=1, source_target_pairs={{0,4},{4,0},{8,12},{12,8},{1,5},{5,1},{9,13},{13,9},{2,6},{6,2},{1... | collective-permute-start | bytes 589832 | tf_op jit(solution)/shard_map/ppermute | solution.py:525
  59.9 3.9 %range_transform.6 = (bf16[2,4,4,48,256]{4,3,2,1,0:T(8,128)(2,1)S(1)}, bf16[2,4,48,256]{3,2,1,0:T(8,128)(2,1)S(1)}, bf16[2,4,48,256]{3,2,1,0:T(8,128)(2,1)S(1)},...) custom-call(s32[3]{0:T(128)S(1)} %copy-done.13, bf16[2,4,256,384]{3,2,1,0:T(8,128)(2,1)S(1)} %interpolate.6.refs_1_.refs_7_, ...), custom_call_target="tpu_custom_call" | custom-call | flops 2415919 | bytes 4718 | tf_op jit(solution)/shard_map/range_transform/pallas_call | solution.py:303
  63.8 5.5 %interpolate.7.refs_1_.refs_7_ = bf16[2,4,256,384]{3,2,1,0:T(8,128)(2,1)S(1)} custom-call(bf16[2,16,256,384]{3,2,1,0:T(8,128)(2,1)S(1)} %bitcast.4, s32[256,384]{1,0:T(8,128)S(1)} %copy-done.6, s32[256,384]{1,0:T(8,128)S(1)} %copy-done.7, bf16[8,256,384]{2,1,0:T(8,128)(2,1)S(1)} %copy-done.2, bf16[2,16,16,384]{3,2,1,0:T(8,128)(2,1)S(1)} %copy-done.10, ...), custom_call_target="tpu_custom_call" | custom-call | flops 26738 | bytes 3145 | tf_op jit(solution)/shard_map/interpolate/pallas_call | solution.py:204
  69.3 5.5 %collective-permute-done.10.refs_7_ = bf16[2,4,48,256]{3,2,1,0:T(8,128)(2,1)S(1)} collective-permute-done((bf16[2,4,48,256]{3,2,1,0:T(8,128)(2,1)S(1)}, bf16[2,4,48,256]{3,2,1,0:T(8,128)(2,1)S(1)}, u32[]{:S(2)}, u32[]{:S(2)}) %collective-permute-start.10) | collective-permute-done | bytes 196640 | tf_op jit(solution)/shard_map/ppermute | solution.py:525
  74.9 1.1 collective-permute-start.17
  76.0 2.0 %collective-permute-start.14 = (bf16[2,4,48,256]{3,2,1,0:T(8,128)(2,1)S(1)}, bf16[2,4,48,256]{3,2,1,0:T(8,128)(2,1)S(1)}, u32[]{:S(2)}, u32[]{:S(2)}) collective-permute-start(bf16[2,4,48,256]{3,2,1,0:T(8,128)(2,1)S(1)} %get-tuple-element.119), channel_id=1, source_target_pairs={{0,12},{4,8},{8,4},{12,0},{1,13},{5,9},{9,5},{13,1},{2,14},{6,10},... | collective-permute-start | bytes 589832 | tf_op jit(solution)/shard_map/ppermute | solution.py:525
  78.0 2.4 %collective-permute-start.16 = (bf16[2,4,48,256]{3,2,1,0:T(8,128)(2,1)S(1)}, bf16[2,4,48,256]{3,2,1,0:T(8,128)(2,1)S(1)}, u32[]{:S(2)}, u32[]{:S(2)}) collective-permute-start(bf16[2,4,48,256]{3,2,1,0:T(8,128)(2,1)S(1)} %get-tuple-element.121), channel_id=1, source_target_pairs={{0,4},{4,0},{8,12},{12,8},{1,5},{5,1},{9,13},{13,9},{2,6},{6,2},{1... | collective-permute-start | bytes 589832 | tf_op jit(solution)/shard_map/ppermute | solution.py:525
  80.4 3.9 %range_transform.7 = (bf16[2,4,4,48,256]{4,3,2,1,0:T(8,128)(2,1)S(1)}, bf16[2,4,48,256]{3,2,1,0:T(8,128)(2,1)S(1)}, bf16[2,4,48,256]{3,2,1,0:T(8,128)(2,1)S(1)},...) custom-call(s32[3]{0:T(128)S(1)} %copy-done.13, bf16[2,4,256,384]{3,2,1,0:T(8,128)(2,1)S(1)} %interpolate.7.refs_1_.refs_7_, ...), custom_call_target="tpu_custom_call" | custom-call | flops 2415919 | bytes 4718 | tf_op jit(solution)/shard_map/range_transform/pallas_call | solution.py:303
  84.2 1.4 collective-permute-done.14.refs_12_
  85.7 9.1 %collective-permute-done.15.refs_11_ = bf16[2,4,48,256]{3,2,1,0:T(8,128)(2,1)S(1)} collective-permute-done((bf16[2,4,48,256]{3,2,1,0:T(8,128)(2,1)S(1)}, bf16[2,4,48,256]{3,2,1,0:T(8,128)(2,1)S(1)}, u32[]{:S(2)}, u32[]{:S(2)}) %collective-permute-start.15) | collective-permute-done | bytes 196640 | tf_op jit(solution)/shard_map/ppermute | solution.py:525
  94.9 1.0 collective-permute-start.21
  95.9 2.0 %collective-permute-start.18 = (bf16[2,4,48,256]{3,2,1,0:T(8,128)(2,1)S(1)}, bf16[2,4,48,256]{3,2,1,0:T(8,128)(2,1)S(1)}, u32[]{:S(2)}, u32[]{:S(2)}) collective-permute-start(bf16[2,4,48,256]{3,2,1,0:T(8,128)(2,1)S(1)} %get-tuple-element.138), channel_id=1, source_target_pairs={{0,12},{4,8},{8,4},{12,0},{1,13},{5,9},{9,5},{13,1},{2,14},{6,10},... | collective-permute-start | bytes 589832 | tf_op jit(solution)/shard_map/ppermute | solution.py:525
  97.9 2.4 %collective-permute-start.20 = (bf16[2,4,48,256]{3,2,1,0:T(8,128)(2,1)S(1)}, bf16[2,4,48,256]{3,2,1,0:T(8,128)(2,1)S(1)}, u32[]{:S(2)}, u32[]{:S(2)}) collective-permute-start(bf16[2,4,48,256]{3,2,1,0:T(8,128)(2,1)S(1)} %get-tuple-element.140), channel_id=1, source_target_pairs={{0,4},{4,0},{8,12},{12,8},{1,5},{5,1},{9,13},{13,9},{2,6},{6,2},{1... | collective-permute-start | bytes 589832 | tf_op jit(solution)/shard_map/ppermute | solution.py:525
  100.3 6.6 %cross_transform.4.refs_10_.refs_2_ = bf16[2,12,48,1024]{3,2,1,0:T(8,128)(2,1)S(1)} custom-call(s32[3]{0:T(128)S(1)} %copy-done.13, bf16[2,4,48,256]{3,2,1,0:T(8,128)(2,1)S(1)} %copy-done.12, bf16[2,4,48,256]{3,2,1,0:T(8,128)(2,1)S(1)} %collective-permute-done.6.refs_2_, bf16[2,4,48,256]{3,2,1,0:T(8,128)(2,1)S(1)} %collective-permute-done.5.refs_3_, ...), custom_call_target="tpu_custom_call" | custom-call | flops 4831838 | bytes 8912 | tf_op jit(solution)/shard_map/cross_transform/pallas_call | solution.py:489
  106.9 6.9 %collective-permute-done.19.refs_3_ = bf16[2,4,48,256]{3,2,1,0:T(8,128)(2,1)S(1)} collective-permute-done((bf16[2,4,48,256]{3,2,1,0:T(8,128)(2,1)S(1)}, bf16[2,4,48,256]{3,2,1,0:T(8,128)(2,1)S(1)}, u32[]{:S(2)}, u32[]{:S(2)}) %collective-permute-start.19) | collective-permute-done | bytes 196640 | tf_op jit(solution)/shard_map/ppermute | solution.py:525
  114.0 1.0 collective-permute-start.28
  115.0 3.5 %first_heights.1 = (bf16[2,8,48,256]{3,2,1,0:T(8,128)(2,1)S(1)}, bf16[2,8,48,256]{3,2,1,0:T(8,128)(2,1)S(1)}, bf16[2,8,48,256]{3,2,1,0:T(8,128)(2,1)S(1)}, bf16[...) custom-call(s32[3]{0:T(128)S(1)} %copy-done.13, ...), custom_call_target="tpu_custom_call" | custom-call | flops 1610612 | bytes 9437 | tf_op jit(solution)/shard_map/first_heights/pallas_call | solution.py:381
  118.6 2.6 %collective-permute-start.23 = (bf16[2,8,48,256]{3,2,1,0:T(8,128)(2,1)S(1)}, bf16[2,8,48,256]{3,2,1,0:T(8,128)(2,1)S(1)}, u32[]{:S(2)}, u32[]{:S(2)}) collective-permute-start(bf16[2,8,48,256]{3,2,1,0:T(8,128)(2,1)S(1)} %get-tuple-element.145), channel_id=1, source_target_pairs={{0,8},{4,12},{8,0},{12,4},{1,9},{5,13},{9,1},{13,5},{2,10},{6,14},... | collective-permute-start | bytes 1179656 | tf_op jit(solution)/shard_map/ppermute | solution.py:525
  121.2 1.8 collective-permute-start.22
  123.0 3.2 %cross_transform.5 = (bf16[2,4,32,1024]{3,2,1,0:T(8,128)(2,1)S(1)}, bf16[2,4,16,1024]{3,2,1,0:T(8,128)(2,1)S(1)}) custom-call(s32[3]{0:T(128)S(1)} %copy-done.13, bf16[2,4,48,256]{3,2,1,0:T(8,128)(2,1)S(1)} %get-tuple-element.151.refs_1_, bf16[2,4,48,256]{3,2,1,0:T(8,128)(2,1)S(1)} %collective-permute-done.20.refs_2_, ...), custom_call_target="tpu_custom_call" | custom-call | flops 1610612 | bytes 5767 | tf_op jit(solution)/shard_map/cross_transform/pallas_call | solution.py:489
  126.2 1.1 collective-permute-start.30
  127.3 7.8 %collective-permute-done.24.refs_2_ = bf16[2,8,48,256]{3,2,1,0:T(8,128)(2,1)S(1)} collective-permute-done((bf16[2,8,48,256]{3,2,1,0:T(8,128)(2,1)S(1)}, bf16[2,8,48,256]{3,2,1,0:T(8,128)(2,1)S(1)}, u32[]{:S(2)}, u32[]{:S(2)}) %collective-permute-start.24) | collective-permute-done | bytes 393248 | tf_op jit(solution)/shard_map/ppermute | solution.py:525
  135.1 13.4 %collective-permute-done.23.refs_3_ = bf16[2,8,48,256]{3,2,1,0:T(8,128)(2,1)S(1)} collective-permute-done((bf16[2,8,48,256]{3,2,1,0:T(8,128)(2,1)S(1)}, bf16[2,8,48,256]{3,2,1,0:T(8,128)(2,1)S(1)}, u32[]{:S(2)}, u32[]{:S(2)}) %collective-permute-start.23) | collective-permute-done | bytes 393248 | tf_op jit(solution)/shard_map/ppermute | solution.py:525
  148.5 6.5 %collective-permute-start.25 = (bf16[2,8,48,256]{3,2,1,0:T(8,128)(2,1)S(1)}, bf16[2,8,48,256]{3,2,1,0:T(8,128)(2,1)S(1)}, u32[]{:S(2)}, u32[]{:S(2)}) collective-permute-start(bf16[2,8,48,256]{3,2,1,0:T(8,128)(2,1)S(1)} %get-tuple-element.157), channel_id=1, source_target_pairs={{0,4},{4,0},{8,12},{12,8},{1,5},{5,1},{9,13},{13,9},{2,6},{6,2},{1... | collective-permute-start | bytes 1179656 | tf_op jit(solution)/shard_map/ppermute | solution.py:525
  155.0 0.9 collective-permute-start.26
  155.8 1.5 collective-permute-start.27
  157.3 5.5 %cross_transform.6.refs_6_ = bf16[2,16,96,1024]{3,2,1,0:T(8,128)(2,1)} custom-call(s32[3]{0:T(128)S(1)} %copy-done.13, bf16[2,8,48,256]{3,2,1,0:T(8,128)(2,1)S(1)} %get-tuple-element.160.refs_7_.refs_1_, bf16[2,8,48,256]{3,2,1,0:T(8,128)(2,1)S(1)} %collective-permute-done.24.refs_2_, bf16[2,8,48,256]{3,2,1,0:T(8,128)(2,1)S(1)} %collective-permute-done.23.refs_3_, ...), custom_call_target="tpu_custom_call" | custom-call | flops 3221225 | bytes 7340 | tf_op jit(solution)/shard_map/cross_transform/pallas_call | solution.py:489
  162.9 5.3 %collective-permute-done.28.refs_4_ = bf16[2,12,48,1024]{3,2,1,0:T(8,128)(2,1)S(1)} collective-permute-done((bf16[2,12,48,1024]{3,2,1,0:T(8,128)(2,1)S(1)}, bf16[2,12,48,1024]{3,2,1,0:T(8,128)(2,1)S(1)}, u32[]{:S(2)}, u32[]{:S(2)}) %collective-permute-start.28) | collective-permute-done | bytes 2359328 | tf_op jit(solution)/shard_map/ppermute | solution.py:525
  168.2 1.0 collective-permute-start.29
  169.2 10.2 %collective-permute-done.30.refs_5_ = bf16[2,4,32,1024]{3,2,1,0:T(8,128)(2,1)S(1)} collective-permute-done((bf16[2,4,32,1024]{3,2,1,0:T(8,128)(2,1)S(1)}, bf16[2,4,32,1024]{3,2,1,0:T(8,128)(2,1)S(1)}, u32[]{:S(2)}, u32[]{:S(2)}) %collective-permute-start.30) | collective-permute-done | bytes 524320 | tf_op jit(solution)/shard_map/ppermute | solution.py:525
  179.4 3.9 %last_heights.2.refs_6_ = bf16[2,16,96,1024]{3,2,1,0:T(8,128)(2,1)} custom-call(s32[3]{0:T(128)S(1)} %copy-done.13, bf16[2,2,256,512]{3,2,1,0:T(8,128)(2,1)S(1)} %copy-done.8, bf16[2,12,48,1024]{3,2,1,0:T(8,128)(2,1)S(1)} %cross_transform.4.refs_10_.refs_2_, ...), custom_call_target="tpu_custom_call", output_to_operand_aliasing={{}: (6, {})} | custom-call | flops 1073741 | bytes 6291 | tf_op jit(solution)/shard_map/last_heights/pallas_call | solution.py:416
  183.3 2.5 %last_heights.3.refs_7_ = bf16[2,16,96,1024]{3,2,1,0:T(8,128)(2,1)} custom-call(s32[3]{0:T(128)S(1)} %copy-done.13, bf16[2,2,256,512]{3,2,1,0:T(8,128)(2,1)S(1)} %copy-done.8, bf16[2,12,48,1024]{3,2,1,0:T(8,128)(2,1)S(1)} %cross_transform.4.refs_10_.refs_2_, bf16[2,4,16,1024]{3,2,1,0:T(8,128)(2,1)S(1)} %get-tuple-element.166.refs_3_, ...), custom_call_target="tpu_custom_call", output_to_operand_aliasing={{}: (6, {})} | custom-call | flops 536870 | bytes 3145 | tf_op jit(solution)/shard_map/last_heights/pallas_call | solution.py:416
  185.7 5.6 %cross_transform.7 = bf16[2,16,96,1024]{3,2,1,0:T(8,128)(2,1)} custom-call(s32[3]{0:T(128)S(1)} %copy-done.13, bf16[2,8,48,256]{3,2,1,0:T(8,128)(2,1)S(1)} %get-tuple-element.156.refs_1_, bf16[2,8,48,256]{3,2,1,0:T(8,128)(2,1)S(1)} %collective-permute-done.25.refs_2_, ...), custom_call_target="tpu_custom_call", output_to_operand_aliasing={{}: (7, {})} | custom-call | flops 3221225 | bytes 7340 | tf_op jit(solution)/shard_map/cross_transform/pallas_call | solution.py:489
  (67 shorter events, 3.3 us)
Async XLA Ops:
  1.1 12.9 %collective-permute-start = (bf16[2,16,8,384]{3,2,1,0:T(8,128)(2,1)S(1)}, bf16[2,16,8,384]{3,2,1,0:T(8,128)(2,1)S(1)}, u32[]{:S(2)}, u32[]{:S(2)}) collective-permute-start(bf16[2,16,8,384]{3,2,1,0:T(8,128)(2,1)S(1)} %get-tuple-element.170), channel_id=1, source_target_pairs={{0,4},{4,8},{8,12},{1,5},{5,9},{9,13},{2,6},{6,10},{10,14},{3,7},{... | collective-permute-start | bytes 589832 | tf_op jit(solution)/shard_map/ppermute | solution.py:536
  6.0 8.3 %collective-permute-start.1 = (bf16[2,16,8,384]{3,2,1,0:T(8,128)(2,1)S(1)}, bf16[2,16,8,384]{3,2,1,0:T(8,128)(2,1)S(1)}, u32[]{:S(2)}, u32[]{:S(2)}) collective-permute-start(bf16[2,16,8,384]{3,2,1,0:T(8,128)(2,1)S(1)} %get-tuple-element.169), channel_id=1, source_target_pairs={{4,0},{8,4},{12,8},{5,1},{9,5},{13,9},{6,2},{10,6},{14,10},{7,3},{... | collective-permute-start | bytes 589832 | tf_op jit(solution)/shard_map/ppermute | solution.py:537
  14.3 0.8 copy-start.9
  17.4 7.3 %collective-permute-start.2 = (bf16[2,4,256,384]{3,2,1,0:T(8,128)(2,1)}, bf16[2,4,256,384]{3,2,1,0:T(8,128)(2,1)}, u32[]{:S(2)}, u32[]{:S(2)}) collective-permute-start(bf16[2,4,256,384]{3,2,1,0:T(8,128)(2,1)} %interpolate_edges.1.refs_5_.refs_1_), channel_id=1, source_target_pairs={{0,1},{1,0},{2,3},{3,2},{4,5},{5,4},{6,7},{7,6},{8,9},{9,8},{10,11... | collective-permute-start | bytes 4718600 | tf_op jit(solution)/shard_map/ppermute | solution.py:525
  24.7 6.7 %copy-start.5 = (bf16[2,4,256,384]{3,2,1,0:T(8,128)(2,1)S(1)}, bf16[2,4,256,384]{3,2,1,0:T(8,128)(2,1)}, u32[]{:S(2)}) copy-start(bf16[2,4,256,384]{3,2,1,0:T(8,128)(2,1)} %interpolate.5.refs_7_.refs_1_) | copy-start | bytes 4718596
  24.7 13.8 %copy-start = (bf16[2,4,96,1536]{3,2,1,0:T(8,128)(2,1)S(1)}, bf16[2,4,96,1536]{3,2,1,0:T(8,128)(2,1)}, u32[]{:S(2)}) copy-start(bf16[2,4,96,1536]{3,2,1,0:T(8,128)(2,1)} %constant.19.clone.refs_3_.refs_4_.refs_5_.refs_6_) | copy-start | bytes 7077892
  24.7 13.8 %copy-start.13 = (s32[3]{0:T(128)S(1)}, s32[3]{0:T(128)}, u32[]{:S(2)}) copy-start(s32[3]{0:T(128)} %pad_add_fusion.refs_0_) | copy-start | bytes 40
  31.4 11.0 %copy-start.2 = (bf16[8,256,384]{2,1,0:T(8,128)(2,1)S(1)}, bf16[8,256,384]{2,1,0:T(8,128)(2,1)}, u32[]{:S(2)}) copy-start(bf16[8,256,384]{2,1,0:T(8,128)(2,1)} %refs_3_.11) | copy-start | bytes 4718596
  31.4 11.0 %copy-start.6 = (s32[256,384]{1,0:T(8,128)S(1)}, s32[256,384]{1,0:T(8,128)}, u32[]{:S(2)}) copy-start(s32[256,384]{1,0:T(8,128)} %refs_1_.10) | copy-start | bytes 1179652
  31.4 11.0 %copy-start.7 = (s32[256,384]{1,0:T(8,128)S(1)}, s32[256,384]{1,0:T(8,128)}, u32[]{:S(2)}) copy-start(s32[256,384]{1,0:T(8,128)} %refs_2_.7) | copy-start | bytes 1179652
  31.4 11.0 %copy-start.10 = (bf16[2,16,16,384]{3,2,1,0:T(8,128)(2,1)S(1)}, bf16[2,16,16,384]{3,2,1,0:T(8,128)(2,1)}, u32[]{:S(2)}) copy-start(bf16[2,16,16,384]{3,2,1,0:T(8,128)(2,1)} %copy-done.9) | copy-start | bytes 1179652
  31.5 7.1 %collective-permute-start.3 = (bf16[2,4,256,384]{3,2,1,0:T(8,128)(2,1)S(1)}, bf16[2,4,256,384]{3,2,1,0:T(8,128)(2,1)S(1)}, u32[]{:S(2)}, u32[]{:S(2)}) collective-permute-start(bf16[2,4,256,384]{3,2,1,0:T(8,128)(2,1)S(1)} %copy-done.5), channel_id=1, source_target_pairs={{0,1},{1,0},{2,3},{3,2},{4,5},{5,4},{6,7},{7,6},{8,9},{9,8},{10,11... | collective-permute-start | bytes 4718600 | tf_op jit(solution)/shard_map/ppermute | solution.py:525
  32.0 22.8 %collective-permute-start.7 = (bf16[2,4,4,48,256]{4,3,2,1,0:T(8,128)(2,1)}, bf16[2,4,4,48,256]{4,3,2,1,0:T(8,128)(2,1)S(1)}, u32[]{:S(2)}, u32[]{:S(2)}) collective-permute-start(bf16[2,4,4,48,256]{4,3,2,1,0:T(8,128)(2,1)} %get-tuple-element.92.refs_2_), channel_id=1, source_target_pairs={{0,2},{2,0},{1,3},{3,1},{4,6},{6,4},{5,7},{7,5},{8,10},{10,8},{9,1... | collective-permute-start | bytes 2359304 | tf_op jit(solution)/shard_map/ppermute | solution.py:525
  33.5 17.2 %collective-permute-start.4 = (bf16[2,4,48,256]{3,2,1,0:T(8,128)(2,1)}, bf16[2,4,48,256]{3,2,1,0:T(8,128)(2,1)S(1)}, u32[]{:S(2)}, u32[]{:S(2)}) collective-permute-start(bf16[2,4,48,256]{3,2,1,0:T(8,128)(2,1)} %get-tuple-element.99), channel_id=1, source_target_pairs={{0,12},{4,8},{8,4},{12,0},{1,13},{5,9},{9,5},{13,1},{2,14},{6,10},... | collective-permute-start | bytes 589832 | tf_op jit(solution)/shard_map/ppermute | solution.py:525
  37.9 16.9 %collective-permute-start.5 = (bf16[2,4,48,256]{3,2,1,0:T(8,128)(2,1)}, bf16[2,4,48,256]{3,2,1,0:T(8,128)(2,1)S(1)}, u32[]{:S(2)}, u32[]{:S(2)}) collective-permute-start(bf16[2,4,48,256]{3,2,1,0:T(8,128)(2,1)} %get-tuple-element.100), channel_id=1, source_target_pairs={{0,8},{4,12},{8,0},{12,4},{1,9},{5,13},{9,1},{13,5},{2,10},{6,14},... | collective-permute-start | bytes 589832 | tf_op jit(solution)/shard_map/ppermute | solution.py:525
  37.9 16.9 %collective-permute-start.6 = (bf16[2,4,48,256]{3,2,1,0:T(8,128)(2,1)}, bf16[2,4,48,256]{3,2,1,0:T(8,128)(2,1)S(1)}, u32[]{:S(2)}, u32[]{:S(2)}) collective-permute-start(bf16[2,4,48,256]{3,2,1,0:T(8,128)(2,1)} %get-tuple-element.101), channel_id=1, source_target_pairs={{0,4},{4,0},{8,12},{12,8},{1,5},{5,1},{9,13},{13,9},{2,6},{6,2},{1... | collective-permute-start | bytes 589832 | tf_op jit(solution)/shard_map/ppermute | solution.py:525
  42.4 2.8 %copy-start.1 = (bf16[2,16,256,384]{3,2,1,0:T(8,128)(2,1)S(1)}, bf16[2,16,256,384]{3,2,1,0:T(8,128)(2,1)}, u32[]{:S(2)}) copy-start(bf16[2,16,256,384]{3,2,1,0:T(8,128)(2,1)} %refs_0_.7) | copy-start | bytes 18874372
  45.2 18.5 %slice-start = ((s8[6291456]{0:T(1024)(128)(4,1)}), s8[4194304]{0:T(1024)(128)(4,1)S(1)}, s32[]{:S(2)}) async-start(s8[6291456]{0:T(1024)(128)(4,1)} %bitcast.3), calls=%async_computation | async-start | bytes 8388608
  54.8 8.9 %slice-start.1 = ((s8[6291456]{0:T(1024)(128)(4,1)}), s8[2097152]{0:T(1024)(128)(4,1)S(1)}, s32[]{:S(2)}) async-start(s8[6291456]{0:T(1024)(128)(4,1)} %bitcast.3), calls=%async_computation.1 | async-start | bytes 4194304
  54.8 5.1 %collective-permute-start.8 = (bf16[2,4,256,384]{3,2,1,0:T(8,128)(2,1)S(1)}, bf16[2,4,256,384]{3,2,1,0:T(8,128)(2,1)S(1)}, u32[]{:S(2)}, u32[]{:S(2)}) collective-permute-start(bf16[2,4,256,384]{3,2,1,0:T(8,128)(2,1)S(1)} %interpolate.6.refs_1_.refs_7_), channel_id=1, source_target_pairs={{0,1},{1,0},{2,3},{3,2},{4,5},{5,4},{6,7},{7,6},{8,9},{9,8},{10,11... | collective-permute-start | bytes 4718600 | tf_op jit(solution)/shard_map/ppermute | solution.py:525
  54.9 20.0 %collective-permute-start.12 = (bf16[2,4,4,48,256]{4,3,2,1,0:T(8,128)(2,1)S(1)}, bf16[2,4,4,48,256]{4,3,2,1,0:T(8,128)(2,1)S(1)}, u32[]{:S(2)}, u32[]{:S(2)}) collective-permute-start(bf16[2,4,4,48,256]{4,3,2,1,0:T(8,128)(2,1)S(1)} %get-tuple-element.102.refs_5_.refs_3_), channel_id=1, source_target_pairs={{0,2},{2,0},{1,3},{3,1},{4,6},{6,4},{5,7},{7,5},{8,10},{10,8},{9,1... | collective-permute-start | bytes 2359304 | tf_op jit(solution)/shard_map/ppermute | solution.py:525
  55.5 13.8 %collective-permute-start.9 = (bf16[2,4,48,256]{3,2,1,0:T(8,128)(2,1)S(1)}, bf16[2,4,48,256]{3,2,1,0:T(8,128)(2,1)S(1)}, u32[]{:S(2)}, u32[]{:S(2)}) collective-permute-start(bf16[2,4,48,256]{3,2,1,0:T(8,128)(2,1)S(1)} %get-tuple-element.109), channel_id=1, source_target_pairs={{0,12},{4,8},{8,4},{12,0},{1,13},{5,9},{9,5},{13,1},{2,14},{6,10},... | collective-permute-start | bytes 589832 | tf_op jit(solution)/shard_map/ppermute | solution.py:525
  58.0 16.8 %collective-permute-start.10 = (bf16[2,4,48,256]{3,2,1,0:T(8,128)(2,1)S(1)}, bf16[2,4,48,256]{3,2,1,0:T(8,128)(2,1)S(1)}, u32[]{:S(2)}, u32[]{:S(2)}) collective-permute-start(bf16[2,4,48,256]{3,2,1,0:T(8,128)(2,1)S(1)} %get-tuple-element.110), channel_id=1, source_target_pairs={{0,8},{4,12},{8,0},{12,4},{1,9},{5,13},{9,1},{13,5},{2,10},{6,14},... | collective-permute-start | bytes 589832 | tf_op jit(solution)/shard_map/ppermute | solution.py:525
  58.0 16.8 %collective-permute-start.11 = (bf16[2,4,48,256]{3,2,1,0:T(8,128)(2,1)S(1)}, bf16[2,4,48,256]{3,2,1,0:T(8,128)(2,1)S(1)}, u32[]{:S(2)}, u32[]{:S(2)}) collective-permute-start(bf16[2,4,48,256]{3,2,1,0:T(8,128)(2,1)S(1)} %get-tuple-element.111), channel_id=1, source_target_pairs={{0,4},{4,0},{8,12},{12,8},{1,5},{5,1},{9,13},{13,9},{2,6},{6,2},{1... | collective-permute-start | bytes 589832 | tf_op jit(solution)/shard_map/ppermute | solution.py:525
  74.9 25.4 %copy-start.3 = (bf16[1024,1024]{1,0:T(8,128)(2,1)S(1)}, bf16[1024,1024]{1,0:T(8,128)(2,1)}, u32[]{:S(2)}) copy-start(bf16[1024,1024]{1,0:T(8,128)(2,1)} %constant.21.clone.refs_14_.refs_6_) | copy-start | bytes 6291460
  74.9 25.4 %copy-start.4 = (bf16[1024,1024]{1,0:T(8,128)(2,1)S(1)}, bf16[1024,1024]{1,0:T(8,128)(2,1)}, u32[]{:S(2)}) copy-start(bf16[1024,1024]{1,0:T(8,128)(2,1)} %constant.20.clone.refs_13_.refs_5_) | copy-start | bytes 6291460
  74.9 25.4 %copy-start.12 = (bf16[2,4,48,256]{3,2,1,0:T(8,128)(2,1)S(1)}, bf16[2,4,48,256]{3,2,1,0:T(8,128)(2,1)}, u32[]{:S(2)}) copy-start(bf16[2,4,48,256]{3,2,1,0:T(8,128)(2,1)} %get-tuple-element.126.refs_1_) | copy-start | bytes 589828
  74.9 5.5 %collective-permute-start.13 = (bf16[2,4,256,384]{3,2,1,0:T(8,128)(2,1)S(1)}, bf16[2,4,256,384]{3,2,1,0:T(8,128)(2,1)S(1)}, u32[]{:S(2)}, u32[]{:S(2)}) collective-permute-start(bf16[2,4,256,384]{3,2,1,0:T(8,128)(2,1)S(1)} %interpolate.7.refs_1_.refs_7_), channel_id=1, source_target_pairs={{0,1},{1,0},{2,3},{3,2},{4,5},{5,4},{6,7},{7,6},{8,9},{9,8},{10,11... | collective-permute-start | bytes 4718600 | tf_op jit(solution)/shard_map/ppermute | solution.py:525
  74.9 20.0 %collective-permute-start.17 = (bf16[2,4,4,48,256]{4,3,2,1,0:T(8,128)(2,1)S(1)}, bf16[2,4,4,48,256]{4,3,2,1,0:T(8,128)(2,1)S(1)}, u32[]{:S(2)}, u32[]{:S(2)}) collective-permute-start(bf16[2,4,4,48,256]{4,3,2,1,0:T(8,128)(2,1)S(1)} %get-tuple-element.112.refs_5_.refs_4_), channel_id=1, source_target_pairs={{0,2},{2,0},{1,3},{3,1},{4,6},{6,4},{5,7},{7,5},{8,10},{10,8},{9,1... | collective-permute-start | bytes 2359304 | tf_op jit(solution)/shard_map/ppermute | solution.py:525
  76.0 9.7 %collective-permute-start.14 = (bf16[2,4,48,256]{3,2,1,0:T(8,128)(2,1)S(1)}, bf16[2,4,48,256]{3,2,1,0:T(8,128)(2,1)S(1)}, u32[]{:S(2)}, u32[]{:S(2)}) collective-permute-start(bf16[2,4,48,256]{3,2,1,0:T(8,128)(2,1)S(1)} %get-tuple-element.119), channel_id=1, source_target_pairs={{0,12},{4,8},{8,4},{12,0},{1,13},{5,9},{9,5},{13,1},{2,14},{6,10},... | collective-permute-start | bytes 589832 | tf_op jit(solution)/shard_map/ppermute | solution.py:525
  78.0 16.8 %collective-permute-start.15 = (bf16[2,4,48,256]{3,2,1,0:T(8,128)(2,1)S(1)}, bf16[2,4,48,256]{3,2,1,0:T(8,128)(2,1)S(1)}, u32[]{:S(2)}, u32[]{:S(2)}) collective-permute-start(bf16[2,4,48,256]{3,2,1,0:T(8,128)(2,1)S(1)} %get-tuple-element.120), channel_id=1, source_target_pairs={{0,8},{4,12},{8,0},{12,4},{1,9},{5,13},{9,1},{13,5},{2,10},{6,14},... | collective-permute-start | bytes 589832 | tf_op jit(solution)/shard_map/ppermute | solution.py:525
  78.0 16.8 %collective-permute-start.16 = (bf16[2,4,48,256]{3,2,1,0:T(8,128)(2,1)S(1)}, bf16[2,4,48,256]{3,2,1,0:T(8,128)(2,1)S(1)}, u32[]{:S(2)}, u32[]{:S(2)}) collective-permute-start(bf16[2,4,48,256]{3,2,1,0:T(8,128)(2,1)S(1)} %get-tuple-element.121), channel_id=1, source_target_pairs={{0,4},{4,0},{8,12},{12,8},{1,5},{5,1},{9,13},{13,9},{2,6},{6,2},{1... | collective-permute-start | bytes 589832 | tf_op jit(solution)/shard_map/ppermute | solution.py:525
  94.9 20.1 %copy-start.8 = (bf16[2,2,256,512]{3,2,1,0:T(8,128)(2,1)S(1)}, bf16[2,2,256,512]{3,2,1,0:T(8,128)(2,1)}, u32[]{:S(2)}) copy-start(bf16[2,2,256,512]{3,2,1,0:T(8,128)(2,1)} %constant.22.clone.refs_1_) | copy-start | bytes 3145732
  94.9 20.1 %copy-start.11 = (bf16[2,4,4,48,256]{4,3,2,1,0:T(8,128)(2,1)S(1)}, bf16[2,4,4,48,256]{4,3,2,1,0:T(8,128)(2,1)}, u32[]{:S(2)}) copy-start(bf16[2,4,4,48,256]{4,3,2,1,0:T(8,128)(2,1)} %get-tuple-element.92.refs_2_) | copy-start | bytes 2359300
  94.9 19.1 %collective-permute-start.21 = (bf16[2,4,4,48,256]{4,3,2,1,0:T(8,128)(2,1)S(1)}, bf16[2,4,4,48,256]{4,3,2,1,0:T(8,128)(2,1)S(1)}, u32[]{:S(2)}, u32[]{:S(2)}) collective-permute-start(bf16[2,4,4,48,256]{4,3,2,1,0:T(8,128)(2,1)S(1)} %get-tuple-element.122.refs_15_.refs_5_), channel_id=1, source_target_pairs={{0,2},{2,0},{1,3},{3,1},{4,6},{6,4},{5,7},{7,5},{8,10},{10,8},{9,1... | collective-permute-start | bytes 2359304 | tf_op jit(solution)/shard_map/ppermute | solution.py:525
  95.9 11.0 %collective-permute-start.18 = (bf16[2,4,48,256]{3,2,1,0:T(8,128)(2,1)S(1)}, bf16[2,4,48,256]{3,2,1,0:T(8,128)(2,1)S(1)}, u32[]{:S(2)}, u32[]{:S(2)}) collective-permute-start(bf16[2,4,48,256]{3,2,1,0:T(8,128)(2,1)S(1)} %get-tuple-element.138), channel_id=1, source_target_pairs={{0,12},{4,8},{8,4},{12,0},{1,13},{5,9},{9,5},{13,1},{2,14},{6,10},... | collective-permute-start | bytes 589832 | tf_op jit(solution)/shard_map/ppermute | solution.py:525
  97.9 16.0 %collective-permute-start.19 = (bf16[2,4,48,256]{3,2,1,0:T(8,128)(2,1)S(1)}, bf16[2,4,48,256]{3,2,1,0:T(8,128)(2,1)S(1)}, u32[]{:S(2)}, u32[]{:S(2)}) collective-permute-start(bf16[2,4,48,256]{3,2,1,0:T(8,128)(2,1)S(1)} %get-tuple-element.139), channel_id=1, source_target_pairs={{0,8},{4,12},{8,0},{12,4},{1,9},{5,13},{9,1},{13,5},{2,10},{6,14},... | collective-permute-start | bytes 589832 | tf_op jit(solution)/shard_map/ppermute | solution.py:525
  97.9 16.0 %collective-permute-start.20 = (bf16[2,4,48,256]{3,2,1,0:T(8,128)(2,1)S(1)}, bf16[2,4,48,256]{3,2,1,0:T(8,128)(2,1)S(1)}, u32[]{:S(2)}, u32[]{:S(2)}) collective-permute-start(bf16[2,4,48,256]{3,2,1,0:T(8,128)(2,1)S(1)} %get-tuple-element.140), channel_id=1, source_target_pairs={{0,4},{4,0},{8,12},{12,8},{1,5},{5,1},{9,13},{13,9},{2,6},{6,2},{1... | collective-permute-start | bytes 589832 | tf_op jit(solution)/shard_map/ppermute | solution.py:525
  114.0 54.2 %collective-permute-start.28 = (bf16[2,12,48,1024]{3,2,1,0:T(8,128)(2,1)S(1)}, bf16[2,12,48,1024]{3,2,1,0:T(8,128)(2,1)S(1)}, u32[]{:S(2)}, u32[]{:S(2)}) collective-permute-start(bf16[2,12,48,1024]{3,2,1,0:T(8,128)(2,1)S(1)} %cross_transform.4.refs_10_.refs_2_), channel_id=1, source_target_pairs={{0,2},{2,0},{1,3},{3,1},{4,6},{6,4},{5,7},{7,5},{8,10},{10,8},{9,1... | collective-permute-start | bytes 7077896 | tf_op jit(solution)/shard_map/ppermute | solution.py:525
  118.5 16.6 %collective-permute-start.24 = (bf16[2,8,48,256]{3,2,1,0:T(8,128)(2,1)S(1)}, bf16[2,8,48,256]{3,2,1,0:T(8,128)(2,1)S(1)}, u32[]{:S(2)}, u32[]{:S(2)}) collective-permute-start(bf16[2,8,48,256]{3,2,1,0:T(8,128)(2,1)S(1)} %get-tuple-element.144), channel_id=1, source_target_pairs={{0,4},{4,0},{8,12},{12,8},{1,5},{5,1},{9,13},{13,9},{2,6},{6,2},{1... | collective-permute-start | bytes 1179656 | tf_op jit(solution)/shard_map/ppermute | solution.py:525
  118.6 29.9 %collective-permute-start.23 = (bf16[2,8,48,256]{3,2,1,0:T(8,128)(2,1)S(1)}, bf16[2,8,48,256]{3,2,1,0:T(8,128)(2,1)S(1)}, u32[]{:S(2)}, u32[]{:S(2)}) collective-permute-start(bf16[2,8,48,256]{3,2,1,0:T(8,128)(2,1)S(1)} %get-tuple-element.145), channel_id=1, source_target_pairs={{0,8},{4,12},{8,0},{12,4},{1,9},{5,13},{9,1},{13,5},{2,10},{6,14},... | collective-permute-start | bytes 1179656 | tf_op jit(solution)/shard_map/ppermute | solution.py:525
  121.2 27.3 %collective-permute-start.22 = (bf16[2,8,48,256]{3,2,1,0:T(8,128)(2,1)S(1)}, bf16[2,8,48,256]{3,2,1,0:T(8,128)(2,1)S(1)}, u32[]{:S(2)}, u32[]{:S(2)}) collective-permute-start(bf16[2,8,48,256]{3,2,1,0:T(8,128)(2,1)S(1)} %get-tuple-element.146), channel_id=1, source_target_pairs={{0,12},{4,8},{8,4},{12,0},{1,13},{5,9},{9,5},{13,1},{2,14},{6,10},... | collective-permute-start | bytes 1179656 | tf_op jit(solution)/shard_map/ppermute | solution.py:525
  126.2 53.2 %collective-permute-start.30 = (bf16[2,4,32,1024]{3,2,1,0:T(8,128)(2,1)S(1)}, bf16[2,4,32,1024]{3,2,1,0:T(8,128)(2,1)S(1)}, u32[]{:S(2)}, u32[]{:S(2)}) collective-permute-start(bf16[2,4,32,1024]{3,2,1,0:T(8,128)(2,1)S(1)} %get-tuple-element.164.refs_7_.refs_3_), channel_id=1, source_target_pairs={{0,2},{2,0},{1,3},{3,1},{4,6},{6,4},{5,7},{7,5},{8,10},{10,8},{9,1... | collective-permute-start | bytes 1572872 | tf_op jit(solution)/shard_map/ppermute | solution.py:525
  148.5 37.3 %collective-permute-start.25 = (bf16[2,8,48,256]{3,2,1,0:T(8,128)(2,1)S(1)}, bf16[2,8,48,256]{3,2,1,0:T(8,128)(2,1)S(1)}, u32[]{:S(2)}, u32[]{:S(2)}) collective-permute-start(bf16[2,8,48,256]{3,2,1,0:T(8,128)(2,1)S(1)} %get-tuple-element.157), channel_id=1, source_target_pairs={{0,4},{4,0},{8,12},{12,8},{1,5},{5,1},{9,13},{13,9},{2,6},{6,2},{1... | collective-permute-start | bytes 1179656 | tf_op jit(solution)/shard_map/ppermute | solution.py:525
  155.0 30.8 %collective-permute-start.26 = (bf16[2,8,48,256]{3,2,1,0:T(8,128)(2,1)S(1)}, bf16[2,8,48,256]{3,2,1,0:T(8,128)(2,1)S(1)}, u32[]{:S(2)}, u32[]{:S(2)}) collective-permute-start(bf16[2,8,48,256]{3,2,1,0:T(8,128)(2,1)S(1)} %get-tuple-element.158), channel_id=1, source_target_pairs={{0,8},{4,12},{8,0},{12,4},{1,9},{5,13},{9,1},{13,5},{2,10},{6,14},... | collective-permute-start | bytes 1179656 | tf_op jit(solution)/shard_map/ppermute | solution.py:525
  155.8 29.9 %collective-permute-start.27 = (bf16[2,8,48,256]{3,2,1,0:T(8,128)(2,1)S(1)}, bf16[2,8,48,256]{3,2,1,0:T(8,128)(2,1)S(1)}, u32[]{:S(2)}, u32[]{:S(2)}) collective-permute-start(bf16[2,8,48,256]{3,2,1,0:T(8,128)(2,1)S(1)} %get-tuple-element.159), channel_id=1, source_target_pairs={{0,12},{4,8},{8,4},{12,0},{1,13},{5,9},{9,5},{13,1},{2,14},{6,10},... | collective-permute-start | bytes 1179656 | tf_op jit(solution)/shard_map/ppermute | solution.py:525
  168.2 15.1 %collective-permute-start.29 = (bf16[2,4,16,1024]{3,2,1,0:T(8,128)(2,1)S(1)}, bf16[2,4,16,1024]{3,2,1,0:T(8,128)(2,1)S(1)}, u32[]{:S(2)}, u32[]{:S(2)}) collective-permute-start(bf16[2,4,16,1024]{3,2,1,0:T(8,128)(2,1)S(1)} %get-tuple-element.166.refs_3_), channel_id=1, source_target_pairs={{0,2},{2,0},{1,3},{3,1},{4,6},{6,4},{5,7},{7,5},{8,10},{10,8},{9,1... | collective-permute-start | bytes 786440 | tf_op jit(solution)/shard_map/ppermute | solution.py:525

commit v6 on v5

--- a/solution.py
+++ b/solution.py
@@ -559,7 +559,14 @@
     range_table = jnp.asarray(np.stack(tables))
     cross_tables = [jnp.asarray(t) for t in host_table(np.arange(A), np.arange(A), A)]
     order = np.concatenate([start + np.arange(count) for start, count in CHUNKS])
-    matrix = jnp.asarray(height_table(cuts, ROWS, order))
+    whole_table = height_table(cuts, ROWS, order)
+    matrix = jnp.asarray(whole_table)
+    by_height = whole_table.reshape(2, 2, 2, cuts // 2, ROWS, -1)
+    pieces, start = [], 0
+    for size in PARTS:
+        piece = by_height[:, :, :, start // 2 : (start + size) // 2]
+        pieces.append(jnp.asarray(piece.reshape(2, 2, size * ROWS, -1)))
+        start += size
 
     bands = (band_offset, tap_count, tap_weight)
     halo = halo_rows(polar)
@@ -601,10 +608,13 @@
     other_first.append(moving[1])
     other_c0 = exchange(c0, "el", 1)
 
-    made = first_heights(ids, matrix, own_first, other_first, PARTS, (c0,))
+    made, before = [], c0
+    for piece, size in zip(pieces, PARTS):
+        made += first_heights(ids, piece, own_first, other_first, (size,), (before,))
+        before = made[-1][0]
     come = to_owners(made[0])
     late = [rest - ROWS, ROWS]
-    c1, c2 = cross_transform(ids, landed[-1:], cross_tables, scale, late, earlier=(made[0][0],))
+    c1, c2 = cross_transform(ids, landed[-1:], cross_tables, scale, late, earlier=(before,))
     other_c1 = exchange(c1, "el", 1)
     shape = (2, cuts, bins, A)
     full_scale = 1.0 / math.sqrt(A * 2 * cuts)

time: 193 us -> 192 us (level)
    pallas_call x1 -> x2, Pallas kernels: 3.54 us -> 5.42 us  [first_heights(): pl.pallas_call(lambda *refs: height_kernel(*refs, chunks=chunks, sets=blo...]
  transfers between devices with their start and end apart: 31 -> 31, of which waited for: 13 -> 13; matrix products, arithmetic and copies ran while one was open for 0% -> 0% of each run, Pallas kernels for 32% -> 33%
where the time goes in v6:
time: 192 us; the launch traced here: 191 us
  Pallas kernels  77.4 us (40%)
  waiting for transfers between devices  62.7 us (33%)
  starting transfers between devices  45.6 us (24%)
  local copies, waits for them, and re-layouts  4.74 us (2%)
    ppermute x29, waiting for transfers between devices, exchange(): lax.ppermute(value, axis, [(i, i ^ s) for i in range(lax.axis_size(axis))])  62.4 us
    ppermute x29, starting transfers between devices, exchange(): lax.ppermute(value, axis, [(i, i ^ s) for i in range(lax.axis_size(axis))])  39.3 us
    pallas_call x4, Pallas kernels, interpolate(): pl.pallas_call(lambda *refs: interp_kernel(*refs, bordered=len(border) ==...  24.3 us
    pallas_call x4, Pallas kernels, cross_transform(): pl.pallas_call(lambda *refs: cross_kernel(*refs, groups=groups, blocks=bl...  20.7 us
    pallas_call x4, Pallas kernels, range_transform(): pl.pallas_call(lambda *refs: range_kernel(*refs, blocks=blocks, earlier=l...  18.3 us
    pallas_call x2, Pallas kernels, last_heights(): pl.pallas_call(lambda *refs: height_kernel(*refs, chunks=chunks, sets=1,...  6.33 us
    pallas_call x2, Pallas kernels, first_heights(): pl.pallas_call(lambda *refs: height_kernel(*refs, chunks=chunks, sets=blo...  5.42 us
    ppermute x1, starting transfers between devices, halo_rows(): lax.ppermute(tail, 'az', [(i, i + 1) for i in range(ends)])  4.94 us
  transfers between devices with their start and end apart: 31, of which 13 were waited for; matrix products, arithmetic and copies ran while one was open for 0% of the time, Pallas kernels for 33%

profile of v6, /device:TPU:0, one launch (start us, length us, event | category | flops | bytes accessed | tf_op | source)
XLA Modules:
  0.0 191.4 jit_solution(6009251333086746950)
XLA Ops:
  0.0 1.1 fusion
  1.1 4.9 %collective-permute-start = (bf16[2,16,8,384]{3,2,1,0:T(8,128)(2,1)S(1)}, bf16[2,16,8,384]{3,2,1,0:T(8,128)(2,1)S(1)}, u32[]{:S(2)}, u32[]{:S(2)}) collective-permute-start(bf16[2,16,8,384]{3,2,1,0:T(8,128)(2,1)S(1)} %get-tuple-element.170), channel_id=1, source_target_pairs={{0,4},{4,8},{8,12},{1,5},{5,9},{9,13},{2,6},{6,10},{10,14},{3,7},{... | collective-permute-start | bytes 589832 | tf_op jit(solution)/shard_map/ppermute | solution.py:536
  6.0 1.3 collective-permute-start.1
  7.3 6.7 %interpolate.4.made_ref = bf16[2,4,256,384]{3,2,1,0:T(8,128)(2,1)} custom-call(bf16[2,16,256,384]{3,2,1,0:T(8,128)(2,1)} %refs_0_.7, s32[256,384]{1,0:T(8,128)} %refs_1_.11, s32[256,384]{1,0:T(8,128)} %refs_2_.7, bf16[8,256,384]{2,1,0:T(8,128)(2,1)} %refs_3_.11), custom_call_target="tpu_custom_call" | custom-call | flops 26738 | bytes 3145 | tf_op jit(solution)/shard_map/interpolate/pallas_call | solution.py:204
  15.1 2.3 %interpolate_edges.1.refs_5_.refs_1_ = bf16[2,4,256,384]{3,2,1,0:T(8,128)(2,1)} custom-call(bf16[2,16,256,384]{3,2,1,0:T(8,128)(2,1)} %refs_0_.7, bf16[2,16,16,384]{3,2,1,0:T(8,128)(2,1)} %copy-done.8, s32[256,384]{1,0:T(8,128)} %refs_1_.11, s32[256,384]{1,0:T(8,128)} %refs_2_.7, bf16[8,256,384]{2,1,0:T(8,128)(2,1)} %refs_3_.11, ...), custom_call_target="tpu_custom_call", output_to_operand_aliasing={{}: (5, {})} | custom-call | flops 3342 | bytes 393 | tf_op jit(solution)/shard_map/interpolate_edges/pallas_call | solution.py:244
  18.1 6.7 %interpolate.5.refs_7_.refs_1_ = bf16[2,4,256,384]{3,2,1,0:T(8,128)(2,1)} custom-call(bf16[2,16,256,384]{3,2,1,0:T(8,128)(2,1)} %refs_0_.7, s32[256,384]{1,0:T(8,128)} %refs_1_.11, s32[256,384]{1,0:T(8,128)} %refs_2_.7, bf16[8,256,384]{2,1,0:T(8,128)(2,1)} %refs_3_.11, bf16[2,16,16,384]{3,2,1,0:T(8,128)(2,1)} %copy-done.8, ...), custom_call_target="tpu_custom_call" | custom-call | flops 26738 | bytes 3145 | tf_op jit(solution)/shard_map/interpolate/pallas_call | solution.py:204
  24.8 6.7 %range_transform.4 = (bf16[2,4,4,48,256]{4,3,2,1,0:T(8,128)(2,1)}, bf16[2,4,48,256]{3,2,1,0:T(8,128)(2,1)}, bf16[2,4,48,256]{3,2,1,0:T(8,128)(2,1)}, bf16[2,4,48...) custom-call(s32[3]{0:T(128)} %pad_add_fusion.refs_0_, bf16[2,4,256,384]{3,2,1,0:T(8,128)(2,1)} %interpolate_edges.1.refs_5_.refs_1_, ...), custom_call_target="tpu_custom_call" | custom-call | flops 2415919 | bytes 4718 | tf_op jit(solution)/shard_map/range_transform/pallas_call | solution.py:303
  32.1 1.5 collective-permute-start.7
  33.6 4.4 %collective-permute-start.4 = (bf16[2,4,48,256]{3,2,1,0:T(8,128)(2,1)}, bf16[2,4,48,256]{3,2,1,0:T(8,128)(2,1)S(1)}, u32[]{:S(2)}, u32[]{:S(2)}) collective-permute-start(bf16[2,4,48,256]{3,2,1,0:T(8,128)(2,1)} %get-tuple-element.99), channel_id=1, source_target_pairs={{0,12},{4,8},{8,4},{12,0},{1,13},{5,9},{9,5},{13,1},{2,14},{6,10},... | collective-permute-start | bytes 589832 | tf_op jit(solution)/shard_map/ppermute | solution.py:525
  38.6 3.9 %range_transform.5 = (bf16[2,4,4,48,256]{4,3,2,1,0:T(8,128)(2,1)S(1)}, bf16[2,4,48,256]{3,2,1,0:T(8,128)(2,1)S(1)}, bf16[2,4,48,256]{3,2,1,0:T(8,128)(2,1)S(1)},...) custom-call(s32[3]{0:T(128)S(1)} %copy-done.15, bf16[2,4,256,384]{3,2,1,0:T(8,128)(2,1)S(1)} %copy-done.5, ...), custom_call_target="tpu_custom_call" | custom-call | flops 2415919 | bytes 4718 | tf_op jit(solution)/shard_map/range_transform/pallas_call | solution.py:303
  42.5 2.8 %copy-done.1 = bf16[2,16,256,384]{3,2,1,0:T(8,128)(2,1)S(1)} copy-done((bf16[2,16,256,384]{3,2,1,0:T(8,128)(2,1)S(1)}, bf16[2,16,256,384]{3,2,1,0:T(8,128)(2,1)}, u32[]{:S(2)}) %copy-start.1) | copy-done | bytes 6291480
  45.3 5.5 %interpolate.6.refs_1_.refs_7_ = bf16[2,4,256,384]{3,2,1,0:T(8,128)(2,1)S(1)} custom-call(bf16[2,16,256,384]{3,2,1,0:T(8,128)(2,1)S(1)} %copy-done.1, s32[256,384]{1,0:T(8,128)S(1)} %copy-done.6, s32[256,384]{1,0:T(8,128)S(1)} %copy-done.7, bf16[8,256,384]{2,1,0:T(8,128)(2,1)S(1)} %copy-done.2, bf16[2,16,16,384]{3,2,1,0:T(8,128)(2,1)S(1)} %copy-done.9, ...), custom_call_target="tpu_custom_call" | custom-call | flops 26738 | bytes 3145 | tf_op jit(solution)/shard_map/interpolate/pallas_call | solution.py:204
  50.8 4.1 %collective-permute-done.5.refs_3_ = bf16[2,4,48,256]{3,2,1,0:T(8,128)(2,1)S(1)} collective-permute-done((bf16[2,4,48,256]{3,2,1,0:T(8,128)(2,1)}, bf16[2,4,48,256]{3,2,1,0:T(8,128)(2,1)S(1)}, u32[]{:S(2)}, u32[]{:S(2)}) %collective-permute-start.5) | collective-permute-done | bytes 196640 | tf_op jit(solution)/shard_map/ppermute | solution.py:525
  55.6 2.5 %collective-permute-start.9 = (bf16[2,4,48,256]{3,2,1,0:T(8,128)(2,1)S(1)}, bf16[2,4,48,256]{3,2,1,0:T(8,128)(2,1)S(1)}, u32[]{:S(2)}, u32[]{:S(2)}) collective-permute-start(bf16[2,4,48,256]{3,2,1,0:T(8,128)(2,1)S(1)} %get-tuple-element.109), channel_id=1, source_target_pairs={{0,12},{4,8},{8,4},{12,0},{1,13},{5,9},{9,5},{13,1},{2,14},{6,10},... | collective-permute-start | bytes 589832 | tf_op jit(solution)/shard_map/ppermute | solution.py:525
  58.0 1.9 %collective-permute-start.11 = (bf16[2,4,48,256]{3,2,1,0:T(8,128)(2,1)S(1)}, bf16[2,4,48,256]{3,2,1,0:T(8,128)(2,1)S(1)}, u32[]{:S(2)}, u32[]{:S(2)}) collective-permute-start(bf16[2,4,48,256]{3,2,1,0:T(8,128)(2,1)S(1)} %get-tuple-element.111), channel_id=1, source_target_pairs={{0,4},{4,0},{8,12},{12,8},{1,5},{5,1},{9,13},{13,9},{2,6},{6,2},{1... | collective-permute-start | bytes 589832 | tf_op jit(solution)/shard_map/ppermute | solution.py:525
  59.9 3.9 %range_transform.6 = (bf16[2,4,4,48,256]{4,3,2,1,0:T(8,128)(2,1)S(1)}, bf16[2,4,48,256]{3,2,1,0:T(8,128)(2,1)S(1)}, bf16[2,4,48,256]{3,2,1,0:T(8,128)(2,1)S(1)},...) custom-call(s32[3]{0:T(128)S(1)} %copy-done.15, bf16[2,4,256,384]{3,2,1,0:T(8,128)(2,1)S(1)} %interpolate.6.refs_1_.refs_7_, ...), custom_call_target="tpu_custom_call" | custom-call | flops 2415919 | bytes 4718 | tf_op jit(solution)/shard_map/range_transform/pallas_call | solution.py:303
  63.8 5.5 %interpolate.7.refs_1_.refs_7_ = bf16[2,4,256,384]{3,2,1,0:T(8,128)(2,1)S(1)} custom-call(bf16[2,16,256,384]{3,2,1,0:T(8,128)(2,1)S(1)} %bitcast.4, s32[256,384]{1,0:T(8,128)S(1)} %copy-done.6, s32[256,384]{1,0:T(8,128)S(1)} %copy-done.7, bf16[8,256,384]{2,1,0:T(8,128)(2,1)S(1)} %copy-done.2, bf16[2,16,16,384]{3,2,1,0:T(8,128)(2,1)S(1)} %copy-done.9, ...), custom_call_target="tpu_custom_call" | custom-call | flops 26738 | bytes 3145 | tf_op jit(solution)/shard_map/interpolate/pallas_call | solution.py:204
  69.3 5.5 %collective-permute-done.10.refs_7_ = bf16[2,4,48,256]{3,2,1,0:T(8,128)(2,1)S(1)} collective-permute-done((bf16[2,4,48,256]{3,2,1,0:T(8,128)(2,1)S(1)}, bf16[2,4,48,256]{3,2,1,0:T(8,128)(2,1)S(1)}, u32[]{:S(2)}, u32[]{:S(2)}) %collective-permute-start.10) | collective-permute-done | bytes 196640 | tf_op jit(solution)/shard_map/ppermute | solution.py:525
  75.0 1.1 collective-permute-start.17
  76.0 2.0 %collective-permute-start.14 = (bf16[2,4,48,256]{3,2,1,0:T(8,128)(2,1)S(1)}, bf16[2,4,48,256]{3,2,1,0:T(8,128)(2,1)S(1)}, u32[]{:S(2)}, u32[]{:S(2)}) collective-permute-start(bf16[2,4,48,256]{3,2,1,0:T(8,128)(2,1)S(1)} %get-tuple-element.119), channel_id=1, source_target_pairs={{0,12},{4,8},{8,4},{12,0},{1,13},{5,9},{9,5},{13,1},{2,14},{6,10},... | collective-permute-start | bytes 589832 | tf_op jit(solution)/shard_map/ppermute | solution.py:525
  78.0 2.4 %collective-permute-start.16 = (bf16[2,4,48,256]{3,2,1,0:T(8,128)(2,1)S(1)}, bf16[2,4,48,256]{3,2,1,0:T(8,128)(2,1)S(1)}, u32[]{:S(2)}, u32[]{:S(2)}) collective-permute-start(bf16[2,4,48,256]{3,2,1,0:T(8,128)(2,1)S(1)} %get-tuple-element.121), channel_id=1, source_target_pairs={{0,4},{4,0},{8,12},{12,8},{1,5},{5,1},{9,13},{13,9},{2,6},{6,2},{1... | collective-permute-start | bytes 589832 | tf_op jit(solution)/shard_map/ppermute | solution.py:525
  80.4 3.9 %range_transform.7 = (bf16[2,4,4,48,256]{4,3,2,1,0:T(8,128)(2,1)S(1)}, bf16[2,4,48,256]{3,2,1,0:T(8,128)(2,1)S(1)}, bf16[2,4,48,256]{3,2,1,0:T(8,128)(2,1)S(1)},...) custom-call(s32[3]{0:T(128)S(1)} %copy-done.15, bf16[2,4,256,384]{3,2,1,0:T(8,128)(2,1)S(1)} %interpolate.7.refs_1_.refs_7_, ...), custom_call_target="tpu_custom_call" | custom-call | flops 2415919 | bytes 4718 | tf_op jit(solution)/shard_map/range_transform/pallas_call | solution.py:303
  84.3 1.4 collective-permute-done.14.refs_12_
  85.7 9.1 %collective-permute-done.15.refs_11_ = bf16[2,4,48,256]{3,2,1,0:T(8,128)(2,1)S(1)} collective-permute-done((bf16[2,4,48,256]{3,2,1,0:T(8,128)(2,1)S(1)}, bf16[2,4,48,256]{3,2,1,0:T(8,128)(2,1)S(1)}, u32[]{:S(2)}, u32[]{:S(2)}) %collective-permute-start.15) | collective-permute-done | bytes 196640 | tf_op jit(solution)/shard_map/ppermute | solution.py:525
  94.9 1.0 collective-permute-start.21
  95.9 2.0 %collective-permute-start.18 = (bf16[2,4,48,256]{3,2,1,0:T(8,128)(2,1)S(1)}, bf16[2,4,48,256]{3,2,1,0:T(8,128)(2,1)S(1)}, u32[]{:S(2)}, u32[]{:S(2)}) collective-permute-start(bf16[2,4,48,256]{3,2,1,0:T(8,128)(2,1)S(1)} %get-tuple-element.138), channel_id=1, source_target_pairs={{0,12},{4,8},{8,4},{12,0},{1,13},{5,9},{9,5},{13,1},{2,14},{6,10},... | collective-permute-start | bytes 589832 | tf_op jit(solution)/shard_map/ppermute | solution.py:525
  97.9 2.4 %collective-permute-start.20 = (bf16[2,4,48,256]{3,2,1,0:T(8,128)(2,1)S(1)}, bf16[2,4,48,256]{3,2,1,0:T(8,128)(2,1)S(1)}, u32[]{:S(2)}, u32[]{:S(2)}) collective-permute-start(bf16[2,4,48,256]{3,2,1,0:T(8,128)(2,1)S(1)} %get-tuple-element.140), channel_id=1, source_target_pairs={{0,4},{4,0},{8,12},{12,8},{1,5},{5,1},{9,13},{13,9},{2,6},{6,2},{1... | collective-permute-start | bytes 589832 | tf_op jit(solution)/shard_map/ppermute | solution.py:525
  100.3 6.6 %cross_transform.4.refs_10_.refs_2_ = bf16[2,12,48,1024]{3,2,1,0:T(8,128)(2,1)S(1)} custom-call(s32[3]{0:T(128)S(1)} %copy-done.15, bf16[2,4,48,256]{3,2,1,0:T(8,128)(2,1)S(1)} %copy-done.14, bf16[2,4,48,256]{3,2,1,0:T(8,128)(2,1)S(1)} %collective-permute-done.6.refs_2_, bf16[2,4,48,256]{3,2,1,0:T(8,128)(2,1)S(1)} %collective-permute-done.5.refs_3_, ...), custom_call_target="tpu_custom_call" | custom-call | flops 4831838 | bytes 8912 | tf_op jit(solution)/shard_map/cross_transform/pallas_call | solution.py:489
  107.0 6.9 %collective-permute-done.19.refs_3_ = bf16[2,4,48,256]{3,2,1,0:T(8,128)(2,1)S(1)} collective-permute-done((bf16[2,4,48,256]{3,2,1,0:T(8,128)(2,1)S(1)}, bf16[2,4,48,256]{3,2,1,0:T(8,128)(2,1)S(1)}, u32[]{:S(2)}, u32[]{:S(2)}) %collective-permute-start.19) | collective-permute-done | bytes 196640 | tf_op jit(solution)/shard_map/ppermute | solution.py:525
  114.0 1.0 collective-permute-start.28
  115.0 2.6 %first_heights.2 = (bf16[2,8,48,256]{3,2,1,0:T(8,128)(2,1)S(1)}, bf16[2,8,48,256]{3,2,1,0:T(8,128)(2,1)S(1)}, bf16[2,8,48,256]{3,2,1,0:T(8,128)(2,1)S(1)}, bf16[2,8,48,256]{3,2,1,0:T(8,128)(2,1)S(1)}) custom-call(s32[3]{0:T(128)S(1)} %copy-done.15, bf16[2,2,128,512]{3,2,1,0:T(8,128)(2,1)S(1)} %copy-done.13, bf16[2,4,4,48,256]{4,3,2,1,0:T(8,128)(2,1)S(1)} %copy-done.11, ...), custom_call_target="tpu_custom_call" | custom-call | flops 1610612 | bytes 9437 | tf_op jit(solution)/shard_map/first_heights/pallas_call | solution.py:381
  117.7 2.6 %collective-permute-start.23 = (bf16[2,8,48,256]{3,2,1,0:T(8,128)(2,1)S(1)}, bf16[2,8,48,256]{3,2,1,0:T(8,128)(2,1)S(1)}, u32[]{:S(2)}, u32[]{:S(2)}) collective-permute-start(bf16[2,8,48,256]{3,2,1,0:T(8,128)(2,1)S(1)} %get-tuple-element.145), channel_id=1, source_target_pairs={{0,8},{4,12},{8,0},{12,4},{1,9},{5,13},{9,1},{13,5},{2,10},{6,14},... | collective-permute-start | bytes 1179656 | tf_op jit(solution)/shard_map/ppermute | solution.py:525
  120.3 1.8 collective-permute-start.22
  122.1 2.8 %first_heights.3 = (bf16[2,8,48,256]{3,2,1,0:T(8,128)(2,1)S(1)}, bf16[2,8,48,256]{3,2,1,0:T(8,128)(2,1)S(1)}, bf16[2,8,48,256]{3,2,1,0:T(8,128)(2,1)S(1)}, bf16[2,8,48,256]{3,2,1,0:T(8,128)(2,1)S(1)}) custom-call(s32[3]{0:T(128)S(1)} %copy-done.15, bf16[2,2,128,512]{3,2,1,0:T(8,128)(2,1)S(1)} %copy-done.12, bf16[2,4,4,48,256]{4,3,2,1,0:T(8,128)(2,1)S(1)} %copy-done.11, ...), custom_call_target="tpu_custom_call" | custom-call | flops 1610612 | bytes 9437 | tf_op jit(solution)/shard_map/first_heights/pallas_call | solution.py:381
  124.9 3.0 %cross_transform.5 = (bf16[2,4,32,1024]{3,2,1,0:T(8,128)(2,1)S(1)}, bf16[2,4,16,1024]{3,2,1,0:T(8,128)(2,1)S(1)}) custom-call(s32[3]{0:T(128)S(1)} %copy-done.15, bf16[2,4,48,256]{3,2,1,0:T(8,128)(2,1)S(1)} %get-tuple-element.151.refs_1_, bf16[2,4,48,256]{3,2,1,0:T(8,128)(2,1)S(1)} %collective-permute-done.20.refs_2_, ...), custom_call_target="tpu_custom_call" | custom-call | flops 1610612 | bytes 5767 | tf_op jit(solution)/shard_map/cross_transform/pallas_call | solution.py:489
  127.9 1.1 collective-permute-start.30
  129.0 5.2 %collective-permute-done.24.refs_2_ = bf16[2,8,48,256]{3,2,1,0:T(8,128)(2,1)S(1)} collective-permute-done((bf16[2,8,48,256]{3,2,1,0:T(8,128)(2,1)S(1)}, bf16[2,8,48,256]{3,2,1,0:T(8,128)(2,1)S(1)}, u32[]{:S(2)}, u32[]{:S(2)}) %collective-permute-start.24) | collective-permute-done | bytes 393248 | tf_op jit(solution)/shard_map/ppermute | solution.py:525
  134.2 13.4 %collective-permute-done.23.refs_3_ = bf16[2,8,48,256]{3,2,1,0:T(8,128)(2,1)S(1)} collective-permute-done((bf16[2,8,48,256]{3,2,1,0:T(8,128)(2,1)S(1)}, bf16[2,8,48,256]{3,2,1,0:T(8,128)(2,1)S(1)}, u32[]{:S(2)}, u32[]{:S(2)}) %collective-permute-start.23) | collective-permute-done | bytes 393248 | tf_op jit(solution)/shard_map/ppermute | solution.py:525
  147.6 6.5 %collective-permute-start.25 = (bf16[2,8,48,256]{3,2,1,0:T(8,128)(2,1)S(1)}, bf16[2,8,48,256]{3,2,1,0:T(8,128)(2,1)S(1)}, u32[]{:S(2)}, u32[]{:S(2)}) collective-permute-start(bf16[2,8,48,256]{3,2,1,0:T(8,128)(2,1)S(1)} %get-tuple-element.157), channel_id=1, source_target_pairs={{0,4},{4,0},{8,12},{12,8},{1,5},{5,1},{9,13},{13,9},{2,6},{6,2},{1... | collective-permute-start | bytes 1179656 | tf_op jit(solution)/shard_map/ppermute | solution.py:525
  154.1 0.9 collective-permute-start.26
  155.0 1.5 collective-permute-start.27
  156.5 5.6 %cross_transform.6.refs_6_ = bf16[2,16,96,1024]{3,2,1,0:T(8,128)(2,1)} custom-call(s32[3]{0:T(128)S(1)} %copy-done.15, bf16[2,8,48,256]{3,2,1,0:T(8,128)(2,1)S(1)} %get-tuple-element.160.refs_10_.refs_1_, bf16[2,8,48,256]{3,2,1,0:T(8,128)(2,1)S(1)} %collective-permute-done.24.refs_2_, bf16[2,8,48,256]{3,2,1,0:T(8,128)(2,1)S(1)} %collective-permute-done.23.refs_3_, ...), custom_call_target="tpu_custom_call" | custom-call | flops 3221225 | bytes 7340 | tf_op jit(solution)/shard_map/cross_transform/pallas_call | solution.py:489
  162.0 6.2 %collective-permute-done.28.refs_4_ = bf16[2,12,48,1024]{3,2,1,0:T(8,128)(2,1)S(1)} collective-permute-done((bf16[2,12,48,1024]{3,2,1,0:T(8,128)(2,1)S(1)}, bf16[2,12,48,1024]{3,2,1,0:T(8,128)(2,1)S(1)}, u32[]{:S(2)}, u32[]{:S(2)}) %collective-permute-start.28) | collective-permute-done | bytes 2359328 | tf_op jit(solution)/shard_map/ppermute | solution.py:525
  168.2 1.0 collective-permute-start.29
  169.2 10.2 %collective-permute-done.30.refs_5_ = bf16[2,4,32,1024]{3,2,1,0:T(8,128)(2,1)S(1)} collective-permute-done((bf16[2,4,32,1024]{3,2,1,0:T(8,128)(2,1)S(1)}, bf16[2,4,32,1024]{3,2,1,0:T(8,128)(2,1)S(1)}, u32[]{:S(2)}, u32[]{:S(2)}) %collective-permute-start.30) | collective-permute-done | bytes 524320 | tf_op jit(solution)/shard_map/ppermute | solution.py:525
  179.5 3.9 %last_heights.2.refs_6_ = bf16[2,16,96,1024]{3,2,1,0:T(8,128)(2,1)} custom-call(s32[3]{0:T(128)S(1)} %copy-done.15, bf16[2,2,256,512]{3,2,1,0:T(8,128)(2,1)S(1)} %copy-done.10, bf16[2,12,48,1024]{3,2,1,0:T(8,128)(2,1)S(1)} %cross_transform.4.refs_10_.refs_2_, ...), custom_call_target="tpu_custom_call", output_to_operand_aliasing={{}: (6, {})} | custom-call | flops 1073741 | bytes 6291 | tf_op jit(solution)/shard_map/last_heights/pallas_call | solution.py:416
  183.3 2.5 %last_heights.3.refs_7_ = bf16[2,16,96,1024]{3,2,1,0:T(8,128)(2,1)} custom-call(s32[3]{0:T(128)S(1)} %copy-done.15, bf16[2,2,256,512]{3,2,1,0:T(8,128)(2,1)S(1)} %copy-done.10, bf16[2,12,48,1024]{3,2,1,0:T(8,128)(2,1)S(1)} %cross_transform.4.refs_10_.refs_2_, ...), custom_call_target="tpu_custom_call", output_to_operand_aliasing={{}: (6, {})} | custom-call | flops 536870 | bytes 3145 | tf_op jit(solution)/shard_map/last_heights/pallas_call | solution.py:416
  185.8 5.6 %cross_transform.7 = bf16[2,16,96,1024]{3,2,1,0:T(8,128)(2,1)} custom-call(s32[3]{0:T(128)S(1)} %copy-done.15, bf16[2,8,48,256]{3,2,1,0:T(8,128)(2,1)S(1)} %get-tuple-element.156.refs_7_.refs_1_, bf16[2,8,48,256]{3,2,1,0:T(8,128)(2,1)S(1)} %collective-permute-done.25.refs_2_, ...), custom_call_target="tpu_custom_call", output_to_operand_aliasing={{}: (7, {})} | custom-call | flops 3221225 | bytes 7340 | tf_op jit(solution)/shard_map/cross_transform/pallas_call | solution.py:489
  (72 shorter events, 4.2 us)
Async XLA Ops:
  1.1 12.9 %collective-permute-start = (bf16[2,16,8,384]{3,2,1,0:T(8,128)(2,1)S(1)}, bf16[2,16,8,384]{3,2,1,0:T(8,128)(2,1)S(1)}, u32[]{:S(2)}, u32[]{:S(2)}) collective-permute-start(bf16[2,16,8,384]{3,2,1,0:T(8,128)(2,1)S(1)} %get-tuple-element.170), channel_id=1, source_target_pairs={{0,4},{4,8},{8,12},{1,5},{5,9},{9,13},{2,6},{6,10},{10,14},{3,7},{... | collective-permute-start | bytes 589832 | tf_op jit(solution)/shard_map/ppermute | solution.py:536
  6.0 8.3 %collective-permute-start.1 = (bf16[2,16,8,384]{3,2,1,0:T(8,128)(2,1)S(1)}, bf16[2,16,8,384]{3,2,1,0:T(8,128)(2,1)S(1)}, u32[]{:S(2)}, u32[]{:S(2)}) collective-permute-start(bf16[2,16,8,384]{3,2,1,0:T(8,128)(2,1)S(1)} %get-tuple-element.169), channel_id=1, source_target_pairs={{4,0},{8,4},{12,8},{5,1},{9,5},{13,9},{6,2},{10,6},{14,10},{7,3},{... | collective-permute-start | bytes 589832 | tf_op jit(solution)/shard_map/ppermute | solution.py:537
  17.4 7.4 %collective-permute-start.2 = (bf16[2,4,256,384]{3,2,1,0:T(8,128)(2,1)}, bf16[2,4,256,384]{3,2,1,0:T(8,128)(2,1)}, u32[]{:S(2)}, u32[]{:S(2)}) collective-permute-start(bf16[2,4,256,384]{3,2,1,0:T(8,128)(2,1)} %interpolate_edges.1.refs_5_.refs_1_), channel_id=1, source_target_pairs={{0,1},{1,0},{2,3},{3,2},{4,5},{5,4},{6,7},{7,6},{8,9},{9,8},{10,11... | collective-permute-start | bytes 4718600 | tf_op jit(solution)/shard_map/ppermute | solution.py:525
  24.8 6.7 %copy-start.5 = (bf16[2,4,256,384]{3,2,1,0:T(8,128)(2,1)S(1)}, bf16[2,4,256,384]{3,2,1,0:T(8,128)(2,1)}, u32[]{:S(2)}) copy-start(bf16[2,4,256,384]{3,2,1,0:T(8,128)(2,1)} %interpolate.5.refs_7_.refs_1_) | copy-start | bytes 4718596
  24.8 13.8 %copy-start = (bf16[2,4,96,1536]{3,2,1,0:T(8,128)(2,1)S(1)}, bf16[2,4,96,1536]{3,2,1,0:T(8,128)(2,1)}, u32[]{:S(2)}) copy-start(bf16[2,4,96,1536]{3,2,1,0:T(8,128)(2,1)} %constant.23.clone.refs_3_.refs_4_.refs_5_.refs_6_) | copy-start | bytes 7077892
  24.8 13.8 %copy-start.15 = (s32[3]{0:T(128)S(1)}, s32[3]{0:T(128)}, u32[]{:S(2)}) copy-start(s32[3]{0:T(128)} %pad_add_fusion.refs_0_) | copy-start | bytes 40
  31.5 11.0 %copy-start.2 = (bf16[8,256,384]{2,1,0:T(8,128)(2,1)S(1)}, bf16[8,256,384]{2,1,0:T(8,128)(2,1)}, u32[]{:S(2)}) copy-start(bf16[8,256,384]{2,1,0:T(8,128)(2,1)} %refs_3_.11) | copy-start | bytes 4718596
  31.5 11.0 %copy-start.6 = (s32[256,384]{1,0:T(8,128)S(1)}, s32[256,384]{1,0:T(8,128)}, u32[]{:S(2)}) copy-start(s32[256,384]{1,0:T(8,128)} %refs_1_.11) | copy-start | bytes 1179652
  31.5 11.0 %copy-start.7 = (s32[256,384]{1,0:T(8,128)S(1)}, s32[256,384]{1,0:T(8,128)}, u32[]{:S(2)}) copy-start(s32[256,384]{1,0:T(8,128)} %refs_2_.7) | copy-start | bytes 1179652
  31.5 11.0 %copy-start.9 = (bf16[2,16,16,384]{3,2,1,0:T(8,128)(2,1)S(1)}, bf16[2,16,16,384]{3,2,1,0:T(8,128)(2,1)}, u32[]{:S(2)}) copy-start(bf16[2,16,16,384]{3,2,1,0:T(8,128)(2,1)} %copy-done.8) | copy-start | bytes 1179652
  31.5 7.0 %collective-permute-start.3 = (bf16[2,4,256,384]{3,2,1,0:T(8,128)(2,1)S(1)}, bf16[2,4,256,384]{3,2,1,0:T(8,128)(2,1)S(1)}, u32[]{:S(2)}, u32[]{:S(2)}) collective-permute-start(bf16[2,4,256,384]{3,2,1,0:T(8,128)(2,1)S(1)} %copy-done.5), channel_id=1, source_target_pairs={{0,1},{1,0},{2,3},{3,2},{4,5},{5,4},{6,7},{7,6},{8,9},{9,8},{10,11... | collective-permute-start | bytes 4718600 | tf_op jit(solution)/shard_map/ppermute | solution.py:525
  32.1 22.8 %collective-permute-start.7 = (bf16[2,4,4,48,256]{4,3,2,1,0:T(8,128)(2,1)}, bf16[2,4,4,48,256]{4,3,2,1,0:T(8,128)(2,1)S(1)}, u32[]{:S(2)}, u32[]{:S(2)}) collective-permute-start(bf16[2,4,4,48,256]{4,3,2,1,0:T(8,128)(2,1)} %get-tuple-element.92.refs_2_), channel_id=1, source_target_pairs={{0,2},{2,0},{1,3},{3,1},{4,6},{6,4},{5,7},{7,5},{8,10},{10,8},{9,1... | collective-permute-start | bytes 2359304 | tf_op jit(solution)/shard_map/ppermute | solution.py:525
  33.6 17.2 %collective-permute-start.4 = (bf16[2,4,48,256]{3,2,1,0:T(8,128)(2,1)}, bf16[2,4,48,256]{3,2,1,0:T(8,128)(2,1)S(1)}, u32[]{:S(2)}, u32[]{:S(2)}) collective-permute-start(bf16[2,4,48,256]{3,2,1,0:T(8,128)(2,1)} %get-tuple-element.99), channel_id=1, source_target_pairs={{0,12},{4,8},{8,4},{12,0},{1,13},{5,9},{9,5},{13,1},{2,14},{6,10},... | collective-permute-start | bytes 589832 | tf_op jit(solution)/shard_map/ppermute | solution.py:525
  38.0 16.9 %collective-permute-start.5 = (bf16[2,4,48,256]{3,2,1,0:T(8,128)(2,1)}, bf16[2,4,48,256]{3,2,1,0:T(8,128)(2,1)S(1)}, u32[]{:S(2)}, u32[]{:S(2)}) collective-permute-start(bf16[2,4,48,256]{3,2,1,0:T(8,128)(2,1)} %get-tuple-element.100), channel_id=1, source_target_pairs={{0,8},{4,12},{8,0},{12,4},{1,9},{5,13},{9,1},{13,5},{2,10},{6,14},... | collective-permute-start | bytes 589832 | tf_op jit(solution)/shard_map/ppermute | solution.py:525
  38.0 16.9 %collective-permute-start.6 = (bf16[2,4,48,256]{3,2,1,0:T(8,128)(2,1)}, bf16[2,4,48,256]{3,2,1,0:T(8,128)(2,1)S(1)}, u32[]{:S(2)}, u32[]{:S(2)}) collective-permute-start(bf16[2,4,48,256]{3,2,1,0:T(8,128)(2,1)} %get-tuple-element.101), channel_id=1, source_target_pairs={{0,4},{4,0},{8,12},{12,8},{1,5},{5,1},{9,13},{13,9},{2,6},{6,2},{1... | collective-permute-start | bytes 589832 | tf_op jit(solution)/shard_map/ppermute | solution.py:525
  42.5 2.8 %copy-start.1 = (bf16[2,16,256,384]{3,2,1,0:T(8,128)(2,1)S(1)}, bf16[2,16,256,384]{3,2,1,0:T(8,128)(2,1)}, u32[]{:S(2)}) copy-start(bf16[2,16,256,384]{3,2,1,0:T(8,128)(2,1)} %refs_0_.7) | copy-start | bytes 18874372
  45.3 18.5 %slice-start = ((s8[6291456]{0:T(1024)(128)(4,1)}), s8[4194304]{0:T(1024)(128)(4,1)S(1)}, s32[]{:S(2)}) async-start(s8[6291456]{0:T(1024)(128)(4,1)} %bitcast.3), calls=%async_computation | async-start | bytes 8388608
  54.9 8.9 %slice-start.1 = ((s8[6291456]{0:T(1024)(128)(4,1)}), s8[2097152]{0:T(1024)(128)(4,1)S(1)}, s32[]{:S(2)}) async-start(s8[6291456]{0:T(1024)(128)(4,1)} %bitcast.3), calls=%async_computation.1 | async-start | bytes 4194304
  54.9 5.1 %collective-permute-start.8 = (bf16[2,4,256,384]{3,2,1,0:T(8,128)(2,1)S(1)}, bf16[2,4,256,384]{3,2,1,0:T(8,128)(2,1)S(1)}, u32[]{:S(2)}, u32[]{:S(2)}) collective-permute-start(bf16[2,4,256,384]{3,2,1,0:T(8,128)(2,1)S(1)} %interpolate.6.refs_1_.refs_7_), channel_id=1, source_target_pairs={{0,1},{1,0},{2,3},{3,2},{4,5},{5,4},{6,7},{7,6},{8,9},{9,8},{10,11... | collective-permute-start | bytes 4718600 | tf_op jit(solution)/shard_map/ppermute | solution.py:525
  55.0 20.0 %collective-permute-start.12 = (bf16[2,4,4,48,256]{4,3,2,1,0:T(8,128)(2,1)S(1)}, bf16[2,4,4,48,256]{4,3,2,1,0:T(8,128)(2,1)S(1)}, u32[]{:S(2)}, u32[]{:S(2)}) collective-permute-start(bf16[2,4,4,48,256]{4,3,2,1,0:T(8,128)(2,1)S(1)} %get-tuple-element.102.refs_5_.refs_3_), channel_id=1, source_target_pairs={{0,2},{2,0},{1,3},{3,1},{4,6},{6,4},{5,7},{7,5},{8,10},{10,8},{9,1... | collective-permute-start | bytes 2359304 | tf_op jit(solution)/shard_map/ppermute | solution.py:525
  55.6 13.8 %collective-permute-start.9 = (bf16[2,4,48,256]{3,2,1,0:T(8,128)(2,1)S(1)}, bf16[2,4,48,256]{3,2,1,0:T(8,128)(2,1)S(1)}, u32[]{:S(2)}, u32[]{:S(2)}) collective-permute-start(bf16[2,4,48,256]{3,2,1,0:T(8,128)(2,1)S(1)} %get-tuple-element.109), channel_id=1, source_target_pairs={{0,12},{4,8},{8,4},{12,0},{1,13},{5,9},{9,5},{13,1},{2,14},{6,10},... | collective-permute-start | bytes 589832 | tf_op jit(solution)/shard_map/ppermute | solution.py:525
  58.0 16.8 %collective-permute-start.10 = (bf16[2,4,48,256]{3,2,1,0:T(8,128)(2,1)S(1)}, bf16[2,4,48,256]{3,2,1,0:T(8,128)(2,1)S(1)}, u32[]{:S(2)}, u32[]{:S(2)}) collective-permute-start(bf16[2,4,48,256]{3,2,1,0:T(8,128)(2,1)S(1)} %get-tuple-element.110), channel_id=1, source_target_pairs={{0,8},{4,12},{8,0},{12,4},{1,9},{5,13},{9,1},{13,5},{2,10},{6,14},... | collective-permute-start | bytes 589832 | tf_op jit(solution)/shard_map/ppermute | solution.py:525
  58.0 16.8 %collective-permute-start.11 = (bf16[2,4,48,256]{3,2,1,0:T(8,128)(2,1)S(1)}, bf16[2,4,48,256]{3,2,1,0:T(8,128)(2,1)S(1)}, u32[]{:S(2)}, u32[]{:S(2)}) collective-permute-start(bf16[2,4,48,256]{3,2,1,0:T(8,128)(2,1)S(1)} %get-tuple-element.111), channel_id=1, source_target_pairs={{0,4},{4,0},{8,12},{12,8},{1,5},{5,1},{9,13},{13,9},{2,6},{6,2},{1... | collective-permute-start | bytes 589832 | tf_op jit(solution)/shard_map/ppermute | solution.py:525
  74.9 25.4 %copy-start.3 = (bf16[1024,1024]{1,0:T(8,128)(2,1)S(1)}, bf16[1024,1024]{1,0:T(8,128)(2,1)}, u32[]{:S(2)}) copy-start(bf16[1024,1024]{1,0:T(8,128)(2,1)} %constant.25.clone.refs_14_.refs_6_) | copy-start | bytes 6291460
  74.9 25.4 %copy-start.4 = (bf16[1024,1024]{1,0:T(8,128)(2,1)S(1)}, bf16[1024,1024]{1,0:T(8,128)(2,1)}, u32[]{:S(2)}) copy-start(bf16[1024,1024]{1,0:T(8,128)(2,1)} %constant.24.clone.refs_13_.refs_5_) | copy-start | bytes 6291460
  74.9 25.4 %copy-start.14 = (bf16[2,4,48,256]{3,2,1,0:T(8,128)(2,1)S(1)}, bf16[2,4,48,256]{3,2,1,0:T(8,128)(2,1)}, u32[]{:S(2)}) copy-start(bf16[2,4,48,256]{3,2,1,0:T(8,128)(2,1)} %get-tuple-element.126.refs_1_) | copy-start | bytes 589828
  74.9 5.5 %collective-permute-start.13 = (bf16[2,4,256,384]{3,2,1,0:T(8,128)(2,1)S(1)}, bf16[2,4,256,384]{3,2,1,0:T(8,128)(2,1)S(1)}, u32[]{:S(2)}, u32[]{:S(2)}) collective-permute-start(bf16[2,4,256,384]{3,2,1,0:T(8,128)(2,1)S(1)} %interpolate.7.refs_1_.refs_7_), channel_id=1, source_target_pairs={{0,1},{1,0},{2,3},{3,2},{4,5},{5,4},{6,7},{7,6},{8,9},{9,8},{10,11... | collective-permute-start | bytes 4718600 | tf_op jit(solution)/shard_map/ppermute | solution.py:525
  75.0 20.0 %collective-permute-start.17 = (bf16[2,4,4,48,256]{4,3,2,1,0:T(8,128)(2,1)S(1)}, bf16[2,4,4,48,256]{4,3,2,1,0:T(8,128)(2,1)S(1)}, u32[]{:S(2)}, u32[]{:S(2)}) collective-permute-start(bf16[2,4,4,48,256]{4,3,2,1,0:T(8,128)(2,1)S(1)} %get-tuple-element.112.refs_5_.refs_4_), channel_id=1, source_target_pairs={{0,2},{2,0},{1,3},{3,1},{4,6},{6,4},{5,7},{7,5},{8,10},{10,8},{9,1... | collective-permute-start | bytes 2359304 | tf_op jit(solution)/shard_map/ppermute | solution.py:525
  76.0 9.7 %collective-permute-start.14 = (bf16[2,4,48,256]{3,2,1,0:T(8,128)(2,1)S(1)}, bf16[2,4,48,256]{3,2,1,0:T(8,128)(2,1)S(1)}, u32[]{:S(2)}, u32[]{:S(2)}) collective-permute-start(bf16[2,4,48,256]{3,2,1,0:T(8,128)(2,1)S(1)} %get-tuple-element.119), channel_id=1, source_target_pairs={{0,12},{4,8},{8,4},{12,0},{1,13},{5,9},{9,5},{13,1},{2,14},{6,10},... | collective-permute-start | bytes 589832 | tf_op jit(solution)/shard_map/ppermute | solution.py:525
  78.0 16.8 %collective-permute-start.15 = (bf16[2,4,48,256]{3,2,1,0:T(8,128)(2,1)S(1)}, bf16[2,4,48,256]{3,2,1,0:T(8,128)(2,1)S(1)}, u32[]{:S(2)}, u32[]{:S(2)}) collective-permute-start(bf16[2,4,48,256]{3,2,1,0:T(8,128)(2,1)S(1)} %get-tuple-element.120), channel_id=1, source_target_pairs={{0,8},{4,12},{8,0},{12,4},{1,9},{5,13},{9,1},{13,5},{2,10},{6,14},... | collective-permute-start | bytes 589832 | tf_op jit(solution)/shard_map/ppermute | solution.py:525
  78.0 16.8 %collective-permute-start.16 = (bf16[2,4,48,256]{3,2,1,0:T(8,128)(2,1)S(1)}, bf16[2,4,48,256]{3,2,1,0:T(8,128)(2,1)S(1)}, u32[]{:S(2)}, u32[]{:S(2)}) collective-permute-start(bf16[2,4,48,256]{3,2,1,0:T(8,128)(2,1)S(1)} %get-tuple-element.121), channel_id=1, source_target_pairs={{0,4},{4,0},{8,12},{12,8},{1,5},{5,1},{9,13},{13,9},{2,6},{6,2},{1... | collective-permute-start | bytes 589832 | tf_op jit(solution)/shard_map/ppermute | solution.py:525
  94.9 20.1 %copy-start.11 = (bf16[2,4,4,48,256]{4,3,2,1,0:T(8,128)(2,1)S(1)}, bf16[2,4,4,48,256]{4,3,2,1,0:T(8,128)(2,1)}, u32[]{:S(2)}) copy-start(bf16[2,4,4,48,256]{4,3,2,1,0:T(8,128)(2,1)} %get-tuple-element.92.refs_2_) | copy-start | bytes 2359300
  94.9 20.1 %copy-start.13 = (bf16[2,2,128,512]{3,2,1,0:T(8,128)(2,1)S(1)}, bf16[2,2,128,512]{3,2,1,0:T(8,128)(2,1)}, u32[]{:S(2)}) copy-start(bf16[2,2,128,512]{3,2,1,0:T(8,128)(2,1)} %constant.27.clone.refs_1_) | copy-start | bytes 1572868
  94.9 19.1 %collective-permute-start.21 = (bf16[2,4,4,48,256]{4,3,2,1,0:T(8,128)(2,1)S(1)}, bf16[2,4,4,48,256]{4,3,2,1,0:T(8,128)(2,1)S(1)}, u32[]{:S(2)}, u32[]{:S(2)}) collective-permute-start(bf16[2,4,4,48,256]{4,3,2,1,0:T(8,128)(2,1)S(1)} %get-tuple-element.122.refs_15_.refs_5_), channel_id=1, source_target_pairs={{0,2},{2,0},{1,3},{3,1},{4,6},{6,4},{5,7},{7,5},{8,10},{10,8},{9,1... | collective-permute-start | bytes 2359304 | tf_op jit(solution)/shard_map/ppermute | solution.py:525
  95.9 11.0 %collective-permute-start.18 = (bf16[2,4,48,256]{3,2,1,0:T(8,128)(2,1)S(1)}, bf16[2,4,48,256]{3,2,1,0:T(8,128)(2,1)S(1)}, u32[]{:S(2)}, u32[]{:S(2)}) collective-permute-start(bf16[2,4,48,256]{3,2,1,0:T(8,128)(2,1)S(1)} %get-tuple-element.138), channel_id=1, source_target_pairs={{0,12},{4,8},{8,4},{12,0},{1,13},{5,9},{9,5},{13,1},{2,14},{6,10},... | collective-permute-start | bytes 589832 | tf_op jit(solution)/shard_map/ppermute | solution.py:525
  97.9 16.0 %collective-permute-start.19 = (bf16[2,4,48,256]{3,2,1,0:T(8,128)(2,1)S(1)}, bf16[2,4,48,256]{3,2,1,0:T(8,128)(2,1)S(1)}, u32[]{:S(2)}, u32[]{:S(2)}) collective-permute-start(bf16[2,4,48,256]{3,2,1,0:T(8,128)(2,1)S(1)} %get-tuple-element.139), channel_id=1, source_target_pairs={{0,8},{4,12},{8,0},{12,4},{1,9},{5,13},{9,1},{13,5},{2,10},{6,14},... | collective-permute-start | bytes 589832 | tf_op jit(solution)/shard_map/ppermute | solution.py:525
  97.9 16.0 %collective-permute-start.20 = (bf16[2,4,48,256]{3,2,1,0:T(8,128)(2,1)S(1)}, bf16[2,4,48,256]{3,2,1,0:T(8,128)(2,1)S(1)}, u32[]{:S(2)}, u32[]{:S(2)}) collective-permute-start(bf16[2,4,48,256]{3,2,1,0:T(8,128)(2,1)S(1)} %get-tuple-element.140), channel_id=1, source_target_pairs={{0,4},{4,0},{8,12},{12,8},{1,5},{5,1},{9,13},{13,9},{2,6},{6,2},{1... | collective-permute-start | bytes 589832 | tf_op jit(solution)/shard_map/ppermute | solution.py:525
  106.9 15.2 %copy-start.12 = (bf16[2,2,128,512]{3,2,1,0:T(8,128)(2,1)S(1)}, bf16[2,2,128,512]{3,2,1,0:T(8,128)(2,1)}, u32[]{:S(2)}) copy-start(bf16[2,2,128,512]{3,2,1,0:T(8,128)(2,1)} %constant.28.clone.refs_1_) | copy-start | bytes 1572868
  114.0 54.2 %collective-permute-start.28 = (bf16[2,12,48,1024]{3,2,1,0:T(8,128)(2,1)S(1)}, bf16[2,12,48,1024]{3,2,1,0:T(8,128)(2,1)S(1)}, u32[]{:S(2)}, u32[]{:S(2)}) collective-permute-start(bf16[2,12,48,1024]{3,2,1,0:T(8,128)(2,1)S(1)} %cross_transform.4.refs_10_.refs_2_), channel_id=1, source_target_pairs={{0,2},{2,0},{1,3},{3,1},{4,6},{6,4},{5,7},{7,5},{8,10},{10,8},{9,1... | collective-permute-start | bytes 7077896 | tf_op jit(solution)/shard_map/ppermute | solution.py:525
  117.7 16.6 %collective-permute-start.24 = (bf16[2,8,48,256]{3,2,1,0:T(8,128)(2,1)S(1)}, bf16[2,8,48,256]{3,2,1,0:T(8,128)(2,1)S(1)}, u32[]{:S(2)}, u32[]{:S(2)}) collective-permute-start(bf16[2,8,48,256]{3,2,1,0:T(8,128)(2,1)S(1)} %get-tuple-element.144), channel_id=1, source_target_pairs={{0,4},{4,0},{8,12},{12,8},{1,5},{5,1},{9,13},{13,9},{2,6},{6,2},{1... | collective-permute-start | bytes 1179656 | tf_op jit(solution)/shard_map/ppermute | solution.py:525
  117.7 29.9 %collective-permute-start.23 = (bf16[2,8,48,256]{3,2,1,0:T(8,128)(2,1)S(1)}, bf16[2,8,48,256]{3,2,1,0:T(8,128)(2,1)S(1)}, u32[]{:S(2)}, u32[]{:S(2)}) collective-permute-start(bf16[2,8,48,256]{3,2,1,0:T(8,128)(2,1)S(1)} %get-tuple-element.145), channel_id=1, source_target_pairs={{0,8},{4,12},{8,0},{12,4},{1,9},{5,13},{9,1},{13,5},{2,10},{6,14},... | collective-permute-start | bytes 1179656 | tf_op jit(solution)/shard_map/ppermute | solution.py:525
  120.3 27.3 %collective-permute-start.22 = (bf16[2,8,48,256]{3,2,1,0:T(8,128)(2,1)S(1)}, bf16[2,8,48,256]{3,2,1,0:T(8,128)(2,1)S(1)}, u32[]{:S(2)}, u32[]{:S(2)}) collective-permute-start(bf16[2,8,48,256]{3,2,1,0:T(8,128)(2,1)S(1)} %get-tuple-element.146), channel_id=1, source_target_pairs={{0,12},{4,8},{8,4},{12,0},{1,13},{5,9},{9,5},{13,1},{2,14},{6,10},... | collective-permute-start | bytes 1179656 | tf_op jit(solution)/shard_map/ppermute | solution.py:525
  127.9 51.5 %collective-permute-start.30 = (bf16[2,4,32,1024]{3,2,1,0:T(8,128)(2,1)S(1)}, bf16[2,4,32,1024]{3,2,1,0:T(8,128)(2,1)S(1)}, u32[]{:S(2)}, u32[]{:S(2)}) collective-permute-start(bf16[2,4,32,1024]{3,2,1,0:T(8,128)(2,1)S(1)} %get-tuple-element.164.refs_7_.refs_3_), channel_id=1, source_target_pairs={{0,2},{2,0},{1,3},{3,1},{4,6},{6,4},{5,7},{7,5},{8,10},{10,8},{9,1... | collective-permute-start | bytes 1572872 | tf_op jit(solution)/shard_map/ppermute | solution.py:525
  147.6 31.8 %copy-start.10 = (bf16[2,2,256,512]{3,2,1,0:T(8,128)(2,1)S(1)}, bf16[2,2,256,512]{3,2,1,0:T(8,128)(2,1)}, u32[]{:S(2)}) copy-start(bf16[2,2,256,512]{3,2,1,0:T(8,128)(2,1)} %constant.26.clone.refs_1_) | copy-start | bytes 3145732
  147.6 38.2 %collective-permute-start.25 = (bf16[2,8,48,256]{3,2,1,0:T(8,128)(2,1)S(1)}, bf16[2,8,48,256]{3,2,1,0:T(8,128)(2,1)S(1)}, u32[]{:S(2)}, u32[]{:S(2)}) collective-permute-start(bf16[2,8,48,256]{3,2,1,0:T(8,128)(2,1)S(1)} %get-tuple-element.157), channel_id=1, source_target_pairs={{0,4},{4,0},{8,12},{12,8},{1,5},{5,1},{9,13},{13,9},{2,6},{6,2},{1... | collective-permute-start | bytes 1179656 | tf_op jit(solution)/shard_map/ppermute | solution.py:525
  154.1 31.7 %collective-permute-start.26 = (bf16[2,8,48,256]{3,2,1,0:T(8,128)(2,1)S(1)}, bf16[2,8,48,256]{3,2,1,0:T(8,128)(2,1)S(1)}, u32[]{:S(2)}, u32[]{:S(2)}) collective-permute-start(bf16[2,8,48,256]{3,2,1,0:T(8,128)(2,1)S(1)} %get-tuple-element.158), channel_id=1, source_target_pairs={{0,8},{4,12},{8,0},{12,4},{1,9},{5,13},{9,1},{13,5},{2,10},{6,14},... | collective-permute-start | bytes 1179656 | tf_op jit(solution)/shard_map/ppermute | solution.py:525
  155.0 30.8 %collective-permute-start.27 = (bf16[2,8,48,256]{3,2,1,0:T(8,128)(2,1)S(1)}, bf16[2,8,48,256]{3,2,1,0:T(8,128)(2,1)S(1)}, u32[]{:S(2)}, u32[]{:S(2)}) collective-permute-start(bf16[2,8,48,256]{3,2,1,0:T(8,128)(2,1)S(1)} %get-tuple-element.159), channel_id=1, source_target_pairs={{0,12},{4,8},{8,4},{12,0},{1,13},{5,9},{9,5},{13,1},{2,14},{6,10},... | collective-permute-start | bytes 1179656 | tf_op jit(solution)/shard_map/ppermute | solution.py:525
  168.2 15.1 %collective-permute-start.29 = (bf16[2,4,16,1024]{3,2,1,0:T(8,128)(2,1)S(1)}, bf16[2,4,16,1024]{3,2,1,0:T(8,128)(2,1)S(1)}, u32[]{:S(2)}, u32[]{:S(2)}) collective-permute-start(bf16[2,4,16,1024]{3,2,1,0:T(8,128)(2,1)S(1)} %get-tuple-element.166.refs_3_), channel_id=1, source_target_pairs={{0,2},{2,0},{1,3},{3,1},{4,6},{6,4},{5,7},{7,5},{8,10},{10,8},{9,1... | collective-permute-start | bytes 786440 | tf_op jit(solution)/shard_map/ppermute | solution.py:525
  (1 other events, 0.8 us)

commit v7 on v6

--- a/solution.py
+++ b/solution.py
@@ -264,41 +264,49 @@
 
 def range_kernel(ids_ref, own_ref, other_ref, *refs, blocks, earlier):
     tables = refs[:blocks]
-    first_ref, *rest = refs[blocks + earlier :]
+    first_ref, *rest = refs[blocks + earlier : -1]
+    mixed_ref = refs[-1]
     cuts, cols = own_ref.shape[1:3]
-    bins = tables[0].shape[2]
+    half = tables[0].shape[3]
     split = first_ref.shape[3]
     scale = 1.0 / math.sqrt(F)
-    table = jnp.concatenate([ref[0, 0] for ref in tables], axis=0)
+    evens, odds = (jnp.concatenate([ref[0, 0, p] for ref in tables], axis=0) for p in range(2))
     for cut in range(cuts):
-        real = [own_ref[0, cut], other_ref[0, cut]]
-        imag = [own_ref[1, cut], other_ref[1, cut]]
-        values = jnp.concatenate(
-            [
-                jnp.concatenate(real + [-v for v in imag], axis=1),
-                jnp.concatenate(imag + real, axis=1),
-            ],
-            axis=0,
-        )
-        product = lax.dot_general(
-            table, values, (((1,), (1,)), ((), ())), preferred_element_type=jnp.float32
-        )
-        product = (product * scale).astype(jnp.bfloat16)
+        for parity, table in ((0, evens), (1, odds)):
+            if parity == 0:
+                real, imag = (own_ref[part, cut] + other_ref[part, cut] for part in range(2))
+            else:
+                real, imag = (own_ref[part, cut] - other_ref[part, cut] for part in range(2))
+            values = jnp.concatenate(
+                [jnp.concatenate([real, -imag], axis=1), jnp.concatenate([imag, real], axis=1)],
+                axis=0,
+            )
+            product = scale * lax.dot_general(
+                table, values, (((1,), (1,)), ((), ())), preferred_element_type=jnp.float32
+            )
+            for s in range(blocks):
+                for tile in range(2 * cols // LANES):
+                    mixed_ref[s, tile, pl.ds(parity, half, stride=2), :] = product[
+                        s * half : (s + 1) * half, tile * LANES : (tile + 1) * LANES
+                    ]
         for s in range(blocks):
-            for part in range(2):
-                value = product[s * bins : (s + 1) * bins, part * cols : (part + 1) * cols]
-                first_ref[part, cut, s] = value[:split]
-                rest[s][part, cut] = value[split:]
+            for tile in range(2 * cols // LANES):
+                part, start = divmod(tile * LANES, cols)
+                lane = pl.ds(start, LANES)
+                value = mixed_ref[s, tile].astype(jnp.bfloat16)
+                first_ref[part, cut, s, :, lane] = value[:split]
+                rest[s][part, cut, :, lane] = value[split:]
 
 
 def range_transform(ids, own, other, table, split, earlier=(), limit=VMEM):
     _, count, cols, freqs = own.shape
-    _, blocks, bins, full = table.shape
+    _, blocks, _, half, full = table.shape
+    bins = 2 * half
     rest = bins - split
     group = 2
 
     def block_of(s):
-        return pl.BlockSpec((1, 1, bins, full), lambda i, ids: (ids[1], ids[0] ^ s, 0, 0))
+        return pl.BlockSpec((1, 1, 2, half, full), lambda i, ids: (ids[1], ids[0] ^ s, 0, 0, 0))
 
     return pl.pallas_call(
         lambda *refs: range_kernel(*refs, blocks=blocks, earlier=len(earlier)),
@@ -312,6 +320,7 @@
                 pl.BlockSpec((2, group, blocks, split, cols), lambda i, ids: (0, i, 0, 0, 0))
             ]
             + [pl.BlockSpec((2, group, rest, cols), lambda i, ids: (0, i, 0, 0))] * blocks,
+            scratch_shapes=[pltpu.VMEM((blocks, 2 * cols // LANES, bins, LANES), jnp.float32)],
         ),
         out_shape=[jax.ShapeDtypeStruct((2, count, blocks, split, cols), jnp.bfloat16)]
         + [jax.ShapeDtypeStruct((2, count, rest, cols), jnp.bfloat16)] * blocks,
@@ -550,11 +559,14 @@
     ids = jnp.stack([lax.axis_index("az"), lax.axis_index("fq"), lax.axis_index("el")])
     tables = []
     for core in range(fq_count):
-        order = np.concatenate([np.arange(freqs) + freqs * (core ^ s) for s in range(fq_count)])
         blocks = []
         for az in range(az_count):
-            ks = (az * fq_count + core) * bins + np.arange(bins)
-            blocks.append(np.concatenate(host_table(ks, order, F), axis=1))
+            pair = []
+            for parity in range(2):
+                ks = (az * fq_count + core) * bins + parity + 2 * np.arange(bins // 2)
+                sign = -1.0 if core and parity else 1.0
+                pair.append(sign * np.concatenate(host_table(ks, np.arange(freqs), F), axis=1))
+            blocks.append(np.stack(pair).astype(ml_dtypes.bfloat16))
         tables.append(np.stack(blocks))
     range_table = jnp.asarray(np.stack(tables))
     cross_tables = [jnp.asarray(t) for t in host_table(np.arange(A), np.arange(A), A)]
@@ -655,6 +667,7 @@
         and cuts == sum(count for _, count in CHUNKS) == sum(PARTS)
         and cols % (2 * LANES) == 0
         and freqs % LANES == 0
+        and 2 * freqs == F
         and bins > SPLIT
         and bins == 2 * SPLIT
         and A % 512 == 0

time: 192 us -> 191 us (level)
  transfers between devices with their start and end apart: 31 -> 31, of which waited for: 13 -> 12; matrix products, arithmetic and copies ran while one was open for 0% -> 0% of each run, Pallas kernels for 33% -> 33%
where the time goes in v7:
time: 191 us
  Pallas kernels  75.9 us (40%)
  waiting for transfers between devices  63.1 us (33%)
  starting transfers between devices  45.8 us (24%)
  local copies, waits for them, and re-layouts  4.74 us (2%)
    ppermute x29, waiting for transfers between devices, exchange(): lax.ppermute(value, axis, [(i, i ^ s) for i in range(lax.axis_size(axis))])  62.8 us
    ppermute x29, starting transfers between devices, exchange(): lax.ppermute(value, axis, [(i, i ^ s) for i in range(lax.axis_size(axis))])  39.6 us
    pallas_call x4, Pallas kernels, interpolate(): pl.pallas_call(lambda *refs: interp_kernel(*refs, bordered=len(border) ==...  24.3 us
    pallas_call x4, Pallas kernels, cross_transform(): pl.pallas_call(lambda *refs: cross_kernel(*refs, groups=groups, blocks=bl...  20.9 us
    pallas_call x4, Pallas kernels, range_transform(): pl.pallas_call(lambda *refs: range_kernel(*refs, blocks=blocks, earlier=l...  16.8 us
    pallas_call x2, Pallas kernels, last_heights(): pl.pallas_call(lambda *refs: height_kernel(*refs, chunks=chunks, sets=1,...  6.32 us
    pallas_call x2, Pallas kernels, first_heights(): pl.pallas_call(lambda *refs: height_kernel(*refs, chunks=chunks, sets=blo...  5.24 us
    ppermute x1, starting transfers between devices, halo_rows(): lax.ppermute(tail, 'az', [(i, i + 1) for i in range(ends)])  4.94 us
  transfers between devices with their start and end apart: 31, of which 12 were waited for; matrix products, arithmetic and copies ran while one was open for 0% of the time, Pallas kernels for 33%

profile of v7, /device:TPU:0, one launch (start us, length us, event | category | flops | bytes accessed | tf_op | source)
XLA Modules:
  0.0 190.6 jit_solution(18235369098368456398)
XLA Ops:
  0.0 1.1 fusion
  1.1 4.9 %collective-permute-start = (bf16[2,16,8,384]{3,2,1,0:T(8,128)(2,1)S(1)}, bf16[2,16,8,384]{3,2,1,0:T(8,128)(2,1)S(1)}, u32[]{:S(2)}, u32[]{:S(2)}) collective-permute-start(bf16[2,16,8,384]{3,2,1,0:T(8,128)(2,1)S(1)} %get-tuple-element.170), channel_id=1, source_target_pairs={{0,4},{4,8},{8,12},{1,5},{5,9},{9,13},{2,6},{6,10},{10,14},{3,7},{... | collective-permute-start | bytes 589832 | tf_op jit(solution)/shard_map/ppermute | solution.py:545
  6.0 1.3 collective-permute-start.1
  7.3 6.7 %interpolate.4.made_ref = bf16[2,4,256,384]{3,2,1,0:T(8,128)(2,1)} custom-call(bf16[2,16,256,384]{3,2,1,0:T(8,128)(2,1)} %refs_0_.7, s32[256,384]{1,0:T(8,128)} %refs_1_.11, s32[256,384]{1,0:T(8,128)} %refs_2_.7, bf16[8,256,384]{2,1,0:T(8,128)(2,1)} %refs_3_.11), custom_call_target="tpu_custom_call" | custom-call | flops 26738 | bytes 3145 | tf_op jit(solution)/shard_map/interpolate/pallas_call | solution.py:204
  15.1 2.3 %interpolate_edges.1.refs_5_.refs_1_ = bf16[2,4,256,384]{3,2,1,0:T(8,128)(2,1)} custom-call(bf16[2,16,256,384]{3,2,1,0:T(8,128)(2,1)} %refs_0_.7, bf16[2,16,16,384]{3,2,1,0:T(8,128)(2,1)} %copy-done.8, s32[256,384]{1,0:T(8,128)} %refs_1_.11, s32[256,384]{1,0:T(8,128)} %refs_2_.7, bf16[8,256,384]{2,1,0:T(8,128)(2,1)} %refs_3_.11, ...), custom_call_target="tpu_custom_call", output_to_operand_aliasing={{}: (5, {})} | custom-call | flops 3342 | bytes 393 | tf_op jit(solution)/shard_map/interpolate_edges/pallas_call | solution.py:244
  18.1 6.7 %interpolate.5.refs_7_.refs_1_ = bf16[2,4,256,384]{3,2,1,0:T(8,128)(2,1)} custom-call(bf16[2,16,256,384]{3,2,1,0:T(8,128)(2,1)} %refs_0_.7, s32[256,384]{1,0:T(8,128)} %refs_1_.11, s32[256,384]{1,0:T(8,128)} %refs_2_.7, bf16[8,256,384]{2,1,0:T(8,128)(2,1)} %refs_3_.11, bf16[2,16,16,384]{3,2,1,0:T(8,128)(2,1)} %copy-done.8, ...), custom_call_target="tpu_custom_call" | custom-call | flops 26738 | bytes 3145 | tf_op jit(solution)/shard_map/interpolate/pallas_call | solution.py:204
  24.8 6.0 %range_transform.4 = (bf16[2,4,4,48,256]{4,3,2,1,0:T(8,128)(2,1)}, bf16[2,4,48,256]{3,2,1,0:T(8,128)(2,1)}, bf16[2,4,48,256]{3,2,1,0:T(8,128)(2,1)}, bf16[2,4,48...) custom-call(s32[3]{0:T(128)} %pad_add_fusion.refs_0_, bf16[2,4,256,384]{3,2,1,0:T(8,128)(2,1)} %interpolate_edges.1.refs_5_.refs_1_, ...), custom_call_target="tpu_custom_call" | custom-call | flops 1207959 | bytes 4718 | tf_op jit(solution)/shard_map/range_transform/pallas_call | solution.py:311
  31.3 1.5 collective-permute-start.7
  32.8 4.4 %collective-permute-start.4 = (bf16[2,4,48,256]{3,2,1,0:T(8,128)(2,1)}, bf16[2,4,48,256]{3,2,1,0:T(8,128)(2,1)S(1)}, u32[]{:S(2)}, u32[]{:S(2)}) collective-permute-start(bf16[2,4,48,256]{3,2,1,0:T(8,128)(2,1)} %get-tuple-element.99), channel_id=1, source_target_pairs={{0,12},{4,8},{8,4},{12,0},{1,13},{5,9},{9,5},{13,1},{2,14},{6,10},... | collective-permute-start | bytes 589832 | tf_op jit(solution)/shard_map/ppermute | solution.py:534
  37.8 3.6 %range_transform.5 = (bf16[2,4,4,48,256]{4,3,2,1,0:T(8,128)(2,1)S(1)}, bf16[2,4,48,256]{3,2,1,0:T(8,128)(2,1)S(1)}, bf16[2,4,48,256]{3,2,1,0:T(8,128)(2,1)S(1)},...) custom-call(s32[3]{0:T(128)S(1)} %copy-done.15, bf16[2,4,256,384]{3,2,1,0:T(8,128)(2,1)S(1)} %copy-done.5, ...), custom_call_target="tpu_custom_call" | custom-call | flops 1207959 | bytes 4718 | tf_op jit(solution)/shard_map/range_transform/pallas_call | solution.py:311
  41.5 2.8 %copy-done.1 = bf16[2,16,256,384]{3,2,1,0:T(8,128)(2,1)S(1)} copy-done((bf16[2,16,256,384]{3,2,1,0:T(8,128)(2,1)S(1)}, bf16[2,16,256,384]{3,2,1,0:T(8,128)(2,1)}, u32[]{:S(2)}) %copy-start.1) | copy-done | bytes 6291480
  44.2 5.5 %interpolate.6.refs_1_.refs_7_ = bf16[2,4,256,384]{3,2,1,0:T(8,128)(2,1)S(1)} custom-call(bf16[2,16,256,384]{3,2,1,0:T(8,128)(2,1)S(1)} %copy-done.1, s32[256,384]{1,0:T(8,128)S(1)} %copy-done.6, s32[256,384]{1,0:T(8,128)S(1)} %copy-done.7, bf16[8,256,384]{2,1,0:T(8,128)(2,1)S(1)} %copy-done.2, bf16[2,16,16,384]{3,2,1,0:T(8,128)(2,1)S(1)} %copy-done.9, ...), custom_call_target="tpu_custom_call" | custom-call | flops 26738 | bytes 3145 | tf_op jit(solution)/shard_map/interpolate/pallas_call | solution.py:204
  49.7 4.4 %collective-permute-done.5.refs_3_ = bf16[2,4,48,256]{3,2,1,0:T(8,128)(2,1)S(1)} collective-permute-done((bf16[2,4,48,256]{3,2,1,0:T(8,128)(2,1)}, bf16[2,4,48,256]{3,2,1,0:T(8,128)(2,1)S(1)}, u32[]{:S(2)}, u32[]{:S(2)}) %collective-permute-start.5) | collective-permute-done | bytes 196640 | tf_op jit(solution)/shard_map/ppermute | solution.py:534
  54.7 2.6 %collective-permute-start.9 = (bf16[2,4,48,256]{3,2,1,0:T(8,128)(2,1)S(1)}, bf16[2,4,48,256]{3,2,1,0:T(8,128)(2,1)S(1)}, u32[]{:S(2)}, u32[]{:S(2)}) collective-permute-start(bf16[2,4,48,256]{3,2,1,0:T(8,128)(2,1)S(1)} %get-tuple-element.109), channel_id=1, source_target_pairs={{0,12},{4,8},{8,4},{12,0},{1,13},{5,9},{9,5},{13,1},{2,14},{6,10},... | collective-permute-start | bytes 589832 | tf_op jit(solution)/shard_map/ppermute | solution.py:534
  57.4 1.7 collective-permute-start.11
  59.1 3.6 %range_transform.6 = (bf16[2,4,4,48,256]{4,3,2,1,0:T(8,128)(2,1)S(1)}, bf16[2,4,48,256]{3,2,1,0:T(8,128)(2,1)S(1)}, bf16[2,4,48,256]{3,2,1,0:T(8,128)(2,1)S(1)},...) custom-call(s32[3]{0:T(128)S(1)} %copy-done.15, bf16[2,4,256,384]{3,2,1,0:T(8,128)(2,1)S(1)} %interpolate.6.refs_1_.refs_7_, ...), custom_call_target="tpu_custom_call" | custom-call | flops 1207959 | bytes 4718 | tf_op jit(solution)/shard_map/range_transform/pallas_call | solution.py:311
  62.8 5.5 %interpolate.7.refs_1_.refs_7_ = bf16[2,4,256,384]{3,2,1,0:T(8,128)(2,1)S(1)} custom-call(bf16[2,16,256,384]{3,2,1,0:T(8,128)(2,1)S(1)} %bitcast.4, s32[256,384]{1,0:T(8,128)S(1)} %copy-done.6, s32[256,384]{1,0:T(8,128)S(1)} %copy-done.7, bf16[8,256,384]{2,1,0:T(8,128)(2,1)S(1)} %copy-done.2, bf16[2,16,16,384]{3,2,1,0:T(8,128)(2,1)S(1)} %copy-done.9, ...), custom_call_target="tpu_custom_call" | custom-call | flops 26738 | bytes 3145 | tf_op jit(solution)/shard_map/interpolate/pallas_call | solution.py:204
  68.3 5.8 %collective-permute-done.10.refs_7_ = bf16[2,4,48,256]{3,2,1,0:T(8,128)(2,1)S(1)} collective-permute-done((bf16[2,4,48,256]{3,2,1,0:T(8,128)(2,1)S(1)}, bf16[2,4,48,256]{3,2,1,0:T(8,128)(2,1)S(1)}, u32[]{:S(2)}, u32[]{:S(2)}) %collective-permute-start.10) | collective-permute-done | bytes 196640 | tf_op jit(solution)/shard_map/ppermute | solution.py:534
  74.2 1.2 collective-permute-start.17
  75.4 2.1 %collective-permute-start.14 = (bf16[2,4,48,256]{3,2,1,0:T(8,128)(2,1)S(1)}, bf16[2,4,48,256]{3,2,1,0:T(8,128)(2,1)S(1)}, u32[]{:S(2)}, u32[]{:S(2)}) collective-permute-start(bf16[2,4,48,256]{3,2,1,0:T(8,128)(2,1)S(1)} %get-tuple-element.119), channel_id=1, source_target_pairs={{0,12},{4,8},{8,4},{12,0},{1,13},{5,9},{9,5},{13,1},{2,14},{6,10},... | collective-permute-start | bytes 589832 | tf_op jit(solution)/shard_map/ppermute | solution.py:534
  77.4 2.3 %collective-permute-start.16 = (bf16[2,4,48,256]{3,2,1,0:T(8,128)(2,1)S(1)}, bf16[2,4,48,256]{3,2,1,0:T(8,128)(2,1)S(1)}, u32[]{:S(2)}, u32[]{:S(2)}) collective-permute-start(bf16[2,4,48,256]{3,2,1,0:T(8,128)(2,1)S(1)} %get-tuple-element.121), channel_id=1, source_target_pairs={{0,4},{4,0},{8,12},{12,8},{1,5},{5,1},{9,13},{13,9},{2,6},{6,2},{1... | collective-permute-start | bytes 589832 | tf_op jit(solution)/shard_map/ppermute | solution.py:534
  79.8 3.6 %range_transform.7 = (bf16[2,4,4,48,256]{4,3,2,1,0:T(8,128)(2,1)S(1)}, bf16[2,4,48,256]{3,2,1,0:T(8,128)(2,1)S(1)}, bf16[2,4,48,256]{3,2,1,0:T(8,128)(2,1)S(1)},...) custom-call(s32[3]{0:T(128)S(1)} %copy-done.15, bf16[2,4,256,384]{3,2,1,0:T(8,128)(2,1)S(1)} %interpolate.7.refs_1_.refs_7_, ...), custom_call_target="tpu_custom_call" | custom-call | flops 1207959 | bytes 4718 | tf_op jit(solution)/shard_map/range_transform/pallas_call | solution.py:311
  83.4 1.7 collective-permute-done.14.refs_12_
  85.1 9.0 %collective-permute-done.15.refs_11_ = bf16[2,4,48,256]{3,2,1,0:T(8,128)(2,1)S(1)} collective-permute-done((bf16[2,4,48,256]{3,2,1,0:T(8,128)(2,1)S(1)}, bf16[2,4,48,256]{3,2,1,0:T(8,128)(2,1)S(1)}, u32[]{:S(2)}, u32[]{:S(2)}) %collective-permute-start.15) | collective-permute-done | bytes 196640 | tf_op jit(solution)/shard_map/ppermute | solution.py:534
  94.2 1.1 collective-permute-start.21
  95.3 2.0 %collective-permute-start.18 = (bf16[2,4,48,256]{3,2,1,0:T(8,128)(2,1)S(1)}, bf16[2,4,48,256]{3,2,1,0:T(8,128)(2,1)S(1)}, u32[]{:S(2)}, u32[]{:S(2)}) collective-permute-start(bf16[2,4,48,256]{3,2,1,0:T(8,128)(2,1)S(1)} %get-tuple-element.138), channel_id=1, source_target_pairs={{0,12},{4,8},{8,4},{12,0},{1,13},{5,9},{9,5},{13,1},{2,14},{6,10},... | collective-permute-start | bytes 589832 | tf_op jit(solution)/shard_map/ppermute | solution.py:534
  97.3 2.3 %collective-permute-start.20 = (bf16[2,4,48,256]{3,2,1,0:T(8,128)(2,1)S(1)}, bf16[2,4,48,256]{3,2,1,0:T(8,128)(2,1)S(1)}, u32[]{:S(2)}, u32[]{:S(2)}) collective-permute-start(bf16[2,4,48,256]{3,2,1,0:T(8,128)(2,1)S(1)} %get-tuple-element.140), channel_id=1, source_target_pairs={{0,4},{4,0},{8,12},{12,8},{1,5},{5,1},{9,13},{13,9},{2,6},{6,2},{1... | collective-permute-start | bytes 589832 | tf_op jit(solution)/shard_map/ppermute | solution.py:534
  99.7 6.6 %cross_transform.4.refs_10_.refs_2_ = bf16[2,12,48,1024]{3,2,1,0:T(8,128)(2,1)S(1)} custom-call(s32[3]{0:T(128)S(1)} %copy-done.15, bf16[2,4,48,256]{3,2,1,0:T(8,128)(2,1)S(1)} %copy-done.14, bf16[2,4,48,256]{3,2,1,0:T(8,128)(2,1)S(1)} %collective-permute-done.6.refs_2_, bf16[2,4,48,256]{3,2,1,0:T(8,128)(2,1)S(1)} %collective-permute-done.5.refs_3_, ...), custom_call_target="tpu_custom_call" | custom-call | flops 4831838 | bytes 8912 | tf_op jit(solution)/shard_map/cross_transform/pallas_call | solution.py:498
  106.3 6.8 %collective-permute-done.19.refs_3_ = bf16[2,4,48,256]{3,2,1,0:T(8,128)(2,1)S(1)} collective-permute-done((bf16[2,4,48,256]{3,2,1,0:T(8,128)(2,1)S(1)}, bf16[2,4,48,256]{3,2,1,0:T(8,128)(2,1)S(1)}, u32[]{:S(2)}, u32[]{:S(2)}) %collective-permute-start.19) | collective-permute-done | bytes 196640 | tf_op jit(solution)/shard_map/ppermute | solution.py:534
  113.3 1.1 collective-permute-start.28
  114.4 2.6 %first_heights.2 = (bf16[2,8,48,256]{3,2,1,0:T(8,128)(2,1)S(1)}, bf16[2,8,48,256]{3,2,1,0:T(8,128)(2,1)S(1)}, bf16[2,8,48,256]{3,2,1,0:T(8,128)(2,1)S(1)}, bf16[2,8,48,256]{3,2,1,0:T(8,128)(2,1)S(1)}) custom-call(s32[3]{0:T(128)S(1)} %copy-done.15, bf16[2,2,128,512]{3,2,1,0:T(8,128)(2,1)S(1)} %copy-done.13, bf16[2,4,4,48,256]{4,3,2,1,0:T(8,128)(2,1)S(1)} %copy-done.11, ...), custom_call_target="tpu_custom_call" | custom-call | flops 1610612 | bytes 9437 | tf_op jit(solution)/shard_map/first_heights/pallas_call | solution.py:390
  117.1 2.6 %collective-permute-start.23 = (bf16[2,8,48,256]{3,2,1,0:T(8,128)(2,1)S(1)}, bf16[2,8,48,256]{3,2,1,0:T(8,128)(2,1)S(1)}, u32[]{:S(2)}, u32[]{:S(2)}) collective-permute-start(bf16[2,8,48,256]{3,2,1,0:T(8,128)(2,1)S(1)} %get-tuple-element.145), channel_id=1, source_target_pairs={{0,8},{4,12},{8,0},{12,4},{1,9},{5,13},{9,1},{13,5},{2,10},{6,14},... | collective-permute-start | bytes 1179656 | tf_op jit(solution)/shard_map/ppermute | solution.py:534
  119.7 1.8 collective-permute-start.22
  121.5 2.6 %first_heights.3 = (bf16[2,8,48,256]{3,2,1,0:T(8,128)(2,1)S(1)}, bf16[2,8,48,256]{3,2,1,0:T(8,128)(2,1)S(1)}, bf16[2,8,48,256]{3,2,1,0:T(8,128)(2,1)S(1)}, bf16[2,8,48,256]{3,2,1,0:T(8,128)(2,1)S(1)}) custom-call(s32[3]{0:T(128)S(1)} %copy-done.15, bf16[2,2,128,512]{3,2,1,0:T(8,128)(2,1)S(1)} %copy-done.12, bf16[2,4,4,48,256]{4,3,2,1,0:T(8,128)(2,1)S(1)} %copy-done.11, ...), custom_call_target="tpu_custom_call" | custom-call | flops 1610612 | bytes 9437 | tf_op jit(solution)/shard_map/first_heights/pallas_call | solution.py:390
  124.1 3.2 %cross_transform.5 = (bf16[2,4,32,1024]{3,2,1,0:T(8,128)(2,1)S(1)}, bf16[2,4,16,1024]{3,2,1,0:T(8,128)(2,1)S(1)}) custom-call(s32[3]{0:T(128)S(1)} %copy-done.15, bf16[2,4,48,256]{3,2,1,0:T(8,128)(2,1)S(1)} %get-tuple-element.151.refs_1_, bf16[2,4,48,256]{3,2,1,0:T(8,128)(2,1)S(1)} %collective-permute-done.20.refs_2_, ...), custom_call_target="tpu_custom_call" | custom-call | flops 1610612 | bytes 5767 | tf_op jit(solution)/shard_map/cross_transform/pallas_call | solution.py:498
  127.3 1.0 collective-permute-start.30
  128.3 5.4 %collective-permute-done.24.refs_2_ = bf16[2,8,48,256]{3,2,1,0:T(8,128)(2,1)S(1)} collective-permute-done((bf16[2,8,48,256]{3,2,1,0:T(8,128)(2,1)S(1)}, bf16[2,8,48,256]{3,2,1,0:T(8,128)(2,1)S(1)}, u32[]{:S(2)}, u32[]{:S(2)}) %collective-permute-start.24) | collective-permute-done | bytes 393248 | tf_op jit(solution)/shard_map/ppermute | solution.py:534
  133.6 13.3 %collective-permute-done.23.refs_3_ = bf16[2,8,48,256]{3,2,1,0:T(8,128)(2,1)S(1)} collective-permute-done((bf16[2,8,48,256]{3,2,1,0:T(8,128)(2,1)S(1)}, bf16[2,8,48,256]{3,2,1,0:T(8,128)(2,1)S(1)}, u32[]{:S(2)}, u32[]{:S(2)}) %collective-permute-start.23) | collective-permute-done | bytes 393248 | tf_op jit(solution)/shard_map/ppermute | solution.py:534
  147.0 6.5 %collective-permute-start.25 = (bf16[2,8,48,256]{3,2,1,0:T(8,128)(2,1)S(1)}, bf16[2,8,48,256]{3,2,1,0:T(8,128)(2,1)S(1)}, u32[]{:S(2)}, u32[]{:S(2)}) collective-permute-start(bf16[2,8,48,256]{3,2,1,0:T(8,128)(2,1)S(1)} %get-tuple-element.157), channel_id=1, source_target_pairs={{0,4},{4,0},{8,12},{12,8},{1,5},{5,1},{9,13},{13,9},{2,6},{6,2},{1... | collective-permute-start | bytes 1179656 | tf_op jit(solution)/shard_map/ppermute | solution.py:534
  153.4 0.9 collective-permute-start.26
  154.3 1.5 collective-permute-start.27
  155.8 5.6 %cross_transform.6.refs_6_ = bf16[2,16,96,1024]{3,2,1,0:T(8,128)(2,1)} custom-call(s32[3]{0:T(128)S(1)} %copy-done.15, bf16[2,8,48,256]{3,2,1,0:T(8,128)(2,1)S(1)} %get-tuple-element.160.refs_10_.refs_1_, bf16[2,8,48,256]{3,2,1,0:T(8,128)(2,1)S(1)} %collective-permute-done.24.refs_2_, bf16[2,8,48,256]{3,2,1,0:T(8,128)(2,1)S(1)} %collective-permute-done.23.refs_3_, ...), custom_call_target="tpu_custom_call" | custom-call | flops 3221225 | bytes 7340 | tf_op jit(solution)/shard_map/cross_transform/pallas_call | solution.py:498
  161.4 6.1 %collective-permute-done.28.refs_4_ = bf16[2,12,48,1024]{3,2,1,0:T(8,128)(2,1)S(1)} collective-permute-done((bf16[2,12,48,1024]{3,2,1,0:T(8,128)(2,1)S(1)}, bf16[2,12,48,1024]{3,2,1,0:T(8,128)(2,1)S(1)}, u32[]{:S(2)}, u32[]{:S(2)}) %collective-permute-start.28) | collective-permute-done | bytes 2359328 | tf_op jit(solution)/shard_map/ppermute | solution.py:534
  167.4 1.1 collective-permute-start.29
  168.6 10.1 %collective-permute-done.30.refs_5_ = bf16[2,4,32,1024]{3,2,1,0:T(8,128)(2,1)S(1)} collective-permute-done((bf16[2,4,32,1024]{3,2,1,0:T(8,128)(2,1)S(1)}, bf16[2,4,32,1024]{3,2,1,0:T(8,128)(2,1)S(1)}, u32[]{:S(2)}, u32[]{:S(2)}) %collective-permute-start.30) | collective-permute-done | bytes 524320 | tf_op jit(solution)/shard_map/ppermute | solution.py:534
  178.7 3.9 %last_heights.2.refs_6_ = bf16[2,16,96,1024]{3,2,1,0:T(8,128)(2,1)} custom-call(s32[3]{0:T(128)S(1)} %copy-done.15, bf16[2,2,256,512]{3,2,1,0:T(8,128)(2,1)S(1)} %copy-done.10, bf16[2,12,48,1024]{3,2,1,0:T(8,128)(2,1)S(1)} %cross_transform.4.refs_10_.refs_2_, ...), custom_call_target="tpu_custom_call", output_to_operand_aliasing={{}: (6, {})} | custom-call | flops 1073741 | bytes 6291 | tf_op jit(solution)/shard_map/last_heights/pallas_call | solution.py:425
  182.5 2.5 %last_heights.3.refs_7_ = bf16[2,16,96,1024]{3,2,1,0:T(8,128)(2,1)} custom-call(s32[3]{0:T(128)S(1)} %copy-done.15, bf16[2,2,256,512]{3,2,1,0:T(8,128)(2,1)S(1)} %copy-done.10, bf16[2,12,48,1024]{3,2,1,0:T(8,128)(2,1)S(1)} %cross_transform.4.refs_10_.refs_2_, ...), custom_call_target="tpu_custom_call", output_to_operand_aliasing={{}: (6, {})} | custom-call | flops 536870 | bytes 3145 | tf_op jit(solution)/shard_map/last_heights/pallas_call | solution.py:425
  185.0 5.6 %cross_transform.7 = bf16[2,16,96,1024]{3,2,1,0:T(8,128)(2,1)} custom-call(s32[3]{0:T(128)S(1)} %copy-done.15, bf16[2,8,48,256]{3,2,1,0:T(8,128)(2,1)S(1)} %get-tuple-element.156.refs_7_.refs_1_, bf16[2,8,48,256]{3,2,1,0:T(8,128)(2,1)S(1)} %collective-permute-done.25.refs_2_, ...), custom_call_target="tpu_custom_call", output_to_operand_aliasing={{}: (7, {})} | custom-call | flops 3221225 | bytes 7340 | tf_op jit(solution)/shard_map/cross_transform/pallas_call | solution.py:498
  (72 shorter events, 3.9 us)
Async XLA Ops:
  1.1 12.9 %collective-permute-start = (bf16[2,16,8,384]{3,2,1,0:T(8,128)(2,1)S(1)}, bf16[2,16,8,384]{3,2,1,0:T(8,128)(2,1)S(1)}, u32[]{:S(2)}, u32[]{:S(2)}) collective-permute-start(bf16[2,16,8,384]{3,2,1,0:T(8,128)(2,1)S(1)} %get-tuple-element.170), channel_id=1, source_target_pairs={{0,4},{4,8},{8,12},{1,5},{5,9},{9,13},{2,6},{6,10},{10,14},{3,7},{... | collective-permute-start | bytes 589832 | tf_op jit(solution)/shard_map/ppermute | solution.py:545
  6.0 8.3 %collective-permute-start.1 = (bf16[2,16,8,384]{3,2,1,0:T(8,128)(2,1)S(1)}, bf16[2,16,8,384]{3,2,1,0:T(8,128)(2,1)S(1)}, u32[]{:S(2)}, u32[]{:S(2)}) collective-permute-start(bf16[2,16,8,384]{3,2,1,0:T(8,128)(2,1)S(1)} %get-tuple-element.169), channel_id=1, source_target_pairs={{4,0},{8,4},{12,8},{5,1},{9,5},{13,9},{6,2},{10,6},{14,10},{7,3},{... | collective-permute-start | bytes 589832 | tf_op jit(solution)/shard_map/ppermute | solution.py:546
  17.4 7.4 %collective-permute-start.2 = (bf16[2,4,256,384]{3,2,1,0:T(8,128)(2,1)}, bf16[2,4,256,384]{3,2,1,0:T(8,128)(2,1)}, u32[]{:S(2)}, u32[]{:S(2)}) collective-permute-start(bf16[2,4,256,384]{3,2,1,0:T(8,128)(2,1)} %interpolate_edges.1.refs_5_.refs_1_), channel_id=1, source_target_pairs={{0,1},{1,0},{2,3},{3,2},{4,5},{5,4},{6,7},{7,6},{8,9},{9,8},{10,11... | collective-permute-start | bytes 4718600 | tf_op jit(solution)/shard_map/ppermute | solution.py:534
  24.8 6.0 %copy-start.5 = (bf16[2,4,256,384]{3,2,1,0:T(8,128)(2,1)S(1)}, bf16[2,4,256,384]{3,2,1,0:T(8,128)(2,1)}, u32[]{:S(2)}) copy-start(bf16[2,4,256,384]{3,2,1,0:T(8,128)(2,1)} %interpolate.5.refs_7_.refs_1_) | copy-start | bytes 4718596
  24.8 13.0 %copy-start = (bf16[2,4,2,48,768]{4,3,2,1,0:T(8,128)(2,1)S(1)}, bf16[2,4,2,48,768]{4,3,2,1,0:T(8,128)(2,1)}, u32[]{:S(2)}) copy-start(bf16[2,4,2,48,768]{4,3,2,1,0:T(8,128)(2,1)} %constant.23.clone.refs_3_.refs_4_.refs_5_.refs_6_) | copy-start | bytes 3538948
  24.8 13.0 %copy-start.15 = (s32[3]{0:T(128)S(1)}, s32[3]{0:T(128)}, u32[]{:S(2)}) copy-start(s32[3]{0:T(128)} %pad_add_fusion.refs_0_) | copy-start | bytes 40
  30.8 10.6 %copy-start.2 = (bf16[8,256,384]{2,1,0:T(8,128)(2,1)S(1)}, bf16[8,256,384]{2,1,0:T(8,128)(2,1)}, u32[]{:S(2)}) copy-start(bf16[8,256,384]{2,1,0:T(8,128)(2,1)} %refs_3_.11) | copy-start | bytes 4718596
  30.8 10.6 %copy-start.6 = (s32[256,384]{1,0:T(8,128)S(1)}, s32[256,384]{1,0:T(8,128)}, u32[]{:S(2)}) copy-start(s32[256,384]{1,0:T(8,128)} %refs_1_.11) | copy-start | bytes 1179652
  30.8 10.6 %copy-start.7 = (s32[256,384]{1,0:T(8,128)S(1)}, s32[256,384]{1,0:T(8,128)}, u32[]{:S(2)}) copy-start(s32[256,384]{1,0:T(8,128)} %refs_2_.7) | copy-start | bytes 1179652
  30.8 10.6 %copy-start.9 = (bf16[2,16,16,384]{3,2,1,0:T(8,128)(2,1)S(1)}, bf16[2,16,16,384]{3,2,1,0:T(8,128)(2,1)}, u32[]{:S(2)}) copy-start(bf16[2,16,16,384]{3,2,1,0:T(8,128)(2,1)} %copy-done.8) | copy-start | bytes 1179652
  30.9 6.9 %collective-permute-start.3 = (bf16[2,4,256,384]{3,2,1,0:T(8,128)(2,1)S(1)}, bf16[2,4,256,384]{3,2,1,0:T(8,128)(2,1)S(1)}, u32[]{:S(2)}, u32[]{:S(2)}) collective-permute-start(bf16[2,4,256,384]{3,2,1,0:T(8,128)(2,1)S(1)} %copy-done.5), channel_id=1, source_target_pairs={{0,1},{1,0},{2,3},{3,2},{4,5},{5,4},{6,7},{7,6},{8,9},{9,8},{10,11... | collective-permute-start | bytes 4718600 | tf_op jit(solution)/shard_map/ppermute | solution.py:534
  31.3 22.8 %collective-permute-start.7 = (bf16[2,4,4,48,256]{4,3,2,1,0:T(8,128)(2,1)}, bf16[2,4,4,48,256]{4,3,2,1,0:T(8,128)(2,1)S(1)}, u32[]{:S(2)}, u32[]{:S(2)}) collective-permute-start(bf16[2,4,4,48,256]{4,3,2,1,0:T(8,128)(2,1)} %get-tuple-element.92.refs_2_), channel_id=1, source_target_pairs={{0,2},{2,0},{1,3},{3,1},{4,6},{6,4},{5,7},{7,5},{8,10},{10,8},{9,1... | collective-permute-start | bytes 2359304 | tf_op jit(solution)/shard_map/ppermute | solution.py:534
  32.8 16.9 %collective-permute-start.4 = (bf16[2,4,48,256]{3,2,1,0:T(8,128)(2,1)}, bf16[2,4,48,256]{3,2,1,0:T(8,128)(2,1)S(1)}, u32[]{:S(2)}, u32[]{:S(2)}) collective-permute-start(bf16[2,4,48,256]{3,2,1,0:T(8,128)(2,1)} %get-tuple-element.99), channel_id=1, source_target_pairs={{0,12},{4,8},{8,4},{12,0},{1,13},{5,9},{9,5},{13,1},{2,14},{6,10},... | collective-permute-start | bytes 589832 | tf_op jit(solution)/shard_map/ppermute | solution.py:534
  37.2 16.9 %collective-permute-start.5 = (bf16[2,4,48,256]{3,2,1,0:T(8,128)(2,1)}, bf16[2,4,48,256]{3,2,1,0:T(8,128)(2,1)S(1)}, u32[]{:S(2)}, u32[]{:S(2)}) collective-permute-start(bf16[2,4,48,256]{3,2,1,0:T(8,128)(2,1)} %get-tuple-element.100), channel_id=1, source_target_pairs={{0,8},{4,12},{8,0},{12,4},{1,9},{5,13},{9,1},{13,5},{2,10},{6,14},... | collective-permute-start | bytes 589832 | tf_op jit(solution)/shard_map/ppermute | solution.py:534
  37.2 16.9 %collective-permute-start.6 = (bf16[2,4,48,256]{3,2,1,0:T(8,128)(2,1)}, bf16[2,4,48,256]{3,2,1,0:T(8,128)(2,1)S(1)}, u32[]{:S(2)}, u32[]{:S(2)}) collective-permute-start(bf16[2,4,48,256]{3,2,1,0:T(8,128)(2,1)} %get-tuple-element.101), channel_id=1, source_target_pairs={{0,4},{4,0},{8,12},{12,8},{1,5},{5,1},{9,13},{13,9},{2,6},{6,2},{1... | collective-permute-start | bytes 589832 | tf_op jit(solution)/shard_map/ppermute | solution.py:534
  37.8 25.0 %slice-start = ((s8[6291456]{0:T(1024)(128)(4,1)}), s8[4194304]{0:T(1024)(128)(4,1)S(1)}, s32[]{:S(2)}) async-start(s8[6291456]{0:T(1024)(128)(4,1)} %bitcast.3), calls=%async_computation | async-start | bytes 8388608
  41.5 2.8 %copy-start.1 = (bf16[2,16,256,384]{3,2,1,0:T(8,128)(2,1)S(1)}, bf16[2,16,256,384]{3,2,1,0:T(8,128)(2,1)}, u32[]{:S(2)}) copy-start(bf16[2,16,256,384]{3,2,1,0:T(8,128)(2,1)} %refs_0_.7) | copy-start | bytes 18874372
  44.2 18.5 %slice-start.1 = ((s8[6291456]{0:T(1024)(128)(4,1)}), s8[2097152]{0:T(1024)(128)(4,1)S(1)}, s32[]{:S(2)}) async-start(s8[6291456]{0:T(1024)(128)(4,1)} %bitcast.3), calls=%async_computation.1 | async-start | bytes 4194304
  54.1 5.0 %collective-permute-start.8 = (bf16[2,4,256,384]{3,2,1,0:T(8,128)(2,1)S(1)}, bf16[2,4,256,384]{3,2,1,0:T(8,128)(2,1)S(1)}, u32[]{:S(2)}, u32[]{:S(2)}) collective-permute-start(bf16[2,4,256,384]{3,2,1,0:T(8,128)(2,1)S(1)} %interpolate.6.refs_1_.refs_7_), channel_id=1, source_target_pairs={{0,1},{1,0},{2,3},{3,2},{4,5},{5,4},{6,7},{7,6},{8,9},{9,8},{10,11... | collective-permute-start | bytes 4718600 | tf_op jit(solution)/shard_map/ppermute | solution.py:534
  54.1 19.9 %collective-permute-start.12 = (bf16[2,4,4,48,256]{4,3,2,1,0:T(8,128)(2,1)S(1)}, bf16[2,4,4,48,256]{4,3,2,1,0:T(8,128)(2,1)S(1)}, u32[]{:S(2)}, u32[]{:S(2)}) collective-permute-start(bf16[2,4,4,48,256]{4,3,2,1,0:T(8,128)(2,1)S(1)} %get-tuple-element.102.refs_5_.refs_3_), channel_id=1, source_target_pairs={{0,2},{2,0},{1,3},{3,1},{4,6},{6,4},{5,7},{7,5},{8,10},{10,8},{9,1... | collective-permute-start | bytes 2359304 | tf_op jit(solution)/shard_map/ppermute | solution.py:534
  54.7 13.5 %collective-permute-start.9 = (bf16[2,4,48,256]{3,2,1,0:T(8,128)(2,1)S(1)}, bf16[2,4,48,256]{3,2,1,0:T(8,128)(2,1)S(1)}, u32[]{:S(2)}, u32[]{:S(2)}) collective-permute-start(bf16[2,4,48,256]{3,2,1,0:T(8,128)(2,1)S(1)} %get-tuple-element.109), channel_id=1, source_target_pairs={{0,12},{4,8},{8,4},{12,0},{1,13},{5,9},{9,5},{13,1},{2,14},{6,10},... | collective-permute-start | bytes 589832 | tf_op jit(solution)/shard_map/ppermute | solution.py:534
  57.4 16.7 %collective-permute-start.10 = (bf16[2,4,48,256]{3,2,1,0:T(8,128)(2,1)S(1)}, bf16[2,4,48,256]{3,2,1,0:T(8,128)(2,1)S(1)}, u32[]{:S(2)}, u32[]{:S(2)}) collective-permute-start(bf16[2,4,48,256]{3,2,1,0:T(8,128)(2,1)S(1)} %get-tuple-element.110), channel_id=1, source_target_pairs={{0,8},{4,12},{8,0},{12,4},{1,9},{5,13},{9,1},{13,5},{2,10},{6,14},... | collective-permute-start | bytes 589832 | tf_op jit(solution)/shard_map/ppermute | solution.py:534
  57.4 16.7 %collective-permute-start.11 = (bf16[2,4,48,256]{3,2,1,0:T(8,128)(2,1)S(1)}, bf16[2,4,48,256]{3,2,1,0:T(8,128)(2,1)S(1)}, u32[]{:S(2)}, u32[]{:S(2)}) collective-permute-start(bf16[2,4,48,256]{3,2,1,0:T(8,128)(2,1)S(1)} %get-tuple-element.111), channel_id=1, source_target_pairs={{0,4},{4,0},{8,12},{12,8},{1,5},{5,1},{9,13},{13,9},{2,6},{6,2},{1... | collective-permute-start | bytes 589832 | tf_op jit(solution)/shard_map/ppermute | solution.py:534
  74.1 25.6 %copy-start.3 = (bf16[1024,1024]{1,0:T(8,128)(2,1)S(1)}, bf16[1024,1024]{1,0:T(8,128)(2,1)}, u32[]{:S(2)}) copy-start(bf16[1024,1024]{1,0:T(8,128)(2,1)} %constant.25.clone.refs_14_.refs_6_) | copy-start | bytes 6291460
  74.1 25.6 %copy-start.4 = (bf16[1024,1024]{1,0:T(8,128)(2,1)S(1)}, bf16[1024,1024]{1,0:T(8,128)(2,1)}, u32[]{:S(2)}) copy-start(bf16[1024,1024]{1,0:T(8,128)(2,1)} %constant.24.clone.refs_13_.refs_5_) | copy-start | bytes 6291460
  74.1 25.6 %copy-start.14 = (bf16[2,4,48,256]{3,2,1,0:T(8,128)(2,1)S(1)}, bf16[2,4,48,256]{3,2,1,0:T(8,128)(2,1)}, u32[]{:S(2)}) copy-start(bf16[2,4,48,256]{3,2,1,0:T(8,128)(2,1)} %get-tuple-element.126.refs_1_) | copy-start | bytes 589828
  74.1 5.7 %collective-permute-start.13 = (bf16[2,4,256,384]{3,2,1,0:T(8,128)(2,1)S(1)}, bf16[2,4,256,384]{3,2,1,0:T(8,128)(2,1)S(1)}, u32[]{:S(2)}, u32[]{:S(2)}) collective-permute-start(bf16[2,4,256,384]{3,2,1,0:T(8,128)(2,1)S(1)} %interpolate.7.refs_1_.refs_7_), channel_id=1, source_target_pairs={{0,1},{1,0},{2,3},{3,2},{4,5},{5,4},{6,7},{7,6},{8,9},{9,8},{10,11... | collective-permute-start | bytes 4718600 | tf_op jit(solution)/shard_map/ppermute | solution.py:534
  74.2 20.0 %collective-permute-start.17 = (bf16[2,4,4,48,256]{4,3,2,1,0:T(8,128)(2,1)S(1)}, bf16[2,4,4,48,256]{4,3,2,1,0:T(8,128)(2,1)S(1)}, u32[]{:S(2)}, u32[]{:S(2)}) collective-permute-start(bf16[2,4,4,48,256]{4,3,2,1,0:T(8,128)(2,1)S(1)} %get-tuple-element.112.refs_5_.refs_4_), channel_id=1, source_target_pairs={{0,2},{2,0},{1,3},{3,1},{4,6},{6,4},{5,7},{7,5},{8,10},{10,8},{9,1... | collective-permute-start | bytes 2359304 | tf_op jit(solution)/shard_map/ppermute | solution.py:534
  75.4 9.7 %collective-permute-start.14 = (bf16[2,4,48,256]{3,2,1,0:T(8,128)(2,1)S(1)}, bf16[2,4,48,256]{3,2,1,0:T(8,128)(2,1)S(1)}, u32[]{:S(2)}, u32[]{:S(2)}) collective-permute-start(bf16[2,4,48,256]{3,2,1,0:T(8,128)(2,1)S(1)} %get-tuple-element.119), channel_id=1, source_target_pairs={{0,12},{4,8},{8,4},{12,0},{1,13},{5,9},{9,5},{13,1},{2,14},{6,10},... | collective-permute-start | bytes 589832 | tf_op jit(solution)/shard_map/ppermute | solution.py:534
  77.4 16.6 %collective-permute-start.15 = (bf16[2,4,48,256]{3,2,1,0:T(8,128)(2,1)S(1)}, bf16[2,4,48,256]{3,2,1,0:T(8,128)(2,1)S(1)}, u32[]{:S(2)}, u32[]{:S(2)}) collective-permute-start(bf16[2,4,48,256]{3,2,1,0:T(8,128)(2,1)S(1)} %get-tuple-element.120), channel_id=1, source_target_pairs={{0,8},{4,12},{8,0},{12,4},{1,9},{5,13},{9,1},{13,5},{2,10},{6,14},... | collective-permute-start | bytes 589832 | tf_op jit(solution)/shard_map/ppermute | solution.py:534
  77.4 16.6 %collective-permute-start.16 = (bf16[2,4,48,256]{3,2,1,0:T(8,128)(2,1)S(1)}, bf16[2,4,48,256]{3,2,1,0:T(8,128)(2,1)S(1)}, u32[]{:S(2)}, u32[]{:S(2)}) collective-permute-start(bf16[2,4,48,256]{3,2,1,0:T(8,128)(2,1)S(1)} %get-tuple-element.121), channel_id=1, source_target_pairs={{0,4},{4,0},{8,12},{12,8},{1,5},{5,1},{9,13},{13,9},{2,6},{6,2},{1... | collective-permute-start | bytes 589832 | tf_op jit(solution)/shard_map/ppermute | solution.py:534
  94.2 20.2 %copy-start.11 = (bf16[2,4,4,48,256]{4,3,2,1,0:T(8,128)(2,1)S(1)}, bf16[2,4,4,48,256]{4,3,2,1,0:T(8,128)(2,1)}, u32[]{:S(2)}) copy-start(bf16[2,4,4,48,256]{4,3,2,1,0:T(8,128)(2,1)} %get-tuple-element.92.refs_2_) | copy-start | bytes 2359300
  94.2 20.2 %copy-start.13 = (bf16[2,2,128,512]{3,2,1,0:T(8,128)(2,1)S(1)}, bf16[2,2,128,512]{3,2,1,0:T(8,128)(2,1)}, u32[]{:S(2)}) copy-start(bf16[2,2,128,512]{3,2,1,0:T(8,128)(2,1)} %constant.27.clone.refs_1_) | copy-start | bytes 1572868
  94.2 19.1 %collective-permute-start.21 = (bf16[2,4,4,48,256]{4,3,2,1,0:T(8,128)(2,1)S(1)}, bf16[2,4,4,48,256]{4,3,2,1,0:T(8,128)(2,1)S(1)}, u32[]{:S(2)}, u32[]{:S(2)}) collective-permute-start(bf16[2,4,4,48,256]{4,3,2,1,0:T(8,128)(2,1)S(1)} %get-tuple-element.122.refs_15_.refs_5_), channel_id=1, source_target_pairs={{0,2},{2,0},{1,3},{3,1},{4,6},{6,4},{5,7},{7,5},{8,10},{10,8},{9,1... | collective-permute-start | bytes 2359304 | tf_op jit(solution)/shard_map/ppermute | solution.py:534
  95.3 11.0 %collective-permute-start.18 = (bf16[2,4,48,256]{3,2,1,0:T(8,128)(2,1)S(1)}, bf16[2,4,48,256]{3,2,1,0:T(8,128)(2,1)S(1)}, u32[]{:S(2)}, u32[]{:S(2)}) collective-permute-start(bf16[2,4,48,256]{3,2,1,0:T(8,128)(2,1)S(1)} %get-tuple-element.138), channel_id=1, source_target_pairs={{0,12},{4,8},{8,4},{12,0},{1,13},{5,9},{9,5},{13,1},{2,14},{6,10},... | collective-permute-start | bytes 589832 | tf_op jit(solution)/shard_map/ppermute | solution.py:534
  97.3 15.8 %collective-permute-start.19 = (bf16[2,4,48,256]{3,2,1,0:T(8,128)(2,1)S(1)}, bf16[2,4,48,256]{3,2,1,0:T(8,128)(2,1)S(1)}, u32[]{:S(2)}, u32[]{:S(2)}) collective-permute-start(bf16[2,4,48,256]{3,2,1,0:T(8,128)(2,1)S(1)} %get-tuple-element.139), channel_id=1, source_target_pairs={{0,8},{4,12},{8,0},{12,4},{1,9},{5,13},{9,1},{13,5},{2,10},{6,14},... | collective-permute-start | bytes 589832 | tf_op jit(solution)/shard_map/ppermute | solution.py:534
  97.3 15.8 %collective-permute-start.20 = (bf16[2,4,48,256]{3,2,1,0:T(8,128)(2,1)S(1)}, bf16[2,4,48,256]{3,2,1,0:T(8,128)(2,1)S(1)}, u32[]{:S(2)}, u32[]{:S(2)}) collective-permute-start(bf16[2,4,48,256]{3,2,1,0:T(8,128)(2,1)S(1)} %get-tuple-element.140), channel_id=1, source_target_pairs={{0,4},{4,0},{8,12},{12,8},{1,5},{5,1},{9,13},{13,9},{2,6},{6,2},{1... | collective-permute-start | bytes 589832 | tf_op jit(solution)/shard_map/ppermute | solution.py:534
  106.3 15.2 %copy-start.12 = (bf16[2,2,128,512]{3,2,1,0:T(8,128)(2,1)S(1)}, bf16[2,2,128,512]{3,2,1,0:T(8,128)(2,1)}, u32[]{:S(2)}) copy-start(bf16[2,2,128,512]{3,2,1,0:T(8,128)(2,1)} %constant.28.clone.refs_1_) | copy-start | bytes 1572868
  113.3 54.2 %collective-permute-start.28 = (bf16[2,12,48,1024]{3,2,1,0:T(8,128)(2,1)S(1)}, bf16[2,12,48,1024]{3,2,1,0:T(8,128)(2,1)S(1)}, u32[]{:S(2)}, u32[]{:S(2)}) collective-permute-start(bf16[2,12,48,1024]{3,2,1,0:T(8,128)(2,1)S(1)} %cross_transform.4.refs_10_.refs_2_), channel_id=1, source_target_pairs={{0,2},{2,0},{1,3},{3,1},{4,6},{6,4},{5,7},{7,5},{8,10},{10,8},{9,1... | collective-permute-start | bytes 7077896 | tf_op jit(solution)/shard_map/ppermute | solution.py:534
  117.0 16.6 %collective-permute-start.24 = (bf16[2,8,48,256]{3,2,1,0:T(8,128)(2,1)S(1)}, bf16[2,8,48,256]{3,2,1,0:T(8,128)(2,1)S(1)}, u32[]{:S(2)}, u32[]{:S(2)}) collective-permute-start(bf16[2,8,48,256]{3,2,1,0:T(8,128)(2,1)S(1)} %get-tuple-element.144), channel_id=1, source_target_pairs={{0,4},{4,0},{8,12},{12,8},{1,5},{5,1},{9,13},{13,9},{2,6},{6,2},{1... | collective-permute-start | bytes 1179656 | tf_op jit(solution)/shard_map/ppermute | solution.py:534
  117.1 29.9 %collective-permute-start.23 = (bf16[2,8,48,256]{3,2,1,0:T(8,128)(2,1)S(1)}, bf16[2,8,48,256]{3,2,1,0:T(8,128)(2,1)S(1)}, u32[]{:S(2)}, u32[]{:S(2)}) collective-permute-start(bf16[2,8,48,256]{3,2,1,0:T(8,128)(2,1)S(1)} %get-tuple-element.145), channel_id=1, source_target_pairs={{0,8},{4,12},{8,0},{12,4},{1,9},{5,13},{9,1},{13,5},{2,10},{6,14},... | collective-permute-start | bytes 1179656 | tf_op jit(solution)/shard_map/ppermute | solution.py:534
  119.7 27.3 %collective-permute-start.22 = (bf16[2,8,48,256]{3,2,1,0:T(8,128)(2,1)S(1)}, bf16[2,8,48,256]{3,2,1,0:T(8,128)(2,1)S(1)}, u32[]{:S(2)}, u32[]{:S(2)}) collective-permute-start(bf16[2,8,48,256]{3,2,1,0:T(8,128)(2,1)S(1)} %get-tuple-element.146), channel_id=1, source_target_pairs={{0,12},{4,8},{8,4},{12,0},{1,13},{5,9},{9,5},{13,1},{2,14},{6,10},... | collective-permute-start | bytes 1179656 | tf_op jit(solution)/shard_map/ppermute | solution.py:534
  127.3 51.4 %collective-permute-start.30 = (bf16[2,4,32,1024]{3,2,1,0:T(8,128)(2,1)S(1)}, bf16[2,4,32,1024]{3,2,1,0:T(8,128)(2,1)S(1)}, u32[]{:S(2)}, u32[]{:S(2)}) collective-permute-start(bf16[2,4,32,1024]{3,2,1,0:T(8,128)(2,1)S(1)} %get-tuple-element.164.refs_7_.refs_3_), channel_id=1, source_target_pairs={{0,2},{2,0},{1,3},{3,1},{4,6},{6,4},{5,7},{7,5},{8,10},{10,8},{9,1... | collective-permute-start | bytes 1572872 | tf_op jit(solution)/shard_map/ppermute | solution.py:534
  147.0 31.7 %copy-start.10 = (bf16[2,2,256,512]{3,2,1,0:T(8,128)(2,1)S(1)}, bf16[2,2,256,512]{3,2,1,0:T(8,128)(2,1)}, u32[]{:S(2)}) copy-start(bf16[2,2,256,512]{3,2,1,0:T(8,128)(2,1)} %constant.26.clone.refs_1_) | copy-start | bytes 3145732
  147.0 38.0 %collective-permute-start.25 = (bf16[2,8,48,256]{3,2,1,0:T(8,128)(2,1)S(1)}, bf16[2,8,48,256]{3,2,1,0:T(8,128)(2,1)S(1)}, u32[]{:S(2)}, u32[]{:S(2)}) collective-permute-start(bf16[2,8,48,256]{3,2,1,0:T(8,128)(2,1)S(1)} %get-tuple-element.157), channel_id=1, source_target_pairs={{0,4},{4,0},{8,12},{12,8},{1,5},{5,1},{9,13},{13,9},{2,6},{6,2},{1... | collective-permute-start | bytes 1179656 | tf_op jit(solution)/shard_map/ppermute | solution.py:534
  153.4 31.6 %collective-permute-start.26 = (bf16[2,8,48,256]{3,2,1,0:T(8,128)(2,1)S(1)}, bf16[2,8,48,256]{3,2,1,0:T(8,128)(2,1)S(1)}, u32[]{:S(2)}, u32[]{:S(2)}) collective-permute-start(bf16[2,8,48,256]{3,2,1,0:T(8,128)(2,1)S(1)} %get-tuple-element.158), channel_id=1, source_target_pairs={{0,8},{4,12},{8,0},{12,4},{1,9},{5,13},{9,1},{13,5},{2,10},{6,14},... | collective-permute-start | bytes 1179656 | tf_op jit(solution)/shard_map/ppermute | solution.py:534
  154.3 30.7 %collective-permute-start.27 = (bf16[2,8,48,256]{3,2,1,0:T(8,128)(2,1)S(1)}, bf16[2,8,48,256]{3,2,1,0:T(8,128)(2,1)S(1)}, u32[]{:S(2)}, u32[]{:S(2)}) collective-permute-start(bf16[2,8,48,256]{3,2,1,0:T(8,128)(2,1)S(1)} %get-tuple-element.159), channel_id=1, source_target_pairs={{0,12},{4,8},{8,4},{12,0},{1,13},{5,9},{9,5},{13,1},{2,14},{6,10},... | collective-permute-start | bytes 1179656 | tf_op jit(solution)/shard_map/ppermute | solution.py:534
  167.4 15.1 %collective-permute-start.29 = (bf16[2,4,16,1024]{3,2,1,0:T(8,128)(2,1)S(1)}, bf16[2,4,16,1024]{3,2,1,0:T(8,128)(2,1)S(1)}, u32[]{:S(2)}, u32[]{:S(2)}) collective-permute-start(bf16[2,4,16,1024]{3,2,1,0:T(8,128)(2,1)S(1)} %get-tuple-element.166.refs_3_), channel_id=1, source_target_pairs={{0,2},{2,0},{1,3},{3,1},{4,6},{6,4},{5,7},{7,5},{8,10},{10,8},{9,1... | collective-permute-start | bytes 786440 | tf_op jit(solution)/shard_map/ppermute | solution.py:534
  (1 other events, 0.8 us)
